TPU v7x, 512 devices: a whole 4x8x8 slice. The times are simulated.
512 devices in a mesh: filt: 16 (over y, z_lo), space: 32 (over x, z_hi, core).
Axes of the slice: x: 4, y: 8, z: 8 (z_hi: 4, z_lo: 2; z = z_hi * 2 + z_lo), core: 2. Of those that a mesh axis runs over, the one named last changes fastest.
Arguments:
- activations: bfloat16 [128, 256, 8, 128], P('filt', 'space'), may hold values from -6 to 6
- cotangent: bfloat16 [128, 256, 8, 128], P('filt', 'space'), may hold values from -6 to 6
- filters: bfloat16 [27, 128, 128], P(None, 'filt'), may hold values from -0.109375 to 0.109375
- bias_terms: bfloat16 [128], P('filt'), may hold values from -3 to 3
Outputs:
- features_out: float32 [128, 256, 8, 128], P('filt', 'space')
- filter_grad: float32 [27, 128, 128], P(None, 'filt', 'space')
All inputs are finite; a program needn't handle non-finite values.
Results may differ from a plain program's by a relative error of at most 0.0003.
Values may be sent and summed in bfloat16 or wider, within the bound.
No kernel may reach another device: no remote copies, remote signals or barrier semaphores. Data moves between devices by JAX's collectives and lax.ppermute only.
A program may use at most 128 MiB of HBM per device.

v0:
```python
import math

import jax
import jax.numpy as jnp
from jax import lax
from jax.sharding import PartitionSpec as P


def padded_2(block, sides, width):
    for axis, dim in sides:
        count = lax.axis_size(axis)
        forward = [(i, i + 1) for i in range(count - 1)]
        backward = [(target, source) for source, target in forward]
        low = lax.ppermute(
            lax.slice_in_dim(block, block.shape[dim] - width, None, axis=dim), axis, forward
        )
        high = lax.ppermute(lax.slice_in_dim(block, 0, width, axis=dim), axis, backward)
        block = jnp.concatenate([low, block, high], axis=dim)
    return block


def tap_offsets(tap_index):
    return (tap_index // 9, tap_index // 3 % 3, tap_index % 3)


def on_device(activations, cotangent, filters, bias_terms):
    block_in, row_count, depth, width = activations.shape
    block_out = filters.shape[1]
    chan_in = filters.shape[2]
    taps = filters.shape[0]
    space_size = lax.axis_size("space")
    scale = jnp.float32(1.0 / math.sqrt(row_count * space_size * depth * width))
    all_chan = lax.all_gather(activations, "filt", axis=0, tiled=True)
    gathered = padded_2(all_chan, (("space", 1),), 1)
    padded = jnp.pad(gathered, ((0, 0), (0, 0), (1, 1), (1, 1)))
    flat_in = padded.reshape(chan_in, -1)
    embeds = []
    for tap_index in range(taps):
        off_x, off_z, off_y = tap_offsets(tap_index)
        embeds.append(
            jnp.pad(cotangent, ((0, 0), (off_x, 2 - off_x), (off_z, 2 - off_z), (off_y, 2 - off_y)))
        )
    embed_mat = jnp.stack(embeds).reshape(taps * block_out, -1)
    partial_value = lax.dot_general(
        embed_mat, flat_in, (((1,), (1,)), ((), ())), preferred_element_type=jnp.float32
    )
    partial_value = partial_value.reshape(taps, block_out, chan_in)
    filter_grad = lax.psum_scatter(partial_value, "space", scatter_dimension=2, tiled=True) * scale
    tap_mat = jnp.dot(
        filters.reshape(taps * block_out, chan_in), flat_in, preferred_element_type=jnp.float32
    )
    tap_mat = tap_mat.reshape(taps, block_out, row_count + 2, depth + 2, width + 2)
    summed = jnp.zeros((block_out, row_count, depth, width), jnp.float32)
    for tap_index in range(taps):
        off_x, off_z, off_y = tap_offsets(tap_index)
        summed = (
            summed
            + tap_mat[
                tap_index,
                :,
                off_x : off_x + row_count,
                off_z : off_z + depth,
                off_y : off_y + width,
            ]
        )
    features_out = summed + bias_terms.astype(jnp.float32)[:, None, None, None]
    return (features_out, filter_grad)


def solution(mesh):
    in_specs = (
        P("filt", "space", None, None),
        P("filt", "space", None, None),
        P(None, "filt", None),
        P("filt"),
    )
    out_specs = (P("filt", "space", None, None), P(None, "filt", "space"))
    return jax.shard_map(
        on_device, mesh=mesh, in_specs=in_specs, out_specs=out_specs, check_vma=False
    )
```

profile of v0, /device:TPU:1, one launch (start us, length us, event | category | flops | bytes accessed | tf_op | source)
XLA Modules:
  0.0 228.8 jit_solution(14467310693240159837)
XLA Ops:
  7.2 0.0 copy-start
  7.2 0.0 copy-start.3
  7.2 0.0 all-gather.2.cloned.1.call-start
  7.2 0.7 all-gather.2.cloned.1.call-update
  7.9 0.0 reduce-scatter.2.cloned.1.call-start
  8.0 1.0 copy.67
  9.0 0.8 bitcast_dynamic-update-slice_fusion.26
  9.8 0.9 bitcast_dynamic-update-slice_fusion.25
  10.7 0.9 bitcast_dynamic-update-slice_fusion.24
  11.6 0.8 bitcast_dynamic-update-slice_fusion.23
  12.4 0.9 bitcast_dynamic-update-slice_fusion.22
  13.4 0.9 bitcast_dynamic-update-slice_fusion.21
  14.3 0.8 bitcast_dynamic-update-slice_fusion.20
  15.1 0.9 bitcast_dynamic-update-slice_fusion.19
  16.1 0.9 bitcast_dynamic-update-slice_fusion.18
  17.0 0.8 bitcast_dynamic-update-slice_fusion.17
  17.8 0.9 bitcast_dynamic-update-slice_fusion.16
  18.7 0.9 bitcast_dynamic-update-slice_fusion.15
  19.6 0.8 bitcast_dynamic-update-slice_fusion.14
  20.4 0.9 bitcast_dynamic-update-slice_fusion.13
  21.4 0.9 bitcast_dynamic-update-slice_fusion.12
  22.3 0.8 bitcast_dynamic-update-slice_fusion.11
  23.1 0.9 bitcast_dynamic-update-slice_fusion.10
  24.0 0.9 bitcast_dynamic-update-slice_fusion.9
  24.9 0.8 bitcast_dynamic-update-slice_fusion.8
  25.7 0.9 bitcast_dynamic-update-slice_fusion.7
  26.7 0.9 bitcast_dynamic-update-slice_fusion.6
  27.6 0.8 bitcast_dynamic-update-slice_fusion.5
  28.4 0.9 bitcast_dynamic-update-slice_fusion.4
  29.3 0.9 bitcast_dynamic-update-slice_fusion.3
  30.2 51.9 %all-gather.2.cloned.1.call-done = bf16[128,8,8,128]{3,2,1,0:T(8,128)(2,1)} async-done(((bf16[8,8,8,128]{3,2,1,0:T(8,128)(2,1)}), bf16[128,8,8,128]{3,2,1,0:T(8,128)(2,1)}) %all-gather.2.cloned.1.call-update) | async-done | bytes 2097168 | tf_op jit(solution)/shard_map/all_gather | solution.py:33
  82.2 3.3 %copy.64 = bf16[128,8,8,128]{0,3,2,1:T(8,128)(2,1)S(1)} copy(bf16[128,8,8,128]{3,2,1,0:T(8,128)(2,1)} %all-gather.2.cloned.1.call-done) | data formatting | bytes 4194304 | tf_op jit(solution)/shard_map/all_gather | solution.py:33
  85.5 0.0 copy-start.2
  85.5 14.6 %collective-permute-start = (bf16[128,1,8,128]{0,3,2,1:T(8,128)(2,1)S(1)}, bf16[128,1,8,128]{0,3,2,1:T(8,128)(2,1)S(1)}, u32[]{:S(2)}, u32[]{:S(2)}) collective-permute-start(bf16[128,1,8,128]{0,3,2,1:T(8,128)(2,1)S(1)} %get-tuple-element.8), channel_id=1, source_target_pairs={{0,1},{1,2},{2,3},{3,4},{4,5},{5,6},{6,7},{7,8},{8,9},{9,10},{10,1... | collective-permute-start | bytes 786440 | tf_op jit(solution)/shard_map/ppermute | solution.py:14
  100.1 2.1 collective-permute-start.1
  102.2 0.8 bitcast_dynamic-update-slice_fusion.2
  103.0 0.0 copy-done.3
  103.0 0.9 bitcast_dynamic-update-slice_fusion.1
  104.0 0.9 bitcast_dynamic-update-slice_fusion
  104.9 1.2 collective-permute-done
  106.1 0.0 copy-done.2
  106.1 5.2 %collective-permute-done.1 = bf16[128,1,8,128]{0,3,2,1:T(8,128)(2,1)S(1)} collective-permute-done((bf16[128,1,8,128]{0,3,2,1:T(8,128)(2,1)S(1)}, bf16[128,1,8,128]{0,3,2,1:T(8,128)(2,1)S(1)}, u32[]{:S(2)}, u32[]{:S(2)}) %collective-permute-start.1) | collective-permute-done | bytes 262176 | tf_op jit(solution)/shard_map/ppermute | solution.py:17
  111.4 4.3 %select_maximum_fusion = bf16[128,10,10,130]{0,3,2,1:T(8,128)(2,1)S(1)} fusion(bf16[128,1,8,128]{0,3,2,1:T(8,128)(2,1)S(1)} %collective-permute-done.1, bf16[128,8,8,128]{0,3,2,1:T(8,128)(2,1)} %copy-done.2, bf16[128,1,8,128]{0,3,2,1:T(8,128)(2,1)S(1)} %collective-permute-done), kind=kLoop, calls=%fused_computation.8 | loop fusion | flops 31616000 | bytes 5949440 | tf_op jit(solution)/shard_map/concatenate | solution.py:18
  115.6 3.1 %reshape.22 = bf16[128,13000]{0,1:T(8,128)(2,1)} reshape(bf16[128,10,10,130]{0,3,2,1:T(8,128)(2,1)S(1)} %select_maximum_fusion) | data formatting | bytes 6656000 | tf_op jit(solution)/shard_map/reshape | solution.py:36
  118.8 8.4 %fusion.8 = f32[27,8,128]{2,1,0:T(8,128)} fusion(bf16[27,8,10,10,130]{4,1,3,0,2:T(8,128)(2,1)} %bitcast_dynamic-update-slice_fusion, bf16[128,10,10,130]{0,3,2,1:T(8,128)(2,1)S(1)} %select_maximum_fusion), kind=kOutput, calls=%fused_computation.15 | convolution fusion | flops 718848000 | bytes 9054592 | tf_op jit(solution)/shard_map/dot_general | solution.py:44
  127.2 1.9 copy.94
  129.1 0.0 reduce-scatter.2.cloned.1.call-update
  129.1 0.0 copy-done
  129.1 8.2 %convolution_bitcast_fusion = f32[216,13000]{1,0:T(8,128)} fusion(bf16[128,13000]{0,1:T(8,128)(2,1)} %reshape.22, bf16[27,8,128]{2,1,0:T(8,128)(2,1)S(1)} %copy-done), kind=kOutput, calls=%fused_computation | convolution fusion | flops 718848000 | bytes 14615296 | tf_op jit(solution)/shard_map/dot_general | solution.py:49
  137.4 0.0 copy-start.1
  137.4 23.9 %reshape.24 = f32[27,8,10,10,130]{4,3,2,1,0:T(8,128)} reshape(f32[216,13000]{1,0:T(8,128)} %convolution_bitcast_fusion) | data formatting | bytes 22464000 | tf_op jit(solution)/shard_map/reshape | solution.py:52
  161.3 8.9 %fusion.12 = f32[8,8,8,128]{3,2,1,0:T(8,128)} fusion(f32[27,8,10,10,130]{4,3,2,1,0:T(8,128)} %reshape.24, f32[8]{0:T(128)S(1)} %convert_element_type.59), kind=kLoop, calls=%fused_computation.45 | loop fusion | flops 1769472 | bytes 7340064 | tf_op jit(solution)/shard_map/add | solution.py:66
  170.2 50.4 %reduce-scatter.2.cloned.1.call-done = f32[27,8,4]{0,1,2:T(8,128)} async-done(((f32[27,8,128]{0,1,2:T(8,128)}), f32[27,8,4]{0,1,2:T(8,128)}) %reduce-scatter.2.cloned.1.call-update) | async-done | bytes 3472 | tf_op jit(solution)/shard_map/reduce_scatter | solution.py:48
  220.6 0.7 broadcast_multiply_fusion
  221.3 0.6 copy.95
  221.9 0.0 copy-done.1
  (2 shorter events, 0.0 us)
Async XLA Ops:
  7.2 122.0 %copy-start = (bf16[27,8,128]{2,1,0:T(8,128)(2,1)S(1)}, bf16[27,8,128]{2,1,0:T(8,128)(2,1)}, u32[]{:S(2)}) copy-start(bf16[27,8,128]{2,1,0:T(8,128)(2,1)} %param.6) | copy-start | bytes 165892
  7.2 95.8 %copy-start.3 = (bf16[8]{0:T(256)(128)(2,1)S(1)}, bf16[8]{0:T(256)(128)(2,1)}, u32[]{:S(2)}) copy-start(bf16[8]{0:T(256)(128)(2,1)} %param.7) | copy-start | bytes 52
  7.2 75.0 %all-gather.2.cloned.1.call-start = ((), (), s32[]{:S(2)}) async-start(), calls=%async_computation.1 | async-start | bytes 2228224 | tf_op jit(solution)/shard_map/all_gather | solution.py:33
  7.9 212.7 %reduce-scatter.2.cloned.1.call-start = ((), (), s32[]{:S(2)}) async-start(), calls=%async_computation.2 | async-start | bytes 540672 | tf_op jit(solution)/shard_map/reduce_scatter | solution.py:48
  85.5 20.6 %copy-start.2 = (bf16[128,8,8,128]{0,3,2,1:T(8,128)(2,1)}, bf16[128,8,8,128]{0,3,2,1:T(8,128)(2,1)S(1)}, u32[]{:S(2)}) copy-start(bf16[128,8,8,128]{0,3,2,1:T(8,128)(2,1)S(1)} %copy.64) | copy-start | bytes 6291460
  85.5 20.6 %collective-permute-start = (bf16[128,1,8,128]{0,3,2,1:T(8,128)(2,1)S(1)}, bf16[128,1,8,128]{0,3,2,1:T(8,128)(2,1)S(1)}, u32[]{:S(2)}, u32[]{:S(2)}) collective-permute-start(bf16[128,1,8,128]{0,3,2,1:T(8,128)(2,1)S(1)} %get-tuple-element.8), channel_id=1, source_target_pairs={{0,1},{1,2},{2,3},{3,4},{4,5},{5,6},{6,7},{7,8},{8,9},{9,10},{10,1... | collective-permute-start | bytes 786440 | tf_op jit(solution)/shard_map/ppermute | solution.py:14
  100.1 11.2 %collective-permute-start.1 = (bf16[128,1,8,128]{0,3,2,1:T(8,128)(2,1)S(1)}, bf16[128,1,8,128]{0,3,2,1:T(8,128)(2,1)S(1)}, u32[]{:S(2)}, u32[]{:S(2)}) collective-permute-start(bf16[128,1,8,128]{0,3,2,1:T(8,128)(2,1)S(1)} %get-tuple-element.9), channel_id=1, source_target_pairs={{1,0},{2,1},{3,2},{4,3},{5,4},{6,5},{7,6},{8,7},{9,8},{10,9},{11,1... | collective-permute-start | bytes 786440 | tf_op jit(solution)/shard_map/ppermute | solution.py:17
  137.4 84.5 %copy-start.1 = (bf16[27,8,128]{2,1,0:T(8,128)(2,1)S(1)}, bf16[27,8,128]{2,1,0:T(8,128)(2,1)}, u32[]{:S(2)}) copy-start(bf16[27,8,128]{2,1,0:T(8,128)(2,1)} %param.6) | copy-start | bytes 165892
Sparse Core Ops, SparseCore 0:
  10.1 72.0 all-gather.1
  129.3 91.2 reduce-scatter.1
where the time goes:
time: 231 us; the launch traced here: 229 us
  waiting for transfers between devices  110 us (48%)
  local copies, waits for them, and re-layouts  57.9 us (25%)
  starting transfers between devices  16.7 us (7%)
  matrix products  16.7 us (7%)
  between operations  14.1 us (6%)
  other arithmetic  13.8 us (6%)
    all_gather x1, waiting for transfers between devices, on_device(): all_chan = lax.all_gather(activations, 'filt', axis=0, tiled=True)  51.9 us
    reduce_scatter x1, waiting for transfers between devices, on_device(): lax.psum_scatter(partial_value, 'space', scatter_dimension=2, tiled=True)  50.4 us
    unnamed x36, local copies, waits for them, and re-layouts  24.6 us
    reshape x1, local copies, waits for them, and re-layouts, on_device(): tap_mat.reshape(taps, block_out, row_count + 2, depth + 2, width + 2)  23.9 us
    ppermute x1, starting transfers between devices, padded_2(): lax.ppermute(lax.slice_in_dim(block, block.shape[dim] - width, None, axis...  14.6 us
    add x1, other arithmetic, on_device(): features_out = summed + bias_terms.astype(jnp.float32)[:, None, None, None]  8.86 us
    dot_general x1, matrix products, on_device(): lax.dot_general(embed_mat, flat_in, (((1,), (1,)), ((), ())), preferred_e...  8.43 us
    dot_general x1, matrix products, on_device(): jnp.dot(filters.reshape(taps * block_out, chan_in), flat_in, preferred_el...  8.24 us
  transfers between devices with their start and end apart: 4, of which 4 were waited for; matrix products, arithmetic and copies ran while one was open for 29% of the time, Pallas kernels for 0%

commit v1 on v0

v1 whole, which is shorter than its diff:
```python
import functools
import math

import jax
import jax.numpy as jnp
from jax import lax
from jax.experimental import pallas as pl
from jax.experimental.pallas import tpu as pltpu
from jax.sharding import Mesh
from jax.sharding import PartitionSpec as P

SPACE = ("x", "zh", "core")
ROWS = 4
DEPTH = 8
WIDTH = 128
STEPS = 8


def local_kernel(place, b0, b1, b2, b3, b4a, b4b, b5, b6, b7, weights, cot, feat, grad):
    y = place[0]
    lane = lax.broadcasted_iota(jnp.int32, (16, WIDTH), 1)

    def block(j, row, z):
        if j == 4:
            return b4a[row, z] if row < 3 else b4b[row - 3, z]
        return (b0, b1, b2, b3, None, b5, b6, b7)[j][row, z]

    turned = pltpu.roll(
        weights[...].astype(jnp.float32).reshape(27 * 16, 128), lax.rem(128 - 16 * y, 128), 1
    ).astype(jnp.bfloat16)
    taps = jnp.concatenate(
        [
            jnp.concatenate(
                [turned[16 * (9 * dx + q) : 16 * (9 * dx + q) + 16] for q in range(9)], axis=0
            )
            for dx in range(3)
        ],
        axis=1,
    )

    total = jnp.zeros((384, 256), jnp.float32)
    gap = jnp.zeros((56, WIDTH), jnp.float32)
    empty = jnp.zeros((16, WIDTH), jnp.float32)
    for row in range(ROWS):
        cells = jnp.concatenate(
            [
                jnp.concatenate(
                    [block(j, row + dx, z) for dx in range(3) for j in range(STEPS)], axis=0
                )
                for z in range(DEPTH)
            ],
            axis=1,
        )
        part = jnp.dot(taps, cells, preferred_element_type=jnp.float32)
        for z in range(DEPTH):
            sums = []
            for dy in range(3):
                acc = None
                for dz in range(3):
                    if 0 <= z + dz - 1 < DEPTH:
                        at = 16 * (3 * dz + dy)
                        lo = WIDTH * (z + dz - 1)
                        term = part[at : at + 16, lo : lo + WIDTH]
                        acc = term if acc is None else acc + term
                sums.append(acc)
            left = jnp.where(lane == 0, 0.0, pltpu.roll(sums[0], 1, 1))
            right = jnp.where(lane == WIDTH - 1, 0.0, pltpu.roll(sums[2], WIDTH - 1, 1))
            feat[:, row, z, :] = sums[1] + left + right
        moved = []
        for z in range(DEPTH):
            here = cot[row, z].astype(jnp.float32)
            ahead = jnp.where(lane == WIDTH - 1, 0.0, pltpu.roll(here, WIDTH - 1, 1))
            behind = jnp.where(lane == 0, 0.0, pltpu.roll(here, 1, 1))
            moved.append((ahead, here, behind))
        spread = []
        for z in range(DEPTH):
            rows = []
            for half in range(2):
                for dz in range(3):
                    for dy in range(3):
                        at = z - dz + 1
                        tile = moved[at][dy] if 0 <= at < DEPTH else empty
                        rows.append(tile[8 * half : 8 * half + 8])
                rows.append(gap)
            spread.append(jnp.concatenate(rows, axis=0).astype(jnp.bfloat16))
        total = total + lax.dot_general(
            cells,
            jnp.concatenate(spread, axis=1),
            (((1,), (1,)), ((), ())),
            preferred_element_type=jnp.float32,
        )
    wide = lax.broadcasted_iota(jnp.int32, (128, WIDTH), 1)
    sub = lax.broadcasted_iota(jnp.int32, (8, WIDTH), 0)
    for half in range(2):
        one, two, three = (
            total[128 * dx : 128 * dx + 128, WIDTH * half : WIDTH * half + WIDTH]
            for dx in range(3)
        )
        one = jnp.where(wide < 72, one, pltpu.roll(three, 72, 1))
        two = jnp.where(wide < 72, two, pltpu.roll(three, 36, 1))
        for k in range(16):
            a, b = one[8 * k : 8 * k + 8], two[8 * k : 8 * k + 8]
            at = lax.rem(y + k // 2, STEPS) * 4 + 2 * (k % 2)
            grad[half, at] = jnp.where(sub < 4, a, pltpu.roll(b, 4, 0))
            grad[half, at + 1] = jnp.where(sub < 4, pltpu.roll(a, 4, 0), b)


def on_device(activations, cotangent, filters, bias_terms):
    y, zl = lax.axis_index("y"), lax.axis_index("zl")
    scale = jnp.float32(1.0 / math.sqrt(activations.shape[1] * 32 * DEPTH * WIDTH))
    acts = jnp.transpose(activations, (1, 2, 0, 3))
    cots = jnp.transpose(cotangent, (1, 2, 0, 3))
    first = zl == 0

    swap = [(0, 1), (1, 0)]
    other = lax.ppermute(lax.dynamic_slice_in_dim(acts, 3 * (1 - zl), 5, 0), "zl", swap)
    own = lax.dynamic_slice_in_dim(acts, 3 * zl, 5, 0)
    last, begin = acts[7:8], acts[0:1]
    pairs_own, pairs_other = [], []
    for s in range(31):
        pairs_own += [(s, s + 1), (32 + s + 1, 32 + s)]
        pairs_other += [(32 + s, s + 1), (s + 1, 32 + s)]
    axes = ("zl",) + SPACE
    edge_own = lax.ppermute(jnp.where(first, last, begin), axes, pairs_own)
    edge_other = lax.ppermute(jnp.where(first, begin, last), axes, pairs_other)

    def rows_of(body, edge):
        return jnp.where(
            first,
            jnp.concatenate([edge, body], axis=0),
            jnp.concatenate([body, edge], axis=0),
        )

    own, other = rows_of(own, edge_own), rows_of(other, edge_other)
    mine = jnp.where(
        first,
        jnp.concatenate([own, other], axis=2),
        jnp.concatenate([other, own], axis=2),
    )

    up = [(i, (i - 1) % STEPS) for i in range(STEPS)]
    down = [(i, (i + 1) % STEPS) for i in range(STEPS)]
    b1, b7 = lax.ppermute(mine, "y", up), lax.ppermute(mine, "y", down)
    b2, b6 = lax.ppermute(b1, "y", up), lax.ppermute(b7, "y", down)
    b3, b5 = lax.ppermute(b2, "y", up), lax.ppermute(b6, "y", down)
    b4a, b4b = lax.ppermute(b3[:3], "y", up), lax.ppermute(b5[3:], "y", down)

    give = jnp.concatenate(
        [lax.dynamic_slice_in_dim(cots, 4 * (1 - zl), 4, 0).reshape(32, 8, WIDTH), filters], axis=0
    )
    got = lax.ppermute(give, "zl", swap)
    keep = lax.dynamic_slice_in_dim(cots, 4 * zl, 4, 0)
    cot = jnp.concatenate([keep, got[:32].reshape(4, 8, 8, WIDTH)], axis=2)
    weights = jnp.concatenate([filters, got[32:]], axis=1)

    vmem = pl.BlockSpec(memory_space=pltpu.VMEM)
    feat, grad = pl.pallas_call(
        local_kernel,
        out_shape=(
            jax.ShapeDtypeStruct((16, ROWS, DEPTH, WIDTH), jnp.float32),
            jax.ShapeDtypeStruct((2, 32, 8, WIDTH), jnp.float32),
        ),
        in_specs=[pl.BlockSpec(memory_space=pltpu.SMEM)] + [vmem] * 11,
        out_specs=(vmem, vmem),
        compiler_params=pltpu.CompilerParams(vmem_limit_bytes=48 * 1024 * 1024),
        cost_estimate=pl.CostEstimate(flops=10**9, bytes_accessed=3 * 10**6, transcendentals=0),
    )(jnp.stack([y, zl]), mine, b1, b2, b3, b4a, b4b, b5, b6, b7, weights, cot)

    part = grad[0] + lax.ppermute(grad[1], "zl", swap)
    got = lax.all_to_all(part, SPACE, 0, 0, tiled=True)
    summed = jnp.sum(got, axis=0) * scale
    low, high = summed[:4], summed[4:]
    filter_grad = jnp.stack(
        [low[:, :72], high[:, :72], jnp.concatenate([low[:, 72:108], high[:, 72:108]], axis=1)]
    )
    filter_grad = filter_grad.reshape(3, 4, 9, 8).transpose(0, 2, 3, 1).reshape(27, 8, 4)

    rest = lax.ppermute(feat[8:], "zl", swap)
    kept = feat[:8]
    features_out = jnp.where(
        first,
        jnp.concatenate([kept, rest], axis=1),
        jnp.concatenate([rest, kept], axis=1),
    ) + bias_terms.astype(jnp.float32)[:, None, None, None]
    return (features_out, filter_grad)


def solution(mesh):
    fine = Mesh(mesh.devices.reshape(8, 2, 4, 4, 2), ("y", "zl", "x", "zh", "core"))
    filt = ("y", "zl")
    in_specs = (
        P(filt, SPACE, None, None),
        P(filt, SPACE, None, None),
        P(None, filt, None),
        P(filt),
    )
    out_specs = (P(filt, SPACE, None, None), P(None, filt, SPACE))
    return jax.shard_map(
        on_device, mesh=fine, in_specs=in_specs, out_specs=out_specs, check_vma=False
    )
```

time: 231 us -> 92.8 us (0.40)
  the two profiles are of different devices: /device:TPU:1 before, /device:TPU:25 now
where the time goes in v1:
time: 92.8 us; the launch traced here: 92.2 us
  starting transfers between devices  63.3 us (68%)
  waiting for transfers between devices  19.9 us (21%)
  local copies, waits for them, and re-layouts  3.74 us (4%)
  Pallas kernels  2.42 us (3%)
  other arithmetic  1.82 us (2%)
  between operations  1 us (1%)
    all_to_all x1, starting transfers between devices, on_device(): got = lax.all_to_all(part, SPACE, 0, 0, tiled=True)  15.8 us
    all_to_all x1, waiting for transfers between devices, on_device(): got = lax.all_to_all(part, SPACE, 0, 0, tiled=True)  10.4 us
    ppermute x2, starting transfers between devices, on_device(): b4a, b4b = (lax.ppermute(b3[:3], 'y', up), lax.ppermute(b5[3:], 'y', down))  7.38 us
    ppermute x2, starting transfers between devices, on_device(): b2, b6 = (lax.ppermute(b1, 'y', up), lax.ppermute(b7, 'y', down))  6.93 us
    ppermute x2, starting transfers between devices, on_device(): b3, b5 = (lax.ppermute(b2, 'y', up), lax.ppermute(b6, 'y', down))  6.49 us
    ppermute x1, starting transfers between devices, on_device(): edge_own = lax.ppermute(jnp.where(first, last, begin), axes, pairs_own)  6.37 us
    ppermute x2, starting transfers between devices, on_device(): b1, b7 = (lax.ppermute(mine, 'y', up), lax.ppermute(mine, 'y', down))  6.34 us
    ppermute x1, starting transfers between devices, on_device(): got = lax.ppermute(give, 'zl', swap)  4.88 us
  transfers between devices with their start and end apart: 15, of which 6 were waited for; matrix products, arithmetic and copies ran while one was open for 2% of the time, Pallas kernels for 0%

profile of v1, /device:TPU:25, one launch (start us, length us, event | category | flops | bytes accessed | tf_op | source)
XLA Modules:
  0.0 92.2 jit_solution(16613746364855035782)
XLA Ops:
  0.6 1.0 %copy.25 = bf16[8,8,8,128]{3,0,2,1:T(8,128)(2,1)S(1)} copy(bf16[8,8,8,128]{3,2,1,0:T(8,128)(2,1)} %param.4) | data formatting | bytes 262144 | tf_op args[0]
  1.7 6.4 %collective-permute-start = (bf16[1,8,8,128]{3,2,1,0:T(8,128)(2,1)S(1)}, bf16[1,8,8,128]{3,2,1,0:T(8,128)(2,1)S(1)}, u32[]{:S(2)}, u32[]{:S(2)}) collective-permute-start(bf16[1,8,8,128]{3,2,1,0:T(8,128)(2,1)S(1)} %get-tuple-element.12), channel_id=1, source_target_pairs={{0,1},{33,32},{1,2},{34,33},{2,3},{35,34},{3,4},{36,35},{4,5},{37,... | collective-permute-start | bytes 49160 | tf_op jit(solution)/shard_map/ppermute | solution.py:124
  8.1 1.9 %collective-permute-start.2 = (bf16[5,8,8,128]{3,2,1,0:T(8,128)(2,1)S(1)}, bf16[5,8,8,128]{3,2,1,0:T(8,128)(2,1)S(1)}, u32[]{:S(2)}, u32[]{:S(2)}) collective-permute-start(bf16[5,8,8,128]{3,2,1,0:T(8,128)(2,1)S(1)} %get-tuple-element.15), channel_id=1, source_target_pairs={{0,32},{32,0},{1,33},{33,1},{2,34},{34,2},{3,35},{35,3},{4,36},{36... | collective-permute-start | bytes 245768 | tf_op jit(solution)/shard_map/ppermute | solution.py:116
  10.0 1.9 %collective-permute-start.1 = (bf16[1,8,8,128]{3,2,1,0:T(8,128)(2,1)S(1)}, bf16[1,8,8,128]{3,2,1,0:T(8,128)(2,1)S(1)}, u32[]{:S(2)}, u32[]{:S(2)}) collective-permute-start(bf16[1,8,8,128]{3,2,1,0:T(8,128)(2,1)S(1)} %get-tuple-element.13), channel_id=1, source_target_pairs={{32,1},{1,32},{33,2},{2,33},{34,3},{3,34},{35,4},{4,35},{36,5},{5,... | collective-permute-start | bytes 49160 | tf_op jit(solution)/shard_map/ppermute | solution.py:125
  11.9 0.0 collective-permute-done
  11.9 3.1 %collective-permute-done.1 = bf16[1,8,8,128]{3,2,1,0:T(8,128)(2,1)S(1)} collective-permute-done((bf16[1,8,8,128]{3,2,1,0:T(8,128)(2,1)S(1)}, bf16[1,8,8,128]{3,2,1,0:T(8,128)(2,1)S(1)}, u32[]{:S(2)}, u32[]{:S(2)}) %collective-permute-start.1) | collective-permute-done | bytes 16416 | tf_op jit(solution)/shard_map/ppermute | solution.py:125
  15.0 0.0 collective-permute-done.2
  15.1 0.0 copy-start.2
  15.1 0.1 maximum_select_fusion.1.b0
  15.1 4.4 %collective-permute-start.7 = (bf16[6,8,16,128]{3,2,1,0:T(8,128)(2,1)S(1)}, bf16[6,8,16,128]{3,2,1,0:T(8,128)(2,1)S(1)}, u32[]{:S(2)}, u32[]{:S(2)}) collective-permute-start(bf16[6,8,16,128]{3,2,1,0:T(8,128)(2,1)S(1)} %maximum_select_fusion.1.b0), channel_id=1, source_target_pairs={{0,64},{64,128},{128,192},{192,256},{256,320},{320,384},{384,448},... | collective-permute-start | bytes 589832 | tf_op jit(solution)/shard_map/ppermute | solution.py:143
  19.6 1.9 %collective-permute-start.3 = (bf16[6,8,16,128]{3,2,1,0:T(8,128)(2,1)S(1)}, bf16[6,8,16,128]{3,2,1,0:T(8,128)(2,1)S(1)}, u32[]{:S(2)}, u32[]{:S(2)}) collective-permute-start(bf16[6,8,16,128]{3,2,1,0:T(8,128)(2,1)S(1)} %maximum_select_fusion.1.b0), channel_id=1, source_target_pairs={{0,448},{64,0},{128,64},{192,128},{256,192},{320,256},{384,320},{4... | collective-permute-start | bytes 589832 | tf_op jit(solution)/shard_map/ppermute | solution.py:143
  21.5 0.7 collective-permute-done.7.b7
  22.2 5.0 %collective-permute-start.8 = (bf16[6,8,16,128]{3,2,1,0:T(8,128)(2,1)S(1)}, bf16[6,8,16,128]{3,2,1,0:T(8,128)(2,1)S(1)}, u32[]{:S(2)}, u32[]{:S(2)}) collective-permute-start(bf16[6,8,16,128]{3,2,1,0:T(8,128)(2,1)S(1)} %collective-permute-done.7.b7), channel_id=1, source_target_pairs={{0,64},{64,128},{128,192},{192,256},{256,320},{320,384},{384,448},... | collective-permute-start | bytes 589832 | tf_op jit(solution)/shard_map/ppermute | solution.py:144
  27.2 0.0 collective-permute-done.3.b1
  27.2 1.9 %collective-permute-start.4 = (bf16[6,8,16,128]{3,2,1,0:T(8,128)(2,1)S(1)}, bf16[6,8,16,128]{3,2,1,0:T(8,128)(2,1)S(1)}, u32[]{:S(2)}, u32[]{:S(2)}) collective-permute-start(bf16[6,8,16,128]{3,2,1,0:T(8,128)(2,1)S(1)} %collective-permute-done.3.b1), channel_id=1, source_target_pairs={{0,448},{64,0},{128,64},{192,128},{256,192},{320,256},{384,320},{4... | collective-permute-start | bytes 589832 | tf_op jit(solution)/shard_map/ppermute | solution.py:144
  29.1 0.0 copy-done.2
  29.1 0.0 copy-start.1
  29.2 0.8 copy-done.1
  30.0 4.9 %collective-permute-start.11 = (bf16[59,8,128]{2,1,0:T(8,128)(2,1)S(1)}, bf16[59,8,128]{2,1,0:T(8,128)(2,1)S(1)}, u32[]{:S(2)}, u32[]{:S(2)}) collective-permute-start(bf16[59,8,128]{2,1,0:T(8,128)(2,1)S(1)} %pad_maximum_fusion.1), channel_id=1, source_target_pairs={{0,32},{32,0},{1,33},{33,1},{2,34},{34,2},{3,35},{35,3},{4,36},{36... | collective-permute-start | bytes 362504 | tf_op jit(solution)/shard_map/ppermute | solution.py:151
  34.9 0.0 collective-permute-done.8.b6
  34.9 4.6 %collective-permute-start.9 = (bf16[6,8,16,128]{3,2,1,0:T(8,128)(2,1)S(1)}, bf16[6,8,16,128]{3,2,1,0:T(8,128)(2,1)S(1)}, u32[]{:S(2)}, u32[]{:S(2)}) collective-permute-start(bf16[6,8,16,128]{3,2,1,0:T(8,128)(2,1)S(1)} %collective-permute-done.8.b6), channel_id=1, source_target_pairs={{0,64},{64,128},{128,192},{192,256},{256,320},{320,384},{384,448},... | collective-permute-start | bytes 589832 | tf_op jit(solution)/shard_map/ppermute | solution.py:145
  39.5 0.0 collective-permute-done.4.b2
  39.5 1.9 %collective-permute-start.5 = (bf16[6,8,16,128]{3,2,1,0:T(8,128)(2,1)S(1)}, bf16[6,8,16,128]{3,2,1,0:T(8,128)(2,1)S(1)}, u32[]{:S(2)}, u32[]{:S(2)}) collective-permute-start(bf16[6,8,16,128]{3,2,1,0:T(8,128)(2,1)S(1)} %collective-permute-done.4.b2), channel_id=1, source_target_pairs={{0,448},{64,0},{128,64},{192,128},{256,192},{320,256},{384,320},{4... | collective-permute-start | bytes 589832 | tf_op jit(solution)/shard_map/ppermute | solution.py:145
  41.4 0.1 pad_add_fusion.place
  41.5 0.0 collective-permute-done.11
  41.5 0.0 copy-start
  41.5 0.6 copy-done
  42.2 0.8 collective-permute-done.9.b5
  43.0 0.0 slice-start
  43.0 5.5 %collective-permute-start.10 = (bf16[3,8,16,128]{3,2,1,0:T(8,128)(2,1)S(1)}, bf16[3,8,16,128]{3,2,1,0:T(8,128)(2,1)S(1)}, u32[]{:S(2)}, u32[]{:S(2)}) collective-permute-start(bf16[3,8,16,128]{3,2,1,0:T(8,128)(2,1)S(1)} %slice.65), channel_id=1, source_target_pairs={{0,64},{64,128},{128,192},{192,256},{256,320},{320,384},{384,448},... | collective-permute-start | bytes 294920 | tf_op jit(solution)/shard_map/ppermute | solution.py:146
  48.5 0.0 collective-permute-done.5.b3
  48.5 1.9 %collective-permute-start.6 = (bf16[3,8,16,128]{3,2,1,0:T(8,128)(2,1)S(1)}, bf16[3,8,16,128]{3,2,1,0:T(8,128)(2,1)S(1)}, u32[]{:S(2)}, u32[]{:S(2)}) collective-permute-start(bf16[3,8,16,128]{3,2,1,0:T(8,128)(2,1)S(1)} %slice.64), channel_id=1, source_target_pairs={{0,448},{64,0},{128,64},{192,128},{256,192},{320,256},{384,320},{4... | collective-permute-start | bytes 294920 | tf_op jit(solution)/shard_map/ppermute | solution.py:146
  50.4 0.0 slice-done
  50.5 0.0 collective-permute-done.10.b4b
  50.5 4.6 %collective-permute-done.6.b4a = bf16[3,8,16,128]{3,2,1,0:T(8,128)(2,1)S(1)} collective-permute-done((bf16[3,8,16,128]{3,2,1,0:T(8,128)(2,1)S(1)}, bf16[3,8,16,128]{3,2,1,0:T(8,128)(2,1)S(1)}, u32[]{:S(2)}, u32[]{:S(2)}) %collective-permute-start.6) | collective-permute-done | bytes 98336 | tf_op jit(solution)/shard_map/ppermute | solution.py:146
  55.1 2.4 %shard_map.59 = (f32[16,4,8,128]{3,2,1,0:T(8,128)S(1)}, f32[2,32,8,128]{3,2,1,0:T(8,128)S(1)}) custom-call(s32[2]{0:T(128)S(1)} %pad_add_fusion.place, bf16[6,8,16,128]{3,2,1,0:T(8,128)(2,1)S(1)} %maximum_select_fusion.1.b0, bf16[6,8,16,128]{3,2,1,0:T(8,128)(2,1)S(1)} %collective-permute-done.3.b1, bf16[6,8,16,128]{3,2,1,0:T(8,128)(2,1)S(1)} %collective-permute-done.4.b2, ...), custom_call_target="tpu_custom_call" | custom-call | flops 1000000000 | bytes 3000000 | tf_op jit(solution)/shard_map/pallas_call | solution.py:157
  57.5 2.0 %collective-permute-start.13 = (f32[32,8,128]{2,1,0:T(8,128)S(1)}, f32[32,8,128]{2,1,0:T(8,128)S(1)}, u32[]{:S(2)}, u32[]{:S(2)}) collective-permute-start(f32[32,8,128]{2,1,0:T(8,128)S(1)} %slice_bitcast_fusion), channel_id=1, source_target_pairs={{0,32},{32,0},{1,33},{33,1},{2,34},{34,2},{3,35},{35,3},{4,36},{36... | collective-permute-start | bytes 393224 | tf_op jit(solution)/shard_map/ppermute | solution.py:169
  59.6 3.3 %collective-permute-start.12 = (f32[8,4,8,128]{3,2,1,0:T(8,128)S(1)}, f32[8,4,8,128]{3,2,1,0:T(8,128)S(1)}, u32[]{:S(2)}, u32[]{:S(2)}) collective-permute-start(f32[8,4,8,128]{3,2,1,0:T(8,128)S(1)} %get-tuple-element.9), channel_id=1, source_target_pairs={{0,32},{32,0},{1,33},{33,1},{2,34},{34,2},{3,35},{35,3},{4,36},{36... | collective-permute-start | bytes 393224 | tf_op jit(solution)/shard_map/ppermute | solution.py:178
  62.8 0.4 collective-permute-done.13
  63.2 0.7 bitcast_add_fusion
  63.9 0.0 copy-start.3
  63.9 15.8 %all-to-all-start = ((f32[32,8,128]{2,1,0:T(8,128)}), f32[32,8,128]{2,1,0:T(8,128)S(1)}, u32[]{:S(2)}, u32[]{:S(2)}) async-start(f32[32,8,128]{2,1,0:T(8,128)} %bitcast_add_fusion), calls=%async_computation | async-start | bytes 262144 | tf_op jit(solution)/shard_map/all_to_all | solution.py:170
  79.7 0.0 copy-done.3
  79.7 0.0 collective-permute-done.12
  79.7 0.8 fusion
  80.5 10.4 %all-to-all-done = f32[32,8,128]{2,1,0:T(8,128)S(1)} async-done(((f32[32,8,128]{2,1,0:T(8,128)}), f32[32,8,128]{2,1,0:T(8,128)S(1)}, u32[]{:S(2)}, u32[]{:S(2)}) %all-to-all-start) | async-done | bytes 131104 | tf_op jit(solution)/shard_map/all_to_all | solution.py:170
  90.9 0.1 fusion.3
  91.0 0.1 pad_maximum_fusion.3
  91.1 0.1 stack.26
  91.2 0.1 stack.24
  91.2 0.1 stack.25
  91.3 0.2 copy.18
  91.5 0.7 reshape.24
  (20 shorter events, 0.3 us)
Async XLA Ops:
  1.7 10.3 %collective-permute-start = (bf16[1,8,8,128]{3,2,1,0:T(8,128)(2,1)S(1)}, bf16[1,8,8,128]{3,2,1,0:T(8,128)(2,1)S(1)}, u32[]{:S(2)}, u32[]{:S(2)}) collective-permute-start(bf16[1,8,8,128]{3,2,1,0:T(8,128)(2,1)S(1)} %get-tuple-element.12), channel_id=1, source_target_pairs={{0,1},{33,32},{1,2},{34,33},{2,3},{35,34},{3,4},{36,35},{4,5},{37,... | collective-permute-start | bytes 49160 | tf_op jit(solution)/shard_map/ppermute | solution.py:124
  8.1 7.0 %collective-permute-start.2 = (bf16[5,8,8,128]{3,2,1,0:T(8,128)(2,1)S(1)}, bf16[5,8,8,128]{3,2,1,0:T(8,128)(2,1)S(1)}, u32[]{:S(2)}, u32[]{:S(2)}) collective-permute-start(bf16[5,8,8,128]{3,2,1,0:T(8,128)(2,1)S(1)} %get-tuple-element.15), channel_id=1, source_target_pairs={{0,32},{32,0},{1,33},{33,1},{2,34},{34,2},{3,35},{35,3},{4,36},{36... | collective-permute-start | bytes 245768 | tf_op jit(solution)/shard_map/ppermute | solution.py:116
  10.0 5.1 %collective-permute-start.1 = (bf16[1,8,8,128]{3,2,1,0:T(8,128)(2,1)S(1)}, bf16[1,8,8,128]{3,2,1,0:T(8,128)(2,1)S(1)}, u32[]{:S(2)}, u32[]{:S(2)}) collective-permute-start(bf16[1,8,8,128]{3,2,1,0:T(8,128)(2,1)S(1)} %get-tuple-element.13), channel_id=1, source_target_pairs={{32,1},{1,32},{33,2},{2,33},{34,3},{3,34},{35,4},{4,35},{36,5},{5,... | collective-permute-start | bytes 49160 | tf_op jit(solution)/shard_map/ppermute | solution.py:125
  15.1 14.1 %copy-start.2 = (bf16[8,8,8,128]{3,2,1,0:T(8,128)(2,1)S(1)}, bf16[8,8,8,128]{3,2,1,0:T(8,128)(2,1)}, u32[]{:S(2)}) copy-start(bf16[8,8,8,128]{3,2,1,0:T(8,128)(2,1)} %param.5) | copy-start | bytes 393220
  15.1 7.0 %collective-permute-start.7 = (bf16[6,8,16,128]{3,2,1,0:T(8,128)(2,1)S(1)}, bf16[6,8,16,128]{3,2,1,0:T(8,128)(2,1)S(1)}, u32[]{:S(2)}, u32[]{:S(2)}) collective-permute-start(bf16[6,8,16,128]{3,2,1,0:T(8,128)(2,1)S(1)} %maximum_select_fusion.1.b0), channel_id=1, source_target_pairs={{0,64},{64,128},{128,192},{192,256},{256,320},{320,384},{384,448},... | collective-permute-start | bytes 589832 | tf_op jit(solution)/shard_map/ppermute | solution.py:143
  19.6 7.6 %collective-permute-start.3 = (bf16[6,8,16,128]{3,2,1,0:T(8,128)(2,1)S(1)}, bf16[6,8,16,128]{3,2,1,0:T(8,128)(2,1)S(1)}, u32[]{:S(2)}, u32[]{:S(2)}) collective-permute-start(bf16[6,8,16,128]{3,2,1,0:T(8,128)(2,1)S(1)} %maximum_select_fusion.1.b0), channel_id=1, source_target_pairs={{0,448},{64,0},{128,64},{192,128},{256,192},{320,256},{384,320},{4... | collective-permute-start | bytes 589832 | tf_op jit(solution)/shard_map/ppermute | solution.py:143
  22.2 12.8 %collective-permute-start.8 = (bf16[6,8,16,128]{3,2,1,0:T(8,128)(2,1)S(1)}, bf16[6,8,16,128]{3,2,1,0:T(8,128)(2,1)S(1)}, u32[]{:S(2)}, u32[]{:S(2)}) collective-permute-start(bf16[6,8,16,128]{3,2,1,0:T(8,128)(2,1)S(1)} %collective-permute-done.7.b7), channel_id=1, source_target_pairs={{0,64},{64,128},{128,192},{192,256},{256,320},{320,384},{384,448},... | collective-permute-start | bytes 589832 | tf_op jit(solution)/shard_map/ppermute | solution.py:144
  27.2 12.3 %collective-permute-start.4 = (bf16[6,8,16,128]{3,2,1,0:T(8,128)(2,1)S(1)}, bf16[6,8,16,128]{3,2,1,0:T(8,128)(2,1)S(1)}, u32[]{:S(2)}, u32[]{:S(2)}) collective-permute-start(bf16[6,8,16,128]{3,2,1,0:T(8,128)(2,1)S(1)} %collective-permute-done.3.b1), channel_id=1, source_target_pairs={{0,448},{64,0},{128,64},{192,128},{256,192},{320,256},{384,320},{4... | collective-permute-start | bytes 589832 | tf_op jit(solution)/shard_map/ppermute | solution.py:144
  29.1 0.8 copy-start.1
  30.0 11.5 %collective-permute-start.11 = (bf16[59,8,128]{2,1,0:T(8,128)(2,1)S(1)}, bf16[59,8,128]{2,1,0:T(8,128)(2,1)S(1)}, u32[]{:S(2)}, u32[]{:S(2)}) collective-permute-start(bf16[59,8,128]{2,1,0:T(8,128)(2,1)S(1)} %pad_maximum_fusion.1), channel_id=1, source_target_pairs={{0,32},{32,0},{1,33},{33,1},{2,34},{34,2},{3,35},{35,3},{4,36},{36... | collective-permute-start | bytes 362504 | tf_op jit(solution)/shard_map/ppermute | solution.py:151
  34.9 8.1 %collective-permute-start.9 = (bf16[6,8,16,128]{3,2,1,0:T(8,128)(2,1)S(1)}, bf16[6,8,16,128]{3,2,1,0:T(8,128)(2,1)S(1)}, u32[]{:S(2)}, u32[]{:S(2)}) collective-permute-start(bf16[6,8,16,128]{3,2,1,0:T(8,128)(2,1)S(1)} %collective-permute-done.8.b6), channel_id=1, source_target_pairs={{0,64},{64,128},{128,192},{192,256},{256,320},{320,384},{384,448},... | collective-permute-start | bytes 589832 | tf_op jit(solution)/shard_map/ppermute | solution.py:145
  39.5 8.9 %collective-permute-start.5 = (bf16[6,8,16,128]{3,2,1,0:T(8,128)(2,1)S(1)}, bf16[6,8,16,128]{3,2,1,0:T(8,128)(2,1)S(1)}, u32[]{:S(2)}, u32[]{:S(2)}) collective-permute-start(bf16[6,8,16,128]{3,2,1,0:T(8,128)(2,1)S(1)} %collective-permute-done.4.b2), channel_id=1, source_target_pairs={{0,448},{64,0},{128,64},{192,128},{256,192},{320,256},{384,320},{4... | collective-permute-start | bytes 589832 | tf_op jit(solution)/shard_map/ppermute | solution.py:145
  41.5 0.6 copy-start
  43.0 7.4 %slice-start = ((bf16[59,8,128]{2,1,0:T(8,128)(2,1)}), bf16[27,8,128]{2,1,0:T(8,128)(2,1)S(1)}, s32[]{:S(2)}) async-start(bf16[59,8,128]{2,1,0:T(8,128)(2,1)} %copy-done), calls=%async_computation.1 | async-start | bytes 110592 | tf_op jit(solution)/shard_map/slice | solution.py:154
  43.0 7.5 %collective-permute-start.10 = (bf16[3,8,16,128]{3,2,1,0:T(8,128)(2,1)S(1)}, bf16[3,8,16,128]{3,2,1,0:T(8,128)(2,1)S(1)}, u32[]{:S(2)}, u32[]{:S(2)}) collective-permute-start(bf16[3,8,16,128]{3,2,1,0:T(8,128)(2,1)S(1)} %slice.65), channel_id=1, source_target_pairs={{0,64},{64,128},{128,192},{192,256},{256,320},{320,384},{384,448},... | collective-permute-start | bytes 294920 | tf_op jit(solution)/shard_map/ppermute | solution.py:146
  48.5 6.6 %collective-permute-start.6 = (bf16[3,8,16,128]{3,2,1,0:T(8,128)(2,1)S(1)}, bf16[3,8,16,128]{3,2,1,0:T(8,128)(2,1)S(1)}, u32[]{:S(2)}, u32[]{:S(2)}) collective-permute-start(bf16[3,8,16,128]{3,2,1,0:T(8,128)(2,1)S(1)} %slice.64), channel_id=1, source_target_pairs={{0,448},{64,0},{128,64},{192,128},{256,192},{320,256},{384,320},{4... | collective-permute-start | bytes 294920 | tf_op jit(solution)/shard_map/ppermute | solution.py:146
  57.5 5.7 %collective-permute-start.13 = (f32[32,8,128]{2,1,0:T(8,128)S(1)}, f32[32,8,128]{2,1,0:T(8,128)S(1)}, u32[]{:S(2)}, u32[]{:S(2)}) collective-permute-start(f32[32,8,128]{2,1,0:T(8,128)S(1)} %slice_bitcast_fusion), channel_id=1, source_target_pairs={{0,32},{32,0},{1,33},{33,1},{2,34},{34,2},{3,35},{35,3},{4,36},{36... | collective-permute-start | bytes 393224 | tf_op jit(solution)/shard_map/ppermute | solution.py:169
  59.6 20.2 %collective-permute-start.12 = (f32[8,4,8,128]{3,2,1,0:T(8,128)S(1)}, f32[8,4,8,128]{3,2,1,0:T(8,128)S(1)}, u32[]{:S(2)}, u32[]{:S(2)}) collective-permute-start(f32[8,4,8,128]{3,2,1,0:T(8,128)S(1)} %get-tuple-element.9), channel_id=1, source_target_pairs={{0,32},{32,0},{1,33},{33,1},{2,34},{34,2},{3,35},{35,3},{4,36},{36... | collective-permute-start | bytes 393224 | tf_op jit(solution)/shard_map/ppermute | solution.py:178
  63.9 15.8 %copy-start.3 = (bf16[8]{0:T(256)(128)(2,1)S(1)}, bf16[8]{0:T(256)(128)(2,1)}, u32[]{:S(2)}) copy-start(bf16[8]{0:T(256)(128)(2,1)} %param.7) | copy-start | bytes 52
  63.9 27.0 %all-to-all-start = ((f32[32,8,128]{2,1,0:T(8,128)}), f32[32,8,128]{2,1,0:T(8,128)S(1)}, u32[]{:S(2)}, u32[]{:S(2)}) async-start(f32[32,8,128]{2,1,0:T(8,128)} %bitcast_add_fusion), calls=%async_computation | async-start | bytes 262144 | tf_op jit(solution)/shard_map/all_to_all | solution.py:170

commit v2 on v1

--- a/solution.py
+++ b/solution.py
@@ -16,15 +16,30 @@
 STEPS = 8
 
 
-def local_kernel(place, b0, b1, b2, b3, b4a, b4b, b5, b6, b7, weights, cot, feat, grad):
+def block_of(blocks, j, row, z):
+    b0, b1, b2, b3, b4a, b4b, b5, b6, b7 = blocks
+    if j == 4:
+        return b4a[row, z] if row < 3 else b4b[row - 3, z]
+    return (b0, b1, b2, b3, None, b5, b6, b7)[j][row, z]
+
+
+def cells_of(blocks, row):
+    return jnp.concatenate(
+        [
+            jnp.concatenate(
+                [block_of(blocks, j, row + dx, z) for dx in range(3) for j in range(STEPS)],
+                axis=0,
+            )
+            for z in range(DEPTH)
+        ],
+        axis=1,
+    )
+
+
+def forward_kernel(place, *refs):
+    *blocks, weights, feat = refs
     y = place[0]
     lane = lax.broadcasted_iota(jnp.int32, (16, WIDTH), 1)
-
-    def block(j, row, z):
-        if j == 4:
-            return b4a[row, z] if row < 3 else b4b[row - 3, z]
-        return (b0, b1, b2, b3, None, b5, b6, b7)[j][row, z]
-
     turned = pltpu.roll(
         weights[...].astype(jnp.float32).reshape(27 * 16, 128), lax.rem(128 - 16 * y, 128), 1
     ).astype(jnp.bfloat16)
@@ -37,21 +52,8 @@
         ],
         axis=1,
     )
-
-    total = jnp.zeros((384, 256), jnp.float32)
-    gap = jnp.zeros((56, WIDTH), jnp.float32)
-    empty = jnp.zeros((16, WIDTH), jnp.float32)
     for row in range(ROWS):
-        cells = jnp.concatenate(
-            [
-                jnp.concatenate(
-                    [block(j, row + dx, z) for dx in range(3) for j in range(STEPS)], axis=0
-                )
-                for z in range(DEPTH)
-            ],
-            axis=1,
-        )
-        part = jnp.dot(taps, cells, preferred_element_type=jnp.float32)
+        part = jnp.dot(taps, cells_of(blocks, row), preferred_element_type=jnp.float32)
         for z in range(DEPTH):
             sums = []
             for dy in range(3):
@@ -66,6 +68,16 @@
             left = jnp.where(lane == 0, 0.0, pltpu.roll(sums[0], 1, 1))
             right = jnp.where(lane == WIDTH - 1, 0.0, pltpu.roll(sums[2], WIDTH - 1, 1))
             feat[:, row, z, :] = sums[1] + left + right
+
+
+def gradient_kernel(place, *refs):
+    *blocks, cot, grad = refs
+    y, zl = place[0], place[1]
+    lane = lax.broadcasted_iota(jnp.int32, (16, WIDTH), 1)
+    total = jnp.zeros((384, 256), jnp.float32)
+    gap = jnp.zeros((56, WIDTH), jnp.float32)
+    empty = jnp.zeros((16, WIDTH), jnp.float32)
+    for row in range(ROWS):
         moved = []
         for z in range(DEPTH):
             here = cot[row, z].astype(jnp.float32)
@@ -84,7 +96,7 @@
                 rows.append(gap)
             spread.append(jnp.concatenate(rows, axis=0).astype(jnp.bfloat16))
         total = total + lax.dot_general(
-            cells,
+            cells_of(blocks, row),
             jnp.concatenate(spread, axis=1),
             (((1,), (1,)), ((), ())),
             preferred_element_type=jnp.float32,
@@ -98,11 +110,12 @@
         )
         one = jnp.where(wide < 72, one, pltpu.roll(three, 72, 1))
         two = jnp.where(wide < 72, two, pltpu.roll(three, 36, 1))
+        base = 32 * lax.rem(zl + half, 2)
         for k in range(16):
             a, b = one[8 * k : 8 * k + 8], two[8 * k : 8 * k + 8]
-            at = lax.rem(y + k // 2, STEPS) * 4 + 2 * (k % 2)
-            grad[half, at] = jnp.where(sub < 4, a, pltpu.roll(b, 4, 0))
-            grad[half, at + 1] = jnp.where(sub < 4, pltpu.roll(a, 4, 0), b)
+            at = base + lax.rem(y + k // 2, STEPS) * 4 + 2 * (k % 2)
+            grad[at] = jnp.where(sub < 4, a, pltpu.roll(b, 4, 0))
+            grad[at + 1] = jnp.where(sub < 4, pltpu.roll(a, 4, 0), b)
 
 
 def on_device(activations, cotangent, filters, bias_terms):
@@ -115,35 +128,29 @@
     swap = [(0, 1), (1, 0)]
     other = lax.ppermute(lax.dynamic_slice_in_dim(acts, 3 * (1 - zl), 5, 0), "zl", swap)
     own = lax.dynamic_slice_in_dim(acts, 3 * zl, 5, 0)
-    last, begin = acts[7:8], acts[0:1]
-    pairs_own, pairs_other = [], []
-    for s in range(31):
-        pairs_own += [(s, s + 1), (32 + s + 1, 32 + s)]
-        pairs_other += [(32 + s, s + 1), (s + 1, 32 + s)]
-    axes = ("zl",) + SPACE
-    edge_own = lax.ppermute(jnp.where(first, last, begin), axes, pairs_own)
-    edge_other = lax.ppermute(jnp.where(first, begin, last), axes, pairs_other)
-
-    def rows_of(body, edge):
-        return jnp.where(
-            first,
-            jnp.concatenate([edge, body], axis=0),
-            jnp.concatenate([body, edge], axis=0),
-        )
-
-    own, other = rows_of(own, edge_own), rows_of(other, edge_other)
-    mine = jnp.where(
+    pairs = []
+    for step in range(31):
+        pairs += [(32 + step, step + 1), (step + 1, 32 + step)]
+
+    body = jnp.where(
         first,
         jnp.concatenate([own, other], axis=2),
         jnp.concatenate([other, own], axis=2),
     )
-
-    up = [(i, (i - 1) % STEPS) for i in range(STEPS)]
-    down = [(i, (i + 1) % STEPS) for i in range(STEPS)]
-    b1, b7 = lax.ppermute(mine, "y", up), lax.ppermute(mine, "y", down)
-    b2, b6 = lax.ppermute(b1, "y", up), lax.ppermute(b7, "y", down)
-    b3, b5 = lax.ppermute(b2, "y", up), lax.ppermute(b6, "y", down)
-    b4a, b4b = lax.ppermute(b3[:3], "y", up), lax.ppermute(b5[3:], "y", down)
+    edge = lax.ppermute(jnp.where(first, body[0:1], body[4:5]), ("zl",) + SPACE, pairs)
+    mine = jnp.where(
+        first,
+        jnp.concatenate([edge, body], axis=0),
+        jnp.concatenate([body, edge], axis=0),
+    )
+
+    def along(block, by):
+        return lax.ppermute(block, "y", [(i, (i - by) % STEPS) for i in range(STEPS)])
+
+    b2, b6 = along(mine, 2), along(mine, -2)
+    b1, b7 = along(mine, 1), along(mine, -1)
+    b3, b5 = along(b2, 1), along(b6, -1)
+    b4a, b4b = along(b2[:3], 2), along(b6[3:], -2)
 
     give = jnp.concatenate(
         [lax.dynamic_slice_in_dim(cots, 4 * (1 - zl), 4, 0).reshape(32, 8, WIDTH), filters], axis=0
@@ -153,21 +160,27 @@
     cot = jnp.concatenate([keep, got[:32].reshape(4, 8, 8, WIDTH)], axis=2)
     weights = jnp.concatenate([filters, got[32:]], axis=1)
 
+    blocks = (mine, b1, b2, b3, b4a, b4b, b5, b6, b7)
+    place = jnp.stack([y, zl])
     vmem = pl.BlockSpec(memory_space=pltpu.VMEM)
-    feat, grad = pl.pallas_call(
-        local_kernel,
-        out_shape=(
-            jax.ShapeDtypeStruct((16, ROWS, DEPTH, WIDTH), jnp.float32),
-            jax.ShapeDtypeStruct((2, 32, 8, WIDTH), jnp.float32),
-        ),
-        in_specs=[pl.BlockSpec(memory_space=pltpu.SMEM)] + [vmem] * 11,
-        out_specs=(vmem, vmem),
+    settings = dict(
+        in_specs=[pl.BlockSpec(memory_space=pltpu.SMEM)] + [vmem] * 10,
+        out_specs=vmem,
         compiler_params=pltpu.CompilerParams(vmem_limit_bytes=48 * 1024 * 1024),
         cost_estimate=pl.CostEstimate(flops=10**9, bytes_accessed=3 * 10**6, transcendentals=0),
-    )(jnp.stack([y, zl]), mine, b1, b2, b3, b4a, b4b, b5, b6, b7, weights, cot)
-
-    part = grad[0] + lax.ppermute(grad[1], "zl", swap)
-    got = lax.all_to_all(part, SPACE, 0, 0, tiled=True)
+    )
+    grad = pl.pallas_call(
+        gradient_kernel,
+        out_shape=jax.ShapeDtypeStruct((64, 8, WIDTH), jnp.float32),
+        **settings,
+    )(place, *blocks, cot)
+    feat = pl.pallas_call(
+        forward_kernel,
+        out_shape=jax.ShapeDtypeStruct((16, ROWS, DEPTH, WIDTH), jnp.float32),
+        **settings,
+    )(place, *blocks, weights)
+
+    got = lax.all_to_all(grad, ("zl",) + SPACE, 0, 0, tiled=True)
     summed = jnp.sum(got, axis=0) * scale
     low, high = summed[:4], summed[4:]
     filter_grad = jnp.stack(

time: 92.8 us -> 86.7 us (0.934)
  the two profiles are of different devices: /device:TPU:25 before, /device:TPU:16 now
where the time goes in v2:
time: 86.7 us; the launch traced here: 86.1 us
  starting transfers between devices  59.3 us (68%)
  waiting for transfers between devices  18.3 us (21%)
  Pallas kernels  3.95 us (5%)
  local copies, waits for them, and re-layouts  2.49 us (3%)
  other arithmetic  1.17 us (1%)
  between operations  0.98 us (1%)
    ppermute x8, starting transfers between devices, along(): lax.ppermute(block, 'y', [(i, (i - by) % STEPS) for i in range(STEPS)])  31.2 us
    all_to_all x1, starting transfers between devices, on_device(): got = lax.all_to_all(grad, ('zl',) + SPACE, 0, 0, tiled=True)  12.8 us
    ppermute x8, waiting for transfers between devices, along(): lax.ppermute(block, 'y', [(i, (i - by) % STEPS) for i in range(STEPS)])  7.32 us
    ppermute x1, starting transfers between devices, on_device(): got = lax.ppermute(give, 'zl', swap)  6.69 us
    ppermute x1, waiting for transfers between devices, on_device(): rest = lax.ppermute(feat[8:], 'zl', swap)  5.75 us
    ppermute x1, starting transfers between devices, on_device(): lax.ppermute(lax.dynamic_slice_in_dim(acts, 3 * (1 - zl), 5, 0), 'zl', swap)  4.28 us
    ppermute x1, starting transfers between devices, on_device(): rest = lax.ppermute(feat[8:], 'zl', swap)  3.58 us
    all_to_all x1, waiting for transfers between devices, on_device(): got = lax.all_to_all(grad, ('zl',) + SPACE, 0, 0, tiled=True)  2.78 us
  transfers between devices with their start and end apart: 13, of which 5 were waited for; matrix products, arithmetic and copies ran while one was open for 1% of the time, Pallas kernels for 2%

profile of v2, /device:TPU:16, one launch (start us, length us, event | category | flops | bytes accessed | tf_op | source)
XLA Modules:
  0.0 86.1 jit_solution(8520113206308251168)
XLA Ops:
  0.6 1.0 %constant_dynamic-slice_fusion.2 = (bf16[8,5,8,128]{3,2,1,0:T(8,128)(2,1)S(1)}, bf16[8,5,8,128]{3,2,1,0:T(8,128)(2,1)S(1)}) fusion(bf16[8,8,8,128]{3,2,1,0:T(8,128)(2,1)} %param.4, s32[]{:T(128)S(6)} %select_n.48, s32[]{:T(128)S(6)} %select_n.49), kind=kLoop, calls=%fused_computation.17 | loop fusion | bytes 327688 | tf_op jit(solution)/shard_map/dynamic-slice
  1.6 4.3 %collective-permute-start = (bf16[5,8,8,128]{3,2,1,0:T(8,128)(2,1)S(1)}, bf16[5,8,8,128]{3,2,1,0:T(8,128)(2,1)S(1)}, u32[]{:S(2)}, u32[]{:S(2)}) collective-permute-start(bf16[5,8,8,128]{3,2,1,0:T(8,128)(2,1)S(1)} %bitcast.23), channel_id=1, source_target_pairs={{0,32},{32,0},{1,33},{33,1},{2,34},{34,2},{3,35},{35,3},{4,36},{36... | collective-permute-start | bytes 245768 | tf_op jit(solution)/shard_map/ppermute | solution.py:129
  6.0 2.4 %collective-permute-done = bf16[5,8,8,128]{3,2,1,0:T(8,128)(2,1)S(1)} collective-permute-done((bf16[5,8,8,128]{3,2,1,0:T(8,128)(2,1)S(1)}, bf16[5,8,8,128]{3,2,1,0:T(8,128)(2,1)S(1)}, u32[]{:S(2)}, u32[]{:S(2)}) %collective-permute-start) | collective-permute-done | bytes 81952 | tf_op jit(solution)/shard_map/ppermute | solution.py:129
  8.4 0.0 copy-start.1
  8.4 0.7 collective-permute-start.1
  9.1 0.2 copy-done.1
  9.3 0.0 copy-start
  9.3 0.0 collective-permute-done.1
  9.4 5.7 %collective-permute-start.6 = (bf16[6,8,16,128]{3,2,1,0:T(8,128)(2,1)S(1)}, bf16[6,8,16,128]{3,2,1,0:T(8,128)(2,1)S(1)}, u32[]{:S(2)}, u32[]{:S(2)}) collective-permute-start(bf16[6,8,16,128]{3,2,1,0:T(8,128)(2,1)S(1)} %maximum_select_fusion.1.refs_0_), channel_id=1, source_target_pairs={{0,128},{64,192},{128,256},{192,320},{256,384},{320,448},{384,0},{... | collective-permute-start | bytes 589832 | tf_op jit(solution)/shard_map/ppermute | solution.py:148
  15.1 3.4 %collective-permute-start.3 = (bf16[6,8,16,128]{3,2,1,0:T(8,128)(2,1)S(1)}, bf16[6,8,16,128]{3,2,1,0:T(8,128)(2,1)S(1)}, u32[]{:S(2)}, u32[]{:S(2)}) collective-permute-start(bf16[6,8,16,128]{3,2,1,0:T(8,128)(2,1)S(1)} %maximum_select_fusion.1.refs_0_), channel_id=1, source_target_pairs={{0,384},{64,448},{128,0},{192,64},{256,128},{320,192},{384,256},{4... | collective-permute-start | bytes 589832 | tf_op jit(solution)/shard_map/ppermute | solution.py:148
  18.5 0.0 copy-done
  18.6 6.7 %collective-permute-start.10 = (bf16[59,8,128]{2,1,0:T(8,128)(2,1)S(1)}, bf16[59,8,128]{2,1,0:T(8,128)(2,1)S(1)}, u32[]{:S(2)}, u32[]{:S(2)}) collective-permute-start(bf16[59,8,128]{2,1,0:T(8,128)(2,1)S(1)} %pad_maximum_fusion.1), channel_id=1, source_target_pairs={{0,32},{32,0},{1,33},{33,1},{2,34},{34,2},{3,35},{35,3},{4,36},{36... | collective-permute-start | bytes 362504 | tf_op jit(solution)/shard_map/ppermute | solution.py:158
  25.3 2.6 %collective-permute-start.9 = (bf16[6,8,16,128]{3,2,1,0:T(8,128)(2,1)S(1)}, bf16[6,8,16,128]{3,2,1,0:T(8,128)(2,1)S(1)}, u32[]{:S(2)}, u32[]{:S(2)}) collective-permute-start(bf16[6,8,16,128]{3,2,1,0:T(8,128)(2,1)S(1)} %maximum_select_fusion.1.refs_0_), channel_id=1, source_target_pairs={{0,64},{64,128},{128,192},{192,256},{256,320},{320,384},{384,448},... | collective-permute-start | bytes 589832 | tf_op jit(solution)/shard_map/ppermute | solution.py:148
  27.9 0.1 pad_add_fusion.place
  28.0 3.2 %collective-permute-start.2 = (bf16[6,8,16,128]{3,2,1,0:T(8,128)(2,1)S(1)}, bf16[6,8,16,128]{3,2,1,0:T(8,128)(2,1)S(1)}, u32[]{:S(2)}, u32[]{:S(2)}) collective-permute-start(bf16[6,8,16,128]{3,2,1,0:T(8,128)(2,1)S(1)} %maximum_select_fusion.1.refs_0_), channel_id=1, source_target_pairs={{0,448},{64,0},{128,64},{192,128},{256,192},{320,256},{384,320},{4... | collective-permute-start | bytes 589832 | tf_op jit(solution)/shard_map/ppermute | solution.py:148
  31.2 0.0 collective-permute-done.10
  31.3 0.0 collective-permute-done.6.refs_7_
  31.3 4.6 %collective-permute-start.8 = (bf16[6,8,16,128]{3,2,1,0:T(8,128)(2,1)S(1)}, bf16[6,8,16,128]{3,2,1,0:T(8,128)(2,1)S(1)}, u32[]{:S(2)}, u32[]{:S(2)}) collective-permute-start(bf16[6,8,16,128]{3,2,1,0:T(8,128)(2,1)S(1)} %collective-permute-done.6.refs_7_), channel_id=1, source_target_pairs={{0,64},{64,128},{128,192},{192,256},{256,320},{320,384},{384,448},... | collective-permute-start | bytes 589832 | tf_op jit(solution)/shard_map/ppermute | solution.py:148
  35.9 0.0 collective-permute-done.3.refs_2_
  35.9 1.9 %collective-permute-start.4 = (bf16[6,8,16,128]{3,2,1,0:T(8,128)(2,1)S(1)}, bf16[6,8,16,128]{3,2,1,0:T(8,128)(2,1)S(1)}, u32[]{:S(2)}, u32[]{:S(2)}) collective-permute-start(bf16[6,8,16,128]{3,2,1,0:T(8,128)(2,1)S(1)} %collective-permute-done.3.refs_2_), channel_id=1, source_target_pairs={{0,448},{64,0},{128,64},{192,128},{256,192},{320,256},{384,320},{4... | collective-permute-start | bytes 589832 | tf_op jit(solution)/shard_map/ppermute | solution.py:148
  37.9 7.8 %collective-permute-start.7 = (bf16[3,8,16,128]{3,2,1,0:T(8,128)(2,1)S(1)}, bf16[3,8,16,128]{3,2,1,0:T(8,128)(2,1)S(1)}, u32[]{:S(2)}, u32[]{:S(2)}) collective-permute-start(bf16[3,8,16,128]{3,2,1,0:T(8,128)(2,1)S(1)} %slice.57), channel_id=1, source_target_pairs={{0,128},{64,192},{128,256},{192,320},{256,384},{320,448},{384,0},{... | collective-permute-start | bytes 294920 | tf_op jit(solution)/shard_map/ppermute | solution.py:148
  45.7 0.0 collective-permute-done.9.refs_8_
  45.7 1.9 %collective-permute-start.5 = (bf16[3,8,16,128]{3,2,1,0:T(8,128)(2,1)S(1)}, bf16[3,8,16,128]{3,2,1,0:T(8,128)(2,1)S(1)}, u32[]{:S(2)}, u32[]{:S(2)}) collective-permute-start(bf16[3,8,16,128]{3,2,1,0:T(8,128)(2,1)S(1)} %slice.56), channel_id=1, source_target_pairs={{0,384},{64,448},{128,0},{192,64},{256,128},{320,192},{384,256},{4... | collective-permute-start | bytes 294920 | tf_op jit(solution)/shard_map/ppermute | solution.py:148
  47.6 0.0 collective-permute-done.2.refs_1_
  47.7 1.2 %collective-permute-done.7.refs_5_ = bf16[3,8,16,128]{3,2,1,0:T(8,128)(2,1)S(1)} collective-permute-done((bf16[3,8,16,128]{3,2,1,0:T(8,128)(2,1)S(1)}, bf16[3,8,16,128]{3,2,1,0:T(8,128)(2,1)S(1)}, u32[]{:S(2)}, u32[]{:S(2)}) %collective-permute-start.7) | collective-permute-done | bytes 98336 | tf_op jit(solution)/shard_map/ppermute | solution.py:148
  48.8 6.1 %collective-permute-done.5.refs_4_ = bf16[3,8,16,128]{3,2,1,0:T(8,128)(2,1)S(1)} collective-permute-done((bf16[3,8,16,128]{3,2,1,0:T(8,128)(2,1)S(1)}, bf16[3,8,16,128]{3,2,1,0:T(8,128)(2,1)S(1)}, u32[]{:S(2)}, u32[]{:S(2)}) %collective-permute-start.5) | collective-permute-done | bytes 98336 | tf_op jit(solution)/shard_map/ppermute | solution.py:148
  55.0 0.0 collective-permute-done.8.refs_6_
  55.0 0.0 collective-permute-done.4.refs_3_
  55.0 2.4 %shard_map.60 = f32[64,8,128]{2,1,0:T(8,128)} custom-call(s32[2]{0:T(128)S(1)} %pad_add_fusion.place, bf16[6,8,16,128]{3,2,1,0:T(8,128)(2,1)S(1)} %maximum_select_fusion.1.refs_0_, bf16[6,8,16,128]{3,2,1,0:T(8,128)(2,1)S(1)} %collective-permute-done.2.refs_1_, bf16[6,8,16,128]{3,2,1,0:T(8,128)(2,1)S(1)} %collective-permute-done.3.refs_2_, ...), custom_call_target="tpu_custom_call" | custom-call | flops 1000000000 | bytes 3000000 | tf_op jit(solution)/shard_map/pallas_call | solution.py:172
  57.4 12.8 %all-to-all-start = ((f32[64,8,128]{2,1,0:T(8,128)}), f32[64,8,128]{2,1,0:T(8,128)S(1)}, u32[]{:S(2)}, u32[]{:S(2)}) async-start(f32[64,8,128]{2,1,0:T(8,128)} %shard_map.60), calls=%async_computation | async-start | bytes 524288 | tf_op jit(solution)/shard_map/all_to_all | solution.py:183
  70.2 1.5 %shard_map.59 = f32[16,4,8,128]{3,2,1,0:T(8,128)S(1)} custom-call(s32[2]{0:T(128)S(1)} %pad_add_fusion.place, bf16[6,8,16,128]{3,2,1,0:T(8,128)(2,1)S(1)} %maximum_select_fusion.1.refs_0_, bf16[6,8,16,128]{3,2,1,0:T(8,128)(2,1)S(1)} %collective-permute-done.2.refs_1_, bf16[6,8,16,128]{3,2,1,0:T(8,128)(2,1)S(1)} %collective-permute-done.3.refs_2_, ...), custom_call_target="tpu_custom_call" | custom-call | flops 1000000000 | bytes 3000000 | tf_op jit(solution)/shard_map/pallas_call | solution.py:177
  71.8 0.0 copy-start.2
  71.8 3.6 %collective-permute-start.11 = (f32[8,4,8,128]{3,2,1,0:T(8,128)S(1)}, f32[8,4,8,128]{3,2,1,0:T(8,128)S(1)}, u32[]{:S(2)}, u32[]{:S(2)}) collective-permute-start(f32[8,4,8,128]{3,2,1,0:T(8,128)S(1)} %get-tuple-element.5), channel_id=1, source_target_pairs={{0,32},{32,0},{1,33},{33,1},{2,34},{34,2},{3,35},{35,3},{4,36},{36... | collective-permute-start | bytes 393224 | tf_op jit(solution)/shard_map/ppermute | solution.py:191
  75.4 0.0 copy-done.2
  75.4 5.8 %collective-permute-done.11 = f32[8,4,8,128]{3,2,1,0:T(8,128)S(1)} collective-permute-done((f32[8,4,8,128]{3,2,1,0:T(8,128)S(1)}, f32[8,4,8,128]{3,2,1,0:T(8,128)S(1)}, u32[]{:S(2)}, u32[]{:S(2)}) %collective-permute-start.11) | collective-permute-done | bytes 131104 | tf_op jit(solution)/shard_map/ppermute | solution.py:191
  81.2 0.8 fusion
  82.0 2.8 %all-to-all-done = f32[64,8,128]{2,1,0:T(8,128)S(1)} async-done(((f32[64,8,128]{2,1,0:T(8,128)}), f32[64,8,128]{2,1,0:T(8,128)S(1)}, u32[]{:S(2)}, u32[]{:S(2)}) %all-to-all-start) | async-done | bytes 262176 | tf_op jit(solution)/shard_map/all_to_all | solution.py:183
  84.8 0.1 reduce_sum.9
  84.8 0.1 fusion.3
  84.9 0.1 stack.24
  85.0 0.1 pad_maximum_fusion.3
  85.1 0.1 stack.26
  85.1 0.1 stack.25
  85.3 0.2 copy.16
  85.4 0.7 reshape.24
  (20 shorter events, 0.3 us)
Async XLA Ops:
  1.6 6.7 %collective-permute-start = (bf16[5,8,8,128]{3,2,1,0:T(8,128)(2,1)S(1)}, bf16[5,8,8,128]{3,2,1,0:T(8,128)(2,1)S(1)}, u32[]{:S(2)}, u32[]{:S(2)}) collective-permute-start(bf16[5,8,8,128]{3,2,1,0:T(8,128)(2,1)S(1)} %bitcast.23), channel_id=1, source_target_pairs={{0,32},{32,0},{1,33},{33,1},{2,34},{34,2},{3,35},{35,3},{4,36},{36... | collective-permute-start | bytes 245768 | tf_op jit(solution)/shard_map/ppermute | solution.py:129
  8.4 0.9 %copy-start.1 = (bf16[8,8,8,128]{3,2,1,0:T(8,128)(2,1)S(1)}, bf16[8,8,8,128]{3,2,1,0:T(8,128)(2,1)}, u32[]{:S(2)}) copy-start(bf16[8,8,8,128]{3,2,1,0:T(8,128)(2,1)} %param.5) | copy-start | bytes 393220
  8.4 0.9 %collective-permute-start.1 = (bf16[1,8,16,128]{3,2,1,0:T(8,128)(2,1)S(1)}, bf16[1,8,16,128]{3,2,1,0:T(8,128)(2,1)S(1)}, u32[]{:S(2)}, u32[]{:S(2)}) collective-permute-start(bf16[1,8,16,128]{3,2,1,0:T(8,128)(2,1)S(1)} %slice_select_fusion), channel_id=1, source_target_pairs={{32,1},{1,32},{33,2},{2,33},{34,3},{3,34},{35,4},{4,35},{36,5},{5,... | collective-permute-start | bytes 98312 | tf_op jit(solution)/shard_map/ppermute | solution.py:140
  9.3 9.2 %copy-start = (bf16[27,8,128]{2,1,0:T(8,128)(2,1)S(1)}, bf16[27,8,128]{2,1,0:T(8,128)(2,1)}, u32[]{:S(2)}) copy-start(bf16[27,8,128]{2,1,0:T(8,128)(2,1)} %param.6) | copy-start | bytes 165892
  9.4 21.9 %collective-permute-start.6 = (bf16[6,8,16,128]{3,2,1,0:T(8,128)(2,1)S(1)}, bf16[6,8,16,128]{3,2,1,0:T(8,128)(2,1)S(1)}, u32[]{:S(2)}, u32[]{:S(2)}) collective-permute-start(bf16[6,8,16,128]{3,2,1,0:T(8,128)(2,1)S(1)} %maximum_select_fusion.1.refs_0_), channel_id=1, source_target_pairs={{0,128},{64,192},{128,256},{192,320},{256,384},{320,448},{384,0},{... | collective-permute-start | bytes 589832 | tf_op jit(solution)/shard_map/ppermute | solution.py:148
  15.1 20.8 %collective-permute-start.3 = (bf16[6,8,16,128]{3,2,1,0:T(8,128)(2,1)S(1)}, bf16[6,8,16,128]{3,2,1,0:T(8,128)(2,1)S(1)}, u32[]{:S(2)}, u32[]{:S(2)}) collective-permute-start(bf16[6,8,16,128]{3,2,1,0:T(8,128)(2,1)S(1)} %maximum_select_fusion.1.refs_0_), channel_id=1, source_target_pairs={{0,384},{64,448},{128,0},{192,64},{256,128},{320,192},{384,256},{4... | collective-permute-start | bytes 589832 | tf_op jit(solution)/shard_map/ppermute | solution.py:148
  18.6 12.7 %collective-permute-start.10 = (bf16[59,8,128]{2,1,0:T(8,128)(2,1)S(1)}, bf16[59,8,128]{2,1,0:T(8,128)(2,1)S(1)}, u32[]{:S(2)}, u32[]{:S(2)}) collective-permute-start(bf16[59,8,128]{2,1,0:T(8,128)(2,1)S(1)} %pad_maximum_fusion.1), channel_id=1, source_target_pairs={{0,32},{32,0},{1,33},{33,1},{2,34},{34,2},{3,35},{35,3},{4,36},{36... | collective-permute-start | bytes 362504 | tf_op jit(solution)/shard_map/ppermute | solution.py:158
  25.3 20.4 %collective-permute-start.9 = (bf16[6,8,16,128]{3,2,1,0:T(8,128)(2,1)S(1)}, bf16[6,8,16,128]{3,2,1,0:T(8,128)(2,1)S(1)}, u32[]{:S(2)}, u32[]{:S(2)}) collective-permute-start(bf16[6,8,16,128]{3,2,1,0:T(8,128)(2,1)S(1)} %maximum_select_fusion.1.refs_0_), channel_id=1, source_target_pairs={{0,64},{64,128},{128,192},{192,256},{256,320},{320,384},{384,448},... | collective-permute-start | bytes 589832 | tf_op jit(solution)/shard_map/ppermute | solution.py:148
  28.0 19.7 %collective-permute-start.2 = (bf16[6,8,16,128]{3,2,1,0:T(8,128)(2,1)S(1)}, bf16[6,8,16,128]{3,2,1,0:T(8,128)(2,1)S(1)}, u32[]{:S(2)}, u32[]{:S(2)}) collective-permute-start(bf16[6,8,16,128]{3,2,1,0:T(8,128)(2,1)S(1)} %maximum_select_fusion.1.refs_0_), channel_id=1, source_target_pairs={{0,448},{64,0},{128,64},{192,128},{256,192},{320,256},{384,320},{4... | collective-permute-start | bytes 589832 | tf_op jit(solution)/shard_map/ppermute | solution.py:148
  31.3 23.7 %collective-permute-start.8 = (bf16[6,8,16,128]{3,2,1,0:T(8,128)(2,1)S(1)}, bf16[6,8,16,128]{3,2,1,0:T(8,128)(2,1)S(1)}, u32[]{:S(2)}, u32[]{:S(2)}) collective-permute-start(bf16[6,8,16,128]{3,2,1,0:T(8,128)(2,1)S(1)} %collective-permute-done.6.refs_7_), channel_id=1, source_target_pairs={{0,64},{64,128},{128,192},{192,256},{256,320},{320,384},{384,448},... | collective-permute-start | bytes 589832 | tf_op jit(solution)/shard_map/ppermute | solution.py:148
  35.9 19.1 %collective-permute-start.4 = (bf16[6,8,16,128]{3,2,1,0:T(8,128)(2,1)S(1)}, bf16[6,8,16,128]{3,2,1,0:T(8,128)(2,1)S(1)}, u32[]{:S(2)}, u32[]{:S(2)}) collective-permute-start(bf16[6,8,16,128]{3,2,1,0:T(8,128)(2,1)S(1)} %collective-permute-done.3.refs_2_), channel_id=1, source_target_pairs={{0,448},{64,0},{128,64},{192,128},{256,192},{320,256},{384,320},{4... | collective-permute-start | bytes 589832 | tf_op jit(solution)/shard_map/ppermute | solution.py:148
  37.9 11.0 %collective-permute-start.7 = (bf16[3,8,16,128]{3,2,1,0:T(8,128)(2,1)S(1)}, bf16[3,8,16,128]{3,2,1,0:T(8,128)(2,1)S(1)}, u32[]{:S(2)}, u32[]{:S(2)}) collective-permute-start(bf16[3,8,16,128]{3,2,1,0:T(8,128)(2,1)S(1)} %slice.57), channel_id=1, source_target_pairs={{0,128},{64,192},{128,256},{192,320},{256,384},{320,448},{384,0},{... | collective-permute-start | bytes 294920 | tf_op jit(solution)/shard_map/ppermute | solution.py:148
  45.7 9.3 %collective-permute-start.5 = (bf16[3,8,16,128]{3,2,1,0:T(8,128)(2,1)S(1)}, bf16[3,8,16,128]{3,2,1,0:T(8,128)(2,1)S(1)}, u32[]{:S(2)}, u32[]{:S(2)}) collective-permute-start(bf16[3,8,16,128]{3,2,1,0:T(8,128)(2,1)S(1)} %slice.56), channel_id=1, source_target_pairs={{0,384},{64,448},{128,0},{192,64},{256,128},{320,192},{384,256},{4... | collective-permute-start | bytes 294920 | tf_op jit(solution)/shard_map/ppermute | solution.py:148
  57.4 27.4 %all-to-all-start = ((f32[64,8,128]{2,1,0:T(8,128)}), f32[64,8,128]{2,1,0:T(8,128)S(1)}, u32[]{:S(2)}, u32[]{:S(2)}) async-start(f32[64,8,128]{2,1,0:T(8,128)} %shard_map.60), calls=%async_computation | async-start | bytes 524288 | tf_op jit(solution)/shard_map/all_to_all | solution.py:183
  71.8 3.6 %copy-start.2 = (bf16[8]{0:T(256)(128)(2,1)S(1)}, bf16[8]{0:T(256)(128)(2,1)}, u32[]{:S(2)}) copy-start(bf16[8]{0:T(256)(128)(2,1)} %param.7) | copy-start | bytes 52
  71.8 9.4 %collective-permute-start.11 = (f32[8,4,8,128]{3,2,1,0:T(8,128)S(1)}, f32[8,4,8,128]{3,2,1,0:T(8,128)S(1)}, u32[]{:S(2)}, u32[]{:S(2)}) collective-permute-start(f32[8,4,8,128]{3,2,1,0:T(8,128)S(1)} %get-tuple-element.5), channel_id=1, source_target_pairs={{0,32},{32,0},{1,33},{33,1},{2,34},{34,2},{3,35},{35,3},{4,36},{36... | collective-permute-start | bytes 393224 | tf_op jit(solution)/shard_map/ppermute | solution.py:191

commit v3 on v2

--- a/solution.py
+++ b/solution.py
@@ -16,18 +16,11 @@
 STEPS = 8
 
 
-def block_of(blocks, j, row, z):
-    b0, b1, b2, b3, b4a, b4b, b5, b6, b7 = blocks
-    if j == 4:
-        return b4a[row, z] if row < 3 else b4b[row - 3, z]
-    return (b0, b1, b2, b3, None, b5, b6, b7)[j][row, z]
-
-
 def cells_of(blocks, row):
     return jnp.concatenate(
         [
             jnp.concatenate(
-                [block_of(blocks, j, row + dx, z) for dx in range(3) for j in range(STEPS)],
+                [blocks[j][row + dx, z] for dx in range(3) for j in range(STEPS)],
                 axis=0,
             )
             for z in range(DEPTH)
@@ -137,7 +130,13 @@
         jnp.concatenate([own, other], axis=2),
         jnp.concatenate([other, own], axis=2),
     )
+    give = jnp.concatenate(
+        [lax.dynamic_slice_in_dim(cots, 4 * (1 - zl), 4, 0).reshape(32, 8, WIDTH), filters], axis=0
+    )
+    got = lax.ppermute(give, "zl", swap)
+
     edge = lax.ppermute(jnp.where(first, body[0:1], body[4:5]), ("zl",) + SPACE, pairs)
+    edge, got = lax.optimization_barrier((edge, got))
     mine = jnp.where(
         first,
         jnp.concatenate([edge, body], axis=0),
@@ -149,22 +148,23 @@
 
     b2, b6 = along(mine, 2), along(mine, -2)
     b1, b7 = along(mine, 1), along(mine, -1)
+    turn = [
+        ((2 * i + c), (2 * ((i + (2 if c else -2)) % STEPS) + c))
+        for i in range(STEPS)
+        for c in range(2)
+    ]
+    b4 = lax.ppermute(jnp.where(lax.axis_index("core") == 0, b2, b6), ("y", "core"), turn)
     b3, b5 = along(b2, 1), along(b6, -1)
-    b4a, b4b = along(b2[:3], 2), along(b6[3:], -2)
-
-    give = jnp.concatenate(
-        [lax.dynamic_slice_in_dim(cots, 4 * (1 - zl), 4, 0).reshape(32, 8, WIDTH), filters], axis=0
-    )
-    got = lax.ppermute(give, "zl", swap)
+
     keep = lax.dynamic_slice_in_dim(cots, 4 * zl, 4, 0)
     cot = jnp.concatenate([keep, got[:32].reshape(4, 8, 8, WIDTH)], axis=2)
     weights = jnp.concatenate([filters, got[32:]], axis=1)
 
-    blocks = (mine, b1, b2, b3, b4a, b4b, b5, b6, b7)
+    blocks = (mine, b1, b2, b3, b4, b5, b6, b7)
     place = jnp.stack([y, zl])
     vmem = pl.BlockSpec(memory_space=pltpu.VMEM)
     settings = dict(
-        in_specs=[pl.BlockSpec(memory_space=pltpu.SMEM)] + [vmem] * 10,
+        in_specs=[pl.BlockSpec(memory_space=pltpu.SMEM)] + [vmem] * 9,
         out_specs=vmem,
         compiler_params=pltpu.CompilerParams(vmem_limit_bytes=48 * 1024 * 1024),
         cost_estimate=pl.CostEstimate(flops=10**9, bytes_accessed=3 * 10**6, transcendentals=0),

time: 86.7 us -> 84.2 us (0.971)
  the two profiles are of different devices: /device:TPU:16 before, /device:TPU:24 now
where the time goes in v3:
time: 84.2 us; the launch traced here: 83.6 us
  starting transfers between devices  49.2 us (58%)
  waiting for transfers between devices  25.2 us (30%)
  Pallas kernels  3.97 us (5%)
  local copies, waits for them, and re-layouts  3.08 us (4%)
  other arithmetic  1.19 us (1%)
  between operations  0.97 us (1%)
    ppermute x6, starting transfers between devices, along(): lax.ppermute(block, 'y', [(i, (i - by) % STEPS) for i in range(STEPS)])  22.4 us
    all_to_all x1, starting transfers between devices, on_device(): got = lax.all_to_all(grad, ('zl',) + SPACE, 0, 0, tiled=True)  14.2 us
    ppermute x6, waiting for transfers between devices, along(): lax.ppermute(block, 'y', [(i, (i - by) % STEPS) for i in range(STEPS)])  11 us
    ppermute x1, waiting for transfers between devices, on_device(): rest = lax.ppermute(feat[8:], 'zl', swap)  5.74 us
    ppermute x1, starting transfers between devices, on_device(): lax.ppermute(lax.dynamic_slice_in_dim(acts, 3 * (1 - zl), 5, 0), 'zl', swap)  4.41 us
    ppermute x1, waiting for transfers between devices, on_device(): got = lax.ppermute(give, 'zl', swap)  4.04 us
    ppermute x1, starting transfers between devices, on_device(): rest = lax.ppermute(feat[8:], 'zl', swap)  3.58 us
    all_to_all x1, waiting for transfers between devices, on_device(): got = lax.all_to_all(grad, ('zl',) + SPACE, 0, 0, tiled=True)  2.78 us
  transfers between devices with their start and end apart: 12, of which 7 were waited for; matrix products, arithmetic and copies ran while one was open for 1% of the time, Pallas kernels for 2%

profile of v3, /device:TPU:24, one launch (start us, length us, event | category | flops | bytes accessed | tf_op | source)
XLA Modules:
  0.0 83.6 jit_solution(16172498064442437649)
XLA Ops:
  0.6 1.0 %constant_dynamic-slice_fusion.2 = (bf16[8,5,8,128]{3,2,1,0:T(8,128)(2,1)S(1)}, bf16[8,5,8,128]{3,2,1,0:T(8,128)(2,1)S(1)}) fusion(bf16[8,8,8,128]{3,2,1,0:T(8,128)(2,1)} %param.4, s32[]{:T(128)S(6)} %select_n.54, s32[]{:T(128)S(6)} %select_n.55), kind=kLoop, calls=%fused_computation.18 | loop fusion | bytes 327688 | tf_op jit(solution)/shard_map/dynamic-slice
  1.6 0.0 copy-start.2
  1.7 4.4 %collective-permute-start = (bf16[5,8,8,128]{3,2,1,0:T(8,128)(2,1)S(1)}, bf16[5,8,8,128]{3,2,1,0:T(8,128)(2,1)S(1)}, u32[]{:S(2)}, u32[]{:S(2)}) collective-permute-start(bf16[5,8,8,128]{3,2,1,0:T(8,128)(2,1)S(1)} %bitcast.23), channel_id=1, source_target_pairs={{0,32},{32,0},{1,33},{33,1},{2,34},{34,2},{3,35},{35,3},{4,36},{36... | collective-permute-start | bytes 245768 | tf_op jit(solution)/shard_map/ppermute | solution.py:122
  6.1 0.0 copy-done.2
  6.1 0.0 copy-start.1
  6.2 0.8 copy-done.1
  6.9 1.9 %collective-permute-start.2 = (bf16[59,8,128]{2,1,0:T(8,128)(2,1)S(1)}, bf16[59,8,128]{2,1,0:T(8,128)(2,1)S(1)}, u32[]{:S(2)}, u32[]{:S(2)}) collective-permute-start(bf16[59,8,128]{2,1,0:T(8,128)(2,1)S(1)} %pad_maximum_fusion.1), channel_id=1, source_target_pairs={{0,32},{32,0},{1,33},{33,1},{2,34},{34,2},{3,35},{35,3},{4,36},{36... | collective-permute-start | bytes 362504 | tf_op jit(solution)/shard_map/ppermute | solution.py:136
  8.9 0.0 collective-permute-done
  9.0 0.7 collective-permute-start.1
  9.7 0.0 collective-permute-done.1
  9.7 4.0 %collective-permute-done.2 = bf16[59,8,128]{2,1,0:T(8,128)(2,1)S(1)} collective-permute-done((bf16[59,8,128]{2,1,0:T(8,128)(2,1)S(1)}, bf16[59,8,128]{2,1,0:T(8,128)(2,1)S(1)}, u32[]{:S(2)}, u32[]{:S(2)}) %collective-permute-start.2) | collective-permute-done | bytes 120864 | tf_op jit(solution)/shard_map/ppermute | solution.py:136
  13.7 0.0 copy-start
  13.7 4.8 %collective-permute-start.6 = (bf16[6,8,16,128]{3,2,1,0:T(8,128)(2,1)S(1)}, bf16[6,8,16,128]{3,2,1,0:T(8,128)(2,1)S(1)}, u32[]{:S(2)}, u32[]{:S(2)}) collective-permute-start(bf16[6,8,16,128]{3,2,1,0:T(8,128)(2,1)S(1)} %maximum_select_fusion.1.refs_0_), channel_id=1, source_target_pairs={{0,128},{64,192},{128,256},{192,320},{256,384},{320,448},{384,0},{... | collective-permute-start | bytes 589832 | tf_op jit(solution)/shard_map/ppermute | solution.py:147
  18.5 1.9 %collective-permute-start.4 = (bf16[6,8,16,128]{3,2,1,0:T(8,128)(2,1)S(1)}, bf16[6,8,16,128]{3,2,1,0:T(8,128)(2,1)S(1)}, u32[]{:S(2)}, u32[]{:S(2)}) collective-permute-start(bf16[6,8,16,128]{3,2,1,0:T(8,128)(2,1)S(1)} %maximum_select_fusion.1.refs_0_), channel_id=1, source_target_pairs={{0,384},{64,448},{128,0},{192,64},{256,128},{320,192},{384,256},{4... | collective-permute-start | bytes 589832 | tf_op jit(solution)/shard_map/ppermute | solution.py:147
  20.5 0.1 pad_add_fusion.place
  20.6 0.0 copy-done
  20.6 0.0 slice-start
  20.6 6.0 %collective-permute-start.9 = (bf16[6,8,16,128]{3,2,1,0:T(8,128)(2,1)S(1)}, bf16[6,8,16,128]{3,2,1,0:T(8,128)(2,1)S(1)}, u32[]{:S(2)}, u32[]{:S(2)}) collective-permute-start(bf16[6,8,16,128]{3,2,1,0:T(8,128)(2,1)S(1)} %maximum_select_fusion.1.refs_0_), channel_id=1, source_target_pairs={{0,64},{64,128},{128,192},{192,256},{256,320},{320,384},{384,448},... | collective-permute-start | bytes 589832 | tf_op jit(solution)/shard_map/ppermute | solution.py:147
  26.7 1.9 %collective-permute-start.3 = (bf16[6,8,16,128]{3,2,1,0:T(8,128)(2,1)S(1)}, bf16[6,8,16,128]{3,2,1,0:T(8,128)(2,1)S(1)}, u32[]{:S(2)}, u32[]{:S(2)}) collective-permute-start(bf16[6,8,16,128]{3,2,1,0:T(8,128)(2,1)S(1)} %maximum_select_fusion.1.refs_0_), channel_id=1, source_target_pairs={{0,448},{64,0},{128,64},{192,128},{256,192},{320,256},{384,320},{4... | collective-permute-start | bytes 589832 | tf_op jit(solution)/shard_map/ppermute | solution.py:147
  28.6 0.0 collective-permute-done.6.refs_6_
  28.6 5.9 %collective-permute-done.4.refs_2_ = bf16[6,8,16,128]{3,2,1,0:T(8,128)(2,1)S(1)} collective-permute-done((bf16[6,8,16,128]{3,2,1,0:T(8,128)(2,1)S(1)}, bf16[6,8,16,128]{3,2,1,0:T(8,128)(2,1)S(1)}, u32[]{:S(2)}, u32[]{:S(2)}) %collective-permute-start.4) | collective-permute-done | bytes 196640 | tf_op jit(solution)/shard_map/ppermute | solution.py:147
  34.5 0.0 slice-start.1
  34.5 2.1 %collective-permute-start.7 = (bf16[6,8,16,128]{3,2,1,0:T(8,128)(2,1)S(1)}, bf16[6,8,16,128]{3,2,1,0:T(8,128)(2,1)S(1)}, u32[]{:S(2)}, u32[]{:S(2)}) collective-permute-start(bf16[6,8,16,128]{3,2,1,0:T(8,128)(2,1)S(1)} %broadcast_select_fusion), channel_id=1, source_target_pairs={{0,384},{1,129},{64,448},{65,193},{128,0},{129,257},{192,64},{193,... | collective-permute-start | bytes 589832 | tf_op jit(solution)/shard_map/ppermute | solution.py:156
  36.6 5.8 %collective-permute-start.8 = (bf16[6,8,16,128]{3,2,1,0:T(8,128)(2,1)S(1)}, bf16[6,8,16,128]{3,2,1,0:T(8,128)(2,1)S(1)}, u32[]{:S(2)}, u32[]{:S(2)}) collective-permute-start(bf16[6,8,16,128]{3,2,1,0:T(8,128)(2,1)S(1)} %collective-permute-done.6.refs_6_), channel_id=1, source_target_pairs={{0,64},{64,128},{128,192},{192,256},{256,320},{320,384},{384,448},... | collective-permute-start | bytes 589832 | tf_op jit(solution)/shard_map/ppermute | solution.py:147
  42.3 1.9 %collective-permute-start.5 = (bf16[6,8,16,128]{3,2,1,0:T(8,128)(2,1)S(1)}, bf16[6,8,16,128]{3,2,1,0:T(8,128)(2,1)S(1)}, u32[]{:S(2)}, u32[]{:S(2)}) collective-permute-start(bf16[6,8,16,128]{3,2,1,0:T(8,128)(2,1)S(1)} %collective-permute-done.4.refs_2_), channel_id=1, source_target_pairs={{0,448},{64,0},{128,64},{192,128},{256,192},{320,256},{384,320},{4... | collective-permute-start | bytes 589832 | tf_op jit(solution)/shard_map/ppermute | solution.py:147
  44.3 0.0 slice-done
  44.3 0.0 slice-done.1
  44.3 0.0 collective-permute-done.9.refs_7_
  44.3 0.0 collective-permute-done.3.refs_1_
  44.4 2.2 %collective-permute-done.8.refs_5_ = bf16[6,8,16,128]{3,2,1,0:T(8,128)(2,1)S(1)} collective-permute-done((bf16[6,8,16,128]{3,2,1,0:T(8,128)(2,1)S(1)}, bf16[6,8,16,128]{3,2,1,0:T(8,128)(2,1)S(1)}, u32[]{:S(2)}, u32[]{:S(2)}) %collective-permute-start.8) | collective-permute-done | bytes 196640 | tf_op jit(solution)/shard_map/ppermute | solution.py:147
  46.6 1.6 %collective-permute-done.7.refs_4_ = bf16[6,8,16,128]{3,2,1,0:T(8,128)(2,1)S(1)} collective-permute-done((bf16[6,8,16,128]{3,2,1,0:T(8,128)(2,1)S(1)}, bf16[6,8,16,128]{3,2,1,0:T(8,128)(2,1)S(1)}, u32[]{:S(2)}, u32[]{:S(2)}) %collective-permute-start.7) | collective-permute-done | bytes 196640 | tf_op jit(solution)/shard_map/ppermute | solution.py:156
  48.2 2.9 %collective-permute-done.5.refs_3_ = bf16[6,8,16,128]{3,2,1,0:T(8,128)(2,1)S(1)} collective-permute-done((bf16[6,8,16,128]{3,2,1,0:T(8,128)(2,1)S(1)}, bf16[6,8,16,128]{3,2,1,0:T(8,128)(2,1)S(1)}, u32[]{:S(2)}, u32[]{:S(2)}) %collective-permute-start.5) | collective-permute-done | bytes 196640 | tf_op jit(solution)/shard_map/ppermute | solution.py:147
  51.1 2.4 %shard_map.60 = f32[64,8,128]{2,1,0:T(8,128)} custom-call(s32[2]{0:T(128)S(1)} %pad_add_fusion.place, bf16[6,8,16,128]{3,2,1,0:T(8,128)(2,1)S(1)} %maximum_select_fusion.1.refs_0_, bf16[6,8,16,128]{3,2,1,0:T(8,128)(2,1)S(1)} %collective-permute-done.3.refs_1_, bf16[6,8,16,128]{3,2,1,0:T(8,128)(2,1)S(1)} %collective-permute-done.4.refs_2_, ...), custom_call_target="tpu_custom_call" | custom-call | flops 1000000000 | bytes 3000000 | tf_op jit(solution)/shard_map/pallas_call | solution.py:172
  53.5 14.2 %all-to-all-start = ((f32[64,8,128]{2,1,0:T(8,128)}), f32[64,8,128]{2,1,0:T(8,128)S(1)}, u32[]{:S(2)}, u32[]{:S(2)}) async-start(f32[64,8,128]{2,1,0:T(8,128)} %shard_map.60), calls=%async_computation | async-start | bytes 524288 | tf_op jit(solution)/shard_map/all_to_all | solution.py:183
  67.7 1.5 %shard_map.59 = f32[16,4,8,128]{3,2,1,0:T(8,128)S(1)} custom-call(s32[2]{0:T(128)S(1)} %pad_add_fusion.place, bf16[6,8,16,128]{3,2,1,0:T(8,128)(2,1)S(1)} %maximum_select_fusion.1.refs_0_, bf16[6,8,16,128]{3,2,1,0:T(8,128)(2,1)S(1)} %collective-permute-done.3.refs_1_, bf16[6,8,16,128]{3,2,1,0:T(8,128)(2,1)S(1)} %collective-permute-done.4.refs_2_, ...), custom_call_target="tpu_custom_call" | custom-call | flops 1000000000 | bytes 3000000 | tf_op jit(solution)/shard_map/pallas_call | solution.py:177
  69.3 0.0 copy-start.3
  69.3 3.6 %collective-permute-start.10 = (f32[8,4,8,128]{3,2,1,0:T(8,128)S(1)}, f32[8,4,8,128]{3,2,1,0:T(8,128)S(1)}, u32[]{:S(2)}, u32[]{:S(2)}) collective-permute-start(f32[8,4,8,128]{3,2,1,0:T(8,128)S(1)} %get-tuple-element.9), channel_id=1, source_target_pairs={{0,32},{32,0},{1,33},{33,1},{2,34},{34,2},{3,35},{35,3},{4,36},{36... | collective-permute-start | bytes 393224 | tf_op jit(solution)/shard_map/ppermute | solution.py:191
  72.9 0.0 copy-done.3
  72.9 5.7 %collective-permute-done.10 = f32[8,4,8,128]{3,2,1,0:T(8,128)S(1)} collective-permute-done((f32[8,4,8,128]{3,2,1,0:T(8,128)S(1)}, f32[8,4,8,128]{3,2,1,0:T(8,128)S(1)}, u32[]{:S(2)}, u32[]{:S(2)}) %collective-permute-start.10) | collective-permute-done | bytes 131104 | tf_op jit(solution)/shard_map/ppermute | solution.py:191
  78.7 0.8 fusion
  79.5 2.8 %all-to-all-done = f32[64,8,128]{2,1,0:T(8,128)S(1)} async-done(((f32[64,8,128]{2,1,0:T(8,128)}), f32[64,8,128]{2,1,0:T(8,128)S(1)}, u32[]{:S(2)}, u32[]{:S(2)}) %all-to-all-start) | async-done | bytes 262176 | tf_op jit(solution)/shard_map/all_to_all | solution.py:183
  82.2 0.1 reduce_sum.9
  82.3 0.1 fusion.3
  82.4 0.1 stack.24
  82.5 0.1 pad_maximum_fusion.3
  82.5 0.1 stack.26
  82.6 0.1 stack.25
  82.7 0.2 copy.16
  82.9 0.7 reshape.24
  (17 shorter events, 0.3 us)
Async XLA Ops:
  1.6 4.5 %copy-start.2 = (bf16[8,8,8,128]{3,2,1,0:T(8,128)(2,1)S(1)}, bf16[8,8,8,128]{3,2,1,0:T(8,128)(2,1)}, u32[]{:S(2)}) copy-start(bf16[8,8,8,128]{3,2,1,0:T(8,128)(2,1)} %param.5) | copy-start | bytes 393220
  1.7 7.2 %collective-permute-start = (bf16[5,8,8,128]{3,2,1,0:T(8,128)(2,1)S(1)}, bf16[5,8,8,128]{3,2,1,0:T(8,128)(2,1)S(1)}, u32[]{:S(2)}, u32[]{:S(2)}) collective-permute-start(bf16[5,8,8,128]{3,2,1,0:T(8,128)(2,1)S(1)} %bitcast.23), channel_id=1, source_target_pairs={{0,32},{32,0},{1,33},{33,1},{2,34},{34,2},{3,35},{35,3},{4,36},{36... | collective-permute-start | bytes 245768 | tf_op jit(solution)/shard_map/ppermute | solution.py:122
  6.1 0.8 copy-start.1
  6.9 6.8 %collective-permute-start.2 = (bf16[59,8,128]{2,1,0:T(8,128)(2,1)S(1)}, bf16[59,8,128]{2,1,0:T(8,128)(2,1)S(1)}, u32[]{:S(2)}, u32[]{:S(2)}) collective-permute-start(bf16[59,8,128]{2,1,0:T(8,128)(2,1)S(1)} %pad_maximum_fusion.1), channel_id=1, source_target_pairs={{0,32},{32,0},{1,33},{33,1},{2,34},{34,2},{3,35},{35,3},{4,36},{36... | collective-permute-start | bytes 362504 | tf_op jit(solution)/shard_map/ppermute | solution.py:136
  9.0 0.7 collective-permute-start.1
  13.7 6.9 %copy-start = (bf16[59,8,128]{2,1,0:T(8,128)(2,1)}, bf16[59,8,128]{2,1,0:T(8,128)(2,1)S(1)}, u32[]{:S(2)}) copy-start(bf16[59,8,128]{2,1,0:T(8,128)(2,1)S(1)} %collective-permute-done.2) | copy-start | bytes 362500
  13.7 14.9 %collective-permute-start.6 = (bf16[6,8,16,128]{3,2,1,0:T(8,128)(2,1)S(1)}, bf16[6,8,16,128]{3,2,1,0:T(8,128)(2,1)S(1)}, u32[]{:S(2)}, u32[]{:S(2)}) collective-permute-start(bf16[6,8,16,128]{3,2,1,0:T(8,128)(2,1)S(1)} %maximum_select_fusion.1.refs_0_), channel_id=1, source_target_pairs={{0,128},{64,192},{128,256},{192,320},{256,384},{320,448},{384,0},{... | collective-permute-start | bytes 589832 | tf_op jit(solution)/shard_map/ppermute | solution.py:147
  18.5 15.9 %collective-permute-start.4 = (bf16[6,8,16,128]{3,2,1,0:T(8,128)(2,1)S(1)}, bf16[6,8,16,128]{3,2,1,0:T(8,128)(2,1)S(1)}, u32[]{:S(2)}, u32[]{:S(2)}) collective-permute-start(bf16[6,8,16,128]{3,2,1,0:T(8,128)(2,1)S(1)} %maximum_select_fusion.1.refs_0_), channel_id=1, source_target_pairs={{0,384},{64,448},{128,0},{192,64},{256,128},{320,192},{384,256},{4... | collective-permute-start | bytes 589832 | tf_op jit(solution)/shard_map/ppermute | solution.py:147
  20.6 23.6 %slice-start = ((bf16[59,8,128]{2,1,0:T(8,128)(2,1)}), bf16[27,8,128]{2,1,0:T(8,128)(2,1)S(1)}, s32[]{:S(2)}) async-start(bf16[59,8,128]{2,1,0:T(8,128)(2,1)} %copy-done), calls=%async_computation.1 | async-start | bytes 110592 | tf_op jit(solution)/shard_map/slice | solution.py:161
  20.6 23.7 %collective-permute-start.9 = (bf16[6,8,16,128]{3,2,1,0:T(8,128)(2,1)S(1)}, bf16[6,8,16,128]{3,2,1,0:T(8,128)(2,1)S(1)}, u32[]{:S(2)}, u32[]{:S(2)}) collective-permute-start(bf16[6,8,16,128]{3,2,1,0:T(8,128)(2,1)S(1)} %maximum_select_fusion.1.refs_0_), channel_id=1, source_target_pairs={{0,64},{64,128},{128,192},{192,256},{256,320},{320,384},{384,448},... | collective-permute-start | bytes 589832 | tf_op jit(solution)/shard_map/ppermute | solution.py:147
  26.7 17.7 %collective-permute-start.3 = (bf16[6,8,16,128]{3,2,1,0:T(8,128)(2,1)S(1)}, bf16[6,8,16,128]{3,2,1,0:T(8,128)(2,1)S(1)}, u32[]{:S(2)}, u32[]{:S(2)}) collective-permute-start(bf16[6,8,16,128]{3,2,1,0:T(8,128)(2,1)S(1)} %maximum_select_fusion.1.refs_0_), channel_id=1, source_target_pairs={{0,448},{64,0},{128,64},{192,128},{256,192},{320,256},{384,320},{4... | collective-permute-start | bytes 589832 | tf_op jit(solution)/shard_map/ppermute | solution.py:147
  34.5 9.8 %slice-start.1 = ((bf16[59,8,128]{2,1,0:T(8,128)(2,1)}), bf16[32,8,128]{2,1,0:T(8,128)(2,1)S(1)}, s32[]{:S(2)}) async-start(bf16[59,8,128]{2,1,0:T(8,128)(2,1)} %copy-done), calls=%async_computation.2 | async-start | bytes 131072 | tf_op jit(solution)/shard_map/slice | solution.py:160
  34.5 13.7 %collective-permute-start.7 = (bf16[6,8,16,128]{3,2,1,0:T(8,128)(2,1)S(1)}, bf16[6,8,16,128]{3,2,1,0:T(8,128)(2,1)S(1)}, u32[]{:S(2)}, u32[]{:S(2)}) collective-permute-start(bf16[6,8,16,128]{3,2,1,0:T(8,128)(2,1)S(1)} %broadcast_select_fusion), channel_id=1, source_target_pairs={{0,384},{1,129},{64,448},{65,193},{128,0},{129,257},{192,64},{193,... | collective-permute-start | bytes 589832 | tf_op jit(solution)/shard_map/ppermute | solution.py:156
  36.6 10.0 %collective-permute-start.8 = (bf16[6,8,16,128]{3,2,1,0:T(8,128)(2,1)S(1)}, bf16[6,8,16,128]{3,2,1,0:T(8,128)(2,1)S(1)}, u32[]{:S(2)}, u32[]{:S(2)}) collective-permute-start(bf16[6,8,16,128]{3,2,1,0:T(8,128)(2,1)S(1)} %collective-permute-done.6.refs_6_), channel_id=1, source_target_pairs={{0,64},{64,128},{128,192},{192,256},{256,320},{320,384},{384,448},... | collective-permute-start | bytes 589832 | tf_op jit(solution)/shard_map/ppermute | solution.py:147
  42.3 8.8 %collective-permute-start.5 = (bf16[6,8,16,128]{3,2,1,0:T(8,128)(2,1)S(1)}, bf16[6,8,16,128]{3,2,1,0:T(8,128)(2,1)S(1)}, u32[]{:S(2)}, u32[]{:S(2)}) collective-permute-start(bf16[6,8,16,128]{3,2,1,0:T(8,128)(2,1)S(1)} %collective-permute-done.4.refs_2_), channel_id=1, source_target_pairs={{0,448},{64,0},{128,64},{192,128},{256,192},{320,256},{384,320},{4... | collective-permute-start | bytes 589832 | tf_op jit(solution)/shard_map/ppermute | solution.py:147
  53.5 28.7 %all-to-all-start = ((f32[64,8,128]{2,1,0:T(8,128)}), f32[64,8,128]{2,1,0:T(8,128)S(1)}, u32[]{:S(2)}, u32[]{:S(2)}) async-start(f32[64,8,128]{2,1,0:T(8,128)} %shard_map.60), calls=%async_computation | async-start | bytes 524288 | tf_op jit(solution)/shard_map/all_to_all | solution.py:183
  69.3 3.6 %copy-start.3 = (bf16[8]{0:T(256)(128)(2,1)S(1)}, bf16[8]{0:T(256)(128)(2,1)}, u32[]{:S(2)}) copy-start(bf16[8]{0:T(256)(128)(2,1)} %param.7) | copy-start | bytes 52
  69.3 9.4 %collective-permute-start.10 = (f32[8,4,8,128]{3,2,1,0:T(8,128)S(1)}, f32[8,4,8,128]{3,2,1,0:T(8,128)S(1)}, u32[]{:S(2)}, u32[]{:S(2)}) collective-permute-start(f32[8,4,8,128]{3,2,1,0:T(8,128)S(1)} %get-tuple-element.9), channel_id=1, source_target_pairs={{0,32},{32,0},{1,33},{33,1},{2,34},{34,2},{3,35},{35,3},{4,36},{36... | collective-permute-start | bytes 393224 | tf_op jit(solution)/shard_map/ppermute | solution.py:191

commit v4 on v3

--- a/solution.py
+++ b/solution.py
@@ -16,12 +16,21 @@
 STEPS = 8
 
 
-def cells_of(blocks, row):
+def fill(rows, place, blocks, edges):
+    zl = place[1]
+    for p, block in enumerate(blocks):
+        rows[p, pl.ds(1 - zl, 5)] = block[...]
+    at = 0
+    for edge in edges:
+        rows[pl.ds(at, edge.shape[0]), 5 * zl] = edge[...]
+        at += edge.shape[0]
+
+
+def cells_of(rows, count, row):
     return jnp.concatenate(
         [
             jnp.concatenate(
-                [blocks[j][row + dx, z] for dx in range(3) for j in range(STEPS)],
-                axis=0,
+                [rows[p, row + dx, z] for dx in range(3) for p in range(count)], axis=0
             )
             for z in range(DEPTH)
         ],
@@ -30,11 +39,12 @@
 
 
 def forward_kernel(place, *refs):
-    *blocks, weights, feat = refs
+    *blocks, edge_a, edge_b, weights, feat, rows = refs
     y = place[0]
+    fill(rows, place, blocks, (edge_a, edge_b))
     lane = lax.broadcasted_iota(jnp.int32, (16, WIDTH), 1)
     turned = pltpu.roll(
-        weights[...].astype(jnp.float32).reshape(27 * 16, 128), lax.rem(128 - 16 * y, 128), 1
+        weights[...].astype(jnp.float32).reshape(27 * 16, 128), lax.rem(128 - 16 * y + 32, 128), 1
     ).astype(jnp.bfloat16)
     taps = jnp.concatenate(
         [
@@ -46,7 +56,7 @@
         axis=1,
     )
     for row in range(ROWS):
-        part = jnp.dot(taps, cells_of(blocks, row), preferred_element_type=jnp.float32)
+        part = jnp.dot(taps, cells_of(rows, STEPS, row), preferred_element_type=jnp.float32)
         for z in range(DEPTH):
             sums = []
             for dy in range(3):
@@ -63,11 +73,14 @@
             feat[:, row, z, :] = sums[1] + left + right
 
 
-def gradient_kernel(place, *refs):
-    *blocks, cot, grad = refs
+def gradient_kernel(skip, count, place, *refs):
+    blocks, (edge, cot, *earlier, grad, rows) = refs[:count], refs[count:]
     y, zl = place[0], place[1]
+    for part in earlier:
+        grad[...] = part[...]
+    fill(rows, place, blocks, (edge,))
     lane = lax.broadcasted_iota(jnp.int32, (16, WIDTH), 1)
-    total = jnp.zeros((384, 256), jnp.float32)
+    total = jnp.zeros((48 * count, 256), jnp.float32)
     gap = jnp.zeros((56, WIDTH), jnp.float32)
     empty = jnp.zeros((16, WIDTH), jnp.float32)
     for row in range(ROWS):
@@ -79,34 +92,35 @@
             moved.append((ahead, here, behind))
         spread = []
         for z in range(DEPTH):
-            rows = []
+            column = []
             for half in range(2):
                 for dz in range(3):
                     for dy in range(3):
                         at = z - dz + 1
                         tile = moved[at][dy] if 0 <= at < DEPTH else empty
-                        rows.append(tile[8 * half : 8 * half + 8])
-                rows.append(gap)
-            spread.append(jnp.concatenate(rows, axis=0).astype(jnp.bfloat16))
+                        column.append(tile[8 * half : 8 * half + 8])
+                column.append(gap)
+            spread.append(jnp.concatenate(column, axis=0).astype(jnp.bfloat16))
         total = total + lax.dot_general(
-            cells_of(blocks, row),
+            cells_of(rows, count, row),
             jnp.concatenate(spread, axis=1),
             (((1,), (1,)), ((), ())),
             preferred_element_type=jnp.float32,
         )
-    wide = lax.broadcasted_iota(jnp.int32, (128, WIDTH), 1)
+    deep = 16 * count
+    wide = lax.broadcasted_iota(jnp.int32, (deep, WIDTH), 1)
     sub = lax.broadcasted_iota(jnp.int32, (8, WIDTH), 0)
     for half in range(2):
         one, two, three = (
-            total[128 * dx : 128 * dx + 128, WIDTH * half : WIDTH * half + WIDTH]
+            total[deep * dx : deep * dx + deep, WIDTH * half : WIDTH * half + WIDTH]
             for dx in range(3)
         )
         one = jnp.where(wide < 72, one, pltpu.roll(three, 72, 1))
         two = jnp.where(wide < 72, two, pltpu.roll(three, 36, 1))
         base = 32 * lax.rem(zl + half, 2)
-        for k in range(16):
+        for k in range(2 * count):
             a, b = one[8 * k : 8 * k + 8], two[8 * k : 8 * k + 8]
-            at = base + lax.rem(y + k // 2, STEPS) * 4 + 2 * (k % 2)
+            at = base + lax.rem(y + skip + k // 2 + 6, STEPS) * 4 + 2 * (k % 2)
             grad[at] = jnp.where(sub < 4, a, pltpu.roll(b, 4, 0))
             grad[at + 1] = jnp.where(sub < 4, pltpu.roll(a, 4, 0), b)
 
@@ -125,7 +139,7 @@
     for step in range(31):
         pairs += [(32 + step, step + 1), (step + 1, 32 + step)]
 
-    body = jnp.where(
+    mine = jnp.where(
         first,
         jnp.concatenate([own, other], axis=2),
         jnp.concatenate([other, own], axis=2),
@@ -135,19 +149,12 @@
     )
     got = lax.ppermute(give, "zl", swap)
 
-    edge = lax.ppermute(jnp.where(first, body[0:1], body[4:5]), ("zl",) + SPACE, pairs)
-    edge, got = lax.optimization_barrier((edge, got))
-    mine = jnp.where(
-        first,
-        jnp.concatenate([edge, body], axis=0),
-        jnp.concatenate([body, edge], axis=0),
-    )
-
     def along(block, by):
         return lax.ppermute(block, "y", [(i, (i - by) % STEPS) for i in range(STEPS)])
 
     b2, b6 = along(mine, 2), along(mine, -2)
-    b1, b7 = along(mine, 1), along(mine, -1)
+    after, got = lax.optimization_barrier((mine, got))
+    b1, b7 = along(after, 1), along(after, -1)
     turn = [
         ((2 * i + c), (2 * ((i + (2 if c else -2)) % STEPS) + c))
         for i in range(STEPS)
@@ -156,29 +163,42 @@
     b4 = lax.ppermute(jnp.where(lax.axis_index("core") == 0, b2, b6), ("y", "core"), turn)
     b3, b5 = along(b2, 1), along(b6, -1)
 
+    def outermost(blocks):
+        return jnp.stack([jnp.where(first, block[0], block[4]) for block in blocks])
+
+    near = (b6, b7, mine, b1, b2)
+    send, b3 = lax.optimization_barrier((outermost(near), b3))
+    far = (b3, b4, b5)
+    edge_a = lax.ppermute(send, ("zl",) + SPACE, pairs)
+    edge_b = lax.ppermute(outermost(far), ("zl",) + SPACE, pairs)
+
     keep = lax.dynamic_slice_in_dim(cots, 4 * zl, 4, 0)
     cot = jnp.concatenate([keep, got[:32].reshape(4, 8, 8, WIDTH)], axis=2)
     weights = jnp.concatenate([filters, got[32:]], axis=1)
 
-    blocks = (mine, b1, b2, b3, b4, b5, b6, b7)
     place = jnp.stack([y, zl])
-    vmem = pl.BlockSpec(memory_space=pltpu.VMEM)
-    settings = dict(
-        in_specs=[pl.BlockSpec(memory_space=pltpu.SMEM)] + [vmem] * 9,
-        out_specs=vmem,
-        compiler_params=pltpu.CompilerParams(vmem_limit_bytes=48 * 1024 * 1024),
-        cost_estimate=pl.CostEstimate(flops=10**9, bytes_accessed=3 * 10**6, transcendentals=0),
-    )
-    grad = pl.pallas_call(
-        gradient_kernel,
-        out_shape=jax.ShapeDtypeStruct((64, 8, WIDTH), jnp.float32),
-        **settings,
-    )(place, *blocks, cot)
-    feat = pl.pallas_call(
-        forward_kernel,
-        out_shape=jax.ShapeDtypeStruct((16, ROWS, DEPTH, WIDTH), jnp.float32),
-        **settings,
-    )(place, *blocks, weights)
+
+    def local(kernel, shape, blocks, *others):
+        vmem = pl.BlockSpec(memory_space=pltpu.VMEM)
+        return pl.pallas_call(
+            kernel,
+            out_shape=jax.ShapeDtypeStruct(shape, jnp.float32),
+            in_specs=[pl.BlockSpec(memory_space=pltpu.SMEM)]
+            + [vmem] * (len(blocks) + len(others)),
+            out_specs=vmem,
+            scratch_shapes=[pltpu.VMEM((len(blocks), 6, DEPTH, 16, WIDTH), jnp.bfloat16)],
+            compiler_params=pltpu.CompilerParams(vmem_limit_bytes=48 * 1024 * 1024),
+            cost_estimate=pl.CostEstimate(
+                flops=10**8 * len(blocks), bytes_accessed=3 * 10**6, transcendentals=0
+            ),
+        )(place, *blocks, *others)
+
+    tiles = (64, 8, WIDTH)
+    grad = local(functools.partial(gradient_kernel, 0, 5), tiles, near, edge_a, cot)
+    grad = local(functools.partial(gradient_kernel, 5, 3), tiles, far, edge_b, cot, grad)
+    feat = local(
+        forward_kernel, (16, ROWS, DEPTH, WIDTH), near + far, edge_a, edge_b, weights
+    )
 
     got = lax.all_to_all(grad, ("zl",) + SPACE, 0, 0, tiled=True)
     summed = jnp.sum(got, axis=0) * scale

time: 84.2 us -> 81.3 us (0.966)
  the two profiles are of different devices: /device:TPU:24 before, /device:TPU:1 now
where the time goes in v4:
time: 81.3 us; the launch traced here: 80.8 us
  starting transfers between devices  59 us (73%)
  waiting for transfers between devices  11.3 us (14%)
  Pallas kernels  5.11 us (6%)
  local copies, waits for them, and re-layouts  3.08 us (4%)
  other arithmetic  1.3 us (2%)
  between operations  1.04 us (1%)
    ppermute x6, starting transfers between devices, along(): lax.ppermute(block, 'y', [(i, (i - by) % STEPS) for i in range(STEPS)])  23.4 us
    all_to_all x1, starting transfers between devices, on_device(): got = lax.all_to_all(grad, ('zl',) + SPACE, 0, 0, tiled=True)  14.3 us
    ppermute x1, waiting for transfers between devices, on_device(): rest = lax.ppermute(feat[8:], 'zl', swap)  5.45 us
    pallas_call x3, Pallas kernels, local(): pl.pallas_call(kernel, out_shape=jax.ShapeDtypeStruct(shape, jnp.float32)...  5.11 us
    ppermute x1, starting transfers between devices, on_device(): lax.ppermute(lax.dynamic_slice_in_dim(acts, 3 * (1 - zl), 5, 0), 'zl', swap)  4.96 us
    ppermute x1, starting transfers between devices, on_device(): edge_a = lax.ppermute(send, ('zl',) + SPACE, pairs)  4.8 us
    ppermute x1, starting transfers between devices, on_device(): edge_b = lax.ppermute(outermost(far), ('zl',) + SPACE, pairs)  3.94 us
    ppermute x6, waiting for transfers between devices, along(): lax.ppermute(block, 'y', [(i, (i - by) % STEPS) for i in range(STEPS)])  3.48 us
  transfers between devices with their start and end apart: 13, of which 5 were waited for; matrix products, arithmetic and copies ran while one was open for 2% of the time, Pallas kernels for 4%

profile of v4, /device:TPU:1, one launch (start us, length us, event | category | flops | bytes accessed | tf_op | source)
XLA Modules:
  0.0 80.8 jit_solution(11111745503496667622)
XLA Ops:
  0.6 1.0 %constant_dynamic-slice_fusion.2 = (bf16[8,5,8,128]{3,2,1,0:T(8,128)(2,1)S(1)}, bf16[8,5,8,128]{3,2,1,0:T(8,128)(2,1)S(1)}) fusion(bf16[8,8,8,128]{3,2,1,0:T(8,128)(2,1)} %param.4, s32[]{:T(128)S(6)} %select_n.80, s32[]{:T(128)S(6)} %select_n.81), kind=kLoop, calls=%fused_computation.30 | loop fusion | bytes 327688 | tf_op jit(solution)/shard_map/dynamic-slice
  1.6 0.0 copy-start.1
  1.7 5.0 %collective-permute-start = (bf16[5,8,8,128]{3,2,1,0:T(8,128)(2,1)S(1)}, bf16[5,8,8,128]{3,2,1,0:T(8,128)(2,1)S(1)}, u32[]{:S(2)}, u32[]{:S(2)}) collective-permute-start(bf16[5,8,8,128]{3,2,1,0:T(8,128)(2,1)S(1)} %bitcast.23), channel_id=1, source_target_pairs={{0,32},{32,0},{1,33},{33,1},{2,34},{34,2},{3,35},{35,3},{4,36},{36... | collective-permute-start | bytes 245768 | tf_op jit(solution)/shard_map/ppermute | solution.py:136
  6.6 0.0 copy-done.1
  6.7 0.0 copy-start
  6.7 0.8 copy-done
  7.5 1.9 %collective-permute-start.2 = (bf16[59,8,128]{2,1,0:T(8,128)(2,1)S(1)}, bf16[59,8,128]{2,1,0:T(8,128)(2,1)S(1)}, u32[]{:S(2)}, u32[]{:S(2)}) collective-permute-start(bf16[59,8,128]{2,1,0:T(8,128)(2,1)S(1)} %pad_maximum_fusion.1), channel_id=1, source_target_pairs={{0,32},{32,0},{1,33},{33,1},{2,34},{34,2},{3,35},{35,3},{4,36},{36... | collective-permute-start | bytes 362504 | tf_op jit(solution)/shard_map/ppermute | solution.py:150
  9.5 0.0 collective-permute-done
  9.5 5.9 %collective-permute-start.5 = (bf16[5,8,16,128]{3,2,1,0:T(8,128)(2,1)S(1)}, bf16[5,8,16,128]{3,2,1,0:T(8,128)(2,1)S(1)}, u32[]{:S(2)}, u32[]{:S(2)}) collective-permute-start(bf16[5,8,16,128]{3,2,1,0:T(8,128)(2,1)S(1)} %maximum_select_fusion.1.refs_2_), channel_id=1, source_target_pairs={{0,384},{64,448},{128,0},{192,64},{256,128},{320,192},{384,256},{4... | collective-permute-start | bytes 491528 | tf_op jit(solution)/shard_map/ppermute | solution.py:153
  15.4 1.9 %collective-permute-start.1 = (bf16[5,8,16,128]{3,2,1,0:T(8,128)(2,1)S(1)}, bf16[5,8,16,128]{3,2,1,0:T(8,128)(2,1)S(1)}, u32[]{:S(2)}, u32[]{:S(2)}) collective-permute-start(bf16[5,8,16,128]{3,2,1,0:T(8,128)(2,1)S(1)} %maximum_select_fusion.1.refs_2_), channel_id=1, source_target_pairs={{0,128},{64,192},{128,256},{192,320},{256,384},{320,448},{384,0},{... | collective-permute-start | bytes 491528 | tf_op jit(solution)/shard_map/ppermute | solution.py:153
  17.3 0.1 pad_add_fusion.place
  17.4 0.0 collective-permute-done.2
  17.5 4.7 %collective-permute-start.4 = (bf16[5,8,16,128]{3,2,1,0:T(8,128)(2,1)S(1)}, bf16[5,8,16,128]{3,2,1,0:T(8,128)(2,1)S(1)}, u32[]{:S(2)}, u32[]{:S(2)}) collective-permute-start(bf16[5,8,16,128]{3,2,1,0:T(8,128)(2,1)S(1)} %maximum_select_fusion.1.refs_2_), channel_id=1, source_target_pairs={{0,448},{64,0},{128,64},{192,128},{256,192},{320,256},{384,320},{4... | collective-permute-start | bytes 491528 | tf_op jit(solution)/shard_map/ppermute | solution.py:153
  22.2 1.9 %collective-permute-start.3 = (bf16[5,8,16,128]{3,2,1,0:T(8,128)(2,1)S(1)}, bf16[5,8,16,128]{3,2,1,0:T(8,128)(2,1)S(1)}, u32[]{:S(2)}, u32[]{:S(2)}) collective-permute-start(bf16[5,8,16,128]{3,2,1,0:T(8,128)(2,1)S(1)} %maximum_select_fusion.1.refs_2_), channel_id=1, source_target_pairs={{0,64},{64,128},{128,192},{192,256},{256,320},{320,384},{384,448},... | collective-permute-start | bytes 491528 | tf_op jit(solution)/shard_map/ppermute | solution.py:153
  24.1 0.0 collective-permute-done.5.refs_4_
  24.2 0.2 collective-permute-done.1.refs_0_
  24.3 2.3 %collective-permute-start.7 = (bf16[5,8,16,128]{3,2,1,0:T(8,128)(2,1)S(1)}, bf16[5,8,16,128]{3,2,1,0:T(8,128)(2,1)S(1)}, u32[]{:S(2)}, u32[]{:S(2)}) collective-permute-start(bf16[5,8,16,128]{3,2,1,0:T(8,128)(2,1)S(1)} %broadcast_select_fusion), channel_id=1, source_target_pairs={{0,384},{1,129},{64,448},{65,193},{128,0},{129,257},{192,64},{193,... | collective-permute-start | bytes 491528 | tf_op jit(solution)/shard_map/ppermute | solution.py:163
  26.7 7.0 %collective-permute-start.6 = (bf16[5,8,16,128]{3,2,1,0:T(8,128)(2,1)S(1)}, bf16[5,8,16,128]{3,2,1,0:T(8,128)(2,1)S(1)}, u32[]{:S(2)}, u32[]{:S(2)}) collective-permute-start(bf16[5,8,16,128]{3,2,1,0:T(8,128)(2,1)S(1)} %collective-permute-done.5.refs_4_), channel_id=1, source_target_pairs={{0,448},{64,0},{128,64},{192,128},{256,192},{320,256},{384,320},{4... | collective-permute-start | bytes 491528 | tf_op jit(solution)/shard_map/ppermute | solution.py:153
  33.7 1.9 %collective-permute-start.8 = (bf16[5,8,16,128]{3,2,1,0:T(8,128)(2,1)S(1)}, bf16[5,8,16,128]{3,2,1,0:T(8,128)(2,1)S(1)}, u32[]{:S(2)}, u32[]{:S(2)}) collective-permute-start(bf16[5,8,16,128]{3,2,1,0:T(8,128)(2,1)S(1)} %collective-permute-done.1.refs_0_), channel_id=1, source_target_pairs={{0,64},{64,128},{128,192},{192,256},{256,320},{320,384},{384,448},... | collective-permute-start | bytes 491528 | tf_op jit(solution)/shard_map/ppermute | solution.py:153
  35.7 0.0 collective-permute-done.3.refs_1_
  35.7 0.0 collective-permute-done.4.refs_3_
  35.8 3.3 %collective-permute-done.6.refs_5_.refs_0_ = bf16[5,8,16,128]{3,2,1,0:T(8,128)(2,1)S(1)} collective-permute-done((bf16[5,8,16,128]{3,2,1,0:T(8,128)(2,1)S(1)}, bf16[5,8,16,128]{3,2,1,0:T(8,128)(2,1)S(1)}, u32[]{:S(2)}, u32[]{:S(2)}) %collective-permute-start.6) | collective-permute-done | bytes 163872 | tf_op jit(solution)/shard_map/ppermute | solution.py:153
  39.1 4.8 %collective-permute-start.9 = (bf16[5,8,16,128]{3,2,1,0:T(8,128)(2,1)S(1)}, bf16[5,8,16,128]{3,2,1,0:T(8,128)(2,1)S(1)}, u32[]{:S(2)}, u32[]{:S(2)}) collective-permute-start(bf16[5,8,16,128]{3,2,1,0:T(8,128)(2,1)S(1)} %fusion.1), channel_id=1, source_target_pairs={{32,1},{1,32},{33,2},{2,33},{34,3},{3,34},{35,4},{4,35},{36,5},{5,... | collective-permute-start | bytes 491528 | tf_op jit(solution)/shard_map/ppermute | solution.py:172
  43.9 0.0 collective-permute-done.7.refs_6_.refs_1_
  44.0 0.0 collective-permute-done.8.refs_7_.refs_2_
  44.0 3.9 %collective-permute-start.10 = (bf16[3,8,16,128]{3,2,1,0:T(8,128)(2,1)S(1)}, bf16[3,8,16,128]{3,2,1,0:T(8,128)(2,1)S(1)}, u32[]{:S(2)}, u32[]{:S(2)}) collective-permute-start(bf16[3,8,16,128]{3,2,1,0:T(8,128)(2,1)S(1)} %pad_maximum_fusion.3), channel_id=1, source_target_pairs={{32,1},{1,32},{33,2},{2,33},{34,3},{3,34},{35,4},{4,35},{36,5},{5,... | collective-permute-start | bytes 294920 | tf_op jit(solution)/shard_map/ppermute | solution.py:173
  48.0 0.0 collective-permute-done.9.refs_8_.refs_5_
  48.0 1.4 %shard_map.60.refs_5_ = f32[64,8,128]{2,1,0:T(8,128)S(1)} custom-call(s32[2]{0:T(128)S(1)} %pad_add_fusion.place, bf16[5,8,16,128]{3,2,1,0:T(8,128)(2,1)S(1)} %collective-permute-done.1.refs_0_, bf16[5,8,16,128]{3,2,1,0:T(8,128)(2,1)S(1)} %collective-permute-done.3.refs_1_, bf16[5,8,16,128]{3,2,1,0:T(8,128)(2,1)S(1)} %maximum_select_fusion.1.refs_2_, ...), custom_call_target="tpu_custom_call" | custom-call | flops 500000000 | bytes 3000000 | tf_op jit(solution)/shard_map/pallas_call | solution.py:183
  49.4 0.8 %collective-permute-done.10.refs_9_.refs_3_ = bf16[3,8,16,128]{3,2,1,0:T(8,128)(2,1)S(1)} collective-permute-done((bf16[3,8,16,128]{3,2,1,0:T(8,128)(2,1)S(1)}, bf16[3,8,16,128]{3,2,1,0:T(8,128)(2,1)S(1)}, u32[]{:S(2)}, u32[]{:S(2)}) %collective-permute-start.10) | collective-permute-done | bytes 98336 | tf_op jit(solution)/shard_map/ppermute | solution.py:173
  50.2 2.1 %shard_map.61 = f32[64,8,128]{2,1,0:T(8,128)} custom-call(s32[2]{0:T(128)S(1)} %pad_add_fusion.place, bf16[5,8,16,128]{3,2,1,0:T(8,128)(2,1)S(1)} %collective-permute-done.6.refs_5_.refs_0_, bf16[5,8,16,128]{3,2,1,0:T(8,128)(2,1)S(1)} %collective-permute-done.7.refs_6_.refs_1_, bf16[5,8,16,128]{3,2,1,0:T(8,128)(2,1)S(1)} %collective-permute-done.8.refs_7_.refs_2_, ...), custom_call_target="tpu_custom_call" | custom-call | flops 300000000 | bytes 3000000 | tf_op jit(solution)/shard_map/pallas_call | solution.py:183
  52.3 14.3 %all-to-all-start = ((f32[64,8,128]{2,1,0:T(8,128)}), f32[64,8,128]{2,1,0:T(8,128)S(1)}, u32[]{:S(2)}, u32[]{:S(2)}) async-start(f32[64,8,128]{2,1,0:T(8,128)} %shard_map.61), calls=%async_computation | async-start | bytes 524288 | tf_op jit(solution)/shard_map/all_to_all | solution.py:203
  66.6 1.6 %shard_map.59 = f32[16,4,8,128]{3,2,1,0:T(8,128)S(1)} custom-call(s32[2]{0:T(128)S(1)} %pad_add_fusion.place, bf16[5,8,16,128]{3,2,1,0:T(8,128)(2,1)S(1)} %collective-permute-done.1.refs_0_, bf16[5,8,16,128]{3,2,1,0:T(8,128)(2,1)S(1)} %collective-permute-done.3.refs_1_, bf16[5,8,16,128]{3,2,1,0:T(8,128)(2,1)S(1)} %maximum_select_fusion.1.refs_2_, ...), custom_call_target="tpu_custom_call" | custom-call | flops 800000000 | bytes 3000000 | tf_op jit(solution)/shard_map/pallas_call | solution.py:183
  68.3 0.0 copy-start.2
  68.3 3.4 %collective-permute-start.11 = (f32[8,4,8,128]{3,2,1,0:T(8,128)S(1)}, f32[8,4,8,128]{3,2,1,0:T(8,128)S(1)}, u32[]{:S(2)}, u32[]{:S(2)}) collective-permute-start(f32[8,4,8,128]{3,2,1,0:T(8,128)S(1)} %get-tuple-element.13), channel_id=1, source_target_pairs={{0,32},{32,0},{1,33},{33,1},{2,34},{34,2},{3,35},{35,3},{4,36},{36... | collective-permute-start | bytes 393224 | tf_op jit(solution)/shard_map/ppermute | solution.py:211
  71.7 0.0 copy-done.2
  71.7 5.5 %collective-permute-done.11 = f32[8,4,8,128]{3,2,1,0:T(8,128)S(1)} collective-permute-done((f32[8,4,8,128]{3,2,1,0:T(8,128)S(1)}, f32[8,4,8,128]{3,2,1,0:T(8,128)S(1)}, u32[]{:S(2)}, u32[]{:S(2)}) %collective-permute-start.11) | collective-permute-done | bytes 131104 | tf_op jit(solution)/shard_map/ppermute | solution.py:211
  77.1 0.8 fusion
  77.9 1.5 %all-to-all-done = f32[64,8,128]{2,1,0:T(8,128)S(1)} async-done(((f32[64,8,128]{2,1,0:T(8,128)}), f32[64,8,128]{2,1,0:T(8,128)S(1)}, u32[]{:S(2)}, u32[]{:S(2)}) %all-to-all-start) | async-done | bytes 262176 | tf_op jit(solution)/shard_map/all_to_all | solution.py:203
  79.4 0.1 reduce_sum.9
  79.5 0.1 fusion.8
  79.6 0.1 stack.40
  79.7 0.1 pad_maximum_fusion.4
  79.7 0.1 stack.42
  79.8 0.1 stack.41
  79.9 0.2 copy.16
  80.1 0.7 reshape.24
  (26 shorter events, 0.4 us)
Async XLA Ops:
  1.6 5.0 %copy-start.1 = (bf16[8,8,8,128]{3,2,1,0:T(8,128)(2,1)S(1)}, bf16[8,8,8,128]{3,2,1,0:T(8,128)(2,1)}, u32[]{:S(2)}) copy-start(bf16[8,8,8,128]{3,2,1,0:T(8,128)(2,1)} %param.5) | copy-start | bytes 393220
  1.7 7.8 %collective-permute-start = (bf16[5,8,8,128]{3,2,1,0:T(8,128)(2,1)S(1)}, bf16[5,8,8,128]{3,2,1,0:T(8,128)(2,1)S(1)}, u32[]{:S(2)}, u32[]{:S(2)}) collective-permute-start(bf16[5,8,8,128]{3,2,1,0:T(8,128)(2,1)S(1)} %bitcast.23), channel_id=1, source_target_pairs={{0,32},{32,0},{1,33},{33,1},{2,34},{34,2},{3,35},{35,3},{4,36},{36... | collective-permute-start | bytes 245768 | tf_op jit(solution)/shard_map/ppermute | solution.py:136
  6.7 0.8 %copy-start = (bf16[27,8,128]{2,1,0:T(8,128)(2,1)S(1)}, bf16[27,8,128]{2,1,0:T(8,128)(2,1)}, u32[]{:S(2)}) copy-start(bf16[27,8,128]{2,1,0:T(8,128)(2,1)} %param.6) | copy-start | bytes 165892
  7.5 10.0 %collective-permute-start.2 = (bf16[59,8,128]{2,1,0:T(8,128)(2,1)S(1)}, bf16[59,8,128]{2,1,0:T(8,128)(2,1)S(1)}, u32[]{:S(2)}, u32[]{:S(2)}) collective-permute-start(bf16[59,8,128]{2,1,0:T(8,128)(2,1)S(1)} %pad_maximum_fusion.1), channel_id=1, source_target_pairs={{0,32},{32,0},{1,33},{33,1},{2,34},{34,2},{3,35},{35,3},{4,36},{36... | collective-permute-start | bytes 362504 | tf_op jit(solution)/shard_map/ppermute | solution.py:150
  9.5 14.6 %collective-permute-start.5 = (bf16[5,8,16,128]{3,2,1,0:T(8,128)(2,1)S(1)}, bf16[5,8,16,128]{3,2,1,0:T(8,128)(2,1)S(1)}, u32[]{:S(2)}, u32[]{:S(2)}) collective-permute-start(bf16[5,8,16,128]{3,2,1,0:T(8,128)(2,1)S(1)} %maximum_select_fusion.1.refs_2_), channel_id=1, source_target_pairs={{0,384},{64,448},{128,0},{192,64},{256,128},{320,192},{384,256},{4... | collective-permute-start | bytes 491528 | tf_op jit(solution)/shard_map/ppermute | solution.py:153
  15.4 8.9 %collective-permute-start.1 = (bf16[5,8,16,128]{3,2,1,0:T(8,128)(2,1)S(1)}, bf16[5,8,16,128]{3,2,1,0:T(8,128)(2,1)S(1)}, u32[]{:S(2)}, u32[]{:S(2)}) collective-permute-start(bf16[5,8,16,128]{3,2,1,0:T(8,128)(2,1)S(1)} %maximum_select_fusion.1.refs_2_), channel_id=1, source_target_pairs={{0,128},{64,192},{128,256},{192,320},{256,384},{320,448},{384,0},{... | collective-permute-start | bytes 491528 | tf_op jit(solution)/shard_map/ppermute | solution.py:153
  17.5 18.2 %collective-permute-start.4 = (bf16[5,8,16,128]{3,2,1,0:T(8,128)(2,1)S(1)}, bf16[5,8,16,128]{3,2,1,0:T(8,128)(2,1)S(1)}, u32[]{:S(2)}, u32[]{:S(2)}) collective-permute-start(bf16[5,8,16,128]{3,2,1,0:T(8,128)(2,1)S(1)} %maximum_select_fusion.1.refs_2_), channel_id=1, source_target_pairs={{0,448},{64,0},{128,64},{192,128},{256,192},{320,256},{384,320},{4... | collective-permute-start | bytes 491528 | tf_op jit(solution)/shard_map/ppermute | solution.py:153
  22.2 13.5 %collective-permute-start.3 = (bf16[5,8,16,128]{3,2,1,0:T(8,128)(2,1)S(1)}, bf16[5,8,16,128]{3,2,1,0:T(8,128)(2,1)S(1)}, u32[]{:S(2)}, u32[]{:S(2)}) collective-permute-start(bf16[5,8,16,128]{3,2,1,0:T(8,128)(2,1)S(1)} %maximum_select_fusion.1.refs_2_), channel_id=1, source_target_pairs={{0,64},{64,128},{128,192},{192,256},{256,320},{320,384},{384,448},... | collective-permute-start | bytes 491528 | tf_op jit(solution)/shard_map/ppermute | solution.py:153
  24.3 19.6 %collective-permute-start.7 = (bf16[5,8,16,128]{3,2,1,0:T(8,128)(2,1)S(1)}, bf16[5,8,16,128]{3,2,1,0:T(8,128)(2,1)S(1)}, u32[]{:S(2)}, u32[]{:S(2)}) collective-permute-start(bf16[5,8,16,128]{3,2,1,0:T(8,128)(2,1)S(1)} %broadcast_select_fusion), channel_id=1, source_target_pairs={{0,384},{1,129},{64,448},{65,193},{128,0},{129,257},{192,64},{193,... | collective-permute-start | bytes 491528 | tf_op jit(solution)/shard_map/ppermute | solution.py:163
  26.7 12.4 %collective-permute-start.6 = (bf16[5,8,16,128]{3,2,1,0:T(8,128)(2,1)S(1)}, bf16[5,8,16,128]{3,2,1,0:T(8,128)(2,1)S(1)}, u32[]{:S(2)}, u32[]{:S(2)}) collective-permute-start(bf16[5,8,16,128]{3,2,1,0:T(8,128)(2,1)S(1)} %collective-permute-done.5.refs_4_), channel_id=1, source_target_pairs={{0,448},{64,0},{128,64},{192,128},{256,192},{320,256},{384,320},{4... | collective-permute-start | bytes 491528 | tf_op jit(solution)/shard_map/ppermute | solution.py:153
  33.7 10.2 %collective-permute-start.8 = (bf16[5,8,16,128]{3,2,1,0:T(8,128)(2,1)S(1)}, bf16[5,8,16,128]{3,2,1,0:T(8,128)(2,1)S(1)}, u32[]{:S(2)}, u32[]{:S(2)}) collective-permute-start(bf16[5,8,16,128]{3,2,1,0:T(8,128)(2,1)S(1)} %collective-permute-done.1.refs_0_), channel_id=1, source_target_pairs={{0,64},{64,128},{128,192},{192,256},{256,320},{320,384},{384,448},... | collective-permute-start | bytes 491528 | tf_op jit(solution)/shard_map/ppermute | solution.py:153
  39.1 8.9 %collective-permute-start.9 = (bf16[5,8,16,128]{3,2,1,0:T(8,128)(2,1)S(1)}, bf16[5,8,16,128]{3,2,1,0:T(8,128)(2,1)S(1)}, u32[]{:S(2)}, u32[]{:S(2)}) collective-permute-start(bf16[5,8,16,128]{3,2,1,0:T(8,128)(2,1)S(1)} %fusion.1), channel_id=1, source_target_pairs={{32,1},{1,32},{33,2},{2,33},{34,3},{3,34},{35,4},{4,35},{36,5},{5,... | collective-permute-start | bytes 491528 | tf_op jit(solution)/shard_map/ppermute | solution.py:172
  44.0 6.2 %collective-permute-start.10 = (bf16[3,8,16,128]{3,2,1,0:T(8,128)(2,1)S(1)}, bf16[3,8,16,128]{3,2,1,0:T(8,128)(2,1)S(1)}, u32[]{:S(2)}, u32[]{:S(2)}) collective-permute-start(bf16[3,8,16,128]{3,2,1,0:T(8,128)(2,1)S(1)} %pad_maximum_fusion.3), channel_id=1, source_target_pairs={{32,1},{1,32},{33,2},{2,33},{34,3},{3,34},{35,4},{4,35},{36,5},{5,... | collective-permute-start | bytes 294920 | tf_op jit(solution)/shard_map/ppermute | solution.py:173
  52.3 27.1 %all-to-all-start = ((f32[64,8,128]{2,1,0:T(8,128)}), f32[64,8,128]{2,1,0:T(8,128)S(1)}, u32[]{:S(2)}, u32[]{:S(2)}) async-start(f32[64,8,128]{2,1,0:T(8,128)} %shard_map.61), calls=%async_computation | async-start | bytes 524288 | tf_op jit(solution)/shard_map/all_to_all | solution.py:203
  68.3 3.4 %copy-start.2 = (bf16[8]{0:T(256)(128)(2,1)S(1)}, bf16[8]{0:T(256)(128)(2,1)}, u32[]{:S(2)}) copy-start(bf16[8]{0:T(256)(128)(2,1)} %param.7) | copy-start | bytes 52
  68.3 8.9 %collective-permute-start.11 = (f32[8,4,8,128]{3,2,1,0:T(8,128)S(1)}, f32[8,4,8,128]{3,2,1,0:T(8,128)S(1)}, u32[]{:S(2)}, u32[]{:S(2)}) collective-permute-start(f32[8,4,8,128]{3,2,1,0:T(8,128)S(1)} %get-tuple-element.13), channel_id=1, source_target_pairs={{0,32},{32,0},{1,33},{33,1},{2,34},{34,2},{3,35},{35,3},{4,36},{36... | collective-permute-start | bytes 393224 | tf_op jit(solution)/shard_map/ppermute | solution.py:211

commit v5 on v4

v5 whole, which is shorter than its diff:
```python
import math

import jax
import jax.numpy as jnp
from jax import lax
from jax.experimental import pallas as pl
from jax.experimental.pallas import tpu as pltpu
from jax.sharding import Mesh
from jax.sharding import PartitionSpec as P

SPACE = ("x", "zh", "core")
ROWS = 4
DEPTH = 8
WIDTH = 128
STEPS = 8


def fill(rows, place, blocks, edge):
    zl = place[1]
    for p, block in enumerate(blocks):
        rows[p, pl.ds(1 - zl, 5)] = block[...]
    rows[:, 5 * zl] = edge


def cells_of(rows, row):
    return jnp.concatenate(
        [
            jnp.concatenate(
                [rows[p, row + dx, z] for dx in range(3) for p in range(STEPS)], axis=0
            )
            for z in range(DEPTH)
        ],
        axis=1,
    )


def forward_kernel(place, *refs):
    *blocks, edge, weights, feat, rows = refs
    y = place[0]
    fill(rows, place, blocks, edge[...])
    lane = lax.broadcasted_iota(jnp.int32, (16, WIDTH), 1)
    turned = pltpu.roll(
        weights[...].astype(jnp.float32).reshape(27 * 16, 128), lax.rem(128 - 16 * y + 32, 128), 1
    ).astype(jnp.bfloat16)
    taps = jnp.concatenate(
        [
            jnp.concatenate(
                [turned[16 * (9 * dx + q) : 16 * (9 * dx + q) + 16] for q in range(9)], axis=0
            )
            for dx in range(3)
        ],
        axis=1,
    )
    for row in range(ROWS):
        part = jnp.dot(taps, cells_of(rows, row), preferred_element_type=jnp.float32)
        for z in range(DEPTH):
            sums = []
            for dy in range(3):
                acc = None
                for dz in range(3):
                    if 0 <= z + dz - 1 < DEPTH:
                        at = 16 * (3 * dz + dy)
                        lo = WIDTH * (z + dz - 1)
                        term = part[at : at + 16, lo : lo + WIDTH]
                        acc = term if acc is None else acc + term
                sums.append(acc)
            left = jnp.where(lane == 0, 0.0, pltpu.roll(sums[0], 1, 1))
            right = jnp.where(lane == WIDTH - 1, 0.0, pltpu.roll(sums[2], WIDTH - 1, 1))
            feat[:, row, z, :] = sums[1] + left + right


def shifted(cot, row):
    lane = lax.broadcasted_iota(jnp.int32, (16, WIDTH), 1)
    gap = jnp.zeros((56, WIDTH), jnp.float32)
    empty = jnp.zeros((16, WIDTH), jnp.float32)
    moved = []
    for z in range(DEPTH):
        here = cot[row, z].astype(jnp.float32)
        ahead = jnp.where(lane == WIDTH - 1, 0.0, pltpu.roll(here, WIDTH - 1, 1))
        behind = jnp.where(lane == 0, 0.0, pltpu.roll(here, 1, 1))
        moved.append((ahead, here, behind))
    columns = []
    for z in range(DEPTH):
        column = []
        for half in range(2):
            for dz in range(3):
                for dy in range(3):
                    at = z - dz + 1
                    tile = moved[at][dy] if 0 <= at < DEPTH else empty
                    column.append(tile[8 * half : 8 * half + 8])
            column.append(gap)
        columns.append(jnp.concatenate(column, axis=0).astype(jnp.bfloat16))
    return jnp.concatenate(columns, axis=1)


def over_cells(a, b):
    return lax.dot_general(a, b, (((1,), (1,)), ((), ())), preferred_element_type=jnp.float32)


def receivers(place, half):
    y, zl = place[0], place[1]
    base = 32 * lax.rem(zl + half, 2)
    return [base + lax.rem(y + k // 2 + 6, STEPS) * 4 + 2 * (k % 2) for k in range(16)]


def pair_of(one, two, k):
    sub = lax.broadcasted_iota(jnp.int32, (8, WIDTH), 0)
    a, b = one[8 * k : 8 * k + 8], two[8 * k : 8 * k + 8]
    return jnp.where(sub < 4, a, pltpu.roll(b, 4, 0)), jnp.where(sub < 4, pltpu.roll(a, 4, 0), b)


def gradient_kernel(place, *refs):
    *blocks, cot, grad, rows = refs
    fill(rows, place, blocks, jnp.zeros((STEPS, DEPTH, 16, WIDTH), jnp.bfloat16))
    total = jnp.zeros((384, 256), jnp.float32)
    for row in range(ROWS):
        total = total + over_cells(cells_of(rows, row), shifted(cot, row))
    wide = lax.broadcasted_iota(jnp.int32, (128, WIDTH), 1)
    for half in range(2):
        one, two, three = (
            total[128 * dx : 128 * dx + 128, WIDTH * half : WIDTH * half + WIDTH]
            for dx in range(3)
        )
        one = jnp.where(wide < 72, one, pltpu.roll(three, 72, 1))
        two = jnp.where(wide < 72, two, pltpu.roll(three, 36, 1))
        for k, at in enumerate(receivers(place, half)):
            grad[at], grad[at + 1] = pair_of(one, two, k)


def edge_kernel(place, edge, cot, earlier, grad):
    zl = place[1]
    cells = jnp.concatenate(
        [jnp.concatenate([edge[p, z] for p in range(STEPS)], axis=0) for z in range(DEPTH)], axis=1
    )
    total = over_cells(cells, shifted(cot, 3 * zl))
    wide = lax.broadcasted_iota(jnp.int32, (128, WIDTH), 1)
    low = zl == 0
    for half in range(2):
        part = total[:, WIDTH * half : WIDTH * half + WIDTH]
        one = jnp.where(low, part, jnp.where(wide < 72, 0.0, pltpu.roll(part, 72, 1)))
        two = jnp.where(
            jnp.logical_or(low, wide < 72), 0.0, pltpu.roll(part, 36, 1)
        )
        for k, at in enumerate(receivers(place, half)):
            first, second = pair_of(one, two, k)
            grad[at] = earlier[at] + first
            grad[at + 1] = earlier[at + 1] + second


def on_device(activations, cotangent, filters, bias_terms):
    y, zl = lax.axis_index("y"), lax.axis_index("zl")
    scale = jnp.float32(1.0 / math.sqrt(activations.shape[1] * 32 * DEPTH * WIDTH))
    acts = jnp.transpose(activations, (1, 2, 0, 3))
    cots = jnp.transpose(cotangent, (1, 2, 0, 3))
    first = zl == 0

    swap = [(0, 1), (1, 0)]
    other = lax.ppermute(lax.dynamic_slice_in_dim(acts, 3 * (1 - zl), 5, 0), "zl", swap)
    own = lax.dynamic_slice_in_dim(acts, 3 * zl, 5, 0)
    pairs = []
    for step in range(31):
        pairs += [(32 + step, step + 1), (step + 1, 32 + step)]

    mine = jnp.where(
        first,
        jnp.concatenate([own, other], axis=2),
        jnp.concatenate([other, own], axis=2),
    )
    give = jnp.concatenate(
        [lax.dynamic_slice_in_dim(cots, 4 * (1 - zl), 4, 0).reshape(32, 8, WIDTH), filters], axis=0
    )
    got = lax.ppermute(give, "zl", swap)

    def along(block, by):
        return lax.ppermute(block, "y", [(i, (i - by) % STEPS) for i in range(STEPS)])

    b2, b6 = along(mine, 2), along(mine, -2)
    keep = lax.dynamic_slice_in_dim(cots, 4 * zl, 4, 0)
    cot = jnp.concatenate([keep, got[:32].reshape(4, 8, 8, WIDTH)], axis=2)
    weights = jnp.concatenate([filters, got[32:]], axis=1)
    after, cot, weights = lax.optimization_barrier((mine, cot, weights))
    b1, b7 = along(after, 1), along(after, -1)
    turn = [
        ((2 * i + c), (2 * ((i + (2 if c else -2)) % STEPS) + c))
        for i in range(STEPS)
        for c in range(2)
    ]
    b4 = lax.ppermute(jnp.where(lax.axis_index("core") == 0, b2, b6), ("y", "core"), turn)
    b3, b5 = along(b2, 1), along(b6, -1)

    blocks = (b6, b7, mine, b1, b2, b3, b4, b5)
    edge = lax.ppermute(
        jnp.stack([jnp.where(first, block[0], block[4]) for block in blocks]),
        ("zl",) + SPACE,
        pairs,
    )

    place = jnp.stack([y, zl])

    def local(kernel, shape, operands, scratch):
        vmem = pl.BlockSpec(memory_space=pltpu.VMEM)
        return pl.pallas_call(
            kernel,
            out_shape=jax.ShapeDtypeStruct(shape, jnp.float32),
            in_specs=[pl.BlockSpec(memory_space=pltpu.SMEM)] + [vmem] * len(operands),
            out_specs=vmem,
            scratch_shapes=scratch,
            compiler_params=pltpu.CompilerParams(vmem_limit_bytes=48 * 1024 * 1024),
            cost_estimate=pl.CostEstimate(
                flops=10**8 * len(operands), bytes_accessed=3 * 10**6, transcendentals=0
            ),
        )(place, *operands)

    tiles = (64, 8, WIDTH)
    rows = [pltpu.VMEM((STEPS, 6, DEPTH, 16, WIDTH), jnp.bfloat16)]
    grad = local(gradient_kernel, tiles, (*blocks, cot), rows)
    grad = local(edge_kernel, tiles, (edge, cot, grad), [])
    feat = local(forward_kernel, (16, ROWS, DEPTH, WIDTH), (*blocks, edge, weights), rows)

    got = lax.all_to_all(grad, ("zl",) + SPACE, 0, 0, tiled=True)
    summed = jnp.sum(got, axis=0) * scale
    low, high = summed[:4], summed[4:]
    filter_grad = jnp.stack(
        [low[:, :72], high[:, :72], jnp.concatenate([low[:, 72:108], high[:, 72:108]], axis=1)]
    )
    filter_grad = filter_grad.reshape(3, 4, 9, 8).transpose(0, 2, 3, 1).reshape(27, 8, 4)

    rest = lax.ppermute(feat[8:], "zl", swap)
    kept = feat[:8]
    features_out = jnp.where(
        first,
        jnp.concatenate([kept, rest], axis=1),
        jnp.concatenate([rest, kept], axis=1),
    ) + bias_terms.astype(jnp.float32)[:, None, None, None]
    return (features_out, filter_grad)


def solution(mesh):
    fine = Mesh(mesh.devices.reshape(8, 2, 4, 4, 2), ("y", "zl", "x", "zh", "core"))
    filt = ("y", "zl")
    in_specs = (
        P(filt, SPACE, None, None),
        P(filt, SPACE, None, None),
        P(None, filt, None),
        P(filt),
    )
    out_specs = (P(filt, SPACE, None, None), P(None, filt, SPACE))
    return jax.shard_map(
        on_device, mesh=fine, in_specs=in_specs, out_specs=out_specs, check_vma=False
    )
```

time: 81.3 us -> 81.1 us (level)
  starting transfers between devices: 59 us -> 53.2 us
  waiting for transfers between devices: 11.3 us -> 16.8 us
    ppermute x6, waiting for transfers between devices: 3.48 us -> 7.69 us  [along(): lax.ppermute(block, 'y', [(i, (i - by) % STEPS) for i in range(STEPS)])]
    ppermute x6, starting transfers between devices: 23.4 us -> 19.6 us  [along(): lax.ppermute(block, 'y', [(i, (i - by) % STEPS) for i in range(STEPS)])]
    ppermute x2 -> x1, starting transfers between devices: 8.74 us -> 5.09 us  [on_device(): lax.ppermute(jnp.stack([jnp.where(first, block[0], block[4]) for block in...]
    ppermute x1, starting transfers between devices: 2.34 us -> 3.98 us  [on_device(): lax.ppermute(jnp.where(lax.axis_index('core') == 0, b2, b6), ('y', 'core'...]
    ppermute x2 -> x1, waiting for transfers between devices: 0.84 us -> 2.2 us  [on_device(): lax.ppermute(jnp.stack([jnp.where(first, block[0], block[4]) for block in...]
  transfers between devices with their start and end apart: 13 -> 12, of which waited for: 5 -> 5; matrix products, arithmetic and copies ran while one was open for 2% -> 2% of each run, Pallas kernels for 4% -> 4%
where the time goes in v5:
time: 81.1 us; the launch traced here: 80.5 us
  starting transfers between devices  53.2 us (66%)
  waiting for transfers between devices  16.8 us (21%)
  Pallas kernels  5.07 us (6%)
  local copies, waits for them, and re-layouts  3.08 us (4%)
  other arithmetic  1.32 us (2%)
  between operations  1.02 us (1%)
    ppermute x6, starting transfers between devices, along(): lax.ppermute(block, 'y', [(i, (i - by) % STEPS) for i in range(STEPS)])  19.6 us
    all_to_all x1, starting transfers between devices, on_device(): got = lax.all_to_all(grad, ('zl',) + SPACE, 0, 0, tiled=True)  14.3 us
    ppermute x6, waiting for transfers between devices, along(): lax.ppermute(block, 'y', [(i, (i - by) % STEPS) for i in range(STEPS)])  7.69 us
    ppermute x1, waiting for transfers between devices, on_device(): rest = lax.ppermute(feat[8:], 'zl', swap)  5.44 us
    ppermute x1, starting transfers between devices, on_device(): lax.ppermute(jnp.stack([jnp.where(first, block[0], block[4]) for block in...  5.09 us
    pallas_call x3, Pallas kernels, local(): pl.pallas_call(kernel, out_shape=jax.ShapeDtypeStruct(shape, jnp.float32)...  5.07 us
    ppermute x1, starting transfers between devices, on_device(): lax.ppermute(lax.dynamic_slice_in_dim(acts, 3 * (1 - zl), 5, 0), 'zl', swap)  4.96 us
    ppermute x1, starting transfers between devices, on_device(): lax.ppermute(jnp.where(lax.axis_index('core') == 0, b2, b6), ('y', 'core'...  3.98 us
  transfers between devices with their start and end apart: 12, of which 5 were waited for; matrix products, arithmetic and copies ran while one was open for 2% of the time, Pallas kernels for 4%

profile of v5, /device:TPU:1, one launch (start us, length us, event | category | flops | bytes accessed | tf_op | source)
XLA Modules:
  0.0 80.5 jit_solution(9637031186392563974)
XLA Ops:
  0.6 1.0 %constant_dynamic-slice_fusion.2 = (bf16[8,5,8,128]{3,2,1,0:T(8,128)(2,1)S(1)}, bf16[8,5,8,128]{3,2,1,0:T(8,128)(2,1)S(1)}) fusion(bf16[8,8,8,128]{3,2,1,0:T(8,128)(2,1)} %param.4, s32[]{:T(128)S(6)} %select_n.80, s32[]{:T(128)S(6)} %select_n.81), kind=kLoop, calls=%fused_computation.32 | loop fusion | bytes 327688 | tf_op jit(solution)/shard_map/dynamic-slice
  1.6 0.0 copy-start.1
  1.7 5.0 %collective-permute-start = (bf16[5,8,8,128]{3,2,1,0:T(8,128)(2,1)S(1)}, bf16[5,8,8,128]{3,2,1,0:T(8,128)(2,1)S(1)}, u32[]{:S(2)}, u32[]{:S(2)}) collective-permute-start(bf16[5,8,8,128]{3,2,1,0:T(8,128)(2,1)S(1)} %bitcast.23), channel_id=1, source_target_pairs={{0,32},{32,0},{1,33},{33,1},{2,34},{34,2},{3,35},{35,3},{4,36},{36... | collective-permute-start | bytes 245768 | tf_op jit(solution)/shard_map/ppermute | solution.py:158
  6.6 0.0 copy-done.1
  6.7 0.0 copy-start
  6.7 0.8 copy-done
  7.5 1.9 %collective-permute-start.2 = (bf16[59,8,128]{2,1,0:T(8,128)(2,1)S(1)}, bf16[59,8,128]{2,1,0:T(8,128)(2,1)S(1)}, u32[]{:S(2)}, u32[]{:S(2)}) collective-permute-start(bf16[59,8,128]{2,1,0:T(8,128)(2,1)S(1)} %pad_maximum_fusion.1), channel_id=1, source_target_pairs={{0,32},{32,0},{1,33},{33,1},{2,34},{34,2},{3,35},{35,3},{4,36},{36... | collective-permute-start | bytes 362504 | tf_op jit(solution)/shard_map/ppermute | solution.py:172
  9.5 0.0 collective-permute-done
  9.6 4.2 %collective-permute-start.1 = (bf16[5,8,16,128]{3,2,1,0:T(8,128)(2,1)S(1)}, bf16[5,8,16,128]{3,2,1,0:T(8,128)(2,1)S(1)}, u32[]{:S(2)}, u32[]{:S(2)}) collective-permute-start(bf16[5,8,16,128]{3,2,1,0:T(8,128)(2,1)S(1)} %maximum_select_fusion.1.refs_2_), channel_id=1, source_target_pairs={{0,128},{64,192},{128,256},{192,320},{256,384},{320,448},{384,0},{... | collective-permute-start | bytes 491528 | tf_op jit(solution)/shard_map/ppermute | solution.py:175
  13.8 3.6 %collective-permute-start.5 = (bf16[5,8,16,128]{3,2,1,0:T(8,128)(2,1)S(1)}, bf16[5,8,16,128]{3,2,1,0:T(8,128)(2,1)S(1)}, u32[]{:S(2)}, u32[]{:S(2)}) collective-permute-start(bf16[5,8,16,128]{3,2,1,0:T(8,128)(2,1)S(1)} %maximum_select_fusion.1.refs_2_), channel_id=1, source_target_pairs={{0,384},{64,448},{128,0},{192,64},{256,128},{320,192},{384,256},{4... | collective-permute-start | bytes 491528 | tf_op jit(solution)/shard_map/ppermute | solution.py:175
  17.4 0.0 collective-permute-done.2
  17.5 2.8 %collective-permute-start.3 = (bf16[5,8,16,128]{3,2,1,0:T(8,128)(2,1)S(1)}, bf16[5,8,16,128]{3,2,1,0:T(8,128)(2,1)S(1)}, u32[]{:S(2)}, u32[]{:S(2)}) collective-permute-start(bf16[5,8,16,128]{3,2,1,0:T(8,128)(2,1)S(1)} %maximum_select_fusion.1.refs_2_), channel_id=1, source_target_pairs={{0,64},{64,128},{128,192},{192,256},{256,320},{320,384},{384,448},... | collective-permute-start | bytes 491528 | tf_op jit(solution)/shard_map/ppermute | solution.py:175
  20.3 3.7 %collective-permute-start.4 = (bf16[5,8,16,128]{3,2,1,0:T(8,128)(2,1)S(1)}, bf16[5,8,16,128]{3,2,1,0:T(8,128)(2,1)S(1)}, u32[]{:S(2)}, u32[]{:S(2)}) collective-permute-start(bf16[5,8,16,128]{3,2,1,0:T(8,128)(2,1)S(1)} %maximum_select_fusion.1.refs_2_), channel_id=1, source_target_pairs={{0,448},{64,0},{128,64},{192,128},{256,192},{320,256},{384,320},{4... | collective-permute-start | bytes 491528 | tf_op jit(solution)/shard_map/ppermute | solution.py:175
  24.0 0.0 collective-permute-done.1.refs_0_
  24.0 3.3 %collective-permute-done.5.refs_4_ = bf16[5,8,16,128]{3,2,1,0:T(8,128)(2,1)S(1)} collective-permute-done((bf16[5,8,16,128]{3,2,1,0:T(8,128)(2,1)S(1)}, bf16[5,8,16,128]{3,2,1,0:T(8,128)(2,1)S(1)}, u32[]{:S(2)}, u32[]{:S(2)}) %collective-permute-start.5) | collective-permute-done | bytes 163872 | tf_op jit(solution)/shard_map/ppermute | solution.py:175
  27.3 4.0 %collective-permute-start.7 = (bf16[5,8,16,128]{3,2,1,0:T(8,128)(2,1)S(1)}, bf16[5,8,16,128]{3,2,1,0:T(8,128)(2,1)S(1)}, u32[]{:S(2)}, u32[]{:S(2)}) collective-permute-start(bf16[5,8,16,128]{3,2,1,0:T(8,128)(2,1)S(1)} %broadcast_select_fusion), channel_id=1, source_target_pairs={{0,384},{1,129},{64,448},{65,193},{128,0},{129,257},{192,64},{193,... | collective-permute-start | bytes 491528 | tf_op jit(solution)/shard_map/ppermute | solution.py:188
  31.3 1.9 %collective-permute-start.6 = (bf16[5,8,16,128]{3,2,1,0:T(8,128)(2,1)S(1)}, bf16[5,8,16,128]{3,2,1,0:T(8,128)(2,1)S(1)}, u32[]{:S(2)}, u32[]{:S(2)}) collective-permute-start(bf16[5,8,16,128]{3,2,1,0:T(8,128)(2,1)S(1)} %collective-permute-done.5.refs_4_), channel_id=1, source_target_pairs={{0,448},{64,0},{128,64},{192,128},{256,192},{320,256},{384,320},{4... | collective-permute-start | bytes 491528 | tf_op jit(solution)/shard_map/ppermute | solution.py:175
  33.2 3.4 %collective-permute-start.8 = (bf16[5,8,16,128]{3,2,1,0:T(8,128)(2,1)S(1)}, bf16[5,8,16,128]{3,2,1,0:T(8,128)(2,1)S(1)}, u32[]{:S(2)}, u32[]{:S(2)}) collective-permute-start(bf16[5,8,16,128]{3,2,1,0:T(8,128)(2,1)S(1)} %collective-permute-done.1.refs_0_), channel_id=1, source_target_pairs={{0,64},{64,128},{128,192},{192,256},{256,320},{320,384},{384,448},... | collective-permute-start | bytes 491528 | tf_op jit(solution)/shard_map/ppermute | solution.py:175
  36.6 0.0 collective-permute-done.3.refs_1_
  36.7 0.0 collective-permute-done.4.refs_3_
  36.8 4.4 %collective-permute-done.6.refs_5_ = bf16[5,8,16,128]{3,2,1,0:T(8,128)(2,1)S(1)} collective-permute-done((bf16[5,8,16,128]{3,2,1,0:T(8,128)(2,1)S(1)}, bf16[5,8,16,128]{3,2,1,0:T(8,128)(2,1)S(1)}, u32[]{:S(2)}, u32[]{:S(2)}) %collective-permute-start.6) | collective-permute-done | bytes 163872 | tf_op jit(solution)/shard_map/ppermute | solution.py:175
  41.2 0.0 collective-permute-done.7.refs_6_
  41.2 0.0 collective-permute-done.8.refs_7_
  41.2 5.1 %collective-permute-start.9 = (bf16[8,8,16,128]{3,2,1,0:T(8,128)(2,1)S(1)}, bf16[8,8,16,128]{3,2,1,0:T(8,128)(2,1)S(1)}, u32[]{:S(2)}, u32[]{:S(2)}) collective-permute-start(bf16[8,8,16,128]{3,2,1,0:T(8,128)(2,1)S(1)} %fusion.1), channel_id=1, source_target_pairs={{32,1},{1,32},{33,2},{2,33},{34,3},{3,34},{35,4},{4,35},{36,5},{5,... | collective-permute-start | bytes 786440 | tf_op jit(solution)/shard_map/ppermute | solution.py:192
  46.3 0.1 pad_add_fusion.place
  46.4 1.8 %shard_map.60.earlier = f32[64,8,128]{2,1,0:T(8,128)S(1)} custom-call(s32[2]{0:T(128)S(1)} %pad_add_fusion.place, bf16[5,8,16,128]{3,2,1,0:T(8,128)(2,1)S(1)} %collective-permute-done.1.refs_0_, bf16[5,8,16,128]{3,2,1,0:T(8,128)(2,1)S(1)} %collective-permute-done.3.refs_1_, bf16[5,8,16,128]{3,2,1,0:T(8,128)(2,1)S(1)} %maximum_select_fusion.1.refs_2_, ...), custom_call_target="tpu_custom_call" | custom-call | flops 900000000 | bytes 3000000 | tf_op jit(solution)/shard_map/pallas_call | solution.py:202
  48.2 2.2 %collective-permute-done.9.refs_8_.edge = bf16[8,8,16,128]{3,2,1,0:T(8,128)(2,1)S(1)} collective-permute-done((bf16[8,8,16,128]{3,2,1,0:T(8,128)(2,1)S(1)}, bf16[8,8,16,128]{3,2,1,0:T(8,128)(2,1)S(1)}, u32[]{:S(2)}, u32[]{:S(2)}) %collective-permute-start.9) | collective-permute-done | bytes 262176 | tf_op jit(solution)/shard_map/ppermute | solution.py:192
  50.4 1.7 %shard_map.61 = f32[64,8,128]{2,1,0:T(8,128)} custom-call(s32[2]{0:T(128)S(1)} %pad_add_fusion.place, bf16[8,8,16,128]{3,2,1,0:T(8,128)(2,1)S(1)} %collective-permute-done.9.refs_8_.edge, bf16[4,8,16,128]{3,2,1,0:T(8,128)(2,1)S(1)} %pad_maximum_fusion.refs_8_.cot, f32[64,8,128]{2,1,0:T(8,128)S(1)} %shard_map.60.earlier), custom_call_target="tpu_custom_call" | custom-call | flops 300000000 | bytes 3000000 | tf_op jit(solution)/shard_map/pallas_call | solution.py:202
  52.1 14.3 %all-to-all-start = ((f32[64,8,128]{2,1,0:T(8,128)}), f32[64,8,128]{2,1,0:T(8,128)S(1)}, u32[]{:S(2)}, u32[]{:S(2)}) async-start(f32[64,8,128]{2,1,0:T(8,128)} %shard_map.61), calls=%async_computation | async-start | bytes 524288 | tf_op jit(solution)/shard_map/all_to_all | solution.py:220
  66.4 1.6 %shard_map.59 = f32[16,4,8,128]{3,2,1,0:T(8,128)S(1)} custom-call(s32[2]{0:T(128)S(1)} %pad_add_fusion.place, bf16[5,8,16,128]{3,2,1,0:T(8,128)(2,1)S(1)} %collective-permute-done.1.refs_0_, bf16[5,8,16,128]{3,2,1,0:T(8,128)(2,1)S(1)} %collective-permute-done.3.refs_1_, bf16[5,8,16,128]{3,2,1,0:T(8,128)(2,1)S(1)} %maximum_select_fusion.1.refs_2_, ...), custom_call_target="tpu_custom_call" | custom-call | flops 1000000000 | bytes 3000000 | tf_op jit(solution)/shard_map/pallas_call | solution.py:202
  68.0 0.0 copy-start.2
  68.0 3.4 %collective-permute-start.10 = (f32[8,4,8,128]{3,2,1,0:T(8,128)S(1)}, f32[8,4,8,128]{3,2,1,0:T(8,128)S(1)}, u32[]{:S(2)}, u32[]{:S(2)}) collective-permute-start(f32[8,4,8,128]{3,2,1,0:T(8,128)S(1)} %get-tuple-element.11), channel_id=1, source_target_pairs={{0,32},{32,0},{1,33},{33,1},{2,34},{34,2},{3,35},{35,3},{4,36},{36... | collective-permute-start | bytes 393224 | tf_op jit(solution)/shard_map/ppermute | solution.py:228
  71.4 0.0 copy-done.2
  71.4 5.4 %collective-permute-done.10 = f32[8,4,8,128]{3,2,1,0:T(8,128)S(1)} collective-permute-done((f32[8,4,8,128]{3,2,1,0:T(8,128)S(1)}, f32[8,4,8,128]{3,2,1,0:T(8,128)S(1)}, u32[]{:S(2)}, u32[]{:S(2)}) %collective-permute-start.10) | collective-permute-done | bytes 131104 | tf_op jit(solution)/shard_map/ppermute | solution.py:228
  76.9 0.8 fusion
  77.7 1.5 %all-to-all-done = f32[64,8,128]{2,1,0:T(8,128)S(1)} async-done(((f32[64,8,128]{2,1,0:T(8,128)}), f32[64,8,128]{2,1,0:T(8,128)S(1)}, u32[]{:S(2)}, u32[]{:S(2)}) %all-to-all-start) | async-done | bytes 262176 | tf_op jit(solution)/shard_map/all_to_all | solution.py:220
  79.2 0.1 reduce_sum.9
  79.2 0.1 fusion.11
  79.3 0.1 pad_maximum_fusion.3
  79.4 0.1 stack.38
  79.5 0.1 stack.37
  79.6 0.1 stack.36
  79.7 0.2 copy.16
  79.8 0.7 reshape.24
  (25 shorter events, 0.4 us)
Async XLA Ops:
  1.6 5.0 %copy-start.1 = (bf16[8,8,8,128]{3,2,1,0:T(8,128)(2,1)S(1)}, bf16[8,8,8,128]{3,2,1,0:T(8,128)(2,1)}, u32[]{:S(2)}) copy-start(bf16[8,8,8,128]{3,2,1,0:T(8,128)(2,1)} %param.5) | copy-start | bytes 393220
  1.7 7.8 %collective-permute-start = (bf16[5,8,8,128]{3,2,1,0:T(8,128)(2,1)S(1)}, bf16[5,8,8,128]{3,2,1,0:T(8,128)(2,1)S(1)}, u32[]{:S(2)}, u32[]{:S(2)}) collective-permute-start(bf16[5,8,8,128]{3,2,1,0:T(8,128)(2,1)S(1)} %bitcast.23), channel_id=1, source_target_pairs={{0,32},{32,0},{1,33},{33,1},{2,34},{34,2},{3,35},{35,3},{4,36},{36... | collective-permute-start | bytes 245768 | tf_op jit(solution)/shard_map/ppermute | solution.py:158
  6.7 0.8 %copy-start = (bf16[27,8,128]{2,1,0:T(8,128)(2,1)S(1)}, bf16[27,8,128]{2,1,0:T(8,128)(2,1)}, u32[]{:S(2)}) copy-start(bf16[27,8,128]{2,1,0:T(8,128)(2,1)} %param.6) | copy-start | bytes 165892
  7.5 9.9 %collective-permute-start.2 = (bf16[59,8,128]{2,1,0:T(8,128)(2,1)S(1)}, bf16[59,8,128]{2,1,0:T(8,128)(2,1)S(1)}, u32[]{:S(2)}, u32[]{:S(2)}) collective-permute-start(bf16[59,8,128]{2,1,0:T(8,128)(2,1)S(1)} %pad_maximum_fusion.1), channel_id=1, source_target_pairs={{0,32},{32,0},{1,33},{33,1},{2,34},{34,2},{3,35},{35,3},{4,36},{36... | collective-permute-start | bytes 362504 | tf_op jit(solution)/shard_map/ppermute | solution.py:172
  9.6 14.4 %collective-permute-start.1 = (bf16[5,8,16,128]{3,2,1,0:T(8,128)(2,1)S(1)}, bf16[5,8,16,128]{3,2,1,0:T(8,128)(2,1)S(1)}, u32[]{:S(2)}, u32[]{:S(2)}) collective-permute-start(bf16[5,8,16,128]{3,2,1,0:T(8,128)(2,1)S(1)} %maximum_select_fusion.1.refs_2_), channel_id=1, source_target_pairs={{0,128},{64,192},{128,256},{192,320},{256,384},{320,448},{384,0},{... | collective-permute-start | bytes 491528 | tf_op jit(solution)/shard_map/ppermute | solution.py:175
  13.8 13.5 %collective-permute-start.5 = (bf16[5,8,16,128]{3,2,1,0:T(8,128)(2,1)S(1)}, bf16[5,8,16,128]{3,2,1,0:T(8,128)(2,1)S(1)}, u32[]{:S(2)}, u32[]{:S(2)}) collective-permute-start(bf16[5,8,16,128]{3,2,1,0:T(8,128)(2,1)S(1)} %maximum_select_fusion.1.refs_2_), channel_id=1, source_target_pairs={{0,384},{64,448},{128,0},{192,64},{256,128},{320,192},{384,256},{4... | collective-permute-start | bytes 491528 | tf_op jit(solution)/shard_map/ppermute | solution.py:175
  17.5 19.2 %collective-permute-start.3 = (bf16[5,8,16,128]{3,2,1,0:T(8,128)(2,1)S(1)}, bf16[5,8,16,128]{3,2,1,0:T(8,128)(2,1)S(1)}, u32[]{:S(2)}, u32[]{:S(2)}) collective-permute-start(bf16[5,8,16,128]{3,2,1,0:T(8,128)(2,1)S(1)} %maximum_select_fusion.1.refs_2_), channel_id=1, source_target_pairs={{0,64},{64,128},{128,192},{192,256},{256,320},{320,384},{384,448},... | collective-permute-start | bytes 491528 | tf_op jit(solution)/shard_map/ppermute | solution.py:175
  20.3 16.4 %collective-permute-start.4 = (bf16[5,8,16,128]{3,2,1,0:T(8,128)(2,1)S(1)}, bf16[5,8,16,128]{3,2,1,0:T(8,128)(2,1)S(1)}, u32[]{:S(2)}, u32[]{:S(2)}) collective-permute-start(bf16[5,8,16,128]{3,2,1,0:T(8,128)(2,1)S(1)} %maximum_select_fusion.1.refs_2_), channel_id=1, source_target_pairs={{0,448},{64,0},{128,64},{192,128},{256,192},{320,256},{384,320},{4... | collective-permute-start | bytes 491528 | tf_op jit(solution)/shard_map/ppermute | solution.py:175
  27.3 13.8 %collective-permute-start.7 = (bf16[5,8,16,128]{3,2,1,0:T(8,128)(2,1)S(1)}, bf16[5,8,16,128]{3,2,1,0:T(8,128)(2,1)S(1)}, u32[]{:S(2)}, u32[]{:S(2)}) collective-permute-start(bf16[5,8,16,128]{3,2,1,0:T(8,128)(2,1)S(1)} %broadcast_select_fusion), channel_id=1, source_target_pairs={{0,384},{1,129},{64,448},{65,193},{128,0},{129,257},{192,64},{193,... | collective-permute-start | bytes 491528 | tf_op jit(solution)/shard_map/ppermute | solution.py:188
  31.3 9.8 %collective-permute-start.6 = (bf16[5,8,16,128]{3,2,1,0:T(8,128)(2,1)S(1)}, bf16[5,8,16,128]{3,2,1,0:T(8,128)(2,1)S(1)}, u32[]{:S(2)}, u32[]{:S(2)}) collective-permute-start(bf16[5,8,16,128]{3,2,1,0:T(8,128)(2,1)S(1)} %collective-permute-done.5.refs_4_), channel_id=1, source_target_pairs={{0,448},{64,0},{128,64},{192,128},{256,192},{320,256},{384,320},{4... | collective-permute-start | bytes 491528 | tf_op jit(solution)/shard_map/ppermute | solution.py:175
  33.2 8.0 %collective-permute-start.8 = (bf16[5,8,16,128]{3,2,1,0:T(8,128)(2,1)S(1)}, bf16[5,8,16,128]{3,2,1,0:T(8,128)(2,1)S(1)}, u32[]{:S(2)}, u32[]{:S(2)}) collective-permute-start(bf16[5,8,16,128]{3,2,1,0:T(8,128)(2,1)S(1)} %collective-permute-done.1.refs_0_), channel_id=1, source_target_pairs={{0,64},{64,128},{128,192},{192,256},{256,320},{320,384},{384,448},... | collective-permute-start | bytes 491528 | tf_op jit(solution)/shard_map/ppermute | solution.py:175
  41.2 9.1 %collective-permute-start.9 = (bf16[8,8,16,128]{3,2,1,0:T(8,128)(2,1)S(1)}, bf16[8,8,16,128]{3,2,1,0:T(8,128)(2,1)S(1)}, u32[]{:S(2)}, u32[]{:S(2)}) collective-permute-start(bf16[8,8,16,128]{3,2,1,0:T(8,128)(2,1)S(1)} %fusion.1), channel_id=1, source_target_pairs={{32,1},{1,32},{33,2},{2,33},{34,3},{3,34},{35,4},{4,35},{36,5},{5,... | collective-permute-start | bytes 786440 | tf_op jit(solution)/shard_map/ppermute | solution.py:192
  52.1 27.1 %all-to-all-start = ((f32[64,8,128]{2,1,0:T(8,128)}), f32[64,8,128]{2,1,0:T(8,128)S(1)}, u32[]{:S(2)}, u32[]{:S(2)}) async-start(f32[64,8,128]{2,1,0:T(8,128)} %shard_map.61), calls=%async_computation | async-start | bytes 524288 | tf_op jit(solution)/shard_map/all_to_all | solution.py:220
  68.0 3.4 %copy-start.2 = (bf16[8]{0:T(256)(128)(2,1)S(1)}, bf16[8]{0:T(256)(128)(2,1)}, u32[]{:S(2)}) copy-start(bf16[8]{0:T(256)(128)(2,1)} %param.7) | copy-start | bytes 52
  68.0 8.9 %collective-permute-start.10 = (f32[8,4,8,128]{3,2,1,0:T(8,128)S(1)}, f32[8,4,8,128]{3,2,1,0:T(8,128)S(1)}, u32[]{:S(2)}, u32[]{:S(2)}) collective-permute-start(f32[8,4,8,128]{3,2,1,0:T(8,128)S(1)} %get-tuple-element.11), channel_id=1, source_target_pairs={{0,32},{32,0},{1,33},{33,1},{2,34},{34,2},{3,35},{35,3},{4,36},{36... | collective-permute-start | bytes 393224 | tf_op jit(solution)/shard_map/ppermute | solution.py:228

commit v6 on v5

--- a/solution.py
+++ b/solution.py
@@ -13,13 +13,15 @@
 DEPTH = 8
 WIDTH = 128
 STEPS = 8
-
-
-def fill(rows, place, blocks, edge):
+SCALE = 1.0 / math.sqrt(256 * DEPTH * WIDTH)
+
+
+def fill(rows, place, blocks, edges):
     zl = place[1]
     for p, block in enumerate(blocks):
         rows[p, pl.ds(1 - zl, 5)] = block[...]
-    rows[:, 5 * zl] = edge
+    rows[0:5, 5 * zl] = edges[0]
+    rows[5:8, 5 * zl] = edges[1]
 
 
 def cells_of(rows, row):
@@ -35,9 +37,9 @@
 
 
 def forward_kernel(place, *refs):
-    *blocks, edge, weights, feat, rows = refs
+    *blocks, near, far, weights, feat, rows = refs
     y = place[0]
-    fill(rows, place, blocks, edge[...])
+    fill(rows, place, blocks, (near[...], far[...]))
     lane = lax.broadcasted_iota(jnp.int32, (16, WIDTH), 1)
     turned = pltpu.roll(
         weights[...].astype(jnp.float32).reshape(27 * 16, 128), lax.rem(128 - 16 * y + 32, 128), 1
@@ -93,6 +95,18 @@
     return jnp.concatenate(columns, axis=1)
 
 
+def edge_cells(near, far):
+    return jnp.concatenate(
+        [
+            jnp.concatenate(
+                [near[p, z] for p in range(5)] + [far[p, z] for p in range(3)], axis=0
+            )
+            for z in range(DEPTH)
+        ],
+        axis=1,
+    )
+
+
 def over_cells(a, b):
     return lax.dot_general(a, b, (((1,), (1,)), ((), ())), preferred_element_type=jnp.float32)
 
@@ -110,11 +124,15 @@
 
 
 def gradient_kernel(place, *refs):
-    *blocks, cot, grad, rows = refs
-    fill(rows, place, blocks, jnp.zeros((STEPS, DEPTH, 16, WIDTH), jnp.bfloat16))
+    *blocks, cot, grad, moved, rows = refs
+    zeros = [jnp.zeros((count, DEPTH, 16, WIDTH), jnp.bfloat16) for count in (5, 3)]
+    fill(rows, place, blocks, zeros)
     total = jnp.zeros((384, 256), jnp.float32)
     for row in range(ROWS):
-        total = total + over_cells(cells_of(rows, row), shifted(cot, row))
+        here = shifted(cot, row)
+        if row in (0, 3):
+            moved[row // 3] = here
+        total = total + over_cells(cells_of(rows, row), here)
     wide = lax.broadcasted_iota(jnp.int32, (128, WIDTH), 1)
     for half in range(2):
         one, two, three = (
@@ -122,24 +140,21 @@
             for dx in range(3)
         )
         one = jnp.where(wide < 72, one, pltpu.roll(three, 72, 1))
-        two = jnp.where(wide < 72, two, pltpu.roll(three, 36, 1))
+        two = jnp.where(wide < 72, two, pltpu.roll(three, 32, 1))
         for k, at in enumerate(receivers(place, half)):
             grad[at], grad[at + 1] = pair_of(one, two, k)
 
 
-def edge_kernel(place, edge, cot, earlier, grad):
+def edge_kernel(place, near, far, moved, earlier, grad):
     zl = place[1]
-    cells = jnp.concatenate(
-        [jnp.concatenate([edge[p, z] for p in range(STEPS)], axis=0) for z in range(DEPTH)], axis=1
-    )
-    total = over_cells(cells, shifted(cot, 3 * zl))
+    total = over_cells(edge_cells(near, far), moved[zl])
     wide = lax.broadcasted_iota(jnp.int32, (128, WIDTH), 1)
     low = zl == 0
     for half in range(2):
         part = total[:, WIDTH * half : WIDTH * half + WIDTH]
         one = jnp.where(low, part, jnp.where(wide < 72, 0.0, pltpu.roll(part, 72, 1)))
         two = jnp.where(
-            jnp.logical_or(low, wide < 72), 0.0, pltpu.roll(part, 36, 1)
+            jnp.logical_or(low, wide < 72), 0.0, pltpu.roll(part, 32, 1)
         )
         for k, at in enumerate(receivers(place, half)):
             first, second = pair_of(one, two, k)
@@ -147,9 +162,15 @@
             grad[at + 1] = earlier[at + 1] + second
 
 
+def finish_kernel(place, got, out):
+    summed = jnp.transpose(jnp.sum(got[...], axis=0) * SCALE)
+    for at, count, lane, start in ((0, 9, 0, 0), (9, 9, 4, 0), (18, 5, 0, 72), (23, 4, 4, 72)):
+        part = summed[start : start + 8 * count, lane : lane + 4]
+        out[at : at + count] = part.reshape(count, 8, 4)
+
+
 def on_device(activations, cotangent, filters, bias_terms):
     y, zl = lax.axis_index("y"), lax.axis_index("zl")
-    scale = jnp.float32(1.0 / math.sqrt(activations.shape[1] * 32 * DEPTH * WIDTH))
     acts = jnp.transpose(activations, (1, 2, 0, 3))
     cots = jnp.transpose(cotangent, (1, 2, 0, 3))
     first = zl == 0
@@ -188,22 +209,29 @@
     b4 = lax.ppermute(jnp.where(lax.axis_index("core") == 0, b2, b6), ("y", "core"), turn)
     b3, b5 = along(b2, 1), along(b6, -1)
 
-    blocks = (b6, b7, mine, b1, b2, b3, b4, b5)
-    edge = lax.ppermute(
-        jnp.stack([jnp.where(first, block[0], block[4]) for block in blocks]),
-        ("zl",) + SPACE,
-        pairs,
-    )
+    def outermost(blocks):
+        return jnp.stack([jnp.where(first, block[0], block[4]) for block in blocks])
+
+    near = (b6, b7, mine, b1, b2)
+    send, b3 = lax.optimization_barrier((outermost(near), b3))
+    far = (b3, b4, b5)
+    edges = (
+        lax.ppermute(send, ("zl",) + SPACE, pairs),
+        lax.ppermute(outermost(far), ("zl",) + SPACE, pairs),
+    )
+    blocks = near + far
+    cot, first_edges = lax.optimization_barrier((cot, edges[0]))
+    edges = (first_edges, edges[1])
 
     place = jnp.stack([y, zl])
 
-    def local(kernel, shape, operands, scratch):
+    def local(kernel, shapes, operands, scratch):
         vmem = pl.BlockSpec(memory_space=pltpu.VMEM)
         return pl.pallas_call(
             kernel,
-            out_shape=jax.ShapeDtypeStruct(shape, jnp.float32),
+            out_shape=shapes,
             in_specs=[pl.BlockSpec(memory_space=pltpu.SMEM)] + [vmem] * len(operands),
-            out_specs=vmem,
+            out_specs=jax.tree.map(lambda _: vmem, shapes),
             scratch_shapes=scratch,
             compiler_params=pltpu.CompilerParams(vmem_limit_bytes=48 * 1024 * 1024),
             cost_estimate=pl.CostEstimate(
@@ -211,19 +239,27 @@
             ),
         )(place, *operands)
 
-    tiles = (64, 8, WIDTH)
+    tiles = jax.ShapeDtypeStruct((64, 8, WIDTH), jnp.float32)
     rows = [pltpu.VMEM((STEPS, 6, DEPTH, 16, WIDTH), jnp.bfloat16)]
-    grad = local(gradient_kernel, tiles, (*blocks, cot), rows)
-    grad = local(edge_kernel, tiles, (edge, cot, grad), [])
-    feat = local(forward_kernel, (16, ROWS, DEPTH, WIDTH), (*blocks, edge, weights), rows)
+    grad, moved = local(
+        gradient_kernel,
+        (tiles, jax.ShapeDtypeStruct((2, 256, DEPTH * WIDTH), jnp.bfloat16)),
+        (*blocks, cot),
+        rows,
+    )
+    grad = local(edge_kernel, tiles, (*edges, moved, grad), [])
+    weights, grad = lax.optimization_barrier((weights, grad))
+    feat = local(
+        forward_kernel,
+        jax.ShapeDtypeStruct((16, ROWS, DEPTH, WIDTH), jnp.float32),
+        (*blocks, *edges, weights),
+        rows,
+    )
 
     got = lax.all_to_all(grad, ("zl",) + SPACE, 0, 0, tiled=True)
-    summed = jnp.sum(got, axis=0) * scale
-    low, high = summed[:4], summed[4:]
-    filter_grad = jnp.stack(
-        [low[:, :72], high[:, :72], jnp.concatenate([low[:, 72:108], high[:, 72:108]], axis=1)]
-    )
-    filter_grad = filter_grad.reshape(3, 4, 9, 8).transpose(0, 2, 3, 1).reshape(27, 8, 4)
+    filter_grad = local(
+        finish_kernel, jax.ShapeDtypeStruct((27, 8, 4), jnp.float32), (got,), []
+    )
 
     rest = lax.ppermute(feat[8:], "zl", swap)
     kept = feat[:8]

time: 81.1 us -> 80.2 us (0.989)
  starting transfers between devices: 53.2 us -> 52 us
    all_to_all x1, starting transfers between devices: 14.3 us -> 12.7 us  [on_device(): got = lax.all_to_all(grad, ('zl',) + SPACE, 0, 0, tiled=True)]
    pallas_call x3 -> x4, Pallas kernels: 5.07 us -> 5.8 us  [local(): pl.pallas_call(kernel, out_shape=shapes, in_specs=[pl.BlockSpec(memory_sp...]
    ppermute x1 -> x2, starting transfers between devices: 5.09 us -> 5.55 us  [the longest x1 3.38 us: on_device(): lax.ppermute(send, ('zl',) + SPACE, pairs)]
    ppermute x1 -> x2, waiting for transfers between devices: 2.2 us -> 1.91 us  [the longest x1 1.02 us: on_device(): lax.ppermute(outermost(far), ('zl',) + SPACE, pairs)]
    unnamed x11 -> x10, local copies, waits for them, and re-layouts: 1.7 us -> 1.58 us
  transfers between devices with their start and end apart: 12 -> 13, of which waited for: 5 -> 6; matrix products, arithmetic and copies ran while one was open for 2% -> 2% of each run, Pallas kernels for 4% -> 4%
where the time goes in v6:
time: 80.2 us; the launch traced here: 79.2 us
  starting transfers between devices  52 us (65%)
  waiting for transfers between devices  16.5 us (21%)
  Pallas kernels  5.8 us (7%)
  local copies, waits for them, and re-layouts  2.64 us (3%)
  other arithmetic  1.13 us (1%)
  between operations  1.03 us (1%)
    ppermute x6, starting transfers between devices, along(): lax.ppermute(block, 'y', [(i, (i - by) % STEPS) for i in range(STEPS)])  19.6 us
    all_to_all x1, starting transfers between devices, on_device(): got = lax.all_to_all(grad, ('zl',) + SPACE, 0, 0, tiled=True)  12.7 us
    ppermute x6, waiting for transfers between devices, along(): lax.ppermute(block, 'y', [(i, (i - by) % STEPS) for i in range(STEPS)])  7.69 us
    pallas_call x4, Pallas kernels, local(): pl.pallas_call(kernel, out_shape=shapes, in_specs=[pl.BlockSpec(memory_sp...  5.8 us
    ppermute x1, waiting for transfers between devices, on_device(): rest = lax.ppermute(feat[8:], 'zl', swap)  5.44 us
    ppermute x1, starting transfers between devices, on_device(): lax.ppermute(lax.dynamic_slice_in_dim(acts, 3 * (1 - zl), 5, 0), 'zl', swap)  4.96 us
    ppermute x1, starting transfers between devices, on_device(): lax.ppermute(jnp.where(lax.axis_index('core') == 0, b2, b6), ('y', 'core'...  3.98 us
    ppermute x1, starting transfers between devices, on_device(): rest = lax.ppermute(feat[8:], 'zl', swap)  3.39 us
  transfers between devices with their start and end apart: 13, of which 6 were waited for; matrix products, arithmetic and copies ran while one was open for 2% of the time, Pallas kernels for 4%

profile of v6, /device:TPU:1, one launch (start us, length us, event | category | flops | bytes accessed | tf_op | source)
XLA Modules:
  0.0 79.2 jit_solution(3523836179997622948)
XLA Ops:
  0.6 1.0 %constant_dynamic-slice_fusion.2 = (bf16[8,5,8,128]{3,2,1,0:T(8,128)(2,1)S(1)}, bf16[8,5,8,128]{3,2,1,0:T(8,128)(2,1)S(1)}) fusion(bf16[8,8,8,128]{3,2,1,0:T(8,128)(2,1)} %param.4, s32[]{:T(128)S(6)} %select_n.80, s32[]{:T(128)S(6)} %select_n.81), kind=kLoop, calls=%fused_computation.27 | loop fusion | bytes 327688 | tf_op jit(solution)/shard_map/dynamic-slice
  1.6 0.0 copy-start.1
  1.7 5.0 %collective-permute-start = (bf16[5,8,8,128]{3,2,1,0:T(8,128)(2,1)S(1)}, bf16[5,8,8,128]{3,2,1,0:T(8,128)(2,1)S(1)}, u32[]{:S(2)}, u32[]{:S(2)}) collective-permute-start(bf16[5,8,8,128]{3,2,1,0:T(8,128)(2,1)S(1)} %bitcast.19), channel_id=1, source_target_pairs={{0,32},{32,0},{1,33},{33,1},{2,34},{34,2},{3,35},{35,3},{4,36},{36... | collective-permute-start | bytes 245768 | tf_op jit(solution)/shard_map/ppermute | solution.py:179
  6.6 0.0 copy-done.1
  6.7 0.0 copy-start
  6.7 0.8 copy-done
  7.5 1.9 %collective-permute-start.2 = (bf16[59,8,128]{2,1,0:T(8,128)(2,1)S(1)}, bf16[59,8,128]{2,1,0:T(8,128)(2,1)S(1)}, u32[]{:S(2)}, u32[]{:S(2)}) collective-permute-start(bf16[59,8,128]{2,1,0:T(8,128)(2,1)S(1)} %pad_maximum_fusion.1), channel_id=1, source_target_pairs={{0,32},{32,0},{1,33},{33,1},{2,34},{34,2},{3,35},{35,3},{4,36},{36... | collective-permute-start | bytes 362504 | tf_op jit(solution)/shard_map/ppermute | solution.py:193
  9.5 0.0 collective-permute-done
  9.6 4.2 %collective-permute-start.1 = (bf16[5,8,16,128]{3,2,1,0:T(8,128)(2,1)S(1)}, bf16[5,8,16,128]{3,2,1,0:T(8,128)(2,1)S(1)}, u32[]{:S(2)}, u32[]{:S(2)}) collective-permute-start(bf16[5,8,16,128]{3,2,1,0:T(8,128)(2,1)S(1)} %maximum_select_fusion.1.refs_2_), channel_id=1, source_target_pairs={{0,128},{64,192},{128,256},{192,320},{256,384},{320,448},{384,0},{... | collective-permute-start | bytes 491528 | tf_op jit(solution)/shard_map/ppermute | solution.py:196
  13.8 3.6 %collective-permute-start.5 = (bf16[5,8,16,128]{3,2,1,0:T(8,128)(2,1)S(1)}, bf16[5,8,16,128]{3,2,1,0:T(8,128)(2,1)S(1)}, u32[]{:S(2)}, u32[]{:S(2)}) collective-permute-start(bf16[5,8,16,128]{3,2,1,0:T(8,128)(2,1)S(1)} %maximum_select_fusion.1.refs_2_), channel_id=1, source_target_pairs={{0,384},{64,448},{128,0},{192,64},{256,128},{320,192},{384,256},{4... | collective-permute-start | bytes 491528 | tf_op jit(solution)/shard_map/ppermute | solution.py:196
  17.4 0.0 collective-permute-done.2
  17.5 2.8 %collective-permute-start.3 = (bf16[5,8,16,128]{3,2,1,0:T(8,128)(2,1)S(1)}, bf16[5,8,16,128]{3,2,1,0:T(8,128)(2,1)S(1)}, u32[]{:S(2)}, u32[]{:S(2)}) collective-permute-start(bf16[5,8,16,128]{3,2,1,0:T(8,128)(2,1)S(1)} %maximum_select_fusion.1.refs_2_), channel_id=1, source_target_pairs={{0,64},{64,128},{128,192},{192,256},{256,320},{320,384},{384,448},... | collective-permute-start | bytes 491528 | tf_op jit(solution)/shard_map/ppermute | solution.py:196
  20.3 3.7 %collective-permute-start.4 = (bf16[5,8,16,128]{3,2,1,0:T(8,128)(2,1)S(1)}, bf16[5,8,16,128]{3,2,1,0:T(8,128)(2,1)S(1)}, u32[]{:S(2)}, u32[]{:S(2)}) collective-permute-start(bf16[5,8,16,128]{3,2,1,0:T(8,128)(2,1)S(1)} %maximum_select_fusion.1.refs_2_), channel_id=1, source_target_pairs={{0,448},{64,0},{128,64},{192,128},{256,192},{320,256},{384,320},{4... | collective-permute-start | bytes 491528 | tf_op jit(solution)/shard_map/ppermute | solution.py:196
  24.0 0.0 collective-permute-done.1.refs_0_
  24.0 3.3 %collective-permute-done.5.refs_4_ = bf16[5,8,16,128]{3,2,1,0:T(8,128)(2,1)S(1)} collective-permute-done((bf16[5,8,16,128]{3,2,1,0:T(8,128)(2,1)S(1)}, bf16[5,8,16,128]{3,2,1,0:T(8,128)(2,1)S(1)}, u32[]{:S(2)}, u32[]{:S(2)}) %collective-permute-start.5) | collective-permute-done | bytes 163872 | tf_op jit(solution)/shard_map/ppermute | solution.py:196
  27.3 4.0 %collective-permute-start.7 = (bf16[5,8,16,128]{3,2,1,0:T(8,128)(2,1)S(1)}, bf16[5,8,16,128]{3,2,1,0:T(8,128)(2,1)S(1)}, u32[]{:S(2)}, u32[]{:S(2)}) collective-permute-start(bf16[5,8,16,128]{3,2,1,0:T(8,128)(2,1)S(1)} %broadcast_select_fusion), channel_id=1, source_target_pairs={{0,384},{1,129},{64,448},{65,193},{128,0},{129,257},{192,64},{193,... | collective-permute-start | bytes 491528 | tf_op jit(solution)/shard_map/ppermute | solution.py:209
  31.3 1.9 %collective-permute-start.6 = (bf16[5,8,16,128]{3,2,1,0:T(8,128)(2,1)S(1)}, bf16[5,8,16,128]{3,2,1,0:T(8,128)(2,1)S(1)}, u32[]{:S(2)}, u32[]{:S(2)}) collective-permute-start(bf16[5,8,16,128]{3,2,1,0:T(8,128)(2,1)S(1)} %collective-permute-done.5.refs_4_), channel_id=1, source_target_pairs={{0,448},{64,0},{128,64},{192,128},{256,192},{320,256},{384,320},{4... | collective-permute-start | bytes 491528 | tf_op jit(solution)/shard_map/ppermute | solution.py:196
  33.2 3.4 %collective-permute-start.8 = (bf16[5,8,16,128]{3,2,1,0:T(8,128)(2,1)S(1)}, bf16[5,8,16,128]{3,2,1,0:T(8,128)(2,1)S(1)}, u32[]{:S(2)}, u32[]{:S(2)}) collective-permute-start(bf16[5,8,16,128]{3,2,1,0:T(8,128)(2,1)S(1)} %collective-permute-done.1.refs_0_), channel_id=1, source_target_pairs={{0,64},{64,128},{128,192},{192,256},{256,320},{320,384},{384,448},... | collective-permute-start | bytes 491528 | tf_op jit(solution)/shard_map/ppermute | solution.py:196
  36.6 0.0 collective-permute-done.3.refs_1_
  36.7 0.0 collective-permute-done.4.refs_3_
  36.8 4.4 %collective-permute-done.6.refs_5_ = bf16[5,8,16,128]{3,2,1,0:T(8,128)(2,1)S(1)} collective-permute-done((bf16[5,8,16,128]{3,2,1,0:T(8,128)(2,1)S(1)}, bf16[5,8,16,128]{3,2,1,0:T(8,128)(2,1)S(1)}, u32[]{:S(2)}, u32[]{:S(2)}) %collective-permute-start.6) | collective-permute-done | bytes 163872 | tf_op jit(solution)/shard_map/ppermute | solution.py:196
  41.1 3.4 %collective-permute-start.9 = (bf16[5,8,16,128]{3,2,1,0:T(8,128)(2,1)S(1)}, bf16[5,8,16,128]{3,2,1,0:T(8,128)(2,1)S(1)}, u32[]{:S(2)}, u32[]{:S(2)}) collective-permute-start(bf16[5,8,16,128]{3,2,1,0:T(8,128)(2,1)S(1)} %fusion.1), channel_id=1, source_target_pairs={{32,1},{1,32},{33,2},{2,33},{34,3},{3,34},{35,4},{4,35},{36,5},{5,... | collective-permute-start | bytes 491528 | tf_op jit(solution)/shard_map/ppermute | solution.py:219
  44.5 0.0 collective-permute-done.8.refs_7_
  44.6 0.0 collective-permute-done.7.refs_6_
  44.6 2.2 %collective-permute-start.10 = (bf16[3,8,16,128]{3,2,1,0:T(8,128)(2,1)S(1)}, bf16[3,8,16,128]{3,2,1,0:T(8,128)(2,1)S(1)}, u32[]{:S(2)}, u32[]{:S(2)}) collective-permute-start(bf16[3,8,16,128]{3,2,1,0:T(8,128)(2,1)S(1)} %pad_maximum_fusion.3), channel_id=1, source_target_pairs={{32,1},{1,32},{33,2},{2,33},{34,3},{3,34},{35,4},{4,35},{36,5},{5,... | collective-permute-start | bytes 294920 | tf_op jit(solution)/shard_map/ppermute | solution.py:220
  46.8 0.1 pad_add_fusion.place
  46.9 0.9 %collective-permute-done.9.near.refs_8_ = bf16[5,8,16,128]{3,2,1,0:T(8,128)(2,1)S(1)} collective-permute-done((bf16[5,8,16,128]{3,2,1,0:T(8,128)(2,1)S(1)}, bf16[5,8,16,128]{3,2,1,0:T(8,128)(2,1)S(1)}, u32[]{:S(2)}, u32[]{:S(2)}) %collective-permute-start.9) | collective-permute-done | bytes 163872 | tf_op jit(solution)/shard_map/ppermute | solution.py:219
  47.8 1.8 %shard_map.59 = (f32[64,8,128]{2,1,0:T(8,128)S(1)}, bf16[2,256,1024]{2,1,0:T(8,128)(2,1)S(1)}) custom-call(s32[2]{0:T(128)S(1)} %pad_add_fusion.place, bf16[5,8,16,128]{3,2,1,0:T(8,128)(2,1)S(1)} %collective-permute-done.1.refs_0_, bf16[5,8,16,128]{3,2,1,0:T(8,128)(2,1)S(1)} %collective-permute-done.3.refs_1_, ...), custom_call_target="tpu_custom_call" | custom-call | flops 900000000 | bytes 3000000 | tf_op jit(solution)/shard_map/pallas_call | solution.py:230
  49.5 1.0 %collective-permute-done.10.far.refs_9_ = bf16[3,8,16,128]{3,2,1,0:T(8,128)(2,1)S(1)} collective-permute-done((bf16[3,8,16,128]{3,2,1,0:T(8,128)(2,1)S(1)}, bf16[3,8,16,128]{3,2,1,0:T(8,128)(2,1)S(1)}, u32[]{:S(2)}, u32[]{:S(2)}) %collective-permute-start.10) | collective-permute-done | bytes 98336 | tf_op jit(solution)/shard_map/ppermute | solution.py:220
  50.6 1.7 %shard_map.60 = f32[64,8,128]{2,1,0:T(8,128)} custom-call(s32[2]{0:T(128)S(1)} %pad_add_fusion.place, bf16[5,8,16,128]{3,2,1,0:T(8,128)(2,1)S(1)} %collective-permute-done.9.near.refs_8_, bf16[3,8,16,128]{3,2,1,0:T(8,128)(2,1)S(1)} %collective-permute-done.10.far.refs_9_, bf16[2,256,1024]{2,1,0:T(8,128)(2,1)S(1)} %get-tuple-element.20.moved, ...), custom_call_target="tpu_custom_call" | custom-call | flops 400000000 | bytes 3000000 | tf_op jit(solution)/shard_map/pallas_call | solution.py:230
  52.2 12.7 %all-to-all-start = ((f32[64,8,128]{2,1,0:T(8,128)}), f32[64,8,128]{2,1,0:T(8,128)S(1)}, u32[]{:S(2)}, u32[]{:S(2)}) async-start(f32[64,8,128]{2,1,0:T(8,128)} %shard_map.60), calls=%async_computation | async-start | bytes 524288 | tf_op jit(solution)/shard_map/all_to_all | solution.py:259
  64.9 1.6 %shard_map.61 = f32[16,4,8,128]{3,2,1,0:T(8,128)S(1)} custom-call(s32[2]{0:T(128)S(1)} %pad_add_fusion.place, bf16[5,8,16,128]{3,2,1,0:T(8,128)(2,1)S(1)} %collective-permute-done.1.refs_0_, bf16[5,8,16,128]{3,2,1,0:T(8,128)(2,1)S(1)} %collective-permute-done.3.refs_1_, bf16[5,8,16,128]{3,2,1,0:T(8,128)(2,1)S(1)} %maximum_select_fusion.1.refs_2_, ...), custom_call_target="tpu_custom_call" | custom-call | flops 1100000000 | bytes 3000000 | tf_op jit(solution)/shard_map/pallas_call | solution.py:230
  66.5 0.0 copy-start.2
  66.5 3.4 %collective-permute-start.11 = (f32[8,4,8,128]{3,2,1,0:T(8,128)S(1)}, f32[8,4,8,128]{3,2,1,0:T(8,128)S(1)}, u32[]{:S(2)}, u32[]{:S(2)}) collective-permute-start(f32[8,4,8,128]{3,2,1,0:T(8,128)S(1)} %get-tuple-element.27), channel_id=1, source_target_pairs={{0,32},{32,0},{1,33},{33,1},{2,34},{34,2},{3,35},{35,3},{4,36},{36... | collective-permute-start | bytes 393224 | tf_op jit(solution)/shard_map/ppermute | solution.py:264
  69.9 0.0 copy-done.2
  70.0 5.4 %collective-permute-done.11 = f32[8,4,8,128]{3,2,1,0:T(8,128)S(1)} collective-permute-done((f32[8,4,8,128]{3,2,1,0:T(8,128)S(1)}, f32[8,4,8,128]{3,2,1,0:T(8,128)S(1)}, u32[]{:S(2)}, u32[]{:S(2)}) %collective-permute-start.11) | collective-permute-done | bytes 131104 | tf_op jit(solution)/shard_map/ppermute | solution.py:264
  75.4 0.8 fusion
  76.2 1.5 %all-to-all-done.got = f32[64,8,128]{2,1,0:T(8,128)S(1)} async-done(((f32[64,8,128]{2,1,0:T(8,128)}), f32[64,8,128]{2,1,0:T(8,128)S(1)}, u32[]{:S(2)}, u32[]{:S(2)}) %all-to-all-start) | async-done | bytes 262176 | tf_op jit(solution)/shard_map/all_to_all | solution.py:259
  77.7 0.8 shard_map.62
  78.5 0.7 copy.10
  (23 shorter events, 0.4 us)
Async XLA Ops:
  1.6 5.0 %copy-start.1 = (bf16[8,8,8,128]{3,2,1,0:T(8,128)(2,1)S(1)}, bf16[8,8,8,128]{3,2,1,0:T(8,128)(2,1)}, u32[]{:S(2)}) copy-start(bf16[8,8,8,128]{3,2,1,0:T(8,128)(2,1)} %param.5) | copy-start | bytes 393220
  1.7 7.8 %collective-permute-start = (bf16[5,8,8,128]{3,2,1,0:T(8,128)(2,1)S(1)}, bf16[5,8,8,128]{3,2,1,0:T(8,128)(2,1)S(1)}, u32[]{:S(2)}, u32[]{:S(2)}) collective-permute-start(bf16[5,8,8,128]{3,2,1,0:T(8,128)(2,1)S(1)} %bitcast.19), channel_id=1, source_target_pairs={{0,32},{32,0},{1,33},{33,1},{2,34},{34,2},{3,35},{35,3},{4,36},{36... | collective-permute-start | bytes 245768 | tf_op jit(solution)/shard_map/ppermute | solution.py:179
  6.7 0.8 %copy-start = (bf16[27,8,128]{2,1,0:T(8,128)(2,1)S(1)}, bf16[27,8,128]{2,1,0:T(8,128)(2,1)}, u32[]{:S(2)}) copy-start(bf16[27,8,128]{2,1,0:T(8,128)(2,1)} %param.6) | copy-start | bytes 165892
  7.5 9.9 %collective-permute-start.2 = (bf16[59,8,128]{2,1,0:T(8,128)(2,1)S(1)}, bf16[59,8,128]{2,1,0:T(8,128)(2,1)S(1)}, u32[]{:S(2)}, u32[]{:S(2)}) collective-permute-start(bf16[59,8,128]{2,1,0:T(8,128)(2,1)S(1)} %pad_maximum_fusion.1), channel_id=1, source_target_pairs={{0,32},{32,0},{1,33},{33,1},{2,34},{34,2},{3,35},{35,3},{4,36},{36... | collective-permute-start | bytes 362504 | tf_op jit(solution)/shard_map/ppermute | solution.py:193
  9.6 14.4 %collective-permute-start.1 = (bf16[5,8,16,128]{3,2,1,0:T(8,128)(2,1)S(1)}, bf16[5,8,16,128]{3,2,1,0:T(8,128)(2,1)S(1)}, u32[]{:S(2)}, u32[]{:S(2)}) collective-permute-start(bf16[5,8,16,128]{3,2,1,0:T(8,128)(2,1)S(1)} %maximum_select_fusion.1.refs_2_), channel_id=1, source_target_pairs={{0,128},{64,192},{128,256},{192,320},{256,384},{320,448},{384,0},{... | collective-permute-start | bytes 491528 | tf_op jit(solution)/shard_map/ppermute | solution.py:196
  13.8 13.5 %collective-permute-start.5 = (bf16[5,8,16,128]{3,2,1,0:T(8,128)(2,1)S(1)}, bf16[5,8,16,128]{3,2,1,0:T(8,128)(2,1)S(1)}, u32[]{:S(2)}, u32[]{:S(2)}) collective-permute-start(bf16[5,8,16,128]{3,2,1,0:T(8,128)(2,1)S(1)} %maximum_select_fusion.1.refs_2_), channel_id=1, source_target_pairs={{0,384},{64,448},{128,0},{192,64},{256,128},{320,192},{384,256},{4... | collective-permute-start | bytes 491528 | tf_op jit(solution)/shard_map/ppermute | solution.py:196
  17.5 19.2 %collective-permute-start.3 = (bf16[5,8,16,128]{3,2,1,0:T(8,128)(2,1)S(1)}, bf16[5,8,16,128]{3,2,1,0:T(8,128)(2,1)S(1)}, u32[]{:S(2)}, u32[]{:S(2)}) collective-permute-start(bf16[5,8,16,128]{3,2,1,0:T(8,128)(2,1)S(1)} %maximum_select_fusion.1.refs_2_), channel_id=1, source_target_pairs={{0,64},{64,128},{128,192},{192,256},{256,320},{320,384},{384,448},... | collective-permute-start | bytes 491528 | tf_op jit(solution)/shard_map/ppermute | solution.py:196
  20.3 16.4 %collective-permute-start.4 = (bf16[5,8,16,128]{3,2,1,0:T(8,128)(2,1)S(1)}, bf16[5,8,16,128]{3,2,1,0:T(8,128)(2,1)S(1)}, u32[]{:S(2)}, u32[]{:S(2)}) collective-permute-start(bf16[5,8,16,128]{3,2,1,0:T(8,128)(2,1)S(1)} %maximum_select_fusion.1.refs_2_), channel_id=1, source_target_pairs={{0,448},{64,0},{128,64},{192,128},{256,192},{320,256},{384,320},{4... | collective-permute-start | bytes 491528 | tf_op jit(solution)/shard_map/ppermute | solution.py:196
  27.3 17.2 %collective-permute-start.7 = (bf16[5,8,16,128]{3,2,1,0:T(8,128)(2,1)S(1)}, bf16[5,8,16,128]{3,2,1,0:T(8,128)(2,1)S(1)}, u32[]{:S(2)}, u32[]{:S(2)}) collective-permute-start(bf16[5,8,16,128]{3,2,1,0:T(8,128)(2,1)S(1)} %broadcast_select_fusion), channel_id=1, source_target_pairs={{0,384},{1,129},{64,448},{65,193},{128,0},{129,257},{192,64},{193,... | collective-permute-start | bytes 491528 | tf_op jit(solution)/shard_map/ppermute | solution.py:209
  31.3 9.8 %collective-permute-start.6 = (bf16[5,8,16,128]{3,2,1,0:T(8,128)(2,1)S(1)}, bf16[5,8,16,128]{3,2,1,0:T(8,128)(2,1)S(1)}, u32[]{:S(2)}, u32[]{:S(2)}) collective-permute-start(bf16[5,8,16,128]{3,2,1,0:T(8,128)(2,1)S(1)} %collective-permute-done.5.refs_4_), channel_id=1, source_target_pairs={{0,448},{64,0},{128,64},{192,128},{256,192},{320,256},{384,320},{4... | collective-permute-start | bytes 491528 | tf_op jit(solution)/shard_map/ppermute | solution.py:196
  33.2 11.3 %collective-permute-start.8 = (bf16[5,8,16,128]{3,2,1,0:T(8,128)(2,1)S(1)}, bf16[5,8,16,128]{3,2,1,0:T(8,128)(2,1)S(1)}, u32[]{:S(2)}, u32[]{:S(2)}) collective-permute-start(bf16[5,8,16,128]{3,2,1,0:T(8,128)(2,1)S(1)} %collective-permute-done.1.refs_0_), channel_id=1, source_target_pairs={{0,64},{64,128},{128,192},{192,256},{256,320},{320,384},{384,448},... | collective-permute-start | bytes 491528 | tf_op jit(solution)/shard_map/ppermute | solution.py:196
  41.1 6.6 %collective-permute-start.9 = (bf16[5,8,16,128]{3,2,1,0:T(8,128)(2,1)S(1)}, bf16[5,8,16,128]{3,2,1,0:T(8,128)(2,1)S(1)}, u32[]{:S(2)}, u32[]{:S(2)}) collective-permute-start(bf16[5,8,16,128]{3,2,1,0:T(8,128)(2,1)S(1)} %fusion.1), channel_id=1, source_target_pairs={{32,1},{1,32},{33,2},{2,33},{34,3},{3,34},{35,4},{4,35},{36,5},{5,... | collective-permute-start | bytes 491528 | tf_op jit(solution)/shard_map/ppermute | solution.py:219
  44.6 5.9 %collective-permute-start.10 = (bf16[3,8,16,128]{3,2,1,0:T(8,128)(2,1)S(1)}, bf16[3,8,16,128]{3,2,1,0:T(8,128)(2,1)S(1)}, u32[]{:S(2)}, u32[]{:S(2)}) collective-permute-start(bf16[3,8,16,128]{3,2,1,0:T(8,128)(2,1)S(1)} %pad_maximum_fusion.3), channel_id=1, source_target_pairs={{32,1},{1,32},{33,2},{2,33},{34,3},{3,34},{35,4},{4,35},{36,5},{5,... | collective-permute-start | bytes 294920 | tf_op jit(solution)/shard_map/ppermute | solution.py:220
  52.2 25.5 %all-to-all-start = ((f32[64,8,128]{2,1,0:T(8,128)}), f32[64,8,128]{2,1,0:T(8,128)S(1)}, u32[]{:S(2)}, u32[]{:S(2)}) async-start(f32[64,8,128]{2,1,0:T(8,128)} %shard_map.60), calls=%async_computation | async-start | bytes 524288 | tf_op jit(solution)/shard_map/all_to_all | solution.py:259
  66.5 3.4 %copy-start.2 = (bf16[8]{0:T(256)(128)(2,1)S(1)}, bf16[8]{0:T(256)(128)(2,1)}, u32[]{:S(2)}) copy-start(bf16[8]{0:T(256)(128)(2,1)} %param.7) | copy-start | bytes 52
  66.5 8.9 %collective-permute-start.11 = (f32[8,4,8,128]{3,2,1,0:T(8,128)S(1)}, f32[8,4,8,128]{3,2,1,0:T(8,128)S(1)}, u32[]{:S(2)}, u32[]{:S(2)}) collective-permute-start(f32[8,4,8,128]{3,2,1,0:T(8,128)S(1)} %get-tuple-element.27), channel_id=1, source_target_pairs={{0,32},{32,0},{1,33},{33,1},{2,34},{34,2},{3,35},{35,3},{4,36},{36... | collective-permute-start | bytes 393224 | tf_op jit(solution)/shard_map/ppermute | solution.py:264

commit v7 on v6

--- a/solution.py
+++ b/solution.py
@@ -162,11 +162,15 @@
             grad[at + 1] = earlier[at + 1] + second
 
 
-def finish_kernel(place, got, out):
-    summed = jnp.transpose(jnp.sum(got[...], axis=0) * SCALE)
-    for at, count, lane, start in ((0, 9, 0, 0), (9, 9, 4, 0), (18, 5, 0, 72), (23, 4, 4, 72)):
-        part = summed[start : start + 8 * count, lane : lane + 4]
-        out[at : at + count] = part.reshape(count, 8, 4)
+def finish_kernel(place, got, out, turned, table):
+    turned[...] = jnp.transpose(jnp.sum(got[...], axis=0) * SCALE)
+    for o in range(8):
+        for at, count, lane, start in ((0, 9, 0, 0), (9, 9, 4, 0), (18, 5, 0, 72), (23, 4, 4, 72)):
+            part = turned[pl.ds(start + o, count, stride=8), :]
+            table[at : at + count, 4 * o : 4 * o + 4] = part[:, lane : lane + 4]
+    done = jnp.transpose(table[...])
+    for o in range(8):
+        out[o] = done[4 * o : 4 * o + 4, :27]
 
 
 def on_device(activations, cotangent, filters, bias_terms):
@@ -213,7 +217,7 @@
         return jnp.stack([jnp.where(first, block[0], block[4]) for block in blocks])
 
     near = (b6, b7, mine, b1, b2)
-    send, b3 = lax.optimization_barrier((outermost(near), b3))
+    send, b4 = lax.optimization_barrier((outermost(near), b4))
     far = (b3, b4, b5)
     edges = (
         lax.ppermute(send, ("zl",) + SPACE, pairs),
@@ -258,8 +262,11 @@
 
     got = lax.all_to_all(grad, ("zl",) + SPACE, 0, 0, tiled=True)
     filter_grad = local(
-        finish_kernel, jax.ShapeDtypeStruct((27, 8, 4), jnp.float32), (got,), []
-    )
+        finish_kernel,
+        jax.ShapeDtypeStruct((8, 4, 27), jnp.float32),
+        (got,),
+        [pltpu.VMEM((WIDTH, 8), jnp.float32), pltpu.VMEM((32, WIDTH), jnp.float32)],
+    ).transpose(2, 0, 1)
 
     rest = lax.ppermute(feat[8:], "zl", swap)
     kept = feat[:8]

time: 80.2 us -> 79.5 us (level)
  waiting for transfers between devices: 16.5 us -> 11.4 us
  starting transfers between devices: 52 us -> 56.9 us
    ppermute x6, waiting for transfers between devices: 7.69 us -> 3.32 us  [along(): lax.ppermute(block, 'y', [(i, (i - by) % STEPS) for i in range(STEPS)])]
    ppermute x1, starting transfers between devices: 3.38 us -> 6.55 us  [on_device(): lax.ppermute(send, ('zl',) + SPACE, pairs)]
    all_to_all x1, starting transfers between devices: 12.7 us -> 13.6 us  [on_device(): got = lax.all_to_all(grad, ('zl',) + SPACE, 0, 0, tiled=True)]
    ppermute x1, waiting for transfers between devices: 0.89 us -> 0.01 us  [on_device(): lax.ppermute(send, ('zl',) + SPACE, pairs)]
  transfers between devices with their start and end apart: 13 -> 13, of which waited for: 6 -> 4; matrix products, arithmetic and copies ran while one was open for 2% -> 2% of each run, Pallas kernels for 4% -> 4%
where the time goes in v7:
time: 79.5 us; the launch traced here: 78.9 us
  starting transfers between devices  56.9 us (72%)
  waiting for transfers between devices  11.4 us (14%)
  Pallas kernels  6.54 us (8%)
  local copies, waits for them, and re-layouts  1.91 us (2%)
  other arithmetic  1.13 us (1%)
  between operations  1.04 us (1%)
    ppermute x6, starting transfers between devices, along(): lax.ppermute(block, 'y', [(i, (i - by) % STEPS) for i in range(STEPS)])  19.6 us
    all_to_all x1, starting transfers between devices, on_device(): got = lax.all_to_all(grad, ('zl',) + SPACE, 0, 0, tiled=True)  13.6 us
    ppermute x1, starting transfers between devices, on_device(): lax.ppermute(send, ('zl',) + SPACE, pairs)  6.55 us
    pallas_call x4, Pallas kernels, local(): pl.pallas_call(kernel, out_shape=shapes, in_specs=[pl.BlockSpec(memory_sp...  6.54 us
    ppermute x1, waiting for transfers between devices, on_device(): rest = lax.ppermute(feat[8:], 'zl', swap)  5.45 us
    ppermute x1, starting transfers between devices, on_device(): lax.ppermute(lax.dynamic_slice_in_dim(acts, 3 * (1 - zl), 5, 0), 'zl', swap)  4.96 us
    ppermute x1, starting transfers between devices, on_device(): lax.ppermute(jnp.where(lax.axis_index('core') == 0, b2, b6), ('y', 'core'...  3.98 us
    ppermute x1, starting transfers between devices, on_device(): rest = lax.ppermute(feat[8:], 'zl', swap)  3.39 us
  transfers between devices with their start and end apart: 13, of which 4 were waited for; matrix products, arithmetic and copies ran while one was open for 2% of the time, Pallas kernels for 4%

profile of v7, /device:TPU:1, one launch (start us, length us, event | category | flops | bytes accessed | tf_op | source)
XLA Modules:
  0.0 78.9 jit_solution(12426106328052171916)
XLA Ops:
  0.6 1.0 %constant_dynamic-slice_fusion.2 = (bf16[8,5,8,128]{3,2,1,0:T(8,128)(2,1)S(1)}, bf16[8,5,8,128]{3,2,1,0:T(8,128)(2,1)S(1)}) fusion(bf16[8,8,8,128]{3,2,1,0:T(8,128)(2,1)} %param.4, s32[]{:T(128)S(6)} %select_n.80, s32[]{:T(128)S(6)} %select_n.81), kind=kLoop, calls=%fused_computation.27 | loop fusion | bytes 327688 | tf_op jit(solution)/shard_map/dynamic-slice
  1.6 0.0 copy-start.1
  1.7 5.0 %collective-permute-start = (bf16[5,8,8,128]{3,2,1,0:T(8,128)(2,1)S(1)}, bf16[5,8,8,128]{3,2,1,0:T(8,128)(2,1)S(1)}, u32[]{:S(2)}, u32[]{:S(2)}) collective-permute-start(bf16[5,8,8,128]{3,2,1,0:T(8,128)(2,1)S(1)} %bitcast.20), channel_id=1, source_target_pairs={{0,32},{32,0},{1,33},{33,1},{2,34},{34,2},{3,35},{35,3},{4,36},{36... | collective-permute-start | bytes 245768 | tf_op jit(solution)/shard_map/ppermute | solution.py:183
  6.6 0.0 copy-done.1
  6.7 0.0 copy-start
  6.7 0.8 copy-done
  7.5 1.9 %collective-permute-start.2 = (bf16[59,8,128]{2,1,0:T(8,128)(2,1)S(1)}, bf16[59,8,128]{2,1,0:T(8,128)(2,1)S(1)}, u32[]{:S(2)}, u32[]{:S(2)}) collective-permute-start(bf16[59,8,128]{2,1,0:T(8,128)(2,1)S(1)} %pad_maximum_fusion.1), channel_id=1, source_target_pairs={{0,32},{32,0},{1,33},{33,1},{2,34},{34,2},{3,35},{35,3},{4,36},{36... | collective-permute-start | bytes 362504 | tf_op jit(solution)/shard_map/ppermute | solution.py:197
  9.5 0.0 collective-permute-done
  9.6 4.2 %collective-permute-start.1 = (bf16[5,8,16,128]{3,2,1,0:T(8,128)(2,1)S(1)}, bf16[5,8,16,128]{3,2,1,0:T(8,128)(2,1)S(1)}, u32[]{:S(2)}, u32[]{:S(2)}) collective-permute-start(bf16[5,8,16,128]{3,2,1,0:T(8,128)(2,1)S(1)} %maximum_select_fusion.1.refs_2_), channel_id=1, source_target_pairs={{0,128},{64,192},{128,256},{192,320},{256,384},{320,448},{384,0},{... | collective-permute-start | bytes 491528 | tf_op jit(solution)/shard_map/ppermute | solution.py:200
  13.8 3.6 %collective-permute-start.5 = (bf16[5,8,16,128]{3,2,1,0:T(8,128)(2,1)S(1)}, bf16[5,8,16,128]{3,2,1,0:T(8,128)(2,1)S(1)}, u32[]{:S(2)}, u32[]{:S(2)}) collective-permute-start(bf16[5,8,16,128]{3,2,1,0:T(8,128)(2,1)S(1)} %maximum_select_fusion.1.refs_2_), channel_id=1, source_target_pairs={{0,384},{64,448},{128,0},{192,64},{256,128},{320,192},{384,256},{4... | collective-permute-start | bytes 491528 | tf_op jit(solution)/shard_map/ppermute | solution.py:200
  17.4 0.0 collective-permute-done.2
  17.5 2.8 %collective-permute-start.3 = (bf16[5,8,16,128]{3,2,1,0:T(8,128)(2,1)S(1)}, bf16[5,8,16,128]{3,2,1,0:T(8,128)(2,1)S(1)}, u32[]{:S(2)}, u32[]{:S(2)}) collective-permute-start(bf16[5,8,16,128]{3,2,1,0:T(8,128)(2,1)S(1)} %maximum_select_fusion.1.refs_2_), channel_id=1, source_target_pairs={{0,64},{64,128},{128,192},{192,256},{256,320},{320,384},{384,448},... | collective-permute-start | bytes 491528 | tf_op jit(solution)/shard_map/ppermute | solution.py:200
  20.3 3.7 %collective-permute-start.4 = (bf16[5,8,16,128]{3,2,1,0:T(8,128)(2,1)S(1)}, bf16[5,8,16,128]{3,2,1,0:T(8,128)(2,1)S(1)}, u32[]{:S(2)}, u32[]{:S(2)}) collective-permute-start(bf16[5,8,16,128]{3,2,1,0:T(8,128)(2,1)S(1)} %maximum_select_fusion.1.refs_2_), channel_id=1, source_target_pairs={{0,448},{64,0},{128,64},{192,128},{256,192},{320,256},{384,320},{4... | collective-permute-start | bytes 491528 | tf_op jit(solution)/shard_map/ppermute | solution.py:200
  24.0 0.0 collective-permute-done.1.refs_0_
  24.0 3.3 %collective-permute-done.5.refs_4_ = bf16[5,8,16,128]{3,2,1,0:T(8,128)(2,1)S(1)} collective-permute-done((bf16[5,8,16,128]{3,2,1,0:T(8,128)(2,1)S(1)}, bf16[5,8,16,128]{3,2,1,0:T(8,128)(2,1)S(1)}, u32[]{:S(2)}, u32[]{:S(2)}) %collective-permute-start.5) | collective-permute-done | bytes 163872 | tf_op jit(solution)/shard_map/ppermute | solution.py:200
  27.3 4.0 %collective-permute-start.7 = (bf16[5,8,16,128]{3,2,1,0:T(8,128)(2,1)S(1)}, bf16[5,8,16,128]{3,2,1,0:T(8,128)(2,1)S(1)}, u32[]{:S(2)}, u32[]{:S(2)}) collective-permute-start(bf16[5,8,16,128]{3,2,1,0:T(8,128)(2,1)S(1)} %broadcast_select_fusion), channel_id=1, source_target_pairs={{0,384},{1,129},{64,448},{65,193},{128,0},{129,257},{192,64},{193,... | collective-permute-start | bytes 491528 | tf_op jit(solution)/shard_map/ppermute | solution.py:213
  31.3 1.9 %collective-permute-start.6 = (bf16[5,8,16,128]{3,2,1,0:T(8,128)(2,1)S(1)}, bf16[5,8,16,128]{3,2,1,0:T(8,128)(2,1)S(1)}, u32[]{:S(2)}, u32[]{:S(2)}) collective-permute-start(bf16[5,8,16,128]{3,2,1,0:T(8,128)(2,1)S(1)} %collective-permute-done.5.refs_4_), channel_id=1, source_target_pairs={{0,448},{64,0},{128,64},{192,128},{256,192},{320,256},{384,320},{4... | collective-permute-start | bytes 491528 | tf_op jit(solution)/shard_map/ppermute | solution.py:200
  33.2 3.4 %collective-permute-start.8 = (bf16[5,8,16,128]{3,2,1,0:T(8,128)(2,1)S(1)}, bf16[5,8,16,128]{3,2,1,0:T(8,128)(2,1)S(1)}, u32[]{:S(2)}, u32[]{:S(2)}) collective-permute-start(bf16[5,8,16,128]{3,2,1,0:T(8,128)(2,1)S(1)} %collective-permute-done.1.refs_0_), channel_id=1, source_target_pairs={{0,64},{64,128},{128,192},{192,256},{256,320},{320,384},{384,448},... | collective-permute-start | bytes 491528 | tf_op jit(solution)/shard_map/ppermute | solution.py:200
  36.6 0.0 collective-permute-done.3.refs_1_
  36.7 0.0 collective-permute-done.4.refs_3_
  36.8 0.0 collective-permute-done.7.refs_6_
  36.8 6.5 %collective-permute-start.9 = (bf16[5,8,16,128]{3,2,1,0:T(8,128)(2,1)S(1)}, bf16[5,8,16,128]{3,2,1,0:T(8,128)(2,1)S(1)}, u32[]{:S(2)}, u32[]{:S(2)}) collective-permute-start(bf16[5,8,16,128]{3,2,1,0:T(8,128)(2,1)S(1)} %fusion.1), channel_id=1, source_target_pairs={{32,1},{1,32},{33,2},{2,33},{34,3},{3,34},{35,4},{4,35},{36,5},{5,... | collective-permute-start | bytes 491528 | tf_op jit(solution)/shard_map/ppermute | solution.py:223
  43.3 0.0 collective-permute-done.8.refs_7_
  43.4 0.0 collective-permute-done.6.refs_5_
  43.4 2.9 %collective-permute-start.10 = (bf16[3,8,16,128]{3,2,1,0:T(8,128)(2,1)S(1)}, bf16[3,8,16,128]{3,2,1,0:T(8,128)(2,1)S(1)}, u32[]{:S(2)}, u32[]{:S(2)}) collective-permute-start(bf16[3,8,16,128]{3,2,1,0:T(8,128)(2,1)S(1)} %pad_maximum_fusion.3), channel_id=1, source_target_pairs={{32,1},{1,32},{33,2},{2,33},{34,3},{3,34},{35,4},{4,35},{36,5},{5,... | collective-permute-start | bytes 294920 | tf_op jit(solution)/shard_map/ppermute | solution.py:224
  46.4 0.1 pad_add_fusion.place
  46.4 0.0 collective-permute-done.9.near.refs_8_
  46.5 1.8 %shard_map.59 = (f32[64,8,128]{2,1,0:T(8,128)S(1)}, bf16[2,256,1024]{2,1,0:T(8,128)(2,1)S(1)}) custom-call(s32[2]{0:T(128)S(1)} %pad_add_fusion.place, bf16[5,8,16,128]{3,2,1,0:T(8,128)(2,1)S(1)} %collective-permute-done.1.refs_0_, bf16[5,8,16,128]{3,2,1,0:T(8,128)(2,1)S(1)} %collective-permute-done.3.refs_1_, ...), custom_call_target="tpu_custom_call" | custom-call | flops 900000000 | bytes 3000000 | tf_op jit(solution)/shard_map/pallas_call | solution.py:234
  48.2 1.1 %collective-permute-done.10.far.refs_9_ = bf16[3,8,16,128]{3,2,1,0:T(8,128)(2,1)S(1)} collective-permute-done((bf16[3,8,16,128]{3,2,1,0:T(8,128)(2,1)S(1)}, bf16[3,8,16,128]{3,2,1,0:T(8,128)(2,1)S(1)}, u32[]{:S(2)}, u32[]{:S(2)}) %collective-permute-start.10) | collective-permute-done | bytes 98336 | tf_op jit(solution)/shard_map/ppermute | solution.py:224
  49.4 1.7 %shard_map.60 = f32[64,8,128]{2,1,0:T(8,128)} custom-call(s32[2]{0:T(128)S(1)} %pad_add_fusion.place, bf16[5,8,16,128]{3,2,1,0:T(8,128)(2,1)S(1)} %collective-permute-done.9.near.refs_8_, bf16[3,8,16,128]{3,2,1,0:T(8,128)(2,1)S(1)} %collective-permute-done.10.far.refs_9_, bf16[2,256,1024]{2,1,0:T(8,128)(2,1)S(1)} %get-tuple-element.20.moved, ...), custom_call_target="tpu_custom_call" | custom-call | flops 400000000 | bytes 3000000 | tf_op jit(solution)/shard_map/pallas_call | solution.py:234
  51.0 13.6 %all-to-all-start = ((f32[64,8,128]{2,1,0:T(8,128)}), f32[64,8,128]{2,1,0:T(8,128)S(1)}, u32[]{:S(2)}, u32[]{:S(2)}) async-start(f32[64,8,128]{2,1,0:T(8,128)} %shard_map.60), calls=%async_computation | async-start | bytes 524288 | tf_op jit(solution)/shard_map/all_to_all | solution.py:263
  64.6 1.6 %shard_map.61 = f32[16,4,8,128]{3,2,1,0:T(8,128)S(1)} custom-call(s32[2]{0:T(128)S(1)} %pad_add_fusion.place, bf16[5,8,16,128]{3,2,1,0:T(8,128)(2,1)S(1)} %collective-permute-done.1.refs_0_, bf16[5,8,16,128]{3,2,1,0:T(8,128)(2,1)S(1)} %collective-permute-done.3.refs_1_, bf16[5,8,16,128]{3,2,1,0:T(8,128)(2,1)S(1)} %maximum_select_fusion.1.refs_2_, ...), custom_call_target="tpu_custom_call" | custom-call | flops 1100000000 | bytes 3000000 | tf_op jit(solution)/shard_map/pallas_call | solution.py:234
  66.2 0.0 copy-start.2
  66.2 3.4 %collective-permute-start.11 = (f32[8,4,8,128]{3,2,1,0:T(8,128)S(1)}, f32[8,4,8,128]{3,2,1,0:T(8,128)S(1)}, u32[]{:S(2)}, u32[]{:S(2)}) collective-permute-start(f32[8,4,8,128]{3,2,1,0:T(8,128)S(1)} %get-tuple-element.25), channel_id=1, source_target_pairs={{0,32},{32,0},{1,33},{33,1},{2,34},{34,2},{3,35},{35,3},{4,36},{36... | collective-permute-start | bytes 393224 | tf_op jit(solution)/shard_map/ppermute | solution.py:271
  69.6 0.0 copy-done.2
  69.7 5.5 %collective-permute-done.11 = f32[8,4,8,128]{3,2,1,0:T(8,128)S(1)} collective-permute-done((f32[8,4,8,128]{3,2,1,0:T(8,128)S(1)}, f32[8,4,8,128]{3,2,1,0:T(8,128)S(1)}, u32[]{:S(2)}, u32[]{:S(2)}) %collective-permute-start.11) | collective-permute-done | bytes 131104 | tf_op jit(solution)/shard_map/ppermute | solution.py:271
  75.1 0.8 fusion
  75.9 1.5 %all-to-all-done.got = f32[64,8,128]{2,1,0:T(8,128)S(1)} async-done(((f32[64,8,128]{2,1,0:T(8,128)}), f32[64,8,128]{2,1,0:T(8,128)S(1)}, u32[]{:S(2)}, u32[]{:S(2)}) %all-to-all-start) | async-done | bytes 262176 | tf_op jit(solution)/shard_map/all_to_all | solution.py:263
  77.4 1.5 %shard_map.62 = f32[8,4,27]{2,1,0:T(4,128)} custom-call(s32[2]{0:T(128)S(1)} %pad_add_fusion.place, f32[64,8,128]{2,1,0:T(8,128)S(1)} %all-to-all-done.got), custom_call_target="tpu_custom_call" | custom-call | flops 100000000 | bytes 3000000 | tf_op jit(solution)/shard_map/pallas_call | solution.py:234
  (23 shorter events, 0.4 us)
Async XLA Ops:
  1.6 5.0 %copy-start.1 = (bf16[8,8,8,128]{3,2,1,0:T(8,128)(2,1)S(1)}, bf16[8,8,8,128]{3,2,1,0:T(8,128)(2,1)}, u32[]{:S(2)}) copy-start(bf16[8,8,8,128]{3,2,1,0:T(8,128)(2,1)} %param.5) | copy-start | bytes 393220
  1.7 7.8 %collective-permute-start = (bf16[5,8,8,128]{3,2,1,0:T(8,128)(2,1)S(1)}, bf16[5,8,8,128]{3,2,1,0:T(8,128)(2,1)S(1)}, u32[]{:S(2)}, u32[]{:S(2)}) collective-permute-start(bf16[5,8,8,128]{3,2,1,0:T(8,128)(2,1)S(1)} %bitcast.20), channel_id=1, source_target_pairs={{0,32},{32,0},{1,33},{33,1},{2,34},{34,2},{3,35},{35,3},{4,36},{36... | collective-permute-start | bytes 245768 | tf_op jit(solution)/shard_map/ppermute | solution.py:183
  6.7 0.8 %copy-start = (bf16[27,8,128]{2,1,0:T(8,128)(2,1)S(1)}, bf16[27,8,128]{2,1,0:T(8,128)(2,1)}, u32[]{:S(2)}) copy-start(bf16[27,8,128]{2,1,0:T(8,128)(2,1)} %param.6) | copy-start | bytes 165892
  7.5 9.9 %collective-permute-start.2 = (bf16[59,8,128]{2,1,0:T(8,128)(2,1)S(1)}, bf16[59,8,128]{2,1,0:T(8,128)(2,1)S(1)}, u32[]{:S(2)}, u32[]{:S(2)}) collective-permute-start(bf16[59,8,128]{2,1,0:T(8,128)(2,1)S(1)} %pad_maximum_fusion.1), channel_id=1, source_target_pairs={{0,32},{32,0},{1,33},{33,1},{2,34},{34,2},{3,35},{35,3},{4,36},{36... | collective-permute-start | bytes 362504 | tf_op jit(solution)/shard_map/ppermute | solution.py:197
  9.6 14.4 %collective-permute-start.1 = (bf16[5,8,16,128]{3,2,1,0:T(8,128)(2,1)S(1)}, bf16[5,8,16,128]{3,2,1,0:T(8,128)(2,1)S(1)}, u32[]{:S(2)}, u32[]{:S(2)}) collective-permute-start(bf16[5,8,16,128]{3,2,1,0:T(8,128)(2,1)S(1)} %maximum_select_fusion.1.refs_2_), channel_id=1, source_target_pairs={{0,128},{64,192},{128,256},{192,320},{256,384},{320,448},{384,0},{... | collective-permute-start | bytes 491528 | tf_op jit(solution)/shard_map/ppermute | solution.py:200
  13.8 13.5 %collective-permute-start.5 = (bf16[5,8,16,128]{3,2,1,0:T(8,128)(2,1)S(1)}, bf16[5,8,16,128]{3,2,1,0:T(8,128)(2,1)S(1)}, u32[]{:S(2)}, u32[]{:S(2)}) collective-permute-start(bf16[5,8,16,128]{3,2,1,0:T(8,128)(2,1)S(1)} %maximum_select_fusion.1.refs_2_), channel_id=1, source_target_pairs={{0,384},{64,448},{128,0},{192,64},{256,128},{320,192},{384,256},{4... | collective-permute-start | bytes 491528 | tf_op jit(solution)/shard_map/ppermute | solution.py:200
  17.5 19.2 %collective-permute-start.3 = (bf16[5,8,16,128]{3,2,1,0:T(8,128)(2,1)S(1)}, bf16[5,8,16,128]{3,2,1,0:T(8,128)(2,1)S(1)}, u32[]{:S(2)}, u32[]{:S(2)}) collective-permute-start(bf16[5,8,16,128]{3,2,1,0:T(8,128)(2,1)S(1)} %maximum_select_fusion.1.refs_2_), channel_id=1, source_target_pairs={{0,64},{64,128},{128,192},{192,256},{256,320},{320,384},{384,448},... | collective-permute-start | bytes 491528 | tf_op jit(solution)/shard_map/ppermute | solution.py:200
  20.3 16.4 %collective-permute-start.4 = (bf16[5,8,16,128]{3,2,1,0:T(8,128)(2,1)S(1)}, bf16[5,8,16,128]{3,2,1,0:T(8,128)(2,1)S(1)}, u32[]{:S(2)}, u32[]{:S(2)}) collective-permute-start(bf16[5,8,16,128]{3,2,1,0:T(8,128)(2,1)S(1)} %maximum_select_fusion.1.refs_2_), channel_id=1, source_target_pairs={{0,448},{64,0},{128,64},{192,128},{256,192},{320,256},{384,320},{4... | collective-permute-start | bytes 491528 | tf_op jit(solution)/shard_map/ppermute | solution.py:200
  27.3 9.4 %collective-permute-start.7 = (bf16[5,8,16,128]{3,2,1,0:T(8,128)(2,1)S(1)}, bf16[5,8,16,128]{3,2,1,0:T(8,128)(2,1)S(1)}, u32[]{:S(2)}, u32[]{:S(2)}) collective-permute-start(bf16[5,8,16,128]{3,2,1,0:T(8,128)(2,1)S(1)} %broadcast_select_fusion), channel_id=1, source_target_pairs={{0,384},{1,129},{64,448},{65,193},{128,0},{129,257},{192,64},{193,... | collective-permute-start | bytes 491528 | tf_op jit(solution)/shard_map/ppermute | solution.py:213
  31.3 12.1 %collective-permute-start.6 = (bf16[5,8,16,128]{3,2,1,0:T(8,128)(2,1)S(1)}, bf16[5,8,16,128]{3,2,1,0:T(8,128)(2,1)S(1)}, u32[]{:S(2)}, u32[]{:S(2)}) collective-permute-start(bf16[5,8,16,128]{3,2,1,0:T(8,128)(2,1)S(1)} %collective-permute-done.5.refs_4_), channel_id=1, source_target_pairs={{0,448},{64,0},{128,64},{192,128},{256,192},{320,256},{384,320},{4... | collective-permute-start | bytes 491528 | tf_op jit(solution)/shard_map/ppermute | solution.py:200
  33.2 10.1 %collective-permute-start.8 = (bf16[5,8,16,128]{3,2,1,0:T(8,128)(2,1)S(1)}, bf16[5,8,16,128]{3,2,1,0:T(8,128)(2,1)S(1)}, u32[]{:S(2)}, u32[]{:S(2)}) collective-permute-start(bf16[5,8,16,128]{3,2,1,0:T(8,128)(2,1)S(1)} %collective-permute-done.1.refs_0_), channel_id=1, source_target_pairs={{0,64},{64,128},{128,192},{192,256},{256,320},{320,384},{384,448},... | collective-permute-start | bytes 491528 | tf_op jit(solution)/shard_map/ppermute | solution.py:200
  36.8 9.7 %collective-permute-start.9 = (bf16[5,8,16,128]{3,2,1,0:T(8,128)(2,1)S(1)}, bf16[5,8,16,128]{3,2,1,0:T(8,128)(2,1)S(1)}, u32[]{:S(2)}, u32[]{:S(2)}) collective-permute-start(bf16[5,8,16,128]{3,2,1,0:T(8,128)(2,1)S(1)} %fusion.1), channel_id=1, source_target_pairs={{32,1},{1,32},{33,2},{2,33},{34,3},{3,34},{35,4},{4,35},{36,5},{5,... | collective-permute-start | bytes 491528 | tf_op jit(solution)/shard_map/ppermute | solution.py:223
  43.4 5.9 %collective-permute-start.10 = (bf16[3,8,16,128]{3,2,1,0:T(8,128)(2,1)S(1)}, bf16[3,8,16,128]{3,2,1,0:T(8,128)(2,1)S(1)}, u32[]{:S(2)}, u32[]{:S(2)}) collective-permute-start(bf16[3,8,16,128]{3,2,1,0:T(8,128)(2,1)S(1)} %pad_maximum_fusion.3), channel_id=1, source_target_pairs={{32,1},{1,32},{33,2},{2,33},{34,3},{3,34},{35,4},{4,35},{36,5},{5,... | collective-permute-start | bytes 294920 | tf_op jit(solution)/shard_map/ppermute | solution.py:224
  51.0 26.4 %all-to-all-start = ((f32[64,8,128]{2,1,0:T(8,128)}), f32[64,8,128]{2,1,0:T(8,128)S(1)}, u32[]{:S(2)}, u32[]{:S(2)}) async-start(f32[64,8,128]{2,1,0:T(8,128)} %shard_map.60), calls=%async_computation | async-start | bytes 524288 | tf_op jit(solution)/shard_map/all_to_all | solution.py:263
  66.2 3.4 %copy-start.2 = (bf16[8]{0:T(256)(128)(2,1)S(1)}, bf16[8]{0:T(256)(128)(2,1)}, u32[]{:S(2)}) copy-start(bf16[8]{0:T(256)(128)(2,1)} %param.7) | copy-start | bytes 52
  66.2 8.9 %collective-permute-start.11 = (f32[8,4,8,128]{3,2,1,0:T(8,128)S(1)}, f32[8,4,8,128]{3,2,1,0:T(8,128)S(1)}, u32[]{:S(2)}, u32[]{:S(2)}) collective-permute-start(f32[8,4,8,128]{3,2,1,0:T(8,128)S(1)} %get-tuple-element.25), channel_id=1, source_target_pairs={{0,32},{32,0},{1,33},{33,1},{2,34},{34,2},{3,35},{35,3},{4,36},{36... | collective-permute-start | bytes 393224 | tf_op jit(solution)/shard_map/ppermute | solution.py:271

commit v8 on v7

--- a/solution.py
+++ b/solution.py
@@ -95,26 +95,13 @@
     return jnp.concatenate(columns, axis=1)
 
 
-def edge_cells(near, far):
-    return jnp.concatenate(
-        [
-            jnp.concatenate(
-                [near[p, z] for p in range(5)] + [far[p, z] for p in range(3)], axis=0
-            )
-            for z in range(DEPTH)
-        ],
-        axis=1,
-    )
-
-
 def over_cells(a, b):
     return lax.dot_general(a, b, (((1,), (1,)), ((), ())), preferred_element_type=jnp.float32)
 
 
-def receivers(place, half):
+def receivers(place, half, p):
     y, zl = place[0], place[1]
-    base = 32 * lax.rem(zl + half, 2)
-    return [base + lax.rem(y + k // 2 + 6, STEPS) * 4 + 2 * (k % 2) for k in range(16)]
+    return 32 * lax.rem(zl + half, 2) + 4 * lax.rem(y + p + 6, STEPS)
 
 
 def pair_of(one, two, k):
@@ -124,9 +111,8 @@
 
 
 def gradient_kernel(place, *refs):
-    *blocks, cot, grad, moved, rows = refs
-    zeros = [jnp.zeros((count, DEPTH, 16, WIDTH), jnp.bfloat16) for count in (5, 3)]
-    fill(rows, place, blocks, zeros)
+    *blocks, edge, cot, grad, later, moved, rows, tiles, sems = refs
+    fill(rows, place, blocks, (edge[...], jnp.zeros((3, DEPTH, 16, WIDTH), jnp.bfloat16)))
     total = jnp.zeros((384, 256), jnp.float32)
     for row in range(ROWS):
         here = shifted(cot, row)
@@ -134,6 +120,7 @@
             moved[row // 3] = here
         total = total + over_cells(cells_of(rows, row), here)
     wide = lax.broadcasted_iota(jnp.int32, (128, WIDTH), 1)
+    copies = []
     for half in range(2):
         one, two, three = (
             total[128 * dx : 128 * dx + 128, WIDTH * half : WIDTH * half + WIDTH]
@@ -141,25 +128,43 @@
         )
         one = jnp.where(wide < 72, one, pltpu.roll(three, 72, 1))
         two = jnp.where(wide < 72, two, pltpu.roll(three, 32, 1))
-        for k, at in enumerate(receivers(place, half)):
-            grad[at], grad[at + 1] = pair_of(one, two, k)
-
-
-def edge_kernel(place, near, far, moved, earlier, grad):
+        for p in range(STEPS):
+            n = 5 * half + p
+            into = tiles.at[n] if p < 5 else later.at[3 * half + p - 5]
+            into[0], into[1] = pair_of(one, two, 2 * p)
+            into[2], into[3] = pair_of(one, two, 2 * p + 1)
+            if p < 5:
+                at = receivers(place, half, p)
+                copies.append(pltpu.make_async_copy(into, grad.at[pl.ds(at, 4)], sems.at[n]))
+                copies[-1].start()
+    for copy in copies:
+        copy.wait()
+
+
+def edge_kernel(place, edge, moved, earlier, _, grad, tiles, sems):
     zl = place[1]
-    total = over_cells(edge_cells(near, far), moved[zl])
-    wide = lax.broadcasted_iota(jnp.int32, (128, WIDTH), 1)
+    cells = jnp.concatenate(
+        [jnp.concatenate([edge[p, z] for p in range(3)], axis=0) for z in range(DEPTH)], axis=1
+    )
+    total = over_cells(cells, moved[zl])
+    wide = lax.broadcasted_iota(jnp.int32, (48, WIDTH), 1)
     low = zl == 0
+    copies = []
     for half in range(2):
         part = total[:, WIDTH * half : WIDTH * half + WIDTH]
         one = jnp.where(low, part, jnp.where(wide < 72, 0.0, pltpu.roll(part, 72, 1)))
-        two = jnp.where(
-            jnp.logical_or(low, wide < 72), 0.0, pltpu.roll(part, 32, 1)
-        )
-        for k, at in enumerate(receivers(place, half)):
-            first, second = pair_of(one, two, k)
-            grad[at] = earlier[at] + first
-            grad[at + 1] = earlier[at + 1] + second
+        two = jnp.where(jnp.logical_or(low, wide < 72), 0.0, pltpu.roll(part, 32, 1))
+        for p in range(3):
+            n = 3 * half + p
+            for k in range(2):
+                first, second = pair_of(one, two, 2 * p + k)
+                tiles[n, 2 * k] = earlier[n, 2 * k] + first
+                tiles[n, 2 * k + 1] = earlier[n, 2 * k + 1] + second
+            at = receivers(place, half, p + 5)
+            copies.append(pltpu.make_async_copy(tiles.at[n], grad.at[pl.ds(at, 4)], sems.at[n]))
+            copies[-1].start()
+    for copy in copies:
+        copy.wait()
 
 
 def finish_kernel(place, got, out, turned, table):
@@ -180,7 +185,9 @@
     first = zl == 0
 
     swap = [(0, 1), (1, 0)]
-    other = lax.ppermute(lax.dynamic_slice_in_dim(acts, 3 * (1 - zl), 5, 0), "zl", swap)
+    other = lax.ppermute(
+        lax.dynamic_slice_in_dim(activations, 3 * (1 - zl), 5, 1), "zl", swap
+    ).transpose(1, 2, 0, 3)
     own = lax.dynamic_slice_in_dim(acts, 3 * zl, 5, 0)
     pairs = []
     for step in range(31):
@@ -224,34 +231,49 @@
         lax.ppermute(outermost(far), ("zl",) + SPACE, pairs),
     )
     blocks = near + far
-    cot, first_edges = lax.optimization_barrier((cot, edges[0]))
-    edges = (first_edges, edges[1])
-
     place = jnp.stack([y, zl])
 
-    def local(kernel, shapes, operands, scratch):
-        vmem = pl.BlockSpec(memory_space=pltpu.VMEM)
+    vmem, hbm = (pl.BlockSpec(memory_space=space) for space in (pltpu.VMEM, pltpu.HBM))
+
+    def local(kernel, shapes, operands, scratch, out_specs=vmem, alias=False):
         return pl.pallas_call(
             kernel,
             out_shape=shapes,
-            in_specs=[pl.BlockSpec(memory_space=pltpu.SMEM)] + [vmem] * len(operands),
-            out_specs=jax.tree.map(lambda _: vmem, shapes),
+            in_specs=[pl.BlockSpec(memory_space=pltpu.SMEM)]
+            + [vmem] * (len(operands) - alias)
+            + [hbm] * alias,
+            out_specs=out_specs,
             scratch_shapes=scratch,
+            input_output_aliases={len(operands): 0} if alias else {},
             compiler_params=pltpu.CompilerParams(vmem_limit_bytes=48 * 1024 * 1024),
             cost_estimate=pl.CostEstimate(
                 flops=10**8 * len(operands), bytes_accessed=3 * 10**6, transcendentals=0
             ),
         )(place, *operands)
 
-    tiles = jax.ShapeDtypeStruct((64, 8, WIDTH), jnp.float32)
+    def tiles_of(*counts):
+        return jax.ShapeDtypeStruct((*counts, 8, WIDTH), jnp.float32)
+
     rows = [pltpu.VMEM((STEPS, 6, DEPTH, 16, WIDTH), jnp.bfloat16)]
-    grad, moved = local(
+    grad, later, moved = local(
         gradient_kernel,
-        (tiles, jax.ShapeDtypeStruct((2, 256, DEPTH * WIDTH), jnp.bfloat16)),
-        (*blocks, cot),
-        rows,
-    )
-    grad = local(edge_kernel, tiles, (*edges, moved, grad), [])
+        (
+            tiles_of(64),
+            tiles_of(6, 4),
+            jax.ShapeDtypeStruct((2, 256, DEPTH * WIDTH), jnp.bfloat16),
+        ),
+        (*blocks, edges[0], cot),
+        rows + [pltpu.VMEM((10, 4, 8, WIDTH), jnp.float32), pltpu.SemaphoreType.DMA((10,))],
+        (hbm, vmem, vmem),
+    )
+    grad = local(
+        edge_kernel,
+        tiles_of(64),
+        (edges[1], moved, later, grad),
+        [pltpu.VMEM((6, 4, 8, WIDTH), jnp.float32), pltpu.SemaphoreType.DMA((6,))],
+        hbm,
+        True,
+    )
     weights, grad = lax.optimization_barrier((weights, grad))
     feat = local(
         forward_kernel,

time: 79.5 us -> 79.7 us (level)
  transfers between devices with their start and end apart: 13 -> 13, of which waited for: 4 -> 4; matrix products, arithmetic and copies ran while one was open for 2% -> 2% of each run, Pallas kernels for 4% -> 5%
where the time goes in v8:
time: 79.7 us; the launch traced here: 78.9 us
  starting transfers between devices  56.9 us (71%)
  waiting for transfers between devices  10.7 us (13%)
  Pallas kernels  7.16 us (9%)
  local copies, waits for them, and re-layouts  1.91 us (2%)
  other arithmetic  1.13 us (1%)
  between operations  1.05 us (1%)
    ppermute x6, starting transfers between devices, along(): lax.ppermute(block, 'y', [(i, (i - by) % STEPS) for i in range(STEPS)])  19.6 us
    all_to_all x1, starting transfers between devices, on_device(): got = lax.all_to_all(grad, ('zl',) + SPACE, 0, 0, tiled=True)  13.6 us
    pallas_call x4, Pallas kernels, local(): pl.pallas_call(kernel, out_shape=shapes, in_specs=[pl.BlockSpec(memory_sp...  7.16 us
    ppermute x1, starting transfers between devices, on_device(): lax.ppermute(send, ('zl',) + SPACE, pairs)  6.55 us
    ppermute x1, waiting for transfers between devices, on_device(): rest = lax.ppermute(feat[8:], 'zl', swap)  5.45 us
    ppermute x1, starting transfers between devices, on_device(): lax.ppermute(lax.dynamic_slice_in_dim(activations, 3 * (1 - zl), 5, 1), '...  4.96 us
    ppermute x1, starting transfers between devices, on_device(): lax.ppermute(jnp.where(lax.axis_index('core') == 0, b2, b6), ('y', 'core'...  3.98 us
    ppermute x1, starting transfers between devices, on_device(): rest = lax.ppermute(feat[8:], 'zl', swap)  3.39 us
  transfers between devices with their start and end apart: 13, of which 4 were waited for; matrix products, arithmetic and copies ran while one was open for 2% of the time, Pallas kernels for 5%

profile of v8, /device:TPU:1, one launch (start us, length us, event | category | flops | bytes accessed | tf_op | source)
XLA Modules:
  0.0 78.9 jit_solution(11835220559542936780)
XLA Ops:
  0.6 1.0 %constant_dynamic-slice_fusion.2 = (bf16[8,5,8,128]{3,2,1,0:T(8,128)(2,1)S(1)}, bf16[8,5,8,128]{3,2,1,0:T(8,128)(2,1)S(1)}) fusion(bf16[8,8,8,128]{3,2,1,0:T(8,128)(2,1)} %param.4, s32[]{:T(128)S(6)} %select_n.80, s32[]{:T(128)S(6)} %select_n.81), kind=kLoop, calls=%fused_computation.26 | loop fusion | bytes 327688 | tf_op jit(solution)/shard_map/dynamic-slice
  1.6 0.0 copy-start.1
  1.7 5.0 %collective-permute-start = (bf16[8,5,8,128]{3,0,2,1:T(8,128)(2,1)S(1)}, bf16[8,5,8,128]{3,0,2,1:T(8,128)(2,1)S(1)}, u32[]{:S(2)}, u32[]{:S(2)}) collective-permute-start(bf16[8,5,8,128]{3,0,2,1:T(8,128)(2,1)S(1)} %copy.12), channel_id=1, source_target_pairs={{0,32},{32,0},{1,33},{33,1},{2,34},{34,2},{3,35},{35,3},{4,36},{36... | collective-permute-start | bytes 245768 | tf_op jit(solution)/shard_map/ppermute | solution.py:188
  6.6 0.0 copy-done.1
  6.7 0.0 copy-start
  6.7 0.8 copy-done
  7.5 1.9 %collective-permute-start.2 = (bf16[59,8,128]{2,1,0:T(8,128)(2,1)S(1)}, bf16[59,8,128]{2,1,0:T(8,128)(2,1)S(1)}, u32[]{:S(2)}, u32[]{:S(2)}) collective-permute-start(bf16[59,8,128]{2,1,0:T(8,128)(2,1)S(1)} %pad_maximum_fusion.1), channel_id=1, source_target_pairs={{0,32},{32,0},{1,33},{33,1},{2,34},{34,2},{3,35},{35,3},{4,36},{36... | collective-permute-start | bytes 362504 | tf_op jit(solution)/shard_map/ppermute | solution.py:204
  9.5 0.0 collective-permute-done
  9.6 4.2 %collective-permute-start.1 = (bf16[5,8,16,128]{3,2,1,0:T(8,128)(2,1)S(1)}, bf16[5,8,16,128]{3,2,1,0:T(8,128)(2,1)S(1)}, u32[]{:S(2)}, u32[]{:S(2)}) collective-permute-start(bf16[5,8,16,128]{3,2,1,0:T(8,128)(2,1)S(1)} %maximum_select_fusion.1.refs_2_), channel_id=1, source_target_pairs={{0,128},{64,192},{128,256},{192,320},{256,384},{320,448},{384,0},{... | collective-permute-start | bytes 491528 | tf_op jit(solution)/shard_map/ppermute | solution.py:207
  13.8 3.6 %collective-permute-start.5 = (bf16[5,8,16,128]{3,2,1,0:T(8,128)(2,1)S(1)}, bf16[5,8,16,128]{3,2,1,0:T(8,128)(2,1)S(1)}, u32[]{:S(2)}, u32[]{:S(2)}) collective-permute-start(bf16[5,8,16,128]{3,2,1,0:T(8,128)(2,1)S(1)} %maximum_select_fusion.1.refs_2_), channel_id=1, source_target_pairs={{0,384},{64,448},{128,0},{192,64},{256,128},{320,192},{384,256},{4... | collective-permute-start | bytes 491528 | tf_op jit(solution)/shard_map/ppermute | solution.py:207
  17.4 0.0 collective-permute-done.2
  17.5 2.8 %collective-permute-start.3 = (bf16[5,8,16,128]{3,2,1,0:T(8,128)(2,1)S(1)}, bf16[5,8,16,128]{3,2,1,0:T(8,128)(2,1)S(1)}, u32[]{:S(2)}, u32[]{:S(2)}) collective-permute-start(bf16[5,8,16,128]{3,2,1,0:T(8,128)(2,1)S(1)} %maximum_select_fusion.1.refs_2_), channel_id=1, source_target_pairs={{0,64},{64,128},{128,192},{192,256},{256,320},{320,384},{384,448},... | collective-permute-start | bytes 491528 | tf_op jit(solution)/shard_map/ppermute | solution.py:207
  20.3 3.7 %collective-permute-start.4 = (bf16[5,8,16,128]{3,2,1,0:T(8,128)(2,1)S(1)}, bf16[5,8,16,128]{3,2,1,0:T(8,128)(2,1)S(1)}, u32[]{:S(2)}, u32[]{:S(2)}) collective-permute-start(bf16[5,8,16,128]{3,2,1,0:T(8,128)(2,1)S(1)} %maximum_select_fusion.1.refs_2_), channel_id=1, source_target_pairs={{0,448},{64,0},{128,64},{192,128},{256,192},{320,256},{384,320},{4... | collective-permute-start | bytes 491528 | tf_op jit(solution)/shard_map/ppermute | solution.py:207
  24.0 0.0 collective-permute-done.1.refs_0_
  24.0 3.3 %collective-permute-done.5.refs_4_ = bf16[5,8,16,128]{3,2,1,0:T(8,128)(2,1)S(1)} collective-permute-done((bf16[5,8,16,128]{3,2,1,0:T(8,128)(2,1)S(1)}, bf16[5,8,16,128]{3,2,1,0:T(8,128)(2,1)S(1)}, u32[]{:S(2)}, u32[]{:S(2)}) %collective-permute-start.5) | collective-permute-done | bytes 163872 | tf_op jit(solution)/shard_map/ppermute | solution.py:207
  27.3 4.0 %collective-permute-start.7 = (bf16[5,8,16,128]{3,2,1,0:T(8,128)(2,1)S(1)}, bf16[5,8,16,128]{3,2,1,0:T(8,128)(2,1)S(1)}, u32[]{:S(2)}, u32[]{:S(2)}) collective-permute-start(bf16[5,8,16,128]{3,2,1,0:T(8,128)(2,1)S(1)} %broadcast_select_fusion), channel_id=1, source_target_pairs={{0,384},{1,129},{64,448},{65,193},{128,0},{129,257},{192,64},{193,... | collective-permute-start | bytes 491528 | tf_op jit(solution)/shard_map/ppermute | solution.py:220
  31.3 1.9 %collective-permute-start.6 = (bf16[5,8,16,128]{3,2,1,0:T(8,128)(2,1)S(1)}, bf16[5,8,16,128]{3,2,1,0:T(8,128)(2,1)S(1)}, u32[]{:S(2)}, u32[]{:S(2)}) collective-permute-start(bf16[5,8,16,128]{3,2,1,0:T(8,128)(2,1)S(1)} %collective-permute-done.5.refs_4_), channel_id=1, source_target_pairs={{0,448},{64,0},{128,64},{192,128},{256,192},{320,256},{384,320},{4... | collective-permute-start | bytes 491528 | tf_op jit(solution)/shard_map/ppermute | solution.py:207
  33.2 3.4 %collective-permute-start.8 = (bf16[5,8,16,128]{3,2,1,0:T(8,128)(2,1)S(1)}, bf16[5,8,16,128]{3,2,1,0:T(8,128)(2,1)S(1)}, u32[]{:S(2)}, u32[]{:S(2)}) collective-permute-start(bf16[5,8,16,128]{3,2,1,0:T(8,128)(2,1)S(1)} %collective-permute-done.1.refs_0_), channel_id=1, source_target_pairs={{0,64},{64,128},{128,192},{192,256},{256,320},{320,384},{384,448},... | collective-permute-start | bytes 491528 | tf_op jit(solution)/shard_map/ppermute | solution.py:207
  36.6 0.0 collective-permute-done.3.refs_1_
  36.7 0.0 collective-permute-done.4.refs_3_
  36.8 0.0 collective-permute-done.7.refs_6_
  36.8 6.5 %collective-permute-start.9 = (bf16[5,8,16,128]{3,2,1,0:T(8,128)(2,1)S(1)}, bf16[5,8,16,128]{3,2,1,0:T(8,128)(2,1)S(1)}, u32[]{:S(2)}, u32[]{:S(2)}) collective-permute-start(bf16[5,8,16,128]{3,2,1,0:T(8,128)(2,1)S(1)} %fusion.1), channel_id=1, source_target_pairs={{32,1},{1,32},{33,2},{2,33},{34,3},{3,34},{35,4},{4,35},{36,5},{5,... | collective-permute-start | bytes 491528 | tf_op jit(solution)/shard_map/ppermute | solution.py:230
  43.3 0.0 collective-permute-done.8.refs_7_
  43.4 0.0 collective-permute-done.6.refs_5_
  43.4 2.9 %collective-permute-start.10 = (bf16[3,8,16,128]{3,2,1,0:T(8,128)(2,1)S(1)}, bf16[3,8,16,128]{3,2,1,0:T(8,128)(2,1)S(1)}, u32[]{:S(2)}, u32[]{:S(2)}) collective-permute-start(bf16[3,8,16,128]{3,2,1,0:T(8,128)(2,1)S(1)} %pad_maximum_fusion.3), channel_id=1, source_target_pairs={{32,1},{1,32},{33,2},{2,33},{34,3},{3,34},{35,4},{4,35},{36,5},{5,... | collective-permute-start | bytes 294920 | tf_op jit(solution)/shard_map/ppermute | solution.py:231
  46.4 0.1 pad_add_fusion.place
  46.4 0.0 collective-permute-done.9.refs_8_
  46.5 2.5 %shard_map.59 = (f32[64,8,128]{2,1,0:T(8,128)}, f32[6,4,8,128]{3,2,1,0:T(8,128)S(1)}, bf16[2,256,1024]{2,1,0:T(8,128)(2,1)S(1)}) custom-call(s32[2]{0:T(128)S(1)} %pad_add_fusion.place, bf16[5,8,16,128]{3,2,1,0:T(8,128)(2,1)S(1)} %collective-permute-done.1.refs_0_, bf16[5,8,16,128]{3,2,1,0:T(8,128)(2,1)S(1)} %collective-permute-done.3.refs_1_, ...), custom_call_target="tpu_custom_call" | custom-call | flops 1000000000 | bytes 3000000 | tf_op jit(solution)/shard_map/pallas_call | solution.py:239
  48.9 0.4 collective-permute-done.10.edge.refs_9_
  49.4 1.6 %shard_map.60 = f32[64,8,128]{2,1,0:T(8,128)} custom-call(s32[2]{0:T(128)S(1)} %pad_add_fusion.place, bf16[3,8,16,128]{3,2,1,0:T(8,128)(2,1)S(1)} %collective-permute-done.10.edge.refs_9_, bf16[2,256,1024]{2,1,0:T(8,128)(2,1)S(1)} %get-tuple-element.17.moved, f32[6,4,8,128]{3,2,1,0:T(8,128)S(1)} %get-tuple-element.18.earlier, ...), custom_call_target="tpu_custom_call", output_to_operand_aliasing={{}: (4, {})} | custom-call | flops 400000000 | bytes 3000000 | tf_op jit(solution)/shard_map/pallas_call | solution.py:239
  50.9 13.6 %all-to-all-start = ((f32[64,8,128]{2,1,0:T(8,128)}), f32[64,8,128]{2,1,0:T(8,128)S(1)}, u32[]{:S(2)}, u32[]{:S(2)}) async-start(f32[64,8,128]{2,1,0:T(8,128)} %shard_map.60), calls=%async_computation | async-start | bytes 524288 | tf_op jit(solution)/shard_map/all_to_all | solution.py:285
  64.5 1.6 %shard_map.61 = f32[16,4,8,128]{3,2,1,0:T(8,128)S(1)} custom-call(s32[2]{0:T(128)S(1)} %pad_add_fusion.place, bf16[5,8,16,128]{3,2,1,0:T(8,128)(2,1)S(1)} %collective-permute-done.1.refs_0_, bf16[5,8,16,128]{3,2,1,0:T(8,128)(2,1)S(1)} %collective-permute-done.3.refs_1_, bf16[5,8,16,128]{3,2,1,0:T(8,128)(2,1)S(1)} %maximum_select_fusion.1.refs_2_, ...), custom_call_target="tpu_custom_call" | custom-call | flops 1100000000 | bytes 3000000 | tf_op jit(solution)/shard_map/pallas_call | solution.py:239
  66.2 0.0 copy-start.2
  66.2 3.4 %collective-permute-start.11 = (f32[8,4,8,128]{3,2,1,0:T(8,128)S(1)}, f32[8,4,8,128]{3,2,1,0:T(8,128)S(1)}, u32[]{:S(2)}, u32[]{:S(2)}) collective-permute-start(f32[8,4,8,128]{3,2,1,0:T(8,128)S(1)} %get-tuple-element.23), channel_id=1, source_target_pairs={{0,32},{32,0},{1,33},{33,1},{2,34},{34,2},{3,35},{35,3},{4,36},{36... | collective-permute-start | bytes 393224 | tf_op jit(solution)/shard_map/ppermute | solution.py:293
  69.6 0.0 copy-done.2
  69.6 5.4 %collective-permute-done.11 = f32[8,4,8,128]{3,2,1,0:T(8,128)S(1)} collective-permute-done((f32[8,4,8,128]{3,2,1,0:T(8,128)S(1)}, f32[8,4,8,128]{3,2,1,0:T(8,128)S(1)}, u32[]{:S(2)}, u32[]{:S(2)}) %collective-permute-start.11) | collective-permute-done | bytes 131104 | tf_op jit(solution)/shard_map/ppermute | solution.py:293
  75.0 0.8 %fusion = f32[8,8,8,128]{3,2,1,0:T(8,128)} fusion(f32[8,4,8,128]{3,2,1,0:T(8,128)S(1)} %collective-permute-done.11, f32[8,4,8,128]{3,2,1,0:T(8,128)S(1)} %get-tuple-element.22, f32[8]{0:T(128)S(1)} %convert_element_type.3, pred[]{:T(512)S(6)} %eq.6), kind=kLoop, calls=%fused_computation.1 | loop fusion | flops 262144 | bytes 524321 | tf_op jit(solution)/shard_map/add | solution.py:295
  75.8 1.5 %all-to-all-done.got = f32[64,8,128]{2,1,0:T(8,128)S(1)} async-done(((f32[64,8,128]{2,1,0:T(8,128)}), f32[64,8,128]{2,1,0:T(8,128)S(1)}, u32[]{:S(2)}, u32[]{:S(2)}) %all-to-all-start) | async-done | bytes 262176 | tf_op jit(solution)/shard_map/all_to_all | solution.py:285
  77.3 1.5 %shard_map.62 = f32[8,4,27]{2,1,0:T(4,128)} custom-call(s32[2]{0:T(128)S(1)} %pad_add_fusion.place, f32[64,8,128]{2,1,0:T(8,128)S(1)} %all-to-all-done.got), custom_call_target="tpu_custom_call" | custom-call | flops 100000000 | bytes 3000000 | tf_op jit(solution)/shard_map/pallas_call | solution.py:239
  (23 shorter events, 0.4 us)
Async XLA Ops:
  1.6 5.0 %copy-start.1 = (bf16[8,8,8,128]{3,2,1,0:T(8,128)(2,1)S(1)}, bf16[8,8,8,128]{3,2,1,0:T(8,128)(2,1)}, u32[]{:S(2)}) copy-start(bf16[8,8,8,128]{3,2,1,0:T(8,128)(2,1)} %param.5) | copy-start | bytes 393220
  1.7 7.8 %collective-permute-start = (bf16[8,5,8,128]{3,0,2,1:T(8,128)(2,1)S(1)}, bf16[8,5,8,128]{3,0,2,1:T(8,128)(2,1)S(1)}, u32[]{:S(2)}, u32[]{:S(2)}) collective-permute-start(bf16[8,5,8,128]{3,0,2,1:T(8,128)(2,1)S(1)} %copy.12), channel_id=1, source_target_pairs={{0,32},{32,0},{1,33},{33,1},{2,34},{34,2},{3,35},{35,3},{4,36},{36... | collective-permute-start | bytes 245768 | tf_op jit(solution)/shard_map/ppermute | solution.py:188
  6.7 0.8 %copy-start = (bf16[27,8,128]{2,1,0:T(8,128)(2,1)S(1)}, bf16[27,8,128]{2,1,0:T(8,128)(2,1)}, u32[]{:S(2)}) copy-start(bf16[27,8,128]{2,1,0:T(8,128)(2,1)} %param.6) | copy-start | bytes 165892
  7.5 9.9 %collective-permute-start.2 = (bf16[59,8,128]{2,1,0:T(8,128)(2,1)S(1)}, bf16[59,8,128]{2,1,0:T(8,128)(2,1)S(1)}, u32[]{:S(2)}, u32[]{:S(2)}) collective-permute-start(bf16[59,8,128]{2,1,0:T(8,128)(2,1)S(1)} %pad_maximum_fusion.1), channel_id=1, source_target_pairs={{0,32},{32,0},{1,33},{33,1},{2,34},{34,2},{3,35},{35,3},{4,36},{36... | collective-permute-start | bytes 362504 | tf_op jit(solution)/shard_map/ppermute | solution.py:204
  9.6 14.4 %collective-permute-start.1 = (bf16[5,8,16,128]{3,2,1,0:T(8,128)(2,1)S(1)}, bf16[5,8,16,128]{3,2,1,0:T(8,128)(2,1)S(1)}, u32[]{:S(2)}, u32[]{:S(2)}) collective-permute-start(bf16[5,8,16,128]{3,2,1,0:T(8,128)(2,1)S(1)} %maximum_select_fusion.1.refs_2_), channel_id=1, source_target_pairs={{0,128},{64,192},{128,256},{192,320},{256,384},{320,448},{384,0},{... | collective-permute-start | bytes 491528 | tf_op jit(solution)/shard_map/ppermute | solution.py:207
  13.8 13.5 %collective-permute-start.5 = (bf16[5,8,16,128]{3,2,1,0:T(8,128)(2,1)S(1)}, bf16[5,8,16,128]{3,2,1,0:T(8,128)(2,1)S(1)}, u32[]{:S(2)}, u32[]{:S(2)}) collective-permute-start(bf16[5,8,16,128]{3,2,1,0:T(8,128)(2,1)S(1)} %maximum_select_fusion.1.refs_2_), channel_id=1, source_target_pairs={{0,384},{64,448},{128,0},{192,64},{256,128},{320,192},{384,256},{4... | collective-permute-start | bytes 491528 | tf_op jit(solution)/shard_map/ppermute | solution.py:207
  17.5 19.2 %collective-permute-start.3 = (bf16[5,8,16,128]{3,2,1,0:T(8,128)(2,1)S(1)}, bf16[5,8,16,128]{3,2,1,0:T(8,128)(2,1)S(1)}, u32[]{:S(2)}, u32[]{:S(2)}) collective-permute-start(bf16[5,8,16,128]{3,2,1,0:T(8,128)(2,1)S(1)} %maximum_select_fusion.1.refs_2_), channel_id=1, source_target_pairs={{0,64},{64,128},{128,192},{192,256},{256,320},{320,384},{384,448},... | collective-permute-start | bytes 491528 | tf_op jit(solution)/shard_map/ppermute | solution.py:207
  20.3 16.4 %collective-permute-start.4 = (bf16[5,8,16,128]{3,2,1,0:T(8,128)(2,1)S(1)}, bf16[5,8,16,128]{3,2,1,0:T(8,128)(2,1)S(1)}, u32[]{:S(2)}, u32[]{:S(2)}) collective-permute-start(bf16[5,8,16,128]{3,2,1,0:T(8,128)(2,1)S(1)} %maximum_select_fusion.1.refs_2_), channel_id=1, source_target_pairs={{0,448},{64,0},{128,64},{192,128},{256,192},{320,256},{384,320},{4... | collective-permute-start | bytes 491528 | tf_op jit(solution)/shard_map/ppermute | solution.py:207
  27.3 9.4 %collective-permute-start.7 = (bf16[5,8,16,128]{3,2,1,0:T(8,128)(2,1)S(1)}, bf16[5,8,16,128]{3,2,1,0:T(8,128)(2,1)S(1)}, u32[]{:S(2)}, u32[]{:S(2)}) collective-permute-start(bf16[5,8,16,128]{3,2,1,0:T(8,128)(2,1)S(1)} %broadcast_select_fusion), channel_id=1, source_target_pairs={{0,384},{1,129},{64,448},{65,193},{128,0},{129,257},{192,64},{193,... | collective-permute-start | bytes 491528 | tf_op jit(solution)/shard_map/ppermute | solution.py:220
  31.3 12.1 %collective-permute-start.6 = (bf16[5,8,16,128]{3,2,1,0:T(8,128)(2,1)S(1)}, bf16[5,8,16,128]{3,2,1,0:T(8,128)(2,1)S(1)}, u32[]{:S(2)}, u32[]{:S(2)}) collective-permute-start(bf16[5,8,16,128]{3,2,1,0:T(8,128)(2,1)S(1)} %collective-permute-done.5.refs_4_), channel_id=1, source_target_pairs={{0,448},{64,0},{128,64},{192,128},{256,192},{320,256},{384,320},{4... | collective-permute-start | bytes 491528 | tf_op jit(solution)/shard_map/ppermute | solution.py:207
  33.2 10.1 %collective-permute-start.8 = (bf16[5,8,16,128]{3,2,1,0:T(8,128)(2,1)S(1)}, bf16[5,8,16,128]{3,2,1,0:T(8,128)(2,1)S(1)}, u32[]{:S(2)}, u32[]{:S(2)}) collective-permute-start(bf16[5,8,16,128]{3,2,1,0:T(8,128)(2,1)S(1)} %collective-permute-done.1.refs_0_), channel_id=1, source_target_pairs={{0,64},{64,128},{128,192},{192,256},{256,320},{320,384},{384,448},... | collective-permute-start | bytes 491528 | tf_op jit(solution)/shard_map/ppermute | solution.py:207
  36.8 9.7 %collective-permute-start.9 = (bf16[5,8,16,128]{3,2,1,0:T(8,128)(2,1)S(1)}, bf16[5,8,16,128]{3,2,1,0:T(8,128)(2,1)S(1)}, u32[]{:S(2)}, u32[]{:S(2)}) collective-permute-start(bf16[5,8,16,128]{3,2,1,0:T(8,128)(2,1)S(1)} %fusion.1), channel_id=1, source_target_pairs={{32,1},{1,32},{33,2},{2,33},{34,3},{3,34},{35,4},{4,35},{36,5},{5,... | collective-permute-start | bytes 491528 | tf_op jit(solution)/shard_map/ppermute | solution.py:230
  43.4 5.9 %collective-permute-start.10 = (bf16[3,8,16,128]{3,2,1,0:T(8,128)(2,1)S(1)}, bf16[3,8,16,128]{3,2,1,0:T(8,128)(2,1)S(1)}, u32[]{:S(2)}, u32[]{:S(2)}) collective-permute-start(bf16[3,8,16,128]{3,2,1,0:T(8,128)(2,1)S(1)} %pad_maximum_fusion.3), channel_id=1, source_target_pairs={{32,1},{1,32},{33,2},{2,33},{34,3},{3,34},{35,4},{4,35},{36,5},{5,... | collective-permute-start | bytes 294920 | tf_op jit(solution)/shard_map/ppermute | solution.py:231
  50.9 26.4 %all-to-all-start = ((f32[64,8,128]{2,1,0:T(8,128)}), f32[64,8,128]{2,1,0:T(8,128)S(1)}, u32[]{:S(2)}, u32[]{:S(2)}) async-start(f32[64,8,128]{2,1,0:T(8,128)} %shard_map.60), calls=%async_computation | async-start | bytes 524288 | tf_op jit(solution)/shard_map/all_to_all | solution.py:285
  66.2 3.4 %copy-start.2 = (bf16[8]{0:T(256)(128)(2,1)S(1)}, bf16[8]{0:T(256)(128)(2,1)}, u32[]{:S(2)}) copy-start(bf16[8]{0:T(256)(128)(2,1)} %param.7) | copy-start | bytes 52
  66.2 8.9 %collective-permute-start.11 = (f32[8,4,8,128]{3,2,1,0:T(8,128)S(1)}, f32[8,4,8,128]{3,2,1,0:T(8,128)S(1)}, u32[]{:S(2)}, u32[]{:S(2)}) collective-permute-start(f32[8,4,8,128]{3,2,1,0:T(8,128)S(1)} %get-tuple-element.23), channel_id=1, source_target_pairs={{0,32},{32,0},{1,33},{33,1},{2,34},{34,2},{3,35},{35,3},{4,36},{36... | collective-permute-start | bytes 393224 | tf_op jit(solution)/shard_map/ppermute | solution.py:293

commit v9 on v7

--- a/solution.py
+++ b/solution.py
@@ -199,12 +199,12 @@
     def along(block, by):
         return lax.ppermute(block, "y", [(i, (i - by) % STEPS) for i in range(STEPS)])
 
-    b2, b6 = along(mine, 2), along(mine, -2)
+    b1, b7 = along(mine, 1), along(mine, -1)
     keep = lax.dynamic_slice_in_dim(cots, 4 * zl, 4, 0)
     cot = jnp.concatenate([keep, got[:32].reshape(4, 8, 8, WIDTH)], axis=2)
     weights = jnp.concatenate([filters, got[32:]], axis=1)
-    after, cot, weights = lax.optimization_barrier((mine, cot, weights))
-    b1, b7 = along(after, 1), along(after, -1)
+    b7, cot, weights = lax.optimization_barrier((b7, cot, weights))
+    b2, b6 = along(b1, 1), along(b7, -1)
     turn = [
         ((2 * i + c), (2 * ((i + (2 if c else -2)) % STEPS) + c))
         for i in range(STEPS)

time: 79.5 us -> 83.1 us (1.045); the launches traced: 78.9 us -> 81.6 us
  starting transfers between devices: 56.9 us -> 60.1 us
    ppermute x1, starting transfers between devices: 2.94 us -> 4.59 us  [on_device(): lax.ppermute(outermost(far), ('zl',) + SPACE, pairs)]
    all_to_all x1, starting transfers between devices: 13.6 us -> 11.9 us  [on_device(): got = lax.all_to_all(grad, ('zl',) + SPACE, 0, 0, tiled=True)]
    ppermute x1, starting transfers between devices: 6.55 us -> 8.14 us  [on_device(): lax.ppermute(send, ('zl',) + SPACE, pairs)]
    ppermute x1, starting transfers between devices: 3.98 us -> 5.19 us  [on_device(): lax.ppermute(jnp.where(lax.axis_index('core') == 0, b2, b6), ('y', 'core'...]
  transfers between devices with their start and end apart: 13 -> 13, of which waited for: 4 -> 6; matrix products, arithmetic and copies ran while one was open for 2% -> 2% of each run, Pallas kernels for 4% -> 4%
where the time goes in v9:
time: 83.1 us; the launch traced here: 81.6 us
  starting transfers between devices  60.1 us (72%)
  waiting for transfers between devices  10.9 us (13%)
  Pallas kernels  6.55 us (8%)
  local copies, waits for them, and re-layouts  1.91 us (2%)
  other arithmetic  1.13 us (1%)
  between operations  1.02 us (1%)
    ppermute x6, starting transfers between devices, along(): lax.ppermute(block, 'y', [(i, (i - by) % STEPS) for i in range(STEPS)])  20 us
    all_to_all x1, starting transfers between devices, on_device(): got = lax.all_to_all(grad, ('zl',) + SPACE, 0, 0, tiled=True)  11.9 us
    ppermute x1, starting transfers between devices, on_device(): lax.ppermute(send, ('zl',) + SPACE, pairs)  8.14 us
    pallas_call x4, Pallas kernels, local(): pl.pallas_call(kernel, out_shape=shapes, in_specs=[pl.BlockSpec(memory_sp...  6.55 us
    ppermute x1, waiting for transfers between devices, on_device(): rest = lax.ppermute(feat[8:], 'zl', swap)  5.45 us
    ppermute x1, starting transfers between devices, on_device(): lax.ppermute(jnp.where(lax.axis_index('core') == 0, b2, b6), ('y', 'core'...  5.19 us
    ppermute x1, starting transfers between devices, on_device(): lax.ppermute(lax.dynamic_slice_in_dim(acts, 3 * (1 - zl), 5, 0), 'zl', swap)  4.96 us
    ppermute x1, starting transfers between devices, on_device(): lax.ppermute(outermost(far), ('zl',) + SPACE, pairs)  4.59 us
  transfers between devices with their start and end apart: 13, of which 6 were waited for; matrix products, arithmetic and copies ran while one was open for 2% of the time, Pallas kernels for 4%

profile of v9, /device:TPU:1, one launch (start us, length us, event | category | flops | bytes accessed | tf_op | source)
XLA Modules:
  0.0 81.6 jit_solution(12911377287090948396)
XLA Ops:
  0.6 1.0 %constant_dynamic-slice_fusion.2 = (bf16[8,5,8,128]{3,2,1,0:T(8,128)(2,1)S(1)}, bf16[8,5,8,128]{3,2,1,0:T(8,128)(2,1)S(1)}) fusion(bf16[8,8,8,128]{3,2,1,0:T(8,128)(2,1)} %param.4, s32[]{:T(128)S(6)} %select_n.80, s32[]{:T(128)S(6)} %select_n.81), kind=kLoop, calls=%fused_computation.26 | loop fusion | bytes 327688 | tf_op jit(solution)/shard_map/dynamic-slice
  1.6 0.0 copy-start.1
  1.7 5.0 %collective-permute-start = (bf16[5,8,8,128]{3,2,1,0:T(8,128)(2,1)S(1)}, bf16[5,8,8,128]{3,2,1,0:T(8,128)(2,1)S(1)}, u32[]{:S(2)}, u32[]{:S(2)}) collective-permute-start(bf16[5,8,8,128]{3,2,1,0:T(8,128)(2,1)S(1)} %bitcast.20), channel_id=1, source_target_pairs={{0,32},{32,0},{1,33},{33,1},{2,34},{34,2},{3,35},{35,3},{4,36},{36... | collective-permute-start | bytes 245768 | tf_op jit(solution)/shard_map/ppermute | solution.py:183
  6.6 0.0 copy-done.1
  6.7 0.0 copy-start
  6.7 0.8 copy-done
  7.5 1.9 %collective-permute-start.2 = (bf16[59,8,128]{2,1,0:T(8,128)(2,1)S(1)}, bf16[59,8,128]{2,1,0:T(8,128)(2,1)S(1)}, u32[]{:S(2)}, u32[]{:S(2)}) collective-permute-start(bf16[59,8,128]{2,1,0:T(8,128)(2,1)S(1)} %pad_maximum_fusion.1), channel_id=1, source_target_pairs={{0,32},{32,0},{1,33},{33,1},{2,34},{34,2},{3,35},{35,3},{4,36},{36... | collective-permute-start | bytes 362504 | tf_op jit(solution)/shard_map/ppermute | solution.py:197
  9.5 0.0 collective-permute-done
  9.6 3.2 %collective-permute-start.1 = (bf16[5,8,16,128]{3,2,1,0:T(8,128)(2,1)S(1)}, bf16[5,8,16,128]{3,2,1,0:T(8,128)(2,1)S(1)}, u32[]{:S(2)}, u32[]{:S(2)}) collective-permute-start(bf16[5,8,16,128]{3,2,1,0:T(8,128)(2,1)S(1)} %maximum_select_fusion.1.refs_2_), channel_id=1, source_target_pairs={{0,64},{64,128},{128,192},{192,256},{256,320},{320,384},{384,448},... | collective-permute-start | bytes 491528 | tf_op jit(solution)/shard_map/ppermute | solution.py:200
  12.8 3.8 %collective-permute-start.4 = (bf16[5,8,16,128]{3,2,1,0:T(8,128)(2,1)S(1)}, bf16[5,8,16,128]{3,2,1,0:T(8,128)(2,1)S(1)}, u32[]{:S(2)}, u32[]{:S(2)}) collective-permute-start(bf16[5,8,16,128]{3,2,1,0:T(8,128)(2,1)S(1)} %maximum_select_fusion.1.refs_2_), channel_id=1, source_target_pairs={{0,448},{64,0},{128,64},{192,128},{256,192},{320,256},{384,320},{4... | collective-permute-start | bytes 491528 | tf_op jit(solution)/shard_map/ppermute | solution.py:200
  16.6 0.0 collective-permute-done.2
  16.7 0.7 collective-permute-done.1.refs_1_
  17.4 1.9 %collective-permute-start.3 = (bf16[5,8,16,128]{3,2,1,0:T(8,128)(2,1)S(1)}, bf16[5,8,16,128]{3,2,1,0:T(8,128)(2,1)S(1)}, u32[]{:S(2)}, u32[]{:S(2)}) collective-permute-start(bf16[5,8,16,128]{3,2,1,0:T(8,128)(2,1)S(1)} %collective-permute-done.1.refs_1_), channel_id=1, source_target_pairs={{0,64},{64,128},{128,192},{192,256},{256,320},{320,384},{384,448},... | collective-permute-start | bytes 491528 | tf_op jit(solution)/shard_map/ppermute | solution.py:200
  19.3 0.0 collective-permute-done.4.refs_3_
  19.3 4.6 %collective-permute-start.5 = (bf16[5,8,16,128]{3,2,1,0:T(8,128)(2,1)S(1)}, bf16[5,8,16,128]{3,2,1,0:T(8,128)(2,1)S(1)}, u32[]{:S(2)}, u32[]{:S(2)}) collective-permute-start(bf16[5,8,16,128]{3,2,1,0:T(8,128)(2,1)S(1)} %collective-permute-done.4.refs_3_), channel_id=1, source_target_pairs={{0,448},{64,0},{128,64},{192,128},{256,192},{320,256},{384,320},{4... | collective-permute-start | bytes 491528 | tf_op jit(solution)/shard_map/ppermute | solution.py:200
  23.9 1.1 %collective-permute-done.3.refs_0_ = bf16[5,8,16,128]{3,2,1,0:T(8,128)(2,1)S(1)} collective-permute-done((bf16[5,8,16,128]{3,2,1,0:T(8,128)(2,1)S(1)}, bf16[5,8,16,128]{3,2,1,0:T(8,128)(2,1)S(1)}, u32[]{:S(2)}, u32[]{:S(2)}) %collective-permute-start.3) | collective-permute-done | bytes 163872 | tf_op jit(solution)/shard_map/ppermute | solution.py:200
  25.1 1.7 %collective-permute-done.5.refs_4_ = bf16[5,8,16,128]{3,2,1,0:T(8,128)(2,1)S(1)} collective-permute-done((bf16[5,8,16,128]{3,2,1,0:T(8,128)(2,1)S(1)}, bf16[5,8,16,128]{3,2,1,0:T(8,128)(2,1)S(1)}, u32[]{:S(2)}, u32[]{:S(2)}) %collective-permute-start.5) | collective-permute-done | bytes 163872 | tf_op jit(solution)/shard_map/ppermute | solution.py:200
  26.8 5.2 %collective-permute-start.7 = (bf16[5,8,16,128]{3,2,1,0:T(8,128)(2,1)S(1)}, bf16[5,8,16,128]{3,2,1,0:T(8,128)(2,1)S(1)}, u32[]{:S(2)}, u32[]{:S(2)}) collective-permute-start(bf16[5,8,16,128]{3,2,1,0:T(8,128)(2,1)S(1)} %broadcast_select_fusion), channel_id=1, source_target_pairs={{0,384},{1,129},{64,448},{65,193},{128,0},{129,257},{192,64},{193,... | collective-permute-start | bytes 491528 | tf_op jit(solution)/shard_map/ppermute | solution.py:213
  32.0 1.9 %collective-permute-start.6 = (bf16[5,8,16,128]{3,2,1,0:T(8,128)(2,1)S(1)}, bf16[5,8,16,128]{3,2,1,0:T(8,128)(2,1)S(1)}, u32[]{:S(2)}, u32[]{:S(2)}) collective-permute-start(bf16[5,8,16,128]{3,2,1,0:T(8,128)(2,1)S(1)} %collective-permute-done.5.refs_4_), channel_id=1, source_target_pairs={{0,448},{64,0},{128,64},{192,128},{256,192},{320,256},{384,320},{4... | collective-permute-start | bytes 491528 | tf_op jit(solution)/shard_map/ppermute | solution.py:200
  33.9 4.6 %collective-permute-start.8 = (bf16[5,8,16,128]{3,2,1,0:T(8,128)(2,1)S(1)}, bf16[5,8,16,128]{3,2,1,0:T(8,128)(2,1)S(1)}, u32[]{:S(2)}, u32[]{:S(2)}) collective-permute-start(bf16[5,8,16,128]{3,2,1,0:T(8,128)(2,1)S(1)} %collective-permute-done.3.refs_0_), channel_id=1, source_target_pairs={{0,64},{64,128},{128,192},{192,256},{256,320},{320,384},{384,448},... | collective-permute-start | bytes 491528 | tf_op jit(solution)/shard_map/ppermute | solution.py:200
  38.6 0.0 collective-permute-done.7.refs_6_
  38.6 8.1 %collective-permute-start.9 = (bf16[5,8,16,128]{3,2,1,0:T(8,128)(2,1)S(1)}, bf16[5,8,16,128]{3,2,1,0:T(8,128)(2,1)S(1)}, u32[]{:S(2)}, u32[]{:S(2)}) collective-permute-start(bf16[5,8,16,128]{3,2,1,0:T(8,128)(2,1)S(1)} %fusion.1), channel_id=1, source_target_pairs={{32,1},{1,32},{33,2},{2,33},{34,3},{3,34},{35,4},{4,35},{36,5},{5,... | collective-permute-start | bytes 491528 | tf_op jit(solution)/shard_map/ppermute | solution.py:223
  46.7 0.0 collective-permute-done.8.refs_7_
  46.8 0.0 collective-permute-done.6.refs_5_
  46.8 4.6 %collective-permute-start.10 = (bf16[3,8,16,128]{3,2,1,0:T(8,128)(2,1)S(1)}, bf16[3,8,16,128]{3,2,1,0:T(8,128)(2,1)S(1)}, u32[]{:S(2)}, u32[]{:S(2)}) collective-permute-start(bf16[3,8,16,128]{3,2,1,0:T(8,128)(2,1)S(1)} %pad_maximum_fusion.3), channel_id=1, source_target_pairs={{32,1},{1,32},{33,2},{2,33},{34,3},{3,34},{35,4},{4,35},{36,5},{5,... | collective-permute-start | bytes 294920 | tf_op jit(solution)/shard_map/ppermute | solution.py:224
  51.4 0.1 pad_add_fusion.place
  51.5 0.0 collective-permute-done.9.near.refs_8_
  51.5 1.8 %shard_map.59 = (f32[64,8,128]{2,1,0:T(8,128)S(1)}, bf16[2,256,1024]{2,1,0:T(8,128)(2,1)S(1)}) custom-call(s32[2]{0:T(128)S(1)} %pad_add_fusion.place, bf16[5,8,16,128]{3,2,1,0:T(8,128)(2,1)S(1)} %collective-permute-done.3.refs_0_, bf16[5,8,16,128]{3,2,1,0:T(8,128)(2,1)S(1)} %collective-permute-done.1.refs_1_, ...), custom_call_target="tpu_custom_call" | custom-call | flops 900000000 | bytes 3000000 | tf_op jit(solution)/shard_map/pallas_call | solution.py:234
  53.3 0.4 collective-permute-done.10.far.refs_9_
  53.7 1.7 %shard_map.60 = f32[64,8,128]{2,1,0:T(8,128)} custom-call(s32[2]{0:T(128)S(1)} %pad_add_fusion.place, bf16[5,8,16,128]{3,2,1,0:T(8,128)(2,1)S(1)} %collective-permute-done.9.near.refs_8_, bf16[3,8,16,128]{3,2,1,0:T(8,128)(2,1)S(1)} %collective-permute-done.10.far.refs_9_, bf16[2,256,1024]{2,1,0:T(8,128)(2,1)S(1)} %get-tuple-element.20.moved, ...), custom_call_target="tpu_custom_call" | custom-call | flops 400000000 | bytes 3000000 | tf_op jit(solution)/shard_map/pallas_call | solution.py:234
  55.4 11.9 %all-to-all-start = ((f32[64,8,128]{2,1,0:T(8,128)}), f32[64,8,128]{2,1,0:T(8,128)S(1)}, u32[]{:S(2)}, u32[]{:S(2)}) async-start(f32[64,8,128]{2,1,0:T(8,128)} %shard_map.60), calls=%async_computation | async-start | bytes 524288 | tf_op jit(solution)/shard_map/all_to_all | solution.py:263
  67.3 1.6 %shard_map.61 = f32[16,4,8,128]{3,2,1,0:T(8,128)S(1)} custom-call(s32[2]{0:T(128)S(1)} %pad_add_fusion.place, bf16[5,8,16,128]{3,2,1,0:T(8,128)(2,1)S(1)} %collective-permute-done.3.refs_0_, bf16[5,8,16,128]{3,2,1,0:T(8,128)(2,1)S(1)} %collective-permute-done.1.refs_1_, bf16[5,8,16,128]{3,2,1,0:T(8,128)(2,1)S(1)} %maximum_select_fusion.1.refs_2_, ...), custom_call_target="tpu_custom_call" | custom-call | flops 1100000000 | bytes 3000000 | tf_op jit(solution)/shard_map/pallas_call | solution.py:234
  68.9 0.0 copy-start.2
  68.9 3.4 %collective-permute-start.11 = (f32[8,4,8,128]{3,2,1,0:T(8,128)S(1)}, f32[8,4,8,128]{3,2,1,0:T(8,128)S(1)}, u32[]{:S(2)}, u32[]{:S(2)}) collective-permute-start(f32[8,4,8,128]{3,2,1,0:T(8,128)S(1)} %get-tuple-element.25), channel_id=1, source_target_pairs={{0,32},{32,0},{1,33},{33,1},{2,34},{34,2},{3,35},{35,3},{4,36},{36... | collective-permute-start | bytes 393224 | tf_op jit(solution)/shard_map/ppermute | solution.py:271
  72.3 0.0 copy-done.2
  72.4 5.5 %collective-permute-done.11 = f32[8,4,8,128]{3,2,1,0:T(8,128)S(1)} collective-permute-done((f32[8,4,8,128]{3,2,1,0:T(8,128)S(1)}, f32[8,4,8,128]{3,2,1,0:T(8,128)S(1)}, u32[]{:S(2)}, u32[]{:S(2)}) %collective-permute-start.11) | collective-permute-done | bytes 131104 | tf_op jit(solution)/shard_map/ppermute | solution.py:271
  77.8 0.8 fusion
  78.6 1.5 %all-to-all-done.got = f32[64,8,128]{2,1,0:T(8,128)S(1)} async-done(((f32[64,8,128]{2,1,0:T(8,128)}), f32[64,8,128]{2,1,0:T(8,128)S(1)}, u32[]{:S(2)}, u32[]{:S(2)}) %all-to-all-start) | async-done | bytes 262176 | tf_op jit(solution)/shard_map/all_to_all | solution.py:263
  80.1 1.5 %shard_map.62 = f32[8,4,27]{2,1,0:T(4,128)} custom-call(s32[2]{0:T(128)S(1)} %pad_add_fusion.place, f32[64,8,128]{2,1,0:T(8,128)S(1)} %all-to-all-done.got), custom_call_target="tpu_custom_call" | custom-call | flops 100000000 | bytes 3000000 | tf_op jit(solution)/shard_map/pallas_call | solution.py:234
  (23 shorter events, 0.4 us)
Async XLA Ops:
  1.6 5.0 %copy-start.1 = (bf16[8,8,8,128]{3,2,1,0:T(8,128)(2,1)S(1)}, bf16[8,8,8,128]{3,2,1,0:T(8,128)(2,1)}, u32[]{:S(2)}) copy-start(bf16[8,8,8,128]{3,2,1,0:T(8,128)(2,1)} %param.5) | copy-start | bytes 393220
  1.7 7.8 %collective-permute-start = (bf16[5,8,8,128]{3,2,1,0:T(8,128)(2,1)S(1)}, bf16[5,8,8,128]{3,2,1,0:T(8,128)(2,1)S(1)}, u32[]{:S(2)}, u32[]{:S(2)}) collective-permute-start(bf16[5,8,8,128]{3,2,1,0:T(8,128)(2,1)S(1)} %bitcast.20), channel_id=1, source_target_pairs={{0,32},{32,0},{1,33},{33,1},{2,34},{34,2},{3,35},{35,3},{4,36},{36... | collective-permute-start | bytes 245768 | tf_op jit(solution)/shard_map/ppermute | solution.py:183
  6.7 0.8 %copy-start = (bf16[27,8,128]{2,1,0:T(8,128)(2,1)S(1)}, bf16[27,8,128]{2,1,0:T(8,128)(2,1)}, u32[]{:S(2)}) copy-start(bf16[27,8,128]{2,1,0:T(8,128)(2,1)} %param.6) | copy-start | bytes 165892
  7.5 9.1 %collective-permute-start.2 = (bf16[59,8,128]{2,1,0:T(8,128)(2,1)S(1)}, bf16[59,8,128]{2,1,0:T(8,128)(2,1)S(1)}, u32[]{:S(2)}, u32[]{:S(2)}) collective-permute-start(bf16[59,8,128]{2,1,0:T(8,128)(2,1)S(1)} %pad_maximum_fusion.1), channel_id=1, source_target_pairs={{0,32},{32,0},{1,33},{33,1},{2,34},{34,2},{3,35},{35,3},{4,36},{36... | collective-permute-start | bytes 362504 | tf_op jit(solution)/shard_map/ppermute | solution.py:197
  9.6 7.8 %collective-permute-start.1 = (bf16[5,8,16,128]{3,2,1,0:T(8,128)(2,1)S(1)}, bf16[5,8,16,128]{3,2,1,0:T(8,128)(2,1)S(1)}, u32[]{:S(2)}, u32[]{:S(2)}) collective-permute-start(bf16[5,8,16,128]{3,2,1,0:T(8,128)(2,1)S(1)} %maximum_select_fusion.1.refs_2_), channel_id=1, source_target_pairs={{0,64},{64,128},{128,192},{192,256},{256,320},{320,384},{384,448},... | collective-permute-start | bytes 491528 | tf_op jit(solution)/shard_map/ppermute | solution.py:200
  12.8 6.5 %collective-permute-start.4 = (bf16[5,8,16,128]{3,2,1,0:T(8,128)(2,1)S(1)}, bf16[5,8,16,128]{3,2,1,0:T(8,128)(2,1)S(1)}, u32[]{:S(2)}, u32[]{:S(2)}) collective-permute-start(bf16[5,8,16,128]{3,2,1,0:T(8,128)(2,1)S(1)} %maximum_select_fusion.1.refs_2_), channel_id=1, source_target_pairs={{0,448},{64,0},{128,64},{192,128},{256,192},{320,256},{384,320},{4... | collective-permute-start | bytes 491528 | tf_op jit(solution)/shard_map/ppermute | solution.py:200
  17.4 7.7 %collective-permute-start.3 = (bf16[5,8,16,128]{3,2,1,0:T(8,128)(2,1)S(1)}, bf16[5,8,16,128]{3,2,1,0:T(8,128)(2,1)S(1)}, u32[]{:S(2)}, u32[]{:S(2)}) collective-permute-start(bf16[5,8,16,128]{3,2,1,0:T(8,128)(2,1)S(1)} %collective-permute-done.1.refs_1_), channel_id=1, source_target_pairs={{0,64},{64,128},{128,192},{192,256},{256,320},{320,384},{384,448},... | collective-permute-start | bytes 491528 | tf_op jit(solution)/shard_map/ppermute | solution.py:200
  19.3 7.5 %collective-permute-start.5 = (bf16[5,8,16,128]{3,2,1,0:T(8,128)(2,1)S(1)}, bf16[5,8,16,128]{3,2,1,0:T(8,128)(2,1)S(1)}, u32[]{:S(2)}, u32[]{:S(2)}) collective-permute-start(bf16[5,8,16,128]{3,2,1,0:T(8,128)(2,1)S(1)} %collective-permute-done.4.refs_3_), channel_id=1, source_target_pairs={{0,448},{64,0},{128,64},{192,128},{256,192},{320,256},{384,320},{4... | collective-permute-start | bytes 491528 | tf_op jit(solution)/shard_map/ppermute | solution.py:200
  26.8 11.8 %collective-permute-start.7 = (bf16[5,8,16,128]{3,2,1,0:T(8,128)(2,1)S(1)}, bf16[5,8,16,128]{3,2,1,0:T(8,128)(2,1)S(1)}, u32[]{:S(2)}, u32[]{:S(2)}) collective-permute-start(bf16[5,8,16,128]{3,2,1,0:T(8,128)(2,1)S(1)} %broadcast_select_fusion), channel_id=1, source_target_pairs={{0,384},{1,129},{64,448},{65,193},{128,0},{129,257},{192,64},{193,... | collective-permute-start | bytes 491528 | tf_op jit(solution)/shard_map/ppermute | solution.py:213
  32.0 14.8 %collective-permute-start.6 = (bf16[5,8,16,128]{3,2,1,0:T(8,128)(2,1)S(1)}, bf16[5,8,16,128]{3,2,1,0:T(8,128)(2,1)S(1)}, u32[]{:S(2)}, u32[]{:S(2)}) collective-permute-start(bf16[5,8,16,128]{3,2,1,0:T(8,128)(2,1)S(1)} %collective-permute-done.5.refs_4_), channel_id=1, source_target_pairs={{0,448},{64,0},{128,64},{192,128},{256,192},{320,256},{384,320},{4... | collective-permute-start | bytes 491528 | tf_op jit(solution)/shard_map/ppermute | solution.py:200
  33.9 12.8 %collective-permute-start.8 = (bf16[5,8,16,128]{3,2,1,0:T(8,128)(2,1)S(1)}, bf16[5,8,16,128]{3,2,1,0:T(8,128)(2,1)S(1)}, u32[]{:S(2)}, u32[]{:S(2)}) collective-permute-start(bf16[5,8,16,128]{3,2,1,0:T(8,128)(2,1)S(1)} %collective-permute-done.3.refs_0_), channel_id=1, source_target_pairs={{0,64},{64,128},{128,192},{192,256},{256,320},{320,384},{384,448},... | collective-permute-start | bytes 491528 | tf_op jit(solution)/shard_map/ppermute | solution.py:200
  38.6 12.9 %collective-permute-start.9 = (bf16[5,8,16,128]{3,2,1,0:T(8,128)(2,1)S(1)}, bf16[5,8,16,128]{3,2,1,0:T(8,128)(2,1)S(1)}, u32[]{:S(2)}, u32[]{:S(2)}) collective-permute-start(bf16[5,8,16,128]{3,2,1,0:T(8,128)(2,1)S(1)} %fusion.1), channel_id=1, source_target_pairs={{32,1},{1,32},{33,2},{2,33},{34,3},{3,34},{35,4},{4,35},{36,5},{5,... | collective-permute-start | bytes 491528 | tf_op jit(solution)/shard_map/ppermute | solution.py:223
  46.8 6.9 %collective-permute-start.10 = (bf16[3,8,16,128]{3,2,1,0:T(8,128)(2,1)S(1)}, bf16[3,8,16,128]{3,2,1,0:T(8,128)(2,1)S(1)}, u32[]{:S(2)}, u32[]{:S(2)}) collective-permute-start(bf16[3,8,16,128]{3,2,1,0:T(8,128)(2,1)S(1)} %pad_maximum_fusion.3), channel_id=1, source_target_pairs={{32,1},{1,32},{33,2},{2,33},{34,3},{3,34},{35,4},{4,35},{36,5},{5,... | collective-permute-start | bytes 294920 | tf_op jit(solution)/shard_map/ppermute | solution.py:224
  55.4 24.7 %all-to-all-start = ((f32[64,8,128]{2,1,0:T(8,128)}), f32[64,8,128]{2,1,0:T(8,128)S(1)}, u32[]{:S(2)}, u32[]{:S(2)}) async-start(f32[64,8,128]{2,1,0:T(8,128)} %shard_map.60), calls=%async_computation | async-start | bytes 524288 | tf_op jit(solution)/shard_map/all_to_all | solution.py:263
  68.9 3.4 %copy-start.2 = (bf16[8]{0:T(256)(128)(2,1)S(1)}, bf16[8]{0:T(256)(128)(2,1)}, u32[]{:S(2)}) copy-start(bf16[8]{0:T(256)(128)(2,1)} %param.7) | copy-start | bytes 52
  68.9 8.9 %collective-permute-start.11 = (f32[8,4,8,128]{3,2,1,0:T(8,128)S(1)}, f32[8,4,8,128]{3,2,1,0:T(8,128)S(1)}, u32[]{:S(2)}, u32[]{:S(2)}) collective-permute-start(f32[8,4,8,128]{3,2,1,0:T(8,128)S(1)} %get-tuple-element.25), channel_id=1, source_target_pairs={{0,32},{32,0},{1,33},{33,1},{2,34},{34,2},{3,35},{35,3},{4,36},{36... | collective-permute-start | bytes 393224 | tf_op jit(solution)/shard_map/ppermute | solution.py:271

commit v10 on v7

--- a/solution.py
+++ b/solution.py
@@ -191,19 +191,15 @@
         jnp.concatenate([own, other], axis=2),
         jnp.concatenate([other, own], axis=2),
     )
-    give = jnp.concatenate(
-        [lax.dynamic_slice_in_dim(cots, 4 * (1 - zl), 4, 0).reshape(32, 8, WIDTH), filters], axis=0
-    )
-    got = lax.ppermute(give, "zl", swap)
+    got = lax.ppermute(lax.dynamic_slice_in_dim(cots, 4 * (1 - zl), 4, 0), "zl", swap)
 
     def along(block, by):
         return lax.ppermute(block, "y", [(i, (i - by) % STEPS) for i in range(STEPS)])
 
     b2, b6 = along(mine, 2), along(mine, -2)
     keep = lax.dynamic_slice_in_dim(cots, 4 * zl, 4, 0)
-    cot = jnp.concatenate([keep, got[:32].reshape(4, 8, 8, WIDTH)], axis=2)
-    weights = jnp.concatenate([filters, got[32:]], axis=1)
-    after, cot, weights = lax.optimization_barrier((mine, cot, weights))
+    cot = jnp.concatenate([keep, got], axis=2)
+    after, cot = lax.optimization_barrier((mine, cot))
     b1, b7 = along(after, 1), along(after, -1)
     turn = [
         ((2 * i + c), (2 * ((i + (2 if c else -2)) % STEPS) + c))
@@ -219,13 +215,19 @@
     near = (b6, b7, mine, b1, b2)
     send, b4 = lax.optimization_barrier((outermost(near), b4))
     far = (b3, b4, b5)
+    carried = jnp.pad(filters.reshape(216, WIDTH), ((0, 8), (0, 0))).reshape(14, 16, WIDTH)
+    carried = jnp.concatenate([send.reshape(40, 16, WIDTH), carried], axis=0)
+    carried = lax.ppermute(carried, ("zl",) + SPACE, pairs + [(63, 0), (0, 63)])
+    cot, carried = lax.optimization_barrier((cot, carried))
+    space = lax.axis_index(SPACE)
+    at_end = jnp.where(first, space == 0, space == 31)
     edges = (
-        lax.ppermute(send, ("zl",) + SPACE, pairs),
+        jnp.where(at_end, 0, carried[:40]).reshape(5, DEPTH, 16, WIDTH),
         lax.ppermute(outermost(far), ("zl",) + SPACE, pairs),
     )
+    theirs = carried[40:].reshape(224, WIDTH)[:216].reshape(27, 8, WIDTH)
+    weights = jnp.concatenate([filters, theirs], axis=1)
     blocks = near + far
-    cot, first_edges = lax.optimization_barrier((cot, edges[0]))
-    edges = (first_edges, edges[1])
 
     place = jnp.stack([y, zl])
 

time: 79.5 us -> 79.8 us (level)
    ppermute x6, waiting for transfers between devices: 3.32 us -> 2.44 us  [along(): lax.ppermute(block, 'y', [(i, (i - by) % STEPS) for i in range(STEPS)])]
  transfers between devices with their start and end apart: 13 -> 13, of which waited for: 4 -> 5; matrix products, arithmetic and copies ran while one was open for 2% -> 2% of each run, Pallas kernels for 4% -> 4%
where the time goes in v10:
time: 79.8 us; the launch traced here: 78.9 us
  starting transfers between devices  57.3 us (72%)
  waiting for transfers between devices  10.9 us (14%)
  Pallas kernels  6.55 us (8%)
  local copies, waits for them, and re-layouts  1.91 us (2%)
  other arithmetic  1.16 us (1%)
  between operations  1.03 us (1%)
    ppermute x6, starting transfers between devices, along(): lax.ppermute(block, 'y', [(i, (i - by) % STEPS) for i in range(STEPS)])  19.7 us
    all_to_all x1, starting transfers between devices, on_device(): got = lax.all_to_all(grad, ('zl',) + SPACE, 0, 0, tiled=True)  13.1 us
    ppermute x1, starting transfers between devices, on_device(): carried = lax.ppermute(carried, ('zl',) + SPACE, pairs + [(63, 0), (0, 63)])  7.33 us
    pallas_call x4, Pallas kernels, local(): pl.pallas_call(kernel, out_shape=shapes, in_specs=[pl.BlockSpec(memory_sp...  6.55 us
    ppermute x1, waiting for transfers between devices, on_device(): rest = lax.ppermute(feat[8:], 'zl', swap)  5.44 us
    ppermute x1, starting transfers between devices, on_device(): lax.ppermute(lax.dynamic_slice_in_dim(acts, 3 * (1 - zl), 5, 0), 'zl', swap)  4.96 us
    ppermute x1, starting transfers between devices, on_device(): lax.ppermute(jnp.where(lax.axis_index('core') == 0, b2, b6), ('y', 'core'...  4.01 us
    ppermute x1, starting transfers between devices, on_device(): rest = lax.ppermute(feat[8:], 'zl', swap)  3.4 us
  transfers between devices with their start and end apart: 13, of which 5 were waited for; matrix products, arithmetic and copies ran while one was open for 2% of the time, Pallas kernels for 4%

profile of v10, /device:TPU:1, one launch (start us, length us, event | category | flops | bytes accessed | tf_op | source)
XLA Modules:
  0.0 78.9 jit_solution(2585320657030656050)
XLA Ops:
  0.6 1.0 %constant_dynamic-slice_fusion.3 = (bf16[8,5,8,128]{3,2,1,0:T(8,128)(2,1)S(1)}, bf16[8,5,8,128]{3,2,1,0:T(8,128)(2,1)S(1)}) fusion(bf16[8,8,8,128]{3,2,1,0:T(8,128)(2,1)} %param.4, s32[]{:T(128)S(6)} %select_n.92, s32[]{:T(128)S(6)} %select_n.93), kind=kLoop, calls=%fused_computation.30 | loop fusion | bytes 327688 | tf_op jit(solution)/shard_map/dynamic-slice
  1.6 0.0 copy-start.1
  1.7 5.0 %collective-permute-start = (bf16[5,8,8,128]{3,2,1,0:T(8,128)(2,1)S(1)}, bf16[5,8,8,128]{3,2,1,0:T(8,128)(2,1)S(1)}, u32[]{:S(2)}, u32[]{:S(2)}) collective-permute-start(bf16[5,8,8,128]{3,2,1,0:T(8,128)(2,1)S(1)} %bitcast.30), channel_id=1, source_target_pairs={{0,32},{32,0},{1,33},{33,1},{2,34},{34,2},{3,35},{35,3},{4,36},{36... | collective-permute-start | bytes 245768 | tf_op jit(solution)/shard_map/ppermute | solution.py:183
  6.6 0.0 copy-done.1
  6.7 1.9 %collective-permute-start.2 = (bf16[4,8,8,128]{3,2,1,0:T(8,128)(2,1)S(1)}, bf16[4,8,8,128]{3,2,1,0:T(8,128)(2,1)S(1)}, u32[]{:S(2)}, u32[]{:S(2)}) collective-permute-start(bf16[4,8,8,128]{3,2,1,0:T(8,128)(2,1)S(1)} %bitcast.31), channel_id=1, source_target_pairs={{0,32},{32,0},{1,33},{33,1},{2,34},{34,2},{3,35},{35,3},{4,36},{36... | collective-permute-start | bytes 196616 | tf_op jit(solution)/shard_map/ppermute | solution.py:194
  8.7 0.0 collective-permute-done
  8.7 4.3 %collective-permute-start.1 = (bf16[5,8,16,128]{3,2,1,0:T(8,128)(2,1)S(1)}, bf16[5,8,16,128]{3,2,1,0:T(8,128)(2,1)S(1)}, u32[]{:S(2)}, u32[]{:S(2)}) collective-permute-start(bf16[5,8,16,128]{3,2,1,0:T(8,128)(2,1)S(1)} %maximum_select_fusion.1.refs_2_), channel_id=1, source_target_pairs={{0,128},{64,192},{128,256},{192,320},{256,384},{320,448},{384,0},{... | collective-permute-start | bytes 491528 | tf_op jit(solution)/shard_map/ppermute | solution.py:197
  13.1 3.6 %collective-permute-start.5 = (bf16[5,8,16,128]{3,2,1,0:T(8,128)(2,1)S(1)}, bf16[5,8,16,128]{3,2,1,0:T(8,128)(2,1)S(1)}, u32[]{:S(2)}, u32[]{:S(2)}) collective-permute-start(bf16[5,8,16,128]{3,2,1,0:T(8,128)(2,1)S(1)} %maximum_select_fusion.1.refs_2_), channel_id=1, source_target_pairs={{0,384},{64,448},{128,0},{192,64},{256,128},{320,192},{384,256},{4... | collective-permute-start | bytes 491528 | tf_op jit(solution)/shard_map/ppermute | solution.py:197
  16.7 0.1 pad_add_fusion.place
  16.7 0.0 copy-start
  16.8 0.8 copy-done
  17.6 0.0 collective-permute-done.2
  17.6 2.8 %collective-permute-start.3 = (bf16[5,8,16,128]{3,2,1,0:T(8,128)(2,1)S(1)}, bf16[5,8,16,128]{3,2,1,0:T(8,128)(2,1)S(1)}, u32[]{:S(2)}, u32[]{:S(2)}) collective-permute-start(bf16[5,8,16,128]{3,2,1,0:T(8,128)(2,1)S(1)} %maximum_select_fusion.1.refs_2_), channel_id=1, source_target_pairs={{0,64},{64,128},{128,192},{192,256},{256,320},{320,384},{384,448},... | collective-permute-start | bytes 491528 | tf_op jit(solution)/shard_map/ppermute | solution.py:197
  20.4 3.7 %collective-permute-start.4 = (bf16[5,8,16,128]{3,2,1,0:T(8,128)(2,1)S(1)}, bf16[5,8,16,128]{3,2,1,0:T(8,128)(2,1)S(1)}, u32[]{:S(2)}, u32[]{:S(2)}) collective-permute-start(bf16[5,8,16,128]{3,2,1,0:T(8,128)(2,1)S(1)} %maximum_select_fusion.1.refs_2_), channel_id=1, source_target_pairs={{0,448},{64,0},{128,64},{192,128},{256,192},{320,256},{384,320},{4... | collective-permute-start | bytes 491528 | tf_op jit(solution)/shard_map/ppermute | solution.py:197
  24.1 0.0 collective-permute-done.1.refs_0_
  24.1 2.4 %collective-permute-done.5.refs_4_ = bf16[5,8,16,128]{3,2,1,0:T(8,128)(2,1)S(1)} collective-permute-done((bf16[5,8,16,128]{3,2,1,0:T(8,128)(2,1)S(1)}, bf16[5,8,16,128]{3,2,1,0:T(8,128)(2,1)S(1)}, u32[]{:S(2)}, u32[]{:S(2)}) %collective-permute-start.5) | collective-permute-done | bytes 163872 | tf_op jit(solution)/shard_map/ppermute | solution.py:197
  26.6 4.0 %collective-permute-start.7 = (bf16[5,8,16,128]{3,2,1,0:T(8,128)(2,1)S(1)}, bf16[5,8,16,128]{3,2,1,0:T(8,128)(2,1)S(1)}, u32[]{:S(2)}, u32[]{:S(2)}) collective-permute-start(bf16[5,8,16,128]{3,2,1,0:T(8,128)(2,1)S(1)} %broadcast_select_fusion), channel_id=1, source_target_pairs={{0,384},{1,129},{64,448},{65,193},{128,0},{129,257},{192,64},{193,... | collective-permute-start | bytes 491528 | tf_op jit(solution)/shard_map/ppermute | solution.py:209
  30.6 1.9 %collective-permute-start.6 = (bf16[5,8,16,128]{3,2,1,0:T(8,128)(2,1)S(1)}, bf16[5,8,16,128]{3,2,1,0:T(8,128)(2,1)S(1)}, u32[]{:S(2)}, u32[]{:S(2)}) collective-permute-start(bf16[5,8,16,128]{3,2,1,0:T(8,128)(2,1)S(1)} %collective-permute-done.5.refs_4_), channel_id=1, source_target_pairs={{0,448},{64,0},{128,64},{192,128},{256,192},{320,256},{384,320},{4... | collective-permute-start | bytes 491528 | tf_op jit(solution)/shard_map/ppermute | solution.py:197
  32.5 3.4 %collective-permute-start.8 = (bf16[5,8,16,128]{3,2,1,0:T(8,128)(2,1)S(1)}, bf16[5,8,16,128]{3,2,1,0:T(8,128)(2,1)S(1)}, u32[]{:S(2)}, u32[]{:S(2)}) collective-permute-start(bf16[5,8,16,128]{3,2,1,0:T(8,128)(2,1)S(1)} %collective-permute-done.1.refs_0_), channel_id=1, source_target_pairs={{0,64},{64,128},{128,192},{192,256},{256,320},{320,384},{384,448},... | collective-permute-start | bytes 491528 | tf_op jit(solution)/shard_map/ppermute | solution.py:197
  35.9 0.0 collective-permute-done.3.refs_1_
  36.0 0.0 collective-permute-done.4.refs_3_
  36.0 0.0 collective-permute-done.7.refs_6_
  36.1 7.3 %collective-permute-start.9 = (bf16[54,16,128]{2,1,0:T(8,128)(2,1)S(1)}, bf16[54,16,128]{2,1,0:T(8,128)(2,1)S(1)}, u32[]{:S(2)}, u32[]{:S(2)}) collective-permute-start(bf16[54,16,128]{2,1,0:T(8,128)(2,1)S(1)} %pad_maximum_fusion), channel_id=1, source_target_pairs={{32,1},{1,32},{33,2},{2,33},{34,3},{3,34},{35,4},{4,35},{36,5},{5,... | collective-permute-start | bytes 663560 | tf_op jit(solution)/shard_map/ppermute | solution.py:220
  43.4 0.0 collective-permute-done.8.refs_7_
  43.4 0.0 collective-permute-done.6.refs_5_
  43.5 2.8 %collective-permute-start.10 = (bf16[3,8,16,128]{3,2,1,0:T(8,128)(2,1)S(1)}, bf16[3,8,16,128]{3,2,1,0:T(8,128)(2,1)S(1)}, u32[]{:S(2)}, u32[]{:S(2)}) collective-permute-start(bf16[3,8,16,128]{3,2,1,0:T(8,128)(2,1)S(1)} %pad_maximum_fusion.3), channel_id=1, source_target_pairs={{32,1},{1,32},{33,2},{2,33},{34,3},{3,34},{35,4},{4,35},{36,5},{5,... | collective-permute-start | bytes 294920 | tf_op jit(solution)/shard_map/ppermute | solution.py:226
  46.3 0.7 collective-permute-done.9
  47.1 1.8 %shard_map.59 = (f32[64,8,128]{2,1,0:T(8,128)S(1)}, bf16[2,256,1024]{2,1,0:T(8,128)(2,1)S(1)}) custom-call(s32[2]{0:T(128)S(1)} %pad_add_fusion.place, bf16[5,8,16,128]{3,2,1,0:T(8,128)(2,1)S(1)} %collective-permute-done.1.refs_0_, bf16[5,8,16,128]{3,2,1,0:T(8,128)(2,1)S(1)} %collective-permute-done.3.refs_1_, ...), custom_call_target="tpu_custom_call" | custom-call | flops 900000000 | bytes 3000000 | tf_op jit(solution)/shard_map/pallas_call | solution.py:236
  48.8 0.9 %collective-permute-done.10.far.refs_9_ = bf16[3,8,16,128]{3,2,1,0:T(8,128)(2,1)S(1)} collective-permute-done((bf16[3,8,16,128]{3,2,1,0:T(8,128)(2,1)S(1)}, bf16[3,8,16,128]{3,2,1,0:T(8,128)(2,1)S(1)}, u32[]{:S(2)}, u32[]{:S(2)}) %collective-permute-start.10) | collective-permute-done | bytes 98336 | tf_op jit(solution)/shard_map/ppermute | solution.py:226
  49.7 1.7 %shard_map.60 = f32[64,8,128]{2,1,0:T(8,128)} custom-call(s32[2]{0:T(128)S(1)} %pad_add_fusion.place, bf16[5,8,16,128]{3,2,1,0:T(8,128)(2,1)S(1)} %bitcast.22, bf16[3,8,16,128]{3,2,1,0:T(8,128)(2,1)S(1)} %collective-permute-done.10.far.refs_9_, bf16[2,256,1024]{2,1,0:T(8,128)(2,1)S(1)} %get-tuple-element.18.moved, f32[64,8,128]{2,1,0:T(8,128)S(1)} %get-tuple-element.19.earlier), custom_call_target="tpu_custom_call" | custom-call | flops 400000000 | bytes 3000000 | tf_op jit(solution)/shard_map/pallas_call | solution.py:236
  51.4 13.1 %all-to-all-start = ((f32[64,8,128]{2,1,0:T(8,128)}), f32[64,8,128]{2,1,0:T(8,128)S(1)}, u32[]{:S(2)}, u32[]{:S(2)}) async-start(f32[64,8,128]{2,1,0:T(8,128)} %shard_map.60), calls=%async_computation | async-start | bytes 524288 | tf_op jit(solution)/shard_map/all_to_all | solution.py:265
  64.5 1.6 %shard_map.61 = f32[16,4,8,128]{3,2,1,0:T(8,128)S(1)} custom-call(s32[2]{0:T(128)S(1)} %pad_add_fusion.place, bf16[5,8,16,128]{3,2,1,0:T(8,128)(2,1)S(1)} %collective-permute-done.1.refs_0_, bf16[5,8,16,128]{3,2,1,0:T(8,128)(2,1)S(1)} %collective-permute-done.3.refs_1_, bf16[5,8,16,128]{3,2,1,0:T(8,128)(2,1)S(1)} %maximum_select_fusion.1.refs_2_, ...), custom_call_target="tpu_custom_call" | custom-call | flops 1100000000 | bytes 3000000 | tf_op jit(solution)/shard_map/pallas_call | solution.py:236
  66.2 0.0 copy-start.2
  66.2 3.4 %collective-permute-start.11 = (f32[8,4,8,128]{3,2,1,0:T(8,128)S(1)}, f32[8,4,8,128]{3,2,1,0:T(8,128)S(1)}, u32[]{:S(2)}, u32[]{:S(2)}) collective-permute-start(f32[8,4,8,128]{3,2,1,0:T(8,128)S(1)} %get-tuple-element.23), channel_id=1, source_target_pairs={{0,32},{32,0},{1,33},{33,1},{2,34},{34,2},{3,35},{35,3},{4,36},{36... | collective-permute-start | bytes 393224 | tf_op jit(solution)/shard_map/ppermute | solution.py:273
  69.6 0.0 copy-done.2
  69.6 5.4 %collective-permute-done.11 = f32[8,4,8,128]{3,2,1,0:T(8,128)S(1)} collective-permute-done((f32[8,4,8,128]{3,2,1,0:T(8,128)S(1)}, f32[8,4,8,128]{3,2,1,0:T(8,128)S(1)}, u32[]{:S(2)}, u32[]{:S(2)}) %collective-permute-start.11) | collective-permute-done | bytes 131104 | tf_op jit(solution)/shard_map/ppermute | solution.py:273
  75.1 0.8 %fusion = f32[8,8,8,128]{3,2,1,0:T(8,128)} fusion(f32[8,4,8,128]{3,2,1,0:T(8,128)S(1)} %collective-permute-done.11, f32[8,4,8,128]{3,2,1,0:T(8,128)S(1)} %get-tuple-element.22, f32[8]{0:T(128)S(1)} %convert_element_type.7, pred[]{:T(512)S(6)} %eq.12), kind=kLoop, calls=%fused_computation.1 | loop fusion | flops 262144 | bytes 524321 | tf_op jit(solution)/shard_map/add | solution.py:275
  75.8 1.5 %all-to-all-done.got = f32[64,8,128]{2,1,0:T(8,128)S(1)} async-done(((f32[64,8,128]{2,1,0:T(8,128)}), f32[64,8,128]{2,1,0:T(8,128)S(1)}, u32[]{:S(2)}, u32[]{:S(2)}) %all-to-all-start) | async-done | bytes 262176 | tf_op jit(solution)/shard_map/all_to_all | solution.py:265
  77.3 1.5 %shard_map.62 = f32[8,4,27]{2,1,0:T(4,128)} custom-call(s32[2]{0:T(128)S(1)} %pad_add_fusion.place, f32[64,8,128]{2,1,0:T(8,128)S(1)} %all-to-all-done.got), custom_call_target="tpu_custom_call" | custom-call | flops 100000000 | bytes 3000000 | tf_op jit(solution)/shard_map/pallas_call | solution.py:236
  (25 shorter events, 0.4 us)
Async XLA Ops:
  1.6 5.0 %copy-start.1 = (bf16[8,8,8,128]{3,2,1,0:T(8,128)(2,1)S(1)}, bf16[8,8,8,128]{3,2,1,0:T(8,128)(2,1)}, u32[]{:S(2)}) copy-start(bf16[8,8,8,128]{3,2,1,0:T(8,128)(2,1)} %param.5) | copy-start | bytes 393220
  1.7 7.0 %collective-permute-start = (bf16[5,8,8,128]{3,2,1,0:T(8,128)(2,1)S(1)}, bf16[5,8,8,128]{3,2,1,0:T(8,128)(2,1)S(1)}, u32[]{:S(2)}, u32[]{:S(2)}) collective-permute-start(bf16[5,8,8,128]{3,2,1,0:T(8,128)(2,1)S(1)} %bitcast.30), channel_id=1, source_target_pairs={{0,32},{32,0},{1,33},{33,1},{2,34},{34,2},{3,35},{35,3},{4,36},{36... | collective-permute-start | bytes 245768 | tf_op jit(solution)/shard_map/ppermute | solution.py:183
  6.7 10.8 %collective-permute-start.2 = (bf16[4,8,8,128]{3,2,1,0:T(8,128)(2,1)S(1)}, bf16[4,8,8,128]{3,2,1,0:T(8,128)(2,1)S(1)}, u32[]{:S(2)}, u32[]{:S(2)}) collective-permute-start(bf16[4,8,8,128]{3,2,1,0:T(8,128)(2,1)S(1)} %bitcast.31), channel_id=1, source_target_pairs={{0,32},{32,0},{1,33},{33,1},{2,34},{34,2},{3,35},{35,3},{4,36},{36... | collective-permute-start | bytes 196616 | tf_op jit(solution)/shard_map/ppermute | solution.py:194
  8.7 15.4 %collective-permute-start.1 = (bf16[5,8,16,128]{3,2,1,0:T(8,128)(2,1)S(1)}, bf16[5,8,16,128]{3,2,1,0:T(8,128)(2,1)S(1)}, u32[]{:S(2)}, u32[]{:S(2)}) collective-permute-start(bf16[5,8,16,128]{3,2,1,0:T(8,128)(2,1)S(1)} %maximum_select_fusion.1.refs_2_), channel_id=1, source_target_pairs={{0,128},{64,192},{128,256},{192,320},{256,384},{320,448},{384,0},{... | collective-permute-start | bytes 491528 | tf_op jit(solution)/shard_map/ppermute | solution.py:197
  13.1 13.5 %collective-permute-start.5 = (bf16[5,8,16,128]{3,2,1,0:T(8,128)(2,1)S(1)}, bf16[5,8,16,128]{3,2,1,0:T(8,128)(2,1)S(1)}, u32[]{:S(2)}, u32[]{:S(2)}) collective-permute-start(bf16[5,8,16,128]{3,2,1,0:T(8,128)(2,1)S(1)} %maximum_select_fusion.1.refs_2_), channel_id=1, source_target_pairs={{0,384},{64,448},{128,0},{192,64},{256,128},{320,192},{384,256},{4... | collective-permute-start | bytes 491528 | tf_op jit(solution)/shard_map/ppermute | solution.py:197
  16.7 0.8 %copy-start = (bf16[27,8,128]{2,1,0:T(8,128)(2,1)S(1)}, bf16[27,8,128]{2,1,0:T(8,128)(2,1)}, u32[]{:S(2)}) copy-start(bf16[27,8,128]{2,1,0:T(8,128)(2,1)} %param.6) | copy-start | bytes 165892
  17.6 18.3 %collective-permute-start.3 = (bf16[5,8,16,128]{3,2,1,0:T(8,128)(2,1)S(1)}, bf16[5,8,16,128]{3,2,1,0:T(8,128)(2,1)S(1)}, u32[]{:S(2)}, u32[]{:S(2)}) collective-permute-start(bf16[5,8,16,128]{3,2,1,0:T(8,128)(2,1)S(1)} %maximum_select_fusion.1.refs_2_), channel_id=1, source_target_pairs={{0,64},{64,128},{128,192},{192,256},{256,320},{320,384},{384,448},... | collective-permute-start | bytes 491528 | tf_op jit(solution)/shard_map/ppermute | solution.py:197
  20.4 15.6 %collective-permute-start.4 = (bf16[5,8,16,128]{3,2,1,0:T(8,128)(2,1)S(1)}, bf16[5,8,16,128]{3,2,1,0:T(8,128)(2,1)S(1)}, u32[]{:S(2)}, u32[]{:S(2)}) collective-permute-start(bf16[5,8,16,128]{3,2,1,0:T(8,128)(2,1)S(1)} %maximum_select_fusion.1.refs_2_), channel_id=1, source_target_pairs={{0,448},{64,0},{128,64},{192,128},{256,192},{320,256},{384,320},{4... | collective-permute-start | bytes 491528 | tf_op jit(solution)/shard_map/ppermute | solution.py:197
  26.6 9.5 %collective-permute-start.7 = (bf16[5,8,16,128]{3,2,1,0:T(8,128)(2,1)S(1)}, bf16[5,8,16,128]{3,2,1,0:T(8,128)(2,1)S(1)}, u32[]{:S(2)}, u32[]{:S(2)}) collective-permute-start(bf16[5,8,16,128]{3,2,1,0:T(8,128)(2,1)S(1)} %broadcast_select_fusion), channel_id=1, source_target_pairs={{0,384},{1,129},{64,448},{65,193},{128,0},{129,257},{192,64},{193,... | collective-permute-start | bytes 491528 | tf_op jit(solution)/shard_map/ppermute | solution.py:209
  30.6 12.9 %collective-permute-start.6 = (bf16[5,8,16,128]{3,2,1,0:T(8,128)(2,1)S(1)}, bf16[5,8,16,128]{3,2,1,0:T(8,128)(2,1)S(1)}, u32[]{:S(2)}, u32[]{:S(2)}) collective-permute-start(bf16[5,8,16,128]{3,2,1,0:T(8,128)(2,1)S(1)} %collective-permute-done.5.refs_4_), channel_id=1, source_target_pairs={{0,448},{64,0},{128,64},{192,128},{256,192},{320,256},{384,320},{4... | collective-permute-start | bytes 491528 | tf_op jit(solution)/shard_map/ppermute | solution.py:197
  32.5 10.9 %collective-permute-start.8 = (bf16[5,8,16,128]{3,2,1,0:T(8,128)(2,1)S(1)}, bf16[5,8,16,128]{3,2,1,0:T(8,128)(2,1)S(1)}, u32[]{:S(2)}, u32[]{:S(2)}) collective-permute-start(bf16[5,8,16,128]{3,2,1,0:T(8,128)(2,1)S(1)} %collective-permute-done.1.refs_0_), channel_id=1, source_target_pairs={{0,64},{64,128},{128,192},{192,256},{256,320},{320,384},{384,448},... | collective-permute-start | bytes 491528 | tf_op jit(solution)/shard_map/ppermute | solution.py:197
  36.1 10.9 %collective-permute-start.9 = (bf16[54,16,128]{2,1,0:T(8,128)(2,1)S(1)}, bf16[54,16,128]{2,1,0:T(8,128)(2,1)S(1)}, u32[]{:S(2)}, u32[]{:S(2)}) collective-permute-start(bf16[54,16,128]{2,1,0:T(8,128)(2,1)S(1)} %pad_maximum_fusion), channel_id=1, source_target_pairs={{32,1},{1,32},{33,2},{2,33},{34,3},{3,34},{35,4},{4,35},{36,5},{5,... | collective-permute-start | bytes 663560 | tf_op jit(solution)/shard_map/ppermute | solution.py:220
  43.5 6.2 %collective-permute-start.10 = (bf16[3,8,16,128]{3,2,1,0:T(8,128)(2,1)S(1)}, bf16[3,8,16,128]{3,2,1,0:T(8,128)(2,1)S(1)}, u32[]{:S(2)}, u32[]{:S(2)}) collective-permute-start(bf16[3,8,16,128]{3,2,1,0:T(8,128)(2,1)S(1)} %pad_maximum_fusion.3), channel_id=1, source_target_pairs={{32,1},{1,32},{33,2},{2,33},{34,3},{3,34},{35,4},{4,35},{36,5},{5,... | collective-permute-start | bytes 294920 | tf_op jit(solution)/shard_map/ppermute | solution.py:226
  51.4 25.9 %all-to-all-start = ((f32[64,8,128]{2,1,0:T(8,128)}), f32[64,8,128]{2,1,0:T(8,128)S(1)}, u32[]{:S(2)}, u32[]{:S(2)}) async-start(f32[64,8,128]{2,1,0:T(8,128)} %shard_map.60), calls=%async_computation | async-start | bytes 524288 | tf_op jit(solution)/shard_map/all_to_all | solution.py:265
  66.2 3.4 %copy-start.2 = (bf16[8]{0:T(256)(128)(2,1)S(1)}, bf16[8]{0:T(256)(128)(2,1)}, u32[]{:S(2)}) copy-start(bf16[8]{0:T(256)(128)(2,1)} %param.7) | copy-start | bytes 52
  66.2 8.9 %collective-permute-start.11 = (f32[8,4,8,128]{3,2,1,0:T(8,128)S(1)}, f32[8,4,8,128]{3,2,1,0:T(8,128)S(1)}, u32[]{:S(2)}, u32[]{:S(2)}) collective-permute-start(f32[8,4,8,128]{3,2,1,0:T(8,128)S(1)} %get-tuple-element.23), channel_id=1, source_target_pairs={{0,32},{32,0},{1,33},{33,1},{2,34},{34,2},{3,35},{35,3},{4,36},{36... | collective-permute-start | bytes 393224 | tf_op jit(solution)/shard_map/ppermute | solution.py:273

commit v11 on v7

--- a/solution.py
+++ b/solution.py
@@ -113,8 +113,8 @@
 
 def receivers(place, half):
     y, zl = place[0], place[1]
-    base = 32 * lax.rem(zl + half, 2)
-    return [base + lax.rem(y + k // 2 + 6, STEPS) * 4 + 2 * (k % 2) for k in range(16)]
+    base = lax.rem(zl + half, 2)
+    return [base + lax.rem(y + k // 2 + 6, STEPS) * 8 + 4 * (k % 2) for k in range(16)]
 
 
 def pair_of(one, two, k):
@@ -142,7 +142,7 @@
         one = jnp.where(wide < 72, one, pltpu.roll(three, 72, 1))
         two = jnp.where(wide < 72, two, pltpu.roll(three, 32, 1))
         for k, at in enumerate(receivers(place, half)):
-            grad[at], grad[at + 1] = pair_of(one, two, k)
+            grad[at], grad[at + 2] = pair_of(one, two, k)
 
 
 def edge_kernel(place, near, far, moved, earlier, grad):
@@ -159,7 +159,7 @@
         for k, at in enumerate(receivers(place, half)):
             first, second = pair_of(one, two, k)
             grad[at] = earlier[at] + first
-            grad[at + 1] = earlier[at + 1] + second
+            grad[at + 2] = earlier[at + 2] + second
 
 
 def finish_kernel(place, got, out, turned, table):
@@ -260,7 +260,7 @@
         rows,
     )
 
-    got = lax.all_to_all(grad, ("zl",) + SPACE, 0, 0, tiled=True)
+    got = lax.all_to_all(grad, SPACE + ("zl",), 0, 0, tiled=True)
     filter_grad = local(
         finish_kernel,
         jax.ShapeDtypeStruct((8, 4, 27), jnp.float32),

time: 79.5 us -> 79.2 us (level)
  no operation moved by 1% of the time
where the time goes in v11:
time: 79.2 us; the launch traced here: 78.7 us
  starting transfers between devices  56.8 us (72%)
  waiting for transfers between devices  11.3 us (14%)
  Pallas kernels  6.54 us (8%)
  local copies, waits for them, and re-layouts  1.91 us (2%)
  other arithmetic  1.13 us (1%)
  between operations  1.04 us (1%)
    ppermute x6, starting transfers between devices, along(): lax.ppermute(block, 'y', [(i, (i - by) % STEPS) for i in range(STEPS)])  19.6 us
    all_to_all x1, starting transfers between devices, on_device(): got = lax.all_to_all(grad, SPACE + ('zl',), 0, 0, tiled=True)  13.6 us
    ppermute x1, starting transfers between devices, on_device(): lax.ppermute(send, ('zl',) + SPACE, pairs)  6.55 us
    pallas_call x4, Pallas kernels, local(): pl.pallas_call(kernel, out_shape=shapes, in_specs=[pl.BlockSpec(memory_sp...  6.54 us
    ppermute x1, waiting for transfers between devices, on_device(): rest = lax.ppermute(feat[8:], 'zl', swap)  5.45 us
    ppermute x1, starting transfers between devices, on_device(): lax.ppermute(lax.dynamic_slice_in_dim(acts, 3 * (1 - zl), 5, 0), 'zl', swap)  4.96 us
    ppermute x1, starting transfers between devices, on_device(): lax.ppermute(jnp.where(lax.axis_index('core') == 0, b2, b6), ('y', 'core'...  3.98 us
    ppermute x6, waiting for transfers between devices, along(): lax.ppermute(block, 'y', [(i, (i - by) % STEPS) for i in range(STEPS)])  3.32 us
  transfers between devices with their start and end apart: 13, of which 4 were waited for; matrix products, arithmetic and copies ran while one was open for 2% of the time, Pallas kernels for 4%

profile of v11, /device:TPU:1, one launch (start us, length us, event | category | flops | bytes accessed | tf_op | source)
XLA Modules:
  0.0 78.7 jit_solution(14435415840278666628)
XLA Ops:
  0.6 1.0 %constant_dynamic-slice_fusion.2 = (bf16[8,5,8,128]{3,2,1,0:T(8,128)(2,1)S(1)}, bf16[8,5,8,128]{3,2,1,0:T(8,128)(2,1)S(1)}) fusion(bf16[8,8,8,128]{3,2,1,0:T(8,128)(2,1)} %param.4, s32[]{:T(128)S(6)} %select_n.80, s32[]{:T(128)S(6)} %select_n.81), kind=kLoop, calls=%fused_computation.27 | loop fusion | bytes 327688 | tf_op jit(solution)/shard_map/dynamic-slice
  1.6 0.0 copy-start.1
  1.7 5.0 %collective-permute-start = (bf16[5,8,8,128]{3,2,1,0:T(8,128)(2,1)S(1)}, bf16[5,8,8,128]{3,2,1,0:T(8,128)(2,1)S(1)}, u32[]{:S(2)}, u32[]{:S(2)}) collective-permute-start(bf16[5,8,8,128]{3,2,1,0:T(8,128)(2,1)S(1)} %bitcast.20), channel_id=1, source_target_pairs={{0,32},{32,0},{1,33},{33,1},{2,34},{34,2},{3,35},{35,3},{4,36},{36... | collective-permute-start | bytes 245768 | tf_op jit(solution)/shard_map/ppermute | solution.py:183
  6.6 0.0 copy-done.1
  6.7 0.0 copy-start
  6.7 0.8 copy-done
  7.5 1.9 %collective-permute-start.2 = (bf16[59,8,128]{2,1,0:T(8,128)(2,1)S(1)}, bf16[59,8,128]{2,1,0:T(8,128)(2,1)S(1)}, u32[]{:S(2)}, u32[]{:S(2)}) collective-permute-start(bf16[59,8,128]{2,1,0:T(8,128)(2,1)S(1)} %pad_maximum_fusion.1), channel_id=1, source_target_pairs={{0,32},{32,0},{1,33},{33,1},{2,34},{34,2},{3,35},{35,3},{4,36},{36... | collective-permute-start | bytes 362504 | tf_op jit(solution)/shard_map/ppermute | solution.py:197
  9.5 0.0 collective-permute-done
  9.6 4.2 %collective-permute-start.1 = (bf16[5,8,16,128]{3,2,1,0:T(8,128)(2,1)S(1)}, bf16[5,8,16,128]{3,2,1,0:T(8,128)(2,1)S(1)}, u32[]{:S(2)}, u32[]{:S(2)}) collective-permute-start(bf16[5,8,16,128]{3,2,1,0:T(8,128)(2,1)S(1)} %maximum_select_fusion.1.refs_2_), channel_id=1, source_target_pairs={{0,128},{64,192},{128,256},{192,320},{256,384},{320,448},{384,0},{... | collective-permute-start | bytes 491528 | tf_op jit(solution)/shard_map/ppermute | solution.py:200
  13.8 3.6 %collective-permute-start.5 = (bf16[5,8,16,128]{3,2,1,0:T(8,128)(2,1)S(1)}, bf16[5,8,16,128]{3,2,1,0:T(8,128)(2,1)S(1)}, u32[]{:S(2)}, u32[]{:S(2)}) collective-permute-start(bf16[5,8,16,128]{3,2,1,0:T(8,128)(2,1)S(1)} %maximum_select_fusion.1.refs_2_), channel_id=1, source_target_pairs={{0,384},{64,448},{128,0},{192,64},{256,128},{320,192},{384,256},{4... | collective-permute-start | bytes 491528 | tf_op jit(solution)/shard_map/ppermute | solution.py:200
  17.4 0.0 collective-permute-done.2
  17.5 2.8 %collective-permute-start.3 = (bf16[5,8,16,128]{3,2,1,0:T(8,128)(2,1)S(1)}, bf16[5,8,16,128]{3,2,1,0:T(8,128)(2,1)S(1)}, u32[]{:S(2)}, u32[]{:S(2)}) collective-permute-start(bf16[5,8,16,128]{3,2,1,0:T(8,128)(2,1)S(1)} %maximum_select_fusion.1.refs_2_), channel_id=1, source_target_pairs={{0,64},{64,128},{128,192},{192,256},{256,320},{320,384},{384,448},... | collective-permute-start | bytes 491528 | tf_op jit(solution)/shard_map/ppermute | solution.py:200
  20.3 3.7 %collective-permute-start.4 = (bf16[5,8,16,128]{3,2,1,0:T(8,128)(2,1)S(1)}, bf16[5,8,16,128]{3,2,1,0:T(8,128)(2,1)S(1)}, u32[]{:S(2)}, u32[]{:S(2)}) collective-permute-start(bf16[5,8,16,128]{3,2,1,0:T(8,128)(2,1)S(1)} %maximum_select_fusion.1.refs_2_), channel_id=1, source_target_pairs={{0,448},{64,0},{128,64},{192,128},{256,192},{320,256},{384,320},{4... | collective-permute-start | bytes 491528 | tf_op jit(solution)/shard_map/ppermute | solution.py:200
  24.0 0.0 collective-permute-done.1.refs_0_
  24.0 3.3 %collective-permute-done.5.refs_4_ = bf16[5,8,16,128]{3,2,1,0:T(8,128)(2,1)S(1)} collective-permute-done((bf16[5,8,16,128]{3,2,1,0:T(8,128)(2,1)S(1)}, bf16[5,8,16,128]{3,2,1,0:T(8,128)(2,1)S(1)}, u32[]{:S(2)}, u32[]{:S(2)}) %collective-permute-start.5) | collective-permute-done | bytes 163872 | tf_op jit(solution)/shard_map/ppermute | solution.py:200
  27.3 4.0 %collective-permute-start.7 = (bf16[5,8,16,128]{3,2,1,0:T(8,128)(2,1)S(1)}, bf16[5,8,16,128]{3,2,1,0:T(8,128)(2,1)S(1)}, u32[]{:S(2)}, u32[]{:S(2)}) collective-permute-start(bf16[5,8,16,128]{3,2,1,0:T(8,128)(2,1)S(1)} %broadcast_select_fusion), channel_id=1, source_target_pairs={{0,384},{1,129},{64,448},{65,193},{128,0},{129,257},{192,64},{193,... | collective-permute-start | bytes 491528 | tf_op jit(solution)/shard_map/ppermute | solution.py:213
  31.3 1.9 %collective-permute-start.6 = (bf16[5,8,16,128]{3,2,1,0:T(8,128)(2,1)S(1)}, bf16[5,8,16,128]{3,2,1,0:T(8,128)(2,1)S(1)}, u32[]{:S(2)}, u32[]{:S(2)}) collective-permute-start(bf16[5,8,16,128]{3,2,1,0:T(8,128)(2,1)S(1)} %collective-permute-done.5.refs_4_), channel_id=1, source_target_pairs={{0,448},{64,0},{128,64},{192,128},{256,192},{320,256},{384,320},{4... | collective-permute-start | bytes 491528 | tf_op jit(solution)/shard_map/ppermute | solution.py:200
  33.2 3.4 %collective-permute-start.8 = (bf16[5,8,16,128]{3,2,1,0:T(8,128)(2,1)S(1)}, bf16[5,8,16,128]{3,2,1,0:T(8,128)(2,1)S(1)}, u32[]{:S(2)}, u32[]{:S(2)}) collective-permute-start(bf16[5,8,16,128]{3,2,1,0:T(8,128)(2,1)S(1)} %collective-permute-done.1.refs_0_), channel_id=1, source_target_pairs={{0,64},{64,128},{128,192},{192,256},{256,320},{320,384},{384,448},... | collective-permute-start | bytes 491528 | tf_op jit(solution)/shard_map/ppermute | solution.py:200
  36.6 0.0 collective-permute-done.3.refs_1_
  36.7 0.0 collective-permute-done.4.refs_3_
  36.8 0.0 collective-permute-done.7.refs_6_
  36.8 6.5 %collective-permute-start.9 = (bf16[5,8,16,128]{3,2,1,0:T(8,128)(2,1)S(1)}, bf16[5,8,16,128]{3,2,1,0:T(8,128)(2,1)S(1)}, u32[]{:S(2)}, u32[]{:S(2)}) collective-permute-start(bf16[5,8,16,128]{3,2,1,0:T(8,128)(2,1)S(1)} %fusion.1), channel_id=1, source_target_pairs={{32,1},{1,32},{33,2},{2,33},{34,3},{3,34},{35,4},{4,35},{36,5},{5,... | collective-permute-start | bytes 491528 | tf_op jit(solution)/shard_map/ppermute | solution.py:223
  43.3 0.0 collective-permute-done.8.refs_7_
  43.4 0.0 collective-permute-done.6.refs_5_
  43.4 2.9 %collective-permute-start.10 = (bf16[3,8,16,128]{3,2,1,0:T(8,128)(2,1)S(1)}, bf16[3,8,16,128]{3,2,1,0:T(8,128)(2,1)S(1)}, u32[]{:S(2)}, u32[]{:S(2)}) collective-permute-start(bf16[3,8,16,128]{3,2,1,0:T(8,128)(2,1)S(1)} %pad_maximum_fusion.3), channel_id=1, source_target_pairs={{32,1},{1,32},{33,2},{2,33},{34,3},{3,34},{35,4},{4,35},{36,5},{5,... | collective-permute-start | bytes 294920 | tf_op jit(solution)/shard_map/ppermute | solution.py:224
  46.4 0.1 pad_add_fusion.place
  46.4 0.0 collective-permute-done.9.near.refs_8_
  46.5 1.8 %shard_map.59 = (f32[64,8,128]{2,1,0:T(8,128)S(1)}, bf16[2,256,1024]{2,1,0:T(8,128)(2,1)S(1)}) custom-call(s32[2]{0:T(128)S(1)} %pad_add_fusion.place, bf16[5,8,16,128]{3,2,1,0:T(8,128)(2,1)S(1)} %collective-permute-done.1.refs_0_, bf16[5,8,16,128]{3,2,1,0:T(8,128)(2,1)S(1)} %collective-permute-done.3.refs_1_, ...), custom_call_target="tpu_custom_call" | custom-call | flops 900000000 | bytes 3000000 | tf_op jit(solution)/shard_map/pallas_call | solution.py:234
  48.2 1.1 %collective-permute-done.10.far.refs_9_ = bf16[3,8,16,128]{3,2,1,0:T(8,128)(2,1)S(1)} collective-permute-done((bf16[3,8,16,128]{3,2,1,0:T(8,128)(2,1)S(1)}, bf16[3,8,16,128]{3,2,1,0:T(8,128)(2,1)S(1)}, u32[]{:S(2)}, u32[]{:S(2)}) %collective-permute-start.10) | collective-permute-done | bytes 98336 | tf_op jit(solution)/shard_map/ppermute | solution.py:224
  49.4 1.7 %shard_map.60 = f32[64,8,128]{2,1,0:T(8,128)} custom-call(s32[2]{0:T(128)S(1)} %pad_add_fusion.place, bf16[5,8,16,128]{3,2,1,0:T(8,128)(2,1)S(1)} %collective-permute-done.9.near.refs_8_, bf16[3,8,16,128]{3,2,1,0:T(8,128)(2,1)S(1)} %collective-permute-done.10.far.refs_9_, bf16[2,256,1024]{2,1,0:T(8,128)(2,1)S(1)} %get-tuple-element.20.moved, ...), custom_call_target="tpu_custom_call" | custom-call | flops 400000000 | bytes 3000000 | tf_op jit(solution)/shard_map/pallas_call | solution.py:234
  51.0 13.6 %all-to-all-start = ((f32[64,8,128]{2,1,0:T(8,128)}), f32[64,8,128]{2,1,0:T(8,128)S(1)}, u32[]{:S(2)}, u32[]{:S(2)}) async-start(f32[64,8,128]{2,1,0:T(8,128)} %shard_map.60), calls=%async_computation | async-start | bytes 524288 | tf_op jit(solution)/shard_map/all_to_all | solution.py:263
  64.6 1.6 %shard_map.61 = f32[16,4,8,128]{3,2,1,0:T(8,128)S(1)} custom-call(s32[2]{0:T(128)S(1)} %pad_add_fusion.place, bf16[5,8,16,128]{3,2,1,0:T(8,128)(2,1)S(1)} %collective-permute-done.1.refs_0_, bf16[5,8,16,128]{3,2,1,0:T(8,128)(2,1)S(1)} %collective-permute-done.3.refs_1_, bf16[5,8,16,128]{3,2,1,0:T(8,128)(2,1)S(1)} %maximum_select_fusion.1.refs_2_, ...), custom_call_target="tpu_custom_call" | custom-call | flops 1100000000 | bytes 3000000 | tf_op jit(solution)/shard_map/pallas_call | solution.py:234
  66.2 0.0 copy-start.2
  66.2 3.3 %collective-permute-start.11 = (f32[8,4,8,128]{3,2,1,0:T(8,128)S(1)}, f32[8,4,8,128]{3,2,1,0:T(8,128)S(1)}, u32[]{:S(2)}, u32[]{:S(2)}) collective-permute-start(f32[8,4,8,128]{3,2,1,0:T(8,128)S(1)} %get-tuple-element.25), channel_id=1, source_target_pairs={{0,32},{32,0},{1,33},{33,1},{2,34},{34,2},{3,35},{35,3},{4,36},{36... | collective-permute-start | bytes 393224 | tf_op jit(solution)/shard_map/ppermute | solution.py:271
  69.5 0.0 copy-done.2
  69.6 5.4 %collective-permute-done.11 = f32[8,4,8,128]{3,2,1,0:T(8,128)S(1)} collective-permute-done((f32[8,4,8,128]{3,2,1,0:T(8,128)S(1)}, f32[8,4,8,128]{3,2,1,0:T(8,128)S(1)}, u32[]{:S(2)}, u32[]{:S(2)}) %collective-permute-start.11) | collective-permute-done | bytes 131104 | tf_op jit(solution)/shard_map/ppermute | solution.py:271
  75.0 0.8 %fusion = f32[8,8,8,128]{3,2,1,0:T(8,128)} fusion(f32[8,4,8,128]{3,2,1,0:T(8,128)S(1)} %collective-permute-done.11, f32[8,4,8,128]{3,2,1,0:T(8,128)S(1)} %get-tuple-element.24, f32[8]{0:T(128)S(1)} %convert_element_type.3, pred[]{:T(512)S(6)} %eq.6), kind=kLoop, calls=%fused_computation.1 | loop fusion | flops 262144 | bytes 524321 | tf_op jit(solution)/shard_map/add | solution.py:273
  75.8 1.3 %all-to-all-done.got = f32[64,8,128]{2,1,0:T(8,128)S(1)} async-done(((f32[64,8,128]{2,1,0:T(8,128)}), f32[64,8,128]{2,1,0:T(8,128)S(1)}, u32[]{:S(2)}, u32[]{:S(2)}) %all-to-all-start) | async-done | bytes 262176 | tf_op jit(solution)/shard_map/all_to_all | solution.py:263
  77.1 1.5 %shard_map.62 = f32[8,4,27]{2,1,0:T(4,128)} custom-call(s32[2]{0:T(128)S(1)} %pad_add_fusion.place, f32[64,8,128]{2,1,0:T(8,128)S(1)} %all-to-all-done.got), custom_call_target="tpu_custom_call" | custom-call | flops 100000000 | bytes 3000000 | tf_op jit(solution)/shard_map/pallas_call | solution.py:234
  (23 shorter events, 0.4 us)
Async XLA Ops:
  1.6 5.0 %copy-start.1 = (bf16[8,8,8,128]{3,2,1,0:T(8,128)(2,1)S(1)}, bf16[8,8,8,128]{3,2,1,0:T(8,128)(2,1)}, u32[]{:S(2)}) copy-start(bf16[8,8,8,128]{3,2,1,0:T(8,128)(2,1)} %param.5) | copy-start | bytes 393220
  1.7 7.8 %collective-permute-start = (bf16[5,8,8,128]{3,2,1,0:T(8,128)(2,1)S(1)}, bf16[5,8,8,128]{3,2,1,0:T(8,128)(2,1)S(1)}, u32[]{:S(2)}, u32[]{:S(2)}) collective-permute-start(bf16[5,8,8,128]{3,2,1,0:T(8,128)(2,1)S(1)} %bitcast.20), channel_id=1, source_target_pairs={{0,32},{32,0},{1,33},{33,1},{2,34},{34,2},{3,35},{35,3},{4,36},{36... | collective-permute-start | bytes 245768 | tf_op jit(solution)/shard_map/ppermute | solution.py:183
  6.7 0.8 %copy-start = (bf16[27,8,128]{2,1,0:T(8,128)(2,1)S(1)}, bf16[27,8,128]{2,1,0:T(8,128)(2,1)}, u32[]{:S(2)}) copy-start(bf16[27,8,128]{2,1,0:T(8,128)(2,1)} %param.6) | copy-start | bytes 165892
  7.5 9.9 %collective-permute-start.2 = (bf16[59,8,128]{2,1,0:T(8,128)(2,1)S(1)}, bf16[59,8,128]{2,1,0:T(8,128)(2,1)S(1)}, u32[]{:S(2)}, u32[]{:S(2)}) collective-permute-start(bf16[59,8,128]{2,1,0:T(8,128)(2,1)S(1)} %pad_maximum_fusion.1), channel_id=1, source_target_pairs={{0,32},{32,0},{1,33},{33,1},{2,34},{34,2},{3,35},{35,3},{4,36},{36... | collective-permute-start | bytes 362504 | tf_op jit(solution)/shard_map/ppermute | solution.py:197
  9.6 14.4 %collective-permute-start.1 = (bf16[5,8,16,128]{3,2,1,0:T(8,128)(2,1)S(1)}, bf16[5,8,16,128]{3,2,1,0:T(8,128)(2,1)S(1)}, u32[]{:S(2)}, u32[]{:S(2)}) collective-permute-start(bf16[5,8,16,128]{3,2,1,0:T(8,128)(2,1)S(1)} %maximum_select_fusion.1.refs_2_), channel_id=1, source_target_pairs={{0,128},{64,192},{128,256},{192,320},{256,384},{320,448},{384,0},{... | collective-permute-start | bytes 491528 | tf_op jit(solution)/shard_map/ppermute | solution.py:200
  13.8 13.5 %collective-permute-start.5 = (bf16[5,8,16,128]{3,2,1,0:T(8,128)(2,1)S(1)}, bf16[5,8,16,128]{3,2,1,0:T(8,128)(2,1)S(1)}, u32[]{:S(2)}, u32[]{:S(2)}) collective-permute-start(bf16[5,8,16,128]{3,2,1,0:T(8,128)(2,1)S(1)} %maximum_select_fusion.1.refs_2_), channel_id=1, source_target_pairs={{0,384},{64,448},{128,0},{192,64},{256,128},{320,192},{384,256},{4... | collective-permute-start | bytes 491528 | tf_op jit(solution)/shard_map/ppermute | solution.py:200
  17.5 19.2 %collective-permute-start.3 = (bf16[5,8,16,128]{3,2,1,0:T(8,128)(2,1)S(1)}, bf16[5,8,16,128]{3,2,1,0:T(8,128)(2,1)S(1)}, u32[]{:S(2)}, u32[]{:S(2)}) collective-permute-start(bf16[5,8,16,128]{3,2,1,0:T(8,128)(2,1)S(1)} %maximum_select_fusion.1.refs_2_), channel_id=1, source_target_pairs={{0,64},{64,128},{128,192},{192,256},{256,320},{320,384},{384,448},... | collective-permute-start | bytes 491528 | tf_op jit(solution)/shard_map/ppermute | solution.py:200
  20.3 16.4 %collective-permute-start.4 = (bf16[5,8,16,128]{3,2,1,0:T(8,128)(2,1)S(1)}, bf16[5,8,16,128]{3,2,1,0:T(8,128)(2,1)S(1)}, u32[]{:S(2)}, u32[]{:S(2)}) collective-permute-start(bf16[5,8,16,128]{3,2,1,0:T(8,128)(2,1)S(1)} %maximum_select_fusion.1.refs_2_), channel_id=1, source_target_pairs={{0,448},{64,0},{128,64},{192,128},{256,192},{320,256},{384,320},{4... | collective-permute-start | bytes 491528 | tf_op jit(solution)/shard_map/ppermute | solution.py:200
  27.3 9.4 %collective-permute-start.7 = (bf16[5,8,16,128]{3,2,1,0:T(8,128)(2,1)S(1)}, bf16[5,8,16,128]{3,2,1,0:T(8,128)(2,1)S(1)}, u32[]{:S(2)}, u32[]{:S(2)}) collective-permute-start(bf16[5,8,16,128]{3,2,1,0:T(8,128)(2,1)S(1)} %broadcast_select_fusion), channel_id=1, source_target_pairs={{0,384},{1,129},{64,448},{65,193},{128,0},{129,257},{192,64},{193,... | collective-permute-start | bytes 491528 | tf_op jit(solution)/shard_map/ppermute | solution.py:213
  31.3 12.1 %collective-permute-start.6 = (bf16[5,8,16,128]{3,2,1,0:T(8,128)(2,1)S(1)}, bf16[5,8,16,128]{3,2,1,0:T(8,128)(2,1)S(1)}, u32[]{:S(2)}, u32[]{:S(2)}) collective-permute-start(bf16[5,8,16,128]{3,2,1,0:T(8,128)(2,1)S(1)} %collective-permute-done.5.refs_4_), channel_id=1, source_target_pairs={{0,448},{64,0},{128,64},{192,128},{256,192},{320,256},{384,320},{4... | collective-permute-start | bytes 491528 | tf_op jit(solution)/shard_map/ppermute | solution.py:200
  33.2 10.1 %collective-permute-start.8 = (bf16[5,8,16,128]{3,2,1,0:T(8,128)(2,1)S(1)}, bf16[5,8,16,128]{3,2,1,0:T(8,128)(2,1)S(1)}, u32[]{:S(2)}, u32[]{:S(2)}) collective-permute-start(bf16[5,8,16,128]{3,2,1,0:T(8,128)(2,1)S(1)} %collective-permute-done.1.refs_0_), channel_id=1, source_target_pairs={{0,64},{64,128},{128,192},{192,256},{256,320},{320,384},{384,448},... | collective-permute-start | bytes 491528 | tf_op jit(solution)/shard_map/ppermute | solution.py:200
  36.8 9.7 %collective-permute-start.9 = (bf16[5,8,16,128]{3,2,1,0:T(8,128)(2,1)S(1)}, bf16[5,8,16,128]{3,2,1,0:T(8,128)(2,1)S(1)}, u32[]{:S(2)}, u32[]{:S(2)}) collective-permute-start(bf16[5,8,16,128]{3,2,1,0:T(8,128)(2,1)S(1)} %fusion.1), channel_id=1, source_target_pairs={{32,1},{1,32},{33,2},{2,33},{34,3},{3,34},{35,4},{4,35},{36,5},{5,... | collective-permute-start | bytes 491528 | tf_op jit(solution)/shard_map/ppermute | solution.py:223
  43.4 5.9 %collective-permute-start.10 = (bf16[3,8,16,128]{3,2,1,0:T(8,128)(2,1)S(1)}, bf16[3,8,16,128]{3,2,1,0:T(8,128)(2,1)S(1)}, u32[]{:S(2)}, u32[]{:S(2)}) collective-permute-start(bf16[3,8,16,128]{3,2,1,0:T(8,128)(2,1)S(1)} %pad_maximum_fusion.3), channel_id=1, source_target_pairs={{32,1},{1,32},{33,2},{2,33},{34,3},{3,34},{35,4},{4,35},{36,5},{5,... | collective-permute-start | bytes 294920 | tf_op jit(solution)/shard_map/ppermute | solution.py:224
  51.0 26.1 %all-to-all-start = ((f32[64,8,128]{2,1,0:T(8,128)}), f32[64,8,128]{2,1,0:T(8,128)S(1)}, u32[]{:S(2)}, u32[]{:S(2)}) async-start(f32[64,8,128]{2,1,0:T(8,128)} %shard_map.60), calls=%async_computation | async-start | bytes 524288 | tf_op jit(solution)/shard_map/all_to_all | solution.py:263
  66.2 3.3 %copy-start.2 = (bf16[8]{0:T(256)(128)(2,1)S(1)}, bf16[8]{0:T(256)(128)(2,1)}, u32[]{:S(2)}) copy-start(bf16[8]{0:T(256)(128)(2,1)} %param.7) | copy-start | bytes 52
  66.2 8.8 %collective-permute-start.11 = (f32[8,4,8,128]{3,2,1,0:T(8,128)S(1)}, f32[8,4,8,128]{3,2,1,0:T(8,128)S(1)}, u32[]{:S(2)}, u32[]{:S(2)}) collective-permute-start(f32[8,4,8,128]{3,2,1,0:T(8,128)S(1)} %get-tuple-element.25), channel_id=1, source_target_pairs={{0,32},{32,0},{1,33},{33,1},{2,34},{34,2},{3,35},{35,3},{4,36},{36... | collective-permute-start | bytes 393224 | tf_op jit(solution)/shard_map/ppermute | solution.py:271

commit v12 on v11

--- a/solution.py
+++ b/solution.py
@@ -269,6 +269,7 @@
     ).transpose(2, 0, 1)
 
     rest = lax.ppermute(feat[8:], "zl", swap)
+    rest, filter_grad = lax.optimization_barrier((rest, filter_grad))
     kept = feat[:8]
     features_out = jnp.where(
         first,

time: 79.2 us -> 80 us (1.010)
    all_to_all x1, waiting for transfers between devices: 1.33 us -> 7.57 us  [on_device(): got = lax.all_to_all(grad, SPACE + ('zl',), 0, 0, tiled=True)]
    ppermute x1, waiting for transfers between devices: 5.45 us -> 0.01 us  [on_device(): rest = lax.ppermute(feat[8:], 'zl', swap)]
  transfers between devices with their start and end apart: 13 -> 13, of which waited for: 4 -> 3; matrix products, arithmetic and copies ran while one was open for 2% -> 1% of each run, Pallas kernels for 4% -> 6%
where the time goes in v12:
time: 80 us; the launch traced here: 79.5 us
  starting transfers between devices  56.8 us (71%)
  waiting for transfers between devices  12 us (15%)
  Pallas kernels  6.55 us (8%)
  local copies, waits for them, and re-layouts  1.91 us (2%)
  other arithmetic  1.13 us (1%)
  between operations  1.04 us (1%)
    ppermute x6, starting transfers between devices, along(): lax.ppermute(block, 'y', [(i, (i - by) % STEPS) for i in range(STEPS)])  19.6 us
    all_to_all x1, starting transfers between devices, on_device(): got = lax.all_to_all(grad, SPACE + ('zl',), 0, 0, tiled=True)  13.6 us
    all_to_all x1, waiting for transfers between devices, on_device(): got = lax.all_to_all(grad, SPACE + ('zl',), 0, 0, tiled=True)  7.57 us
    ppermute x1, starting transfers between devices, on_device(): lax.ppermute(send, ('zl',) + SPACE, pairs)  6.55 us
    pallas_call x4, Pallas kernels, local(): pl.pallas_call(kernel, out_shape=shapes, in_specs=[pl.BlockSpec(memory_sp...  6.55 us
    ppermute x1, starting transfers between devices, on_device(): lax.ppermute(lax.dynamic_slice_in_dim(acts, 3 * (1 - zl), 5, 0), 'zl', swap)  4.96 us
    ppermute x1, starting transfers between devices, on_device(): lax.ppermute(jnp.where(lax.axis_index('core') == 0, b2, b6), ('y', 'core'...  3.98 us
    ppermute x6, waiting for transfers between devices, along(): lax.ppermute(block, 'y', [(i, (i - by) % STEPS) for i in range(STEPS)])  3.32 us
  transfers between devices with their start and end apart: 13, of which 3 were waited for; matrix products, arithmetic and copies ran while one was open for 1% of the time, Pallas kernels for 6%

profile of v12, /device:TPU:1, one launch (start us, length us, event | category | flops | bytes accessed | tf_op | source)
XLA Modules:
  0.0 79.5 jit_solution(11522239851990283016)
XLA Ops:
  0.6 1.0 %constant_dynamic-slice_fusion.2 = (bf16[8,5,8,128]{3,2,1,0:T(8,128)(2,1)S(1)}, bf16[8,5,8,128]{3,2,1,0:T(8,128)(2,1)S(1)}) fusion(bf16[8,8,8,128]{3,2,1,0:T(8,128)(2,1)} %param.4, s32[]{:T(128)S(6)} %select_n.80, s32[]{:T(128)S(6)} %select_n.81), kind=kLoop, calls=%fused_computation.27 | loop fusion | bytes 327688 | tf_op jit(solution)/shard_map/dynamic-slice
  1.6 0.0 copy-start.1
  1.7 5.0 %collective-permute-start = (bf16[5,8,8,128]{3,2,1,0:T(8,128)(2,1)S(1)}, bf16[5,8,8,128]{3,2,1,0:T(8,128)(2,1)S(1)}, u32[]{:S(2)}, u32[]{:S(2)}) collective-permute-start(bf16[5,8,8,128]{3,2,1,0:T(8,128)(2,1)S(1)} %bitcast.20), channel_id=1, source_target_pairs={{0,32},{32,0},{1,33},{33,1},{2,34},{34,2},{3,35},{35,3},{4,36},{36... | collective-permute-start | bytes 245768 | tf_op jit(solution)/shard_map/ppermute | solution.py:183
  6.6 0.0 copy-done.1
  6.7 0.0 copy-start
  6.7 0.8 copy-done
  7.5 1.9 %collective-permute-start.2 = (bf16[59,8,128]{2,1,0:T(8,128)(2,1)S(1)}, bf16[59,8,128]{2,1,0:T(8,128)(2,1)S(1)}, u32[]{:S(2)}, u32[]{:S(2)}) collective-permute-start(bf16[59,8,128]{2,1,0:T(8,128)(2,1)S(1)} %pad_maximum_fusion.1), channel_id=1, source_target_pairs={{0,32},{32,0},{1,33},{33,1},{2,34},{34,2},{3,35},{35,3},{4,36},{36... | collective-permute-start | bytes 362504 | tf_op jit(solution)/shard_map/ppermute | solution.py:197
  9.5 0.0 collective-permute-done
  9.6 4.2 %collective-permute-start.1 = (bf16[5,8,16,128]{3,2,1,0:T(8,128)(2,1)S(1)}, bf16[5,8,16,128]{3,2,1,0:T(8,128)(2,1)S(1)}, u32[]{:S(2)}, u32[]{:S(2)}) collective-permute-start(bf16[5,8,16,128]{3,2,1,0:T(8,128)(2,1)S(1)} %maximum_select_fusion.1.refs_2_), channel_id=1, source_target_pairs={{0,128},{64,192},{128,256},{192,320},{256,384},{320,448},{384,0},{... | collective-permute-start | bytes 491528 | tf_op jit(solution)/shard_map/ppermute | solution.py:200
  13.8 3.6 %collective-permute-start.5 = (bf16[5,8,16,128]{3,2,1,0:T(8,128)(2,1)S(1)}, bf16[5,8,16,128]{3,2,1,0:T(8,128)(2,1)S(1)}, u32[]{:S(2)}, u32[]{:S(2)}) collective-permute-start(bf16[5,8,16,128]{3,2,1,0:T(8,128)(2,1)S(1)} %maximum_select_fusion.1.refs_2_), channel_id=1, source_target_pairs={{0,384},{64,448},{128,0},{192,64},{256,128},{320,192},{384,256},{4... | collective-permute-start | bytes 491528 | tf_op jit(solution)/shard_map/ppermute | solution.py:200
  17.4 0.0 collective-permute-done.2
  17.5 2.8 %collective-permute-start.3 = (bf16[5,8,16,128]{3,2,1,0:T(8,128)(2,1)S(1)}, bf16[5,8,16,128]{3,2,1,0:T(8,128)(2,1)S(1)}, u32[]{:S(2)}, u32[]{:S(2)}) collective-permute-start(bf16[5,8,16,128]{3,2,1,0:T(8,128)(2,1)S(1)} %maximum_select_fusion.1.refs_2_), channel_id=1, source_target_pairs={{0,64},{64,128},{128,192},{192,256},{256,320},{320,384},{384,448},... | collective-permute-start | bytes 491528 | tf_op jit(solution)/shard_map/ppermute | solution.py:200
  20.3 3.7 %collective-permute-start.4 = (bf16[5,8,16,128]{3,2,1,0:T(8,128)(2,1)S(1)}, bf16[5,8,16,128]{3,2,1,0:T(8,128)(2,1)S(1)}, u32[]{:S(2)}, u32[]{:S(2)}) collective-permute-start(bf16[5,8,16,128]{3,2,1,0:T(8,128)(2,1)S(1)} %maximum_select_fusion.1.refs_2_), channel_id=1, source_target_pairs={{0,448},{64,0},{128,64},{192,128},{256,192},{320,256},{384,320},{4... | collective-permute-start | bytes 491528 | tf_op jit(solution)/shard_map/ppermute | solution.py:200
  24.0 0.0 collective-permute-done.1.refs_0_
  24.0 3.3 %collective-permute-done.5.refs_4_ = bf16[5,8,16,128]{3,2,1,0:T(8,128)(2,1)S(1)} collective-permute-done((bf16[5,8,16,128]{3,2,1,0:T(8,128)(2,1)S(1)}, bf16[5,8,16,128]{3,2,1,0:T(8,128)(2,1)S(1)}, u32[]{:S(2)}, u32[]{:S(2)}) %collective-permute-start.5) | collective-permute-done | bytes 163872 | tf_op jit(solution)/shard_map/ppermute | solution.py:200
  27.3 4.0 %collective-permute-start.7 = (bf16[5,8,16,128]{3,2,1,0:T(8,128)(2,1)S(1)}, bf16[5,8,16,128]{3,2,1,0:T(8,128)(2,1)S(1)}, u32[]{:S(2)}, u32[]{:S(2)}) collective-permute-start(bf16[5,8,16,128]{3,2,1,0:T(8,128)(2,1)S(1)} %broadcast_select_fusion), channel_id=1, source_target_pairs={{0,384},{1,129},{64,448},{65,193},{128,0},{129,257},{192,64},{193,... | collective-permute-start | bytes 491528 | tf_op jit(solution)/shard_map/ppermute | solution.py:213
  31.3 1.9 %collective-permute-start.6 = (bf16[5,8,16,128]{3,2,1,0:T(8,128)(2,1)S(1)}, bf16[5,8,16,128]{3,2,1,0:T(8,128)(2,1)S(1)}, u32[]{:S(2)}, u32[]{:S(2)}) collective-permute-start(bf16[5,8,16,128]{3,2,1,0:T(8,128)(2,1)S(1)} %collective-permute-done.5.refs_4_), channel_id=1, source_target_pairs={{0,448},{64,0},{128,64},{192,128},{256,192},{320,256},{384,320},{4... | collective-permute-start | bytes 491528 | tf_op jit(solution)/shard_map/ppermute | solution.py:200
  33.2 3.4 %collective-permute-start.8 = (bf16[5,8,16,128]{3,2,1,0:T(8,128)(2,1)S(1)}, bf16[5,8,16,128]{3,2,1,0:T(8,128)(2,1)S(1)}, u32[]{:S(2)}, u32[]{:S(2)}) collective-permute-start(bf16[5,8,16,128]{3,2,1,0:T(8,128)(2,1)S(1)} %collective-permute-done.1.refs_0_), channel_id=1, source_target_pairs={{0,64},{64,128},{128,192},{192,256},{256,320},{320,384},{384,448},... | collective-permute-start | bytes 491528 | tf_op jit(solution)/shard_map/ppermute | solution.py:200
  36.6 0.0 collective-permute-done.3.refs_1_
  36.7 0.0 collective-permute-done.4.refs_3_
  36.8 0.0 collective-permute-done.7.refs_6_
  36.8 6.5 %collective-permute-start.9 = (bf16[5,8,16,128]{3,2,1,0:T(8,128)(2,1)S(1)}, bf16[5,8,16,128]{3,2,1,0:T(8,128)(2,1)S(1)}, u32[]{:S(2)}, u32[]{:S(2)}) collective-permute-start(bf16[5,8,16,128]{3,2,1,0:T(8,128)(2,1)S(1)} %fusion.1), channel_id=1, source_target_pairs={{32,1},{1,32},{33,2},{2,33},{34,3},{3,34},{35,4},{4,35},{36,5},{5,... | collective-permute-start | bytes 491528 | tf_op jit(solution)/shard_map/ppermute | solution.py:223
  43.3 0.0 collective-permute-done.8.refs_7_
  43.4 0.0 collective-permute-done.6.refs_5_
  43.4 2.9 %collective-permute-start.10 = (bf16[3,8,16,128]{3,2,1,0:T(8,128)(2,1)S(1)}, bf16[3,8,16,128]{3,2,1,0:T(8,128)(2,1)S(1)}, u32[]{:S(2)}, u32[]{:S(2)}) collective-permute-start(bf16[3,8,16,128]{3,2,1,0:T(8,128)(2,1)S(1)} %pad_maximum_fusion.3), channel_id=1, source_target_pairs={{32,1},{1,32},{33,2},{2,33},{34,3},{3,34},{35,4},{4,35},{36,5},{5,... | collective-permute-start | bytes 294920 | tf_op jit(solution)/shard_map/ppermute | solution.py:224
  46.4 0.1 pad_add_fusion.place
  46.4 0.0 collective-permute-done.9.near.refs_8_
  46.5 1.8 %shard_map.59 = (f32[64,8,128]{2,1,0:T(8,128)S(1)}, bf16[2,256,1024]{2,1,0:T(8,128)(2,1)S(1)}) custom-call(s32[2]{0:T(128)S(1)} %pad_add_fusion.place, bf16[5,8,16,128]{3,2,1,0:T(8,128)(2,1)S(1)} %collective-permute-done.1.refs_0_, bf16[5,8,16,128]{3,2,1,0:T(8,128)(2,1)S(1)} %collective-permute-done.3.refs_1_, ...), custom_call_target="tpu_custom_call" | custom-call | flops 900000000 | bytes 3000000 | tf_op jit(solution)/shard_map/pallas_call | solution.py:234
  48.2 1.1 %collective-permute-done.10.far.refs_9_ = bf16[3,8,16,128]{3,2,1,0:T(8,128)(2,1)S(1)} collective-permute-done((bf16[3,8,16,128]{3,2,1,0:T(8,128)(2,1)S(1)}, bf16[3,8,16,128]{3,2,1,0:T(8,128)(2,1)S(1)}, u32[]{:S(2)}, u32[]{:S(2)}) %collective-permute-start.10) | collective-permute-done | bytes 98336 | tf_op jit(solution)/shard_map/ppermute | solution.py:224
  49.4 1.7 %shard_map.60 = f32[64,8,128]{2,1,0:T(8,128)} custom-call(s32[2]{0:T(128)S(1)} %pad_add_fusion.place, bf16[5,8,16,128]{3,2,1,0:T(8,128)(2,1)S(1)} %collective-permute-done.9.near.refs_8_, bf16[3,8,16,128]{3,2,1,0:T(8,128)(2,1)S(1)} %collective-permute-done.10.far.refs_9_, bf16[2,256,1024]{2,1,0:T(8,128)(2,1)S(1)} %get-tuple-element.22.moved, ...), custom_call_target="tpu_custom_call" | custom-call | flops 400000000 | bytes 3000000 | tf_op jit(solution)/shard_map/pallas_call | solution.py:234
  51.0 13.6 %all-to-all-start = ((f32[64,8,128]{2,1,0:T(8,128)}), f32[64,8,128]{2,1,0:T(8,128)S(1)}, u32[]{:S(2)}, u32[]{:S(2)}) async-start(f32[64,8,128]{2,1,0:T(8,128)} %shard_map.60), calls=%async_computation | async-start | bytes 524288 | tf_op jit(solution)/shard_map/all_to_all | solution.py:263
  64.6 1.6 %shard_map.61 = f32[16,4,8,128]{3,2,1,0:T(8,128)S(1)} custom-call(s32[2]{0:T(128)S(1)} %pad_add_fusion.place, bf16[5,8,16,128]{3,2,1,0:T(8,128)(2,1)S(1)} %collective-permute-done.1.refs_0_, bf16[5,8,16,128]{3,2,1,0:T(8,128)(2,1)S(1)} %collective-permute-done.3.refs_1_, bf16[5,8,16,128]{3,2,1,0:T(8,128)(2,1)S(1)} %maximum_select_fusion.1.refs_2_, ...), custom_call_target="tpu_custom_call" | custom-call | flops 1100000000 | bytes 3000000 | tf_op jit(solution)/shard_map/pallas_call | solution.py:234
  66.2 0.0 copy-start.2
  66.2 3.3 %collective-permute-start.11 = (f32[8,4,8,128]{3,2,1,0:T(8,128)S(1)}, f32[8,4,8,128]{3,2,1,0:T(8,128)S(1)}, u32[]{:S(2)}, u32[]{:S(2)}) collective-permute-start(f32[8,4,8,128]{3,2,1,0:T(8,128)S(1)} %get-tuple-element.29), channel_id=1, source_target_pairs={{0,32},{32,0},{1,33},{33,1},{2,34},{34,2},{3,35},{35,3},{4,36},{36... | collective-permute-start | bytes 393224 | tf_op jit(solution)/shard_map/ppermute | solution.py:271
  69.6 0.0 copy-done.2
  69.6 7.6 %all-to-all-done.got = f32[64,8,128]{2,1,0:T(8,128)S(1)} async-done(((f32[64,8,128]{2,1,0:T(8,128)}), f32[64,8,128]{2,1,0:T(8,128)S(1)}, u32[]{:S(2)}, u32[]{:S(2)}) %all-to-all-start) | async-done | bytes 262176 | tf_op jit(solution)/shard_map/all_to_all | solution.py:263
  77.1 1.5 %shard_map.62 = f32[8,4,27]{2,1,0:T(4,128)} custom-call(s32[2]{0:T(128)S(1)} %pad_add_fusion.place, f32[64,8,128]{2,1,0:T(8,128)S(1)} %all-to-all-done.got), custom_call_target="tpu_custom_call" | custom-call | flops 100000000 | bytes 3000000 | tf_op jit(solution)/shard_map/pallas_call | solution.py:234
  78.7 0.0 collective-permute-done.11
  78.7 0.8 fusion
  (23 shorter events, 0.4 us)
Async XLA Ops:
  1.6 5.0 %copy-start.1 = (bf16[8,8,8,128]{3,2,1,0:T(8,128)(2,1)S(1)}, bf16[8,8,8,128]{3,2,1,0:T(8,128)(2,1)}, u32[]{:S(2)}) copy-start(bf16[8,8,8,128]{3,2,1,0:T(8,128)(2,1)} %param.5) | copy-start | bytes 393220
  1.7 7.8 %collective-permute-start = (bf16[5,8,8,128]{3,2,1,0:T(8,128)(2,1)S(1)}, bf16[5,8,8,128]{3,2,1,0:T(8,128)(2,1)S(1)}, u32[]{:S(2)}, u32[]{:S(2)}) collective-permute-start(bf16[5,8,8,128]{3,2,1,0:T(8,128)(2,1)S(1)} %bitcast.20), channel_id=1, source_target_pairs={{0,32},{32,0},{1,33},{33,1},{2,34},{34,2},{3,35},{35,3},{4,36},{36... | collective-permute-start | bytes 245768 | tf_op jit(solution)/shard_map/ppermute | solution.py:183
  6.7 0.8 %copy-start = (bf16[27,8,128]{2,1,0:T(8,128)(2,1)S(1)}, bf16[27,8,128]{2,1,0:T(8,128)(2,1)}, u32[]{:S(2)}) copy-start(bf16[27,8,128]{2,1,0:T(8,128)(2,1)} %param.6) | copy-start | bytes 165892
  7.5 9.9 %collective-permute-start.2 = (bf16[59,8,128]{2,1,0:T(8,128)(2,1)S(1)}, bf16[59,8,128]{2,1,0:T(8,128)(2,1)S(1)}, u32[]{:S(2)}, u32[]{:S(2)}) collective-permute-start(bf16[59,8,128]{2,1,0:T(8,128)(2,1)S(1)} %pad_maximum_fusion.1), channel_id=1, source_target_pairs={{0,32},{32,0},{1,33},{33,1},{2,34},{34,2},{3,35},{35,3},{4,36},{36... | collective-permute-start | bytes 362504 | tf_op jit(solution)/shard_map/ppermute | solution.py:197
  9.6 14.4 %collective-permute-start.1 = (bf16[5,8,16,128]{3,2,1,0:T(8,128)(2,1)S(1)}, bf16[5,8,16,128]{3,2,1,0:T(8,128)(2,1)S(1)}, u32[]{:S(2)}, u32[]{:S(2)}) collective-permute-start(bf16[5,8,16,128]{3,2,1,0:T(8,128)(2,1)S(1)} %maximum_select_fusion.1.refs_2_), channel_id=1, source_target_pairs={{0,128},{64,192},{128,256},{192,320},{256,384},{320,448},{384,0},{... | collective-permute-start | bytes 491528 | tf_op jit(solution)/shard_map/ppermute | solution.py:200
  13.8 13.5 %collective-permute-start.5 = (bf16[5,8,16,128]{3,2,1,0:T(8,128)(2,1)S(1)}, bf16[5,8,16,128]{3,2,1,0:T(8,128)(2,1)S(1)}, u32[]{:S(2)}, u32[]{:S(2)}) collective-permute-start(bf16[5,8,16,128]{3,2,1,0:T(8,128)(2,1)S(1)} %maximum_select_fusion.1.refs_2_), channel_id=1, source_target_pairs={{0,384},{64,448},{128,0},{192,64},{256,128},{320,192},{384,256},{4... | collective-permute-start | bytes 491528 | tf_op jit(solution)/shard_map/ppermute | solution.py:200
  17.5 19.2 %collective-permute-start.3 = (bf16[5,8,16,128]{3,2,1,0:T(8,128)(2,1)S(1)}, bf16[5,8,16,128]{3,2,1,0:T(8,128)(2,1)S(1)}, u32[]{:S(2)}, u32[]{:S(2)}) collective-permute-start(bf16[5,8,16,128]{3,2,1,0:T(8,128)(2,1)S(1)} %maximum_select_fusion.1.refs_2_), channel_id=1, source_target_pairs={{0,64},{64,128},{128,192},{192,256},{256,320},{320,384},{384,448},... | collective-permute-start | bytes 491528 | tf_op jit(solution)/shard_map/ppermute | solution.py:200
  20.3 16.4 %collective-permute-start.4 = (bf16[5,8,16,128]{3,2,1,0:T(8,128)(2,1)S(1)}, bf16[5,8,16,128]{3,2,1,0:T(8,128)(2,1)S(1)}, u32[]{:S(2)}, u32[]{:S(2)}) collective-permute-start(bf16[5,8,16,128]{3,2,1,0:T(8,128)(2,1)S(1)} %maximum_select_fusion.1.refs_2_), channel_id=1, source_target_pairs={{0,448},{64,0},{128,64},{192,128},{256,192},{320,256},{384,320},{4... | collective-permute-start | bytes 491528 | tf_op jit(solution)/shard_map/ppermute | solution.py:200
  27.3 9.4 %collective-permute-start.7 = (bf16[5,8,16,128]{3,2,1,0:T(8,128)(2,1)S(1)}, bf16[5,8,16,128]{3,2,1,0:T(8,128)(2,1)S(1)}, u32[]{:S(2)}, u32[]{:S(2)}) collective-permute-start(bf16[5,8,16,128]{3,2,1,0:T(8,128)(2,1)S(1)} %broadcast_select_fusion), channel_id=1, source_target_pairs={{0,384},{1,129},{64,448},{65,193},{128,0},{129,257},{192,64},{193,... | collective-permute-start | bytes 491528 | tf_op jit(solution)/shard_map/ppermute | solution.py:213
  31.3 12.1 %collective-permute-start.6 = (bf16[5,8,16,128]{3,2,1,0:T(8,128)(2,1)S(1)}, bf16[5,8,16,128]{3,2,1,0:T(8,128)(2,1)S(1)}, u32[]{:S(2)}, u32[]{:S(2)}) collective-permute-start(bf16[5,8,16,128]{3,2,1,0:T(8,128)(2,1)S(1)} %collective-permute-done.5.refs_4_), channel_id=1, source_target_pairs={{0,448},{64,0},{128,64},{192,128},{256,192},{320,256},{384,320},{4... | collective-permute-start | bytes 491528 | tf_op jit(solution)/shard_map/ppermute | solution.py:200
  33.2 10.1 %collective-permute-start.8 = (bf16[5,8,16,128]{3,2,1,0:T(8,128)(2,1)S(1)}, bf16[5,8,16,128]{3,2,1,0:T(8,128)(2,1)S(1)}, u32[]{:S(2)}, u32[]{:S(2)}) collective-permute-start(bf16[5,8,16,128]{3,2,1,0:T(8,128)(2,1)S(1)} %collective-permute-done.1.refs_0_), channel_id=1, source_target_pairs={{0,64},{64,128},{128,192},{192,256},{256,320},{320,384},{384,448},... | collective-permute-start | bytes 491528 | tf_op jit(solution)/shard_map/ppermute | solution.py:200
  36.8 9.7 %collective-permute-start.9 = (bf16[5,8,16,128]{3,2,1,0:T(8,128)(2,1)S(1)}, bf16[5,8,16,128]{3,2,1,0:T(8,128)(2,1)S(1)}, u32[]{:S(2)}, u32[]{:S(2)}) collective-permute-start(bf16[5,8,16,128]{3,2,1,0:T(8,128)(2,1)S(1)} %fusion.1), channel_id=1, source_target_pairs={{32,1},{1,32},{33,2},{2,33},{34,3},{3,34},{35,4},{4,35},{36,5},{5,... | collective-permute-start | bytes 491528 | tf_op jit(solution)/shard_map/ppermute | solution.py:223
  43.4 5.9 %collective-permute-start.10 = (bf16[3,8,16,128]{3,2,1,0:T(8,128)(2,1)S(1)}, bf16[3,8,16,128]{3,2,1,0:T(8,128)(2,1)S(1)}, u32[]{:S(2)}, u32[]{:S(2)}) collective-permute-start(bf16[3,8,16,128]{3,2,1,0:T(8,128)(2,1)S(1)} %pad_maximum_fusion.3), channel_id=1, source_target_pairs={{32,1},{1,32},{33,2},{2,33},{34,3},{3,34},{35,4},{4,35},{36,5},{5,... | collective-permute-start | bytes 294920 | tf_op jit(solution)/shard_map/ppermute | solution.py:224
  51.0 26.1 %all-to-all-start = ((f32[64,8,128]{2,1,0:T(8,128)}), f32[64,8,128]{2,1,0:T(8,128)S(1)}, u32[]{:S(2)}, u32[]{:S(2)}) async-start(f32[64,8,128]{2,1,0:T(8,128)} %shard_map.60), calls=%async_computation | async-start | bytes 524288 | tf_op jit(solution)/shard_map/all_to_all | solution.py:263
  66.2 3.3 %copy-start.2 = (bf16[8]{0:T(256)(128)(2,1)S(1)}, bf16[8]{0:T(256)(128)(2,1)}, u32[]{:S(2)}) copy-start(bf16[8]{0:T(256)(128)(2,1)} %param.7) | copy-start | bytes 52
  66.2 12.4 %collective-permute-start.11 = (f32[8,4,8,128]{3,2,1,0:T(8,128)S(1)}, f32[8,4,8,128]{3,2,1,0:T(8,128)S(1)}, u32[]{:S(2)}, u32[]{:S(2)}) collective-permute-start(f32[8,4,8,128]{3,2,1,0:T(8,128)S(1)} %get-tuple-element.29), channel_id=1, source_target_pairs={{0,32},{32,0},{1,33},{33,1},{2,34},{34,2},{3,35},{35,3},{4,36},{36... | collective-permute-start | bytes 393224 | tf_op jit(solution)/shard_map/ppermute | solution.py:271
